TPU v7x, 32 devices: a whole 2x2x4 slice. The times are simulated.
32 devices in a mesh: grp: 2 (over y), row: 2 (over x), col: 4 (over z), dep: 2 (over core).
Axes of the slice: x: 2, y: 2, z: 4, core: 2. Of those that a mesh axis runs over, the one named last changes fastest.
Arguments:
- left_blocks: bfloat16 [4, 4, 2, 64, 128, 128], P(('grp', 'row'), 'col', 'dep'), parts along dimension 0
- right_blocks: bfloat16 [4, 4, 2, 56, 128, 128], P(('grp', 'row'), 'col', 'dep'), parts along dimension 0
- triples: int32 [4, 4, 2, 7, 3, 64], P(('grp', 'row'), 'col', 'dep'), parts along dimension 0, may hold values from 0 to 224, as said below
Outputs:
- squared: bfloat16 [4, 4, 2, 112, 128, 128], P(('grp', 'row'), 'col', 'dep'), parts along dimension 0
There are 2 independent parts, one for each index of `grp`. A program takes and returns all parts, laid end to end along the dimension named above; each array names one. Nothing has to cross between parts.
Inputs may be any that keep to these rules, and one draw needn't show every extreme that they name: `triples`: index 0 names a slot of the left panel, index 1 a slot of the right panels laid end to end, index 2 a slot of the cell's result blocks over all layers, or 224 for an unused entry (then indices 0 and 1 are 0). The lists are exactly the products X(i, k) X(k, j) of one matrix X with 7 blocks in every block row, each counted once over all layers and steps; left and right slots that name the same block hold equal values.
All inputs are finite; a program needn't handle non-finite values.
Results may differ from a plain program's by a relative error of at most 0.001.
Values may be sent and summed in bfloat16 or wider, within the bound.
No kernel may reach another device: no remote copies, remote signals or barrier semaphores. Data moves between devices by JAX's collectives and lax.ppermute only.
A program may use at most 128 MiB of HBM per device.

v0:
```python
import jax
import jax.numpy as jnp
from jax import lax
from jax.sharding import PartitionSpec as P

NBQ = 32


def passed_along(value, axis, steps):
    count = lax.axis_size(axis)
    pairs = [(source, (source + steps) % count) for source in range(count)]
    return lax.ppermute(value, axis, pairs)


def add_products(accumulated, left_panel, gathered, step_list):
    left_rows = jnp.take(left_panel, step_list[0], axis=0)
    right_rows = jnp.take(gathered, step_list[1], axis=0)
    products = jnp.einsum("tij,tjk->tik", left_rows, right_rows, preferred_element_type=jnp.float32)
    return accumulated.at[step_list[2]].add(products)


def local(left_blocks, right_blocks, triples):
    left_panel = left_blocks[0, 0, 0]
    right_own = right_blocks[0, 0, 0]
    step_lists = triples[0, 0, 0]
    step_count = step_lists.shape[0]
    centre = step_count // 2
    block_width = left_panel.shape[1]
    row_count = lax.axis_size("row")
    row_hits = (2 * step_count - 2 + row_count) // row_count
    out_count = row_hits * NBQ
    gathered = lax.all_gather(right_own, "row", axis=0, tiled=True)
    accumulated = jnp.zeros((out_count + 1, block_width, block_width), jnp.float32)
    accumulated = add_products(accumulated, left_panel, gathered, step_lists[centre])
    upward = left_panel
    downward = left_panel
    for distance in range(1, centre + 1):
        upward = passed_along(upward, "col", -1)
        accumulated = add_products(accumulated, upward, gathered, step_lists[centre + distance])
        downward = passed_along(downward, "col", 1)
        accumulated = add_products(accumulated, downward, gathered, step_lists[centre - distance])
    reduced = lax.psum_scatter(accumulated[:out_count], "dep", scatter_dimension=0, tiled=True)
    return reduced.astype(jnp.bfloat16)[None, None, None]


def solution(mesh):
    return jax.shard_map(
        local,
        mesh=mesh,
        in_specs=(
            P(("grp", "row"), "col", "dep", None, None, None),
            P(("grp", "row"), "col", "dep", None, None, None),
            P(("grp", "row"), "col", "dep", None, None, None),
        ),
        out_specs=P(("grp", "row"), "col", "dep", None, None, None),
        check_vma=False,
    )
```

profile of v0, /device:TPU:1, one launch (start us, length us, event | category | flops | bytes accessed | tf_op | source)
XLA Modules:
  0.0 371.4 jit_solution(16201991396776120407)
XLA Ops:
  10.8 44.6 %collective-permute-done = bf16[64,128,128]{2,1,0:T(8,128)(2,1)} collective-permute-done((bf16[64,128,128]{2,1,0:T(8,128)(2,1)}, bf16[64,128,128]{2,1,0:T(8,128)(2,1)}, u32[]{:S(2)}, u32[]{:S(2)}) %collective-permute-start) | collective-permute-done | bytes 2097184 | tf_op jit(solution)/shard_map/ppermute | solution.py:12
  59.4 41.8 %collective-permute-done.1 = bf16[64,128,128]{2,1,0:T(8,128)(2,1)} collective-permute-done((bf16[64,128,128]{2,1,0:T(8,128)(2,1)}, bf16[64,128,128]{2,1,0:T(8,128)(2,1)}, u32[]{:S(2)}, u32[]{:S(2)}) %collective-permute-start.1) | collective-permute-done | bytes 2097184 | tf_op jit(solution)/shard_map/ppermute | solution.py:12
  123.8 4.2 %gather_fusion.5 = bf16[64,128,128]{2,1,0:T(8,128)(2,1)} fusion(bf16[112,128,128]{2,1,0:T(8,128)(2,1)} %bitcast.77, s32[1024]{0:T(1024)S(1)} %get-tuple-element.76), kind=kCustom, calls=%fused_computation.9.clone | custom fusion | bytes 4194560 | tf_op jit(solution)/shard_map/jit(_take)/gather | solution.py:17
  136.3 4.2 %gather_fusion.11 = bf16[64,128,128]{2,1,0:T(8,128)(2,1)} fusion(bf16[112,128,128]{2,1,0:T(8,128)(2,1)} %bitcast.80, s32[1024]{0:T(1024)S(1)} %get-tuple-element.70), kind=kCustom, calls=%fused_computation.12.clone | custom fusion | bytes 4194560 | tf_op jit(solution)/shard_map/jit(_take)/gather | solution.py:17
  143.5 4.4 %collective-permute-done.2 = bf16[64,128,128]{2,1,0:T(8,128)(2,1)} collective-permute-done((bf16[64,128,128]{2,1,0:T(8,128)(2,1)}, bf16[64,128,128]{2,1,0:T(8,128)(2,1)}, u32[]{:S(2)}, u32[]{:S(2)}) %collective-permute-start.2) | collective-permute-done | bytes 2097184 | tf_op jit(solution)/shard_map/ppermute | solution.py:12
  149.3 5.0 %fusion.18 = f32[64,128,128]{2,1,0:T(8,128)} fusion(bf16[64,128,128]{2,1,0:T(8,128)(2,1)} %gather_fusion.1, bf16[64,128,128]{2,1,0:T(8,128)(2,1)} %gather_fusion, pred[64]{0:T(512)(128)(4,1)S(1)} %get-tuple-element.55, pred[64]{0:T(512)(128)(4,1)S(1)} %get-tuple-element.57), kind=kOutput, calls=%fused_computation.40 | convolution fusion | flops 270532608 | bytes 8388736 | tf_op jit(solution)/shard_map/tij,tjk->tik/dot_general | solution.py:18
  154.3 7.1 %broadcast_in_dim.31 = f32[225,128,128]{2,1,0:T(8,128)} broadcast(f32[]{:T(128)} %constant.19.clone.1), dimensions={} | broadcast | bytes 14745604 | tf_op jit(solution)/shard_map/broadcast_in_dim | solution.py:33
  161.4 14.0 %scatter_fusion = f32[225,128,128]{2,1,0:T(8,128)} fusion(f32[225,128,128]{2,1,0:T(8,128)} %broadcast_in_dim.31, s32[64]{0:T(128)S(1)} %get-tuple-element.67, f32[64,128,128]{2,1,0:T(8,128)} %fusion.18), kind=kCustom, calls=%fused_computation.14 | custom fusion | flops 1048576 | bytes 12583168 | tf_op jit(solution)/shard_map/scatter-add | solution.py:19
  175.4 15.8 %collective-permute-done.3 = bf16[64,128,128]{2,1,0:T(8,128)(2,1)} collective-permute-done((bf16[64,128,128]{2,1,0:T(8,128)(2,1)}, bf16[64,128,128]{2,1,0:T(8,128)(2,1)}, u32[]{:S(2)}, u32[]{:S(2)}) %collective-permute-start.3) | collective-permute-done | bytes 2097184 | tf_op jit(solution)/shard_map/ppermute | solution.py:12
  192.5 5.0 %fusion.15 = f32[64,128,128]{2,1,0:T(8,128)} fusion(bf16[64,128,128]{2,1,0:T(8,128)(2,1)} %gather_fusion.3, bf16[64,128,128]{2,1,0:T(8,128)(2,1)} %gather_fusion.2, pred[64]{0:T(512)(128)(4,1)S(1)} %get-tuple-element.51, pred[64]{0:T(512)(128)(4,1)S(1)} %get-tuple-element.53), kind=kOutput, calls=%fused_computation.37 | convolution fusion | flops 270532608 | bytes 8388736 | tf_op jit(solution)/shard_map/tij,tjk->tik/dot_general | solution.py:18
  197.4 13.7 %scatter_fusion.1 = f32[225,128,128]{2,1,0:T(8,128)} fusion(f32[225,128,128]{2,1,0:T(8,128)} %scatter_fusion, s32[64]{0:T(128)S(1)} %get-tuple-element.66, f32[64,128,128]{2,1,0:T(8,128)} %fusion.15), kind=kCustom, calls=%fused_computation.15 | custom fusion | flops 1048576 | bytes 12583168 | tf_op jit(solution)/shard_map/scatter-add | solution.py:19
  211.1 5.0 %fusion.12 = f32[64,128,128]{2,1,0:T(8,128)} fusion(bf16[64,128,128]{2,1,0:T(8,128)(2,1)} %gather_fusion.5, bf16[64,128,128]{2,1,0:T(8,128)(2,1)} %gather_fusion.4, pred[64]{0:T(512)(128)(4,1)S(1)} %get-tuple-element.47, pred[64]{0:T(512)(128)(4,1)S(1)} %get-tuple-element.49), kind=kOutput, calls=%fused_computation.34 | convolution fusion | flops 270532608 | bytes 8388736 | tf_op jit(solution)/shard_map/tij,tjk->tik/dot_general | solution.py:18
  216.1 13.6 %scatter_fusion.2 = f32[225,128,128]{2,1,0:T(8,128)} fusion(f32[225,128,128]{2,1,0:T(8,128)} %scatter_fusion.1, s32[64]{0:T(128)S(1)} %get-tuple-element.65, f32[64,128,128]{2,1,0:T(8,128)} %fusion.12), kind=kCustom, calls=%fused_computation.16 | custom fusion | flops 1048576 | bytes 12583168 | tf_op jit(solution)/shard_map/scatter-add | solution.py:19
  233.5 5.0 %fusion.9 = f32[64,128,128]{2,1,0:T(8,128)} fusion(bf16[64,128,128]{2,1,0:T(8,128)(2,1)} %gather_fusion.7, bf16[64,128,128]{2,1,0:T(8,128)(2,1)} %gather_fusion.6, pred[64]{0:T(512)(128)(4,1)S(1)} %get-tuple-element.43, pred[64]{0:T(512)(128)(4,1)S(1)} %get-tuple-element.45), kind=kOutput, calls=%fused_computation.31 | convolution fusion | flops 270532608 | bytes 8388736 | tf_op jit(solution)/shard_map/tij,tjk->tik/dot_general | solution.py:18
  238.4 13.9 %scatter_fusion.3 = f32[225,128,128]{2,1,0:T(8,128)} fusion(f32[225,128,128]{2,1,0:T(8,128)} %scatter_fusion.2, s32[64]{0:T(128)S(1)} %get-tuple-element.64, f32[64,128,128]{2,1,0:T(8,128)} %fusion.9), kind=kCustom, calls=%fused_computation.17 | custom fusion | flops 1048576 | bytes 12583168 | tf_op jit(solution)/shard_map/scatter-add | solution.py:19
  256.0 5.0 %fusion.6 = f32[64,128,128]{2,1,0:T(8,128)} fusion(bf16[64,128,128]{2,1,0:T(8,128)(2,1)} %gather_fusion.9, bf16[64,128,128]{2,1,0:T(8,128)(2,1)} %gather_fusion.8, pred[64]{0:T(512)(128)(4,1)S(1)} %get-tuple-element.39, pred[64]{0:T(512)(128)(4,1)S(1)} %get-tuple-element.41), kind=kOutput, calls=%fused_computation.28 | convolution fusion | flops 270532608 | bytes 8388736 | tf_op jit(solution)/shard_map/tij,tjk->tik/dot_general | solution.py:18
  261.0 13.9 %scatter_fusion.4 = f32[225,128,128]{2,1,0:T(8,128)} fusion(f32[225,128,128]{2,1,0:T(8,128)} %scatter_fusion.3, s32[64]{0:T(128)S(1)} %get-tuple-element.63, f32[64,128,128]{2,1,0:T(8,128)} %fusion.6), kind=kCustom, calls=%fused_computation.18 | custom fusion | flops 1048576 | bytes 12583168 | tf_op jit(solution)/shard_map/scatter-add | solution.py:19
  278.7 5.0 %fusion.3 = f32[64,128,128]{2,1,0:T(8,128)} fusion(bf16[64,128,128]{2,1,0:T(8,128)(2,1)} %gather_fusion.11, bf16[64,128,128]{2,1,0:T(8,128)(2,1)} %gather_fusion.10, pred[64]{0:T(512)(128)(4,1)S(1)} %get-tuple-element.35, pred[64]{0:T(512)(128)(4,1)S(1)} %get-tuple-element.37), kind=kOutput, calls=%fused_computation.25 | convolution fusion | flops 270532608 | bytes 8388736 | tf_op jit(solution)/shard_map/tij,tjk->tik/dot_general | solution.py:18
  283.7 13.7 %scatter_fusion.5 = f32[225,128,128]{2,1,0:T(8,128)} fusion(f32[225,128,128]{2,1,0:T(8,128)} %scatter_fusion.4, s32[64]{0:T(128)S(1)} %get-tuple-element.62, f32[64,128,128]{2,1,0:T(8,128)} %fusion.3), kind=kCustom, calls=%fused_computation.19 | custom fusion | flops 1048576 | bytes 12583168 | tf_op jit(solution)/shard_map/scatter-add | solution.py:19
  301.1 4.3 %fusion = f32[64,128,128]{2,1,0:T(8,128)} fusion(bf16[64,128,128]{2,1,0:T(8,128)(2,1)S(1)} %gather_fusion.13, bf16[64,128,128]{2,1,0:T(8,128)(2,1)} %gather_fusion.12, pred[64]{0:T(512)(128)(4,1)S(1)} %get-tuple-element.59, pred[64]{0:T(512)(128)(4,1)S(1)} %get-tuple-element.6), kind=kOutput, calls=%fused_computation.22 | convolution fusion | flops 270532608 | bytes 8388736 | tf_op jit(solution)/shard_map/tij,tjk->tik/dot_general | solution.py:18
  305.4 13.7 %scatter_fusion.6 = f32[225,128,128]{2,1,0:T(8,128)} fusion(f32[225,128,128]{2,1,0:T(8,128)} %scatter_fusion.5, s32[64]{0:T(128)S(1)} %get-tuple-element.61, f32[64,128,128]{2,1,0:T(8,128)} %fusion), kind=kCustom, calls=%fused_computation.20 | custom fusion | flops 1048576 | bytes 12583168 | tf_op jit(solution)/shard_map/scatter-add | solution.py:19
  319.1 13.1 %slice.172 = f32[224,128,128]{2,1,0:T(8,128)} slice(f32[225,128,128]{2,1,0:T(8,128)} %scatter_fusion.6), slice={[0:224], [0:128], [0:128]} | slice | bytes 29360128 | tf_op jit(solution)/shard_map/slice | solution.py:42
  332.2 26.6 %reduce-scatter.2.cloned.1.call-done = f32[112,128,128]{2,1,0:T(8,128)} async-done(((f32[224,128,128]{2,1,0:T(8,128)}), f32[112,128,128]{2,1,0:T(8,128)}) %reduce-scatter.2.cloned.1.call-update) | async-done | bytes 7340048 | tf_op jit(solution)/shard_map/reduce_scatter | solution.py:42
  358.8 5.8 %convert_bitcast_fusion = bf16[1,1,1,112,128,128]{5,4,3,2,1,0:T(8,128)(2,1)} fusion(f32[112,128,128]{2,1,0:T(8,128)} %reduce-scatter.2.cloned.1.call-done), kind=kLoop, calls=%fused_computation.21 | loop fusion | flops 1835008 | bytes 11010048 | tf_op jit(solution)/shard_map/broadcast_in_dim | solution.py:43
  (34 shorter events, 59.8 us)
Async XLA Ops:
  6.5 108.9 %all-gather.3.cloned.1.call-start = ((), (), s32[]{:S(2)}) async-start(), calls=%async_computation.2 | async-start | bytes 5505024 | tf_op jit(solution)/shard_map/all_gather | solution.py:32
  6.5 48.9 %collective-permute-start = (bf16[64,128,128]{2,1,0:T(8,128)(2,1)}, bf16[64,128,128]{2,1,0:T(8,128)(2,1)}, u32[]{:S(2)}, u32[]{:S(2)}) collective-permute-start(bf16[64,128,128]{2,1,0:T(8,128)(2,1)} %bitcast.82), channel_id=1, source_target_pairs={{0,6},{2,0},{4,2},{6,4},{1,7},{3,1},{5,3},{7,5},{8,14},{10,8},{12,... | collective-permute-start | bytes 6291464 | tf_op jit(solution)/shard_map/ppermute | solution.py:12
  10.7 90.5 %collective-permute-start.1 = (bf16[64,128,128]{2,1,0:T(8,128)(2,1)}, bf16[64,128,128]{2,1,0:T(8,128)(2,1)}, u32[]{:S(2)}, u32[]{:S(2)}) collective-permute-start(bf16[64,128,128]{2,1,0:T(8,128)(2,1)} %bitcast.83), channel_id=1, source_target_pairs={{0,2},{2,4},{4,6},{6,0},{1,3},{3,5},{5,7},{7,1},{8,10},{10,12},{12... | collective-permute-start | bytes 6291464 | tf_op jit(solution)/shard_map/ppermute | solution.py:12
  10.7 348.0 %reduce-scatter.2.cloned.1.call-start = ((), (), s32[]{:S(2)}) async-start(), calls=%async_computation.1 | async-start | bytes 22020096 | tf_op jit(solution)/shard_map/reduce_scatter | solution.py:42
  55.4 92.5 %collective-permute-start.2 = (bf16[64,128,128]{2,1,0:T(8,128)(2,1)}, bf16[64,128,128]{2,1,0:T(8,128)(2,1)}, u32[]{:S(2)}, u32[]{:S(2)}) collective-permute-start(bf16[64,128,128]{2,1,0:T(8,128)(2,1)} %collective-permute-done), channel_id=1, source_target_pairs={{0,6},{2,0},{4,2},{6,4},{1,7},{3,1},{5,3},{7,5},{8,14},{10,8},{12,... | collective-permute-start | bytes 6291464 | tf_op jit(solution)/shard_map/ppermute | solution.py:12
  101.2 89.9 %collective-permute-start.3 = (bf16[64,128,128]{2,1,0:T(8,128)(2,1)}, bf16[64,128,128]{2,1,0:T(8,128)(2,1)}, u32[]{:S(2)}, u32[]{:S(2)}) collective-permute-start(bf16[64,128,128]{2,1,0:T(8,128)(2,1)} %collective-permute-done.1), channel_id=1, source_target_pairs={{0,2},{2,4},{4,6},{6,0},{1,3},{3,5},{5,7},{7,1},{8,10},{10,12},{12... | collective-permute-start | bytes 6291464 | tf_op jit(solution)/shard_map/ppermute | solution.py:12
  147.9 127.1 %collective-permute-start.4 = (bf16[64,128,128]{2,1,0:T(8,128)(2,1)}, bf16[64,128,128]{2,1,0:T(8,128)(2,1)}, u32[]{:S(2)}, u32[]{:S(2)}) collective-permute-start(bf16[64,128,128]{2,1,0:T(8,128)(2,1)} %collective-permute-done.2), channel_id=1, source_target_pairs={{0,6},{2,0},{4,2},{6,4},{1,7},{3,1},{5,3},{7,5},{8,14},{10,8},{12,... | collective-permute-start | bytes 6291464 | tf_op jit(solution)/shard_map/ppermute | solution.py:12
  191.1 106.2 %collective-permute-start.5 = (bf16[64,128,128]{2,1,0:T(8,128)(2,1)}, bf16[64,128,128]{2,1,0:T(8,128)(2,1)}, u32[]{:S(2)}, u32[]{:S(2)}) collective-permute-start(bf16[64,128,128]{2,1,0:T(8,128)(2,1)} %collective-permute-done.3), channel_id=1, source_target_pairs={{0,2},{2,4},{4,6},{6,0},{1,3},{3,5},{5,7},{7,1},{8,10},{10,12},{12... | collective-permute-start | bytes 6291464 | tf_op jit(solution)/shard_map/ppermute | solution.py:12
Sparse Core Ops, SparseCore 0:
  10.8 52.5 all-gather.2
  332.3 26.4 reduce-scatter.1
where the time goes:
time: 373 us; the launch traced here: 371 us
  waiting for transfers between devices  133 us (36%)
  other arithmetic  104 us (28%)
  local copies, waits for them, and re-layouts  74.3 us (20%)
  matrix products  34.2 us (9%)
  between operations  13.5 us (4%)
  starting transfers between devices  12.3 us (3%)
    ppermute x6, waiting for transfers between devices, passed_along(): return lax.ppermute(value, axis, pairs)  107 us
    scatter-add x7, other arithmetic, add_products(): return accumulated.at[step_list[2]].add(products)  96.5 us
    dot_general x7, matrix products, add_products(): jnp.einsum('tij,tjk->tik', left_rows, right_rows, preferred_element_type=...  34.2 us
    gather x7, local copies, waits for them, and re-layouts, add_products(): right_rows = jnp.take(gathered, step_list[1], axis=0)  28.1 us
    reduce_scatter x1, waiting for transfers between devices, local(): lax.psum_scatter(accumulated[:out_count], 'dep', scatter_dimension=0, til...  26.6 us
    gather x7, local copies, waits for them, and re-layouts, add_products(): left_rows = jnp.take(left_panel, step_list[0], axis=0)  26.1 us
    slice x1, local copies, waits for them, and re-layouts, local(): accumulated[:out_count]  13.1 us
    ppermute x6, starting transfers between devices, passed_along(): return lax.ppermute(value, axis, pairs)  12.3 us
  transfers between devices with their start and end apart: 8, of which 5 were waited for; matrix products, arithmetic and copies ran while one was open for 46% of the time, Pallas kernels for 0%

commit v1 on v0

v1 whole, which is shorter than its diff:
```python
import functools

import jax
import jax.numpy as jnp
from jax import lax
from jax.experimental import pallas as pl
from jax.experimental.pallas import tpu as pltpu
from jax.sharding import PartitionSpec as P

NBQ = 32
UNROLL = 4


def stage_kernel(panels, first, last, *refs):
    lists, todo = refs[0], refs[-1]
    lefts = refs[1 : 1 + 2 * panels]
    rights = refs[1 + 2 * panels : 3 + 2 * panels]
    work = refs[-2]
    half = work.shape[0] - 1
    if first:
        work[...] = jnp.zeros_like(work)
    else:
        work[...] = refs[3 + 2 * panels][...]
    for panel in range(panels):
        for layer in range(2):
            row = 2 * panel + layer
            left, right = lefts[row], rights[layer]

            def keep(index, count):
                entry = lists[row, index]
                todo[count] = entry
                return count + (entry >= 0).astype(jnp.int32)

            count = lax.fori_loop(0, lists.shape[1], keep, jnp.int32(0))
            for extra in range(UNROLL - 1):
                todo[count + extra] = jnp.int32(half << 20)

            def several(group, carry):
                for lane in range(UNROLL):
                    entry = todo[group * UNROLL + lane]
                    product = jnp.dot(
                        left[entry & 1023], right[(entry >> 10) & 1023], preferred_element_type=jnp.float32
                    )
                    work[entry >> 20] += product
                return carry

            lax.fori_loop(0, (count + UNROLL - 1) // UNROLL, several, jnp.int32(0))
    if last:
        out = refs[-3]
        out[...] = work[:half].astype(out.dtype)


def stage(lists, lefts, rights, given, half, last):
    width = rights[0].shape[1]
    first = given is None
    operands = [lists, *lefts, *rights] + ([] if first else [given])
    vmem = pl.BlockSpec(memory_space=pltpu.VMEM)
    if last:
        out_shape = jax.ShapeDtypeStruct((half, width, width), jnp.bfloat16)
        scratch = [pltpu.VMEM((half + 1, width, width), jnp.float32)]
    else:
        out_shape = jax.ShapeDtypeStruct((half + 1, width, width), jnp.float32)
        scratch = []
    return pl.pallas_call(
        functools.partial(stage_kernel, len(lefts) // 2, first, last),
        out_shape=out_shape,
        in_specs=[pl.BlockSpec(memory_space=pltpu.SMEM)] + [vmem] * (len(operands) - 1),
        out_specs=vmem,
        scratch_shapes=scratch + [pltpu.SMEM((lists.shape[1] + UNROLL,), jnp.int32)],
        compiler_params=pltpu.CompilerParams(vmem_limit_bytes=56 << 20),
        cost_estimate=pl.CostEstimate(
            flops=lists.size * width**3, bytes_accessed=32 << 20, transcendentals=0
        ),
    )(*operands)


def local(left_blocks, right_blocks, triples):
    own = left_blocks[0, 0, 0]
    right_own = right_blocks[0, 0, 0]
    step_lists = triples[0, 0, 0]
    slots = own.shape[0]
    step_count = step_lists.shape[0]
    centre = step_count // 2
    columns = lax.axis_size("col")
    place = lax.axis_index("col")
    layer = lax.axis_index("dep")
    cyclic = columns >= step_count
    reach = centre if cyclic else columns - 1

    swap = [(0, 1), (1, 0)]
    row_count = lax.axis_size("row")
    half = (2 * step_count - 2 + row_count) // row_count * NBQ // 2
    other_lists = lax.ppermute(step_lists, "dep", swap)
    both = jnp.stack([step_lists, other_lists])
    result = both[:, :, 2] - layer * half
    wanted = (result >= 0) & (result < half)
    packed = jnp.where(wanted, both[:, :, 0] | (both[:, :, 1] << 10) | (result << 20), -1)

    right_here = lax.all_gather(right_own, "row", axis=0, tiled=True)
    right_there = lax.ppermute(right_here, "dep", swap)
    rights = [right_here, right_there]

    steps_of = [[s for s in range(step_count) if (s - centre - q) % columns == 0] for q in range(columns)]
    most = max(len(steps) for steps in steps_of)
    nothing = jnp.full((2, slots), -1, jnp.int32)

    def lists_of(offset):
        steps = steps_of[offset % columns]
        rows = [packed[:, s] for s in steps] + [nothing] * (most - len(steps))
        return jnp.concatenate(rows, axis=1)

    def doubled(panel):
        return [panel, lax.ppermute(panel, "dep", swap)]

    def forward(panel, round_index):
        if cyclic:
            return lax.ppermute(panel, "col", [(i, (i + 1) % columns) for i in range(columns)])
        return lax.ppermute(panel, "col", [(i, i + 1) for i in range(round_index - 1, columns - 1)])

    def backward(panel, round_index):
        if cyclic:
            return lax.ppermute(panel, "col", [(i, (i - 1) % columns) for i in range(columns)])
        return lax.ppermute(panel, "col", [(i + 1, i) for i in range(columns - round_index)])

    rising, falling = own, own
    total = None
    lefts, lists = doubled(own), [lists_of(0)]
    for distance in range(1, reach + 1):
        rising = forward(rising, distance)
        falling = backward(falling, distance)
        from_left, from_right = lists_of(-distance), lists_of(distance)
        if not cyclic:
            from_left = jnp.where(place >= distance, from_left, -1)
            from_right = jnp.where(place + distance < columns, from_right, -1)
        if not cyclic and 2 * distance >= columns:
            lefts += doubled(jnp.where(place >= distance, rising, falling))
            lists += [jnp.where(place >= distance, from_left, from_right)]
        else:
            lefts += doubled(rising) + doubled(falling)
            lists += [from_left, from_right]
        last = distance == reach
        total = stage(jnp.concatenate(lists), lefts, rights, total, half, last)
        lefts, lists = [], []
    return total[None, None, None]


def solution(mesh):
    return jax.shard_map(
        local,
        mesh=mesh,
        in_specs=(
            P(("grp", "row"), "col", "dep", None, None, None),
            P(("grp", "row"), "col", "dep", None, None, None),
            P(("grp", "row"), "col", "dep", None, None, None),
        ),
        out_specs=P(("grp", "row"), "col", "dep", None, None, None),
        check_vma=False,
    )
```

time: 373 us -> 231 us (0.62)
  other arithmetic: 104 us -> 6.26 us
  local copies, waits for them, and re-layouts: 74.3 us -> 0.74 us
  Pallas kernels: 0 us -> 57.7 us
  matrix products: 34.2 us -> 0 us
  starting transfers between devices: 12.3 us -> 20.8 us
  waiting for transfers between devices: 133 us -> 128 us
    scatter-add x7 -> x0, other arithmetic: 96.5 us -> none  [add_products(): return accumulated.at[step_list[2]].add(products)]
    pallas_call x0 -> x3, Pallas kernels: none -> 57.7 us  [stage(): pl.pallas_call(functools.partial(stage_kernel, len(lefts) // 2, first, la...]
    gather x14 -> x0, local copies, waits for them, and re-layouts: 54.2 us -> none  [the longest x7 28.1 us: add_products(): right_rows = jnp.take(gathered, step_list[1], axis=0)]
    dot_general x7 -> x0, matrix products: 34.2 us -> none  [add_products(): jnp.einsum('tij,tjk->tik', left_rows, right_rows, preferred_element_type=...]
    reduce_scatter x1 -> x0, waiting for transfers between devices: 26.6 us -> none  [local(): lax.psum_scatter(accumulated[:out_count], 'dep', scatter_dimension=0, til...]
    ppermute x6 -> x13, waiting for transfers between devices: 107 us -> 128 us  [the longest x3 85.6 us: backward(): lax.ppermute(panel, 'col', [(i + 1, i) for i in range(columns - round_ind...]
    slice x1 -> x0, local copies, waits for them, and re-layouts: 13.1 us -> none  [local(): accumulated[:out_count]]
    ppermute x6 -> x13, starting transfers between devices: 12.3 us -> 20.8 us  [the longest x3 9.47 us: forward(): lax.ppermute(panel, 'col', [(i, i + 1) for i in range(round_index - 1, co...]
  transfers between devices with their start and end apart: 8 -> 14, of which waited for: 5 -> 5; matrix products, arithmetic and copies ran while one was open for 46% -> 3% of each run, Pallas kernels for 0% -> 17%
where the time goes in v1:
time: 231 us; the launch traced here: 227 us
  waiting for transfers between devices  128 us (55%)
  Pallas kernels  57.7 us (25%)
  starting transfers between devices  20.8 us (9%)
  between operations  13.5 us (6%)
  other arithmetic  6.26 us (3%)
    ppermute x3, waiting for transfers between devices, backward(): lax.ppermute(panel, 'col', [(i + 1, i) for i in range(columns - round_ind...  85.6 us
    pallas_call x3, Pallas kernels, stage(): pl.pallas_call(functools.partial(stage_kernel, len(lefts) // 2, first, la...  57.7 us
    ppermute x3, waiting for transfers between devices, forward(): lax.ppermute(panel, 'col', [(i, i + 1) for i in range(round_index - 1, co...  41.9 us
    ppermute x3, starting transfers between devices, forward(): lax.ppermute(panel, 'col', [(i, i + 1) for i in range(round_index - 1, co...  9.47 us
    ppermute x5, starting transfers between devices, doubled(): return [panel, lax.ppermute(panel, 'dep', swap)]  6.93 us
    select_n x2, other arithmetic, local(): lefts += doubled(jnp.where(place >= distance, rising, falling))  4.94 us
  transfers between devices with their start and end apart: 14, of which 5 were waited for; matrix products, arithmetic and copies ran while one was open for 3% of the time, Pallas kernels for 17%

profile of v1, /device:TPU:1, one launch (start us, length us, event | category | flops | bytes accessed | tf_op | source)
XLA Modules:
  0.0 227.3 jit_solution(123323776732644731)
XLA Ops:
  6.5 5.4 %collective-permute-start.1 = (bf16[64,128,128]{2,1,0:T(8,128)(2,1)}, bf16[64,128,128]{2,1,0:T(8,128)(2,1)}, u32[]{:S(2)}, u32[]{:S(2)}) collective-permute-start(bf16[64,128,128]{2,1,0:T(8,128)(2,1)} %bitcast.29), channel_id=1, source_target_pairs={{0,2},{2,4},{4,6},{1,3},{3,5},{5,7},{8,10},{10,12},{12,14},{9,11},... | collective-permute-start | bytes 6291464 | tf_op jit(solution)/shard_map/ppermute | solution.py:118
  12.0 1.3 collective-permute-start.4
  13.3 41.9 %collective-permute-done.1.refs_3_ = bf16[64,128,128]{2,1,0:T(8,128)(2,1)} collective-permute-done((bf16[64,128,128]{2,1,0:T(8,128)(2,1)}, bf16[64,128,128]{2,1,0:T(8,128)(2,1)}, u32[]{:S(2)}, u32[]{:S(2)}) %collective-permute-start.1) | collective-permute-done | bytes 2097184 | tf_op jit(solution)/shard_map/ppermute | solution.py:118
  55.2 2.0 collective-permute-start.2
  57.1 3.2 %collective-permute-done.4.refs_5_ = bf16[64,128,128]{2,1,0:T(8,128)(2,1)} collective-permute-done((bf16[64,128,128]{2,1,0:T(8,128)(2,1)}, bf16[64,128,128]{2,1,0:T(8,128)(2,1)}, u32[]{:S(2)}, u32[]{:S(2)}) %collective-permute-start.4) | collective-permute-done | bytes 2097184 | tf_op jit(solution)/shard_map/ppermute | solution.py:123
  60.3 1.3 collective-permute-start.5
  61.6 2.1 collective-permute-start.3
  63.7 44.2 %collective-permute-done.5 = bf16[64,128,128]{2,1,0:T(8,128)(2,1)} collective-permute-done((bf16[64,128,128]{2,1,0:T(8,128)(2,1)}, bf16[64,128,128]{2,1,0:T(8,128)(2,1)}, u32[]{:S(2)}, u32[]{:S(2)}) %collective-permute-start.5) | collective-permute-done | bytes 2097184 | tf_op jit(solution)/shard_map/ppermute | solution.py:123
  107.9 1.3 collective-permute-start.6
  109.2 2.8 %collective-permute-start.10 = (bf16[64,128,128]{2,1,0:T(8,128)(2,1)}, bf16[64,128,128]{2,1,0:T(8,128)(2,1)}, u32[]{:S(2)}, u32[]{:S(2)}) collective-permute-start(bf16[64,128,128]{2,1,0:T(8,128)(2,1)} %bitcast.31), channel_id=1, source_target_pairs={{0,1},{1,0},{2,3},{3,2},{4,5},{5,4},{6,7},{7,6},{8,9},{9,8},{10,11... | collective-permute-start | bytes 6291464 | tf_op jit(solution)/shard_map/ppermute | solution.py:113
  112.1 0.7 copy.12
  112.8 0.4 collective-permute-start
  113.2 1.8 broadcast_select_fusion.refs_1_
  115.1 0.8 collective-permute-done
  115.8 0.4 collective-permute-start.11
  116.2 0.1 collective-permute-start.12
  116.3 38.2 %collective-permute-done.6 = bf16[64,128,128]{2,1,0:T(8,128)(2,1)} collective-permute-done((bf16[64,128,128]{2,1,0:T(8,128)(2,1)}, bf16[64,128,128]{2,1,0:T(8,128)(2,1)}, u32[]{:S(2)}, u32[]{:S(2)}) %collective-permute-start.6) | collective-permute-done | bytes 2097184 | tf_op jit(solution)/shard_map/ppermute | solution.py:123
  154.6 3.6 %collective-permute-start.9 = (bf16[64,128,128]{2,1,0:T(8,128)(2,1)S(1)}, bf16[64,128,128]{2,1,0:T(8,128)(2,1)}, u32[]{:S(2)}, u32[]{:S(2)}) collective-permute-start(bf16[64,128,128]{2,1,0:T(8,128)(2,1)S(1)} %broadcast_select_fusion.refs_1_), channel_id=1, source_target_pairs={{0,1},{1,0},{2,3},{3,2},{4,5},{5,4},{6,7},{7,6},{8,9},{9,8},{10,11... | collective-permute-start | bytes 6291464 | tf_op jit(solution)/shard_map/ppermute | solution.py:113
  158.2 3.1 %broadcast_select_fusion.1.refs_1_ = bf16[64,128,128]{2,1,0:T(8,128)(2,1)} fusion(bf16[64,128,128]{2,1,0:T(8,128)(2,1)} %collective-permute-done.3, bf16[64,128,128]{2,1,0:T(8,128)(2,1)} %collective-permute-done.6, pred[]{:T(512)S(6)} %ge.20), kind=kLoop, calls=%fused_computation.1 | loop fusion | flops 1048576 | bytes 6291457 | tf_op jit(solution)/shard_map/jit(_where)/select_n | solution.py:136
  161.4 0.7 broadcast_select_fusion.3
  162.1 0.6 fusion.6.refs_0_
  162.7 23.1 %shard_map.37.refs_5_ = f32[113,128,128]{2,1,0:T(8,128)} custom-call(s32[6,128]{1,0:T(8,128)} %fusion.6.refs_0_, bf16[64,128,128]{2,1,0:T(8,128)(2,1)} %bitcast.32, bf16[64,128,128]{2,1,0:T(8,128)(2,1)} %collective-permute-done.10.refs_2_, bf16[64,128,128]{2,1,0:T(8,128)(2,1)} %collective-permute-done.1.refs_3_, ...), custom_call_target="tpu_custom_call" | custom-call | flops 1610612736 | bytes 33554432 | tf_op jit(solution)/shard_map/pallas_call | solution.py:64
  185.8 16.3 %shard_map.38.refs_5_ = f32[113,128,128]{2,1,0:T(8,128)} custom-call(s32[2,128]{1,0:T(2,128)} %get-tuple-element.15.refs_0_, bf16[64,128,128]{2,1,0:T(8,128)(2,1)} %copy-done, bf16[64,128,128]{2,1,0:T(8,128)(2,1)} %collective-permute-done.9.refs_2_, bf16[112,128,128]{2,1,0:T(8,128)(2,1)} %bitcast.27, ...), custom_call_target="tpu_custom_call" | custom-call | flops 536870912 | bytes 33554432 | tf_op jit(solution)/shard_map/pallas_call | solution.py:64
  202.1 18.4 %shard_map.39 = bf16[112,128,128]{2,1,0:T(8,128)(2,1)} custom-call(s32[2,128]{1,0:T(2,128)} %get-tuple-element.13.refs_0_, bf16[64,128,128]{2,1,0:T(8,128)(2,1)} %broadcast_select_fusion.1.refs_1_, bf16[64,128,128]{2,1,0:T(8,128)(2,1)} %collective-permute-done.7.refs_2_, bf16[112,128,128]{2,1,0:T(8,128)(2,1)} %bitcast.28, ...), custom_call_target="tpu_custom_call" | custom-call | flops 536870912 | bytes 33554432 | tf_op jit(solution)/shard_map/pallas_call | solution.py:64
  (20 shorter events, 0.2 us)
Async XLA Ops:
  6.5 105.5 %all-gather.3.cloned.1.call-start = ((), (), s32[]{:S(2)}) async-start(), calls=%async_computation | async-start | bytes 5505024 | tf_op jit(solution)/shard_map/all_gather | solution.py:99
  6.5 48.6 %collective-permute-start.1 = (bf16[64,128,128]{2,1,0:T(8,128)(2,1)}, bf16[64,128,128]{2,1,0:T(8,128)(2,1)}, u32[]{:S(2)}, u32[]{:S(2)}) collective-permute-start(bf16[64,128,128]{2,1,0:T(8,128)(2,1)} %bitcast.29), channel_id=1, source_target_pairs={{0,2},{2,4},{4,6},{1,3},{3,5},{5,7},{8,10},{10,12},{12,14},{9,11},... | collective-permute-start | bytes 6291464 | tf_op jit(solution)/shard_map/ppermute | solution.py:118
  12.0 48.4 %collective-permute-start.4 = (bf16[64,128,128]{2,1,0:T(8,128)(2,1)}, bf16[64,128,128]{2,1,0:T(8,128)(2,1)}, u32[]{:S(2)}, u32[]{:S(2)}) collective-permute-start(bf16[64,128,128]{2,1,0:T(8,128)(2,1)} %bitcast.30), channel_id=1, source_target_pairs={{2,0},{4,2},{6,4},{3,1},{5,3},{7,5},{10,8},{12,10},{14,12},{11,9},... | collective-permute-start | bytes 6291464 | tf_op jit(solution)/shard_map/ppermute | solution.py:123
  55.2 6.5 %collective-permute-start.2 = (bf16[64,128,128]{2,1,0:T(8,128)(2,1)}, bf16[64,128,128]{2,1,0:T(8,128)(2,1)}, u32[]{:S(2)}, u32[]{:S(2)}) collective-permute-start(bf16[64,128,128]{2,1,0:T(8,128)(2,1)} %collective-permute-done.1.refs_3_), channel_id=1, source_target_pairs={{2,4},{4,6},{3,5},{5,7},{10,12},{12,14},{11,13},{13,15},{18,20},{2... | collective-permute-start | bytes 6291464 | tf_op jit(solution)/shard_map/ppermute | solution.py:118
  60.3 47.6 %collective-permute-start.5 = (bf16[64,128,128]{2,1,0:T(8,128)(2,1)}, bf16[64,128,128]{2,1,0:T(8,128)(2,1)}, u32[]{:S(2)}, u32[]{:S(2)}) collective-permute-start(bf16[64,128,128]{2,1,0:T(8,128)(2,1)} %collective-permute-done.4.refs_5_), channel_id=1, source_target_pairs={{2,0},{4,2},{3,1},{5,3},{10,8},{12,10},{11,9},{13,11},{18,16},{20,... | collective-permute-start | bytes 6291464 | tf_op jit(solution)/shard_map/ppermute | solution.py:123
  61.6 54.6 %collective-permute-start.3 = (bf16[64,128,128]{2,1,0:T(8,128)(2,1)}, bf16[64,128,128]{2,1,0:T(8,128)(2,1)}, u32[]{:S(2)}, u32[]{:S(2)}) collective-permute-start(bf16[64,128,128]{2,1,0:T(8,128)(2,1)} %collective-permute-done.2), channel_id=1, source_target_pairs={{4,6},{5,7},{12,14},{13,15},{20,22},{21,23},{28,30},{29,31}} | collective-permute-start | bytes 6291464 | tf_op jit(solution)/shard_map/ppermute | solution.py:118
  107.9 46.6 %collective-permute-start.6 = (bf16[64,128,128]{2,1,0:T(8,128)(2,1)}, bf16[64,128,128]{2,1,0:T(8,128)(2,1)}, u32[]{:S(2)}, u32[]{:S(2)}) collective-permute-start(bf16[64,128,128]{2,1,0:T(8,128)(2,1)} %collective-permute-done.5), channel_id=1, source_target_pairs={{2,0},{3,1},{10,8},{11,9},{18,16},{19,17},{26,24},{27,25}} | collective-permute-start | bytes 6291464 | tf_op jit(solution)/shard_map/ppermute | solution.py:123
  109.2 52.1 %collective-permute-start.10 = (bf16[64,128,128]{2,1,0:T(8,128)(2,1)}, bf16[64,128,128]{2,1,0:T(8,128)(2,1)}, u32[]{:S(2)}, u32[]{:S(2)}) collective-permute-start(bf16[64,128,128]{2,1,0:T(8,128)(2,1)} %bitcast.31), channel_id=1, source_target_pairs={{0,1},{1,0},{2,3},{3,2},{4,5},{5,4},{6,7},{7,6},{8,9},{9,8},{10,11... | collective-permute-start | bytes 6291464 | tf_op jit(solution)/shard_map/ppermute | solution.py:113
  112.0 50.7 %collective-permute-start.8 = (bf16[112,128,128]{2,1,0:T(8,128)(2,1)}, bf16[112,128,128]{2,1,0:T(8,128)(2,1)}, u32[]{:S(2)}, u32[]{:S(2)}) collective-permute-start(bf16[112,128,128]{2,1,0:T(8,128)(2,1)} %bitcast.25), channel_id=1, source_target_pairs={{0,1},{1,0},{2,3},{3,2},{4,5},{5,4},{6,7},{7,6},{8,9},{9,8},{10,11... | collective-permute-start | bytes 11010056 | tf_op jit(solution)/shard_map/ppermute | solution.py:100
  112.8 3.0 %collective-permute-start = (s32[7,3,64]{2,0,1:T(8,128)S(1)}, s32[7,3,64]{2,0,1:T(8,128)S(1)}, u32[]{:S(2)}, u32[]{:S(2)}) collective-permute-start(s32[7,3,64]{2,0,1:T(8,128)S(1)} %bitcast.36), channel_id=1, source_target_pairs={{0,1},{1,0},{2,3},{3,2},{4,5},{5,4},{6,7},{7,6},{8,9},{9,8},{10,11... | collective-permute-start | bytes 16136 | tf_op jit(solution)/shard_map/ppermute | solution.py:93
  115.0 46.3 %copy-start = (bf16[64,128,128]{2,1,0:T(8,128)(2,1)}, bf16[64,128,128]{2,1,0:T(8,128)(2,1)S(1)}, u32[]{:S(2)}) copy-start(bf16[64,128,128]{2,1,0:T(8,128)(2,1)S(1)} %broadcast_select_fusion.refs_1_) | copy-start | bytes 6291460
  115.1 46.3 %copy-start.1 = (s32[1,1,1,7,3,64]{5,2,4,3,1,0:T(1,128)S(1)}, s32[1,1,1,7,3,64]{5,2,4,3,1,0:T(1,128)}, u32[]{:S(2)}) copy-start(s32[1,1,1,7,3,64]{5,2,4,3,1,0:T(1,128)} %param.5) | copy-start | bytes 16132
  115.8 46.9 %collective-permute-start.11 = (bf16[64,128,128]{2,1,0:T(8,128)(2,1)}, bf16[64,128,128]{2,1,0:T(8,128)(2,1)}, u32[]{:S(2)}, u32[]{:S(2)}) collective-permute-start(bf16[64,128,128]{2,1,0:T(8,128)(2,1)} %collective-permute-done.1.refs_3_), channel_id=1, source_target_pairs={{0,1},{1,0},{2,3},{3,2},{4,5},{5,4},{6,7},{7,6},{8,9},{9,8},{10,11... | collective-permute-start | bytes 6291464 | tf_op jit(solution)/shard_map/ppermute | solution.py:113
  116.2 46.5 %collective-permute-start.12 = (bf16[64,128,128]{2,1,0:T(8,128)(2,1)}, bf16[64,128,128]{2,1,0:T(8,128)(2,1)}, u32[]{:S(2)}, u32[]{:S(2)}) collective-permute-start(bf16[64,128,128]{2,1,0:T(8,128)(2,1)} %collective-permute-done.4.refs_5_), channel_id=1, source_target_pairs={{0,1},{1,0},{2,3},{3,2},{4,5},{5,4},{6,7},{7,6},{8,9},{9,8},{10,11... | collective-permute-start | bytes 6291464 | tf_op jit(solution)/shard_map/ppermute | solution.py:113
  154.6 31.3 %collective-permute-start.9 = (bf16[64,128,128]{2,1,0:T(8,128)(2,1)S(1)}, bf16[64,128,128]{2,1,0:T(8,128)(2,1)}, u32[]{:S(2)}, u32[]{:S(2)}) collective-permute-start(bf16[64,128,128]{2,1,0:T(8,128)(2,1)S(1)} %broadcast_select_fusion.refs_1_), channel_id=1, source_target_pairs={{0,1},{1,0},{2,3},{3,2},{4,5},{5,4},{6,7},{7,6},{8,9},{9,8},{10,11... | collective-permute-start | bytes 6291464 | tf_op jit(solution)/shard_map/ppermute | solution.py:113
  161.3 40.8 %collective-permute-start.7 = (bf16[64,128,128]{2,1,0:T(8,128)(2,1)}, bf16[64,128,128]{2,1,0:T(8,128)(2,1)}, u32[]{:S(2)}, u32[]{:S(2)}) collective-permute-start(bf16[64,128,128]{2,1,0:T(8,128)(2,1)} %broadcast_select_fusion.1.refs_1_), channel_id=1, source_target_pairs={{0,1},{1,0},{2,3},{3,2},{4,5},{5,4},{6,7},{7,6},{8,9},{9,8},{10,11... | collective-permute-start | bytes 6291464 | tf_op jit(solution)/shard_map/ppermute | solution.py:113
Sparse Core Ops, SparseCore 0:
  13.4 53.3 all-gather.2

commit v2 on v0

v2 whole, which is shorter than its diff:
```python
import functools

import jax
import jax.numpy as jnp
from jax import lax
from jax.experimental import pallas as pl
from jax.experimental.pallas import tpu as pltpu
from jax.sharding import PartitionSpec as P

NBQ = 32
UNROLL = 4


def adding_kernel(left_count, right_count, given_count, rows, *refs):
    lists, refs = refs[0], refs[1:]
    lefts, refs = refs[:left_count], refs[left_count:]
    rights, refs = refs[:right_count], refs[right_count:]
    givens, refs = refs[:given_count], refs[given_count:]
    out, work, left_all, right_all, todo, sems, out_sem = refs
    half = work.shape[0] - 1
    copies = []
    for group, target in ((rights, right_all), (lefts, left_all)):
        start = 0
        for source in group:
            count = source.shape[0]
            copies.append(pltpu.make_async_copy(source, target.at[pl.ds(start, count)], sems.at[len(copies)]))
            start += count
    if givens:
        copies.append(pltpu.make_async_copy(givens[0], work, sems.at[len(copies)]))
    for copy in copies:
        copy.start()

    def keep(index, count):
        entry = lists[index]
        todo[count] = entry
        return count + (entry >= 0).astype(jnp.int32)

    count = lax.fori_loop(0, lists.shape[0], keep, jnp.int32(0), unroll=8)
    for extra in range(UNROLL - 1):
        todo[count + extra] = jnp.int32(half)
    if not givens:
        work[...] = jnp.zeros_like(work)
    for copy in copies:
        copy.wait()

    def several(group, carry):
        entries = [todo[group * UNROLL + lane] for lane in range(UNROLL)]
        products = [
            jnp.dot(
                left_all[(entry >> 10) & 1023], right_all[entry >> 20], preferred_element_type=jnp.float32
            )
            for entry in entries
        ]
        for entry, product in zip(entries, products):
            work[entry & 1023] += product
        return carry

    lax.fori_loop(0, (count + UNROLL - 1) // UNROLL, several, jnp.int32(0))
    if out.dtype == work.dtype:
        copy = pltpu.make_async_copy(work, out, out_sem)
        copy.start()
        copy.wait()
    else:
        out[...] = work[:half].astype(out.dtype)


def add_products(lists, lefts, rights, givens, half, last):
    width = rights[0].shape[2]
    rows = lefts[0].shape[1]
    left_slots = sum(panel.shape[0] for panel in lefts)
    right_slots = sum(panel.shape[0] for panel in rights)
    assert left_slots <= 1024 and right_slots <= 1024 and half < 1024
    anywhere = pl.BlockSpec(memory_space=pl.ANY)
    out_shape = (
        jax.ShapeDtypeStruct((half, rows, width), jnp.bfloat16)
        if last
        else jax.ShapeDtypeStruct((half + 1, rows, width), jnp.float32)
    )
    operands = [*lefts, *rights, *givens]
    return pl.pallas_call(
        functools.partial(adding_kernel, len(lefts), len(rights), len(givens), rows),
        out_shape=out_shape,
        in_specs=[pl.BlockSpec(memory_space=pltpu.SMEM)] + [anywhere] * len(operands),
        out_specs=pl.BlockSpec(memory_space=pltpu.VMEM) if last else anywhere,
        scratch_shapes=[
            pltpu.VMEM((half + 1, rows, width), jnp.float32),
            pltpu.VMEM((left_slots, rows, width), jnp.bfloat16),
            pltpu.VMEM((right_slots, width, width), jnp.bfloat16),
            pltpu.SMEM((lists.shape[0] + UNROLL,), jnp.int32),
            pltpu.SemaphoreType.DMA((len(operands),)),
            pltpu.SemaphoreType.DMA,
        ],
        compiler_params=pltpu.CompilerParams(vmem_limit_bytes=56 << 20),
        cost_estimate=pl.CostEstimate(
            flops=lists.size * rows * width**2, bytes_accessed=32 << 20, transcendentals=0
        ),
    )(lists, *operands)


def swapped(value):
    return lax.ppermute(value, "dep", [(0, 1), (1, 0)])


def local(left_blocks, right_blocks, triples):
    own = left_blocks[0, 0, 0]
    right_own = right_blocks[0, 0, 0]
    step_lists = triples[0, 0, 0]
    slots = own.shape[0]
    part = right_own.shape[0]
    step_count = step_lists.shape[0]
    centre = step_count // 2
    columns, row_count = lax.axis_size("col"), lax.axis_size("row")
    place, layer = lax.axis_index("col"), lax.axis_index("dep")
    cyclic = columns >= step_count
    reach = centre if cyclic else columns - 1
    half = (2 * step_count - 2 + row_count) // row_count * NBQ // 2

    right_slots = row_count * part
    if row_count == 2:
        met = lax.ppermute(right_own, "row", [(0, 1), (1, 0)])
        rights = [right_own, met, swapped(right_own), swapped(met)]
        turn = lax.axis_index("row") * part
    else:
        gathered = lax.all_gather(right_own, "row", axis=0, tiled=True)
        rights = [gathered, swapped(gathered)]
        turn = 0

    both = jnp.stack([step_lists, swapped(step_lists)])
    result = both[:, :, 2] - layer * half
    wanted = (result >= 0) & (result < half)
    order = jnp.arange(2, dtype=jnp.int32)[:, None, None]
    second = (both[:, :, 1] - turn) % right_slots + order * right_slots
    first = both[:, :, 0] + (order ^ layer) * slots
    packed = jnp.where(wanted, second << 20 | first << 10 | result, -1)

    def listed(offset, panel, valid=True):
        rows = [packed[:, s] for s in range(step_count) if (s - centre - offset) % columns == 0]
        entries = jnp.concatenate(rows, axis=1).reshape(-1)
        return jnp.where(valid & (entries >= 0), entries + (panel * 2 * slots << 10), -1)

    def paired(panel):
        return lax.all_gather(panel, "dep", axis=0, tiled=True)

    if cyclic:
        rising, falling, total = own, own, None
        lefts, lists = [paired(own)], [listed(0, 0)]
        for distance in range(1, reach + 1):
            rising = lax.ppermute(rising, "col", [(i, (i + 1) % columns) for i in range(columns)])
            falling = lax.ppermute(falling, "col", [(i, (i - 1) % columns) for i in range(columns)])
            lists += [listed(-distance, len(lefts)), listed(distance, len(lefts) + 1)]
            lefts += [paired(rising), paired(falling)]
            givens = [] if total is None else [total]
            total = add_products(jnp.concatenate(lists), lefts, rights, givens, half, distance == reach)
            lefts, lists = [], []
        return total[None, None, None]

    assert columns == 4
    rising = lax.ppermute(own, "col", [(0, 1), (1, 2), (2, 3)])
    falling = lax.ppermute(own, "col", [(1, 0), (2, 1), (3, 2)])
    own_pair = paired(own)
    rising, falling, rights, own_pair = lax.optimization_barrier((rising, falling, rights, own_pair))
    rising_two = lax.ppermute(rising, "col", [(1, 2), (2, 3)])
    falling_two = lax.ppermute(falling, "col", [(1, 0), (2, 1)])
    near = [listed(0, 0), listed(-1, 1, place > 0), listed(1, 2, place < 3)]
    total = add_products(
        jnp.concatenate(near), [own_pair, paired(rising), paired(falling)], rights, [], half, False
    )
    rising_two, falling_two, total = lax.optimization_barrier((rising_two, falling_two, total))
    rising_three = lax.ppermute(rising_two, "col", [(2, 3)])
    falling_three = lax.ppermute(falling_two, "col", [(1, 0)])
    two = jnp.where(place > 1, rising_two, falling_two)
    three = jnp.where(place > 1, rising_three, falling_three)
    far = [listed(2, 0), jnp.where(place == 3, listed(1, 1), listed(-1, 1, place == 0))]
    total = add_products(jnp.concatenate(far), [paired(two), paired(three)], rights, [total], half, True)
    return total[None, None, None]


def solution(mesh):
    return jax.shard_map(
        local,
        mesh=mesh,
        in_specs=(
            P(("grp", "row"), "col", "dep", None, None, None),
            P(("grp", "row"), "col", "dep", None, None, None),
            P(("grp", "row"), "col", "dep", None, None, None),
        ),
        out_specs=P(("grp", "row"), "col", "dep", None, None, None),
        check_vma=False,
    )
```

time: 373 us -> 215 us (0.58)
  other arithmetic: 104 us -> 6.1 us
  local copies, waits for them, and re-layouts: 74.3 us -> 2.18 us
  Pallas kernels: 0 us -> 39.4 us
  matrix products: 34.2 us -> 0 us
  starting transfers between devices: 12.3 us -> 17.9 us
    scatter-add x7 -> x0, other arithmetic: 96.5 us -> none  [add_products(): return accumulated.at[step_list[2]].add(products)]
    gather x14 -> x0, local copies, waits for them, and re-layouts: 54.2 us -> none  [the longest x7 28.1 us: add_products(): right_rows = jnp.take(gathered, step_list[1], axis=0)]
    all_gather x1 -> x5, waiting for transfers between devices: 0.01 us -> 50.7 us  [paired(): return lax.all_gather(panel, 'dep', axis=0, tiled=True)]
    pallas_call x0 -> x2, Pallas kernels: none -> 39.4 us  [add_products(): pl.pallas_call(functools.partial(adding_kernel, len(lefts), len(rights),...]
    dot_general x7 -> x0, matrix products: 34.2 us -> none  [add_products(): jnp.einsum('tij,tjk->tik', left_rows, right_rows, preferred_element_type=...]
    reduce_scatter x1 -> x0, waiting for transfers between devices: 26.6 us -> none  [local(): lax.psum_scatter(accumulated[:out_count], 'dep', scatter_dimension=0, til...]
    ppermute x6 -> x10, waiting for transfers between devices: 107 us -> 83.2 us  [the longest x1 43.1 us: local(): falling_three = lax.ppermute(falling_two, 'col', [(1, 0)])]
    slice x1, local copies, waits for them, and re-layouts: 13.1 us -> 0.01 us  [listed(): packed[:, s]]
  transfers between devices with their start and end apart: 8 -> 15, of which waited for: 5 -> 9; matrix products, arithmetic and copies ran while one was open for 46% -> 1% of each run, Pallas kernels for 0% -> 8%
where the time goes in v2:
time: 215 us; the launch traced here: 214 us
  waiting for transfers between devices  135 us (63%)
  Pallas kernels  39.4 us (18%)
  starting transfers between devices  17.9 us (8%)
  between operations  13.3 us (6%)
  other arithmetic  6.1 us (3%)
  local copies, waits for them, and re-layouts  2.18 us (1%)
    all_gather x5, waiting for transfers between devices, paired(): return lax.all_gather(panel, 'dep', axis=0, tiled=True)  50.7 us
    ppermute x1, waiting for transfers between devices, local(): falling_three = lax.ppermute(falling_two, 'col', [(1, 0)])  43.1 us
    pallas_call x2, Pallas kernels, add_products(): pl.pallas_call(functools.partial(adding_kernel, len(lefts), len(rights),...  39.4 us
    ppermute x1, waiting for transfers between devices, local(): met = lax.ppermute(right_own, 'row', [(0, 1), (1, 0)])  31.7 us
    ppermute x1, waiting for transfers between devices, local(): falling = lax.ppermute(own, 'col', [(1, 0), (2, 1), (3, 2)])  5.96 us
    ppermute x1, starting transfers between devices, local(): rising = lax.ppermute(own, 'col', [(0, 1), (1, 2), (2, 3)])  5.32 us
    ppermute x3, starting transfers between devices, swapped(): return lax.ppermute(value, 'dep', [(0, 1), (1, 0)])  4.97 us
  transfers between devices with their start and end apart: 15, of which 9 were waited for; matrix products, arithmetic and copies ran while one was open for 1% of the time, Pallas kernels for 8%

profile of v2, /device:TPU:1, one launch (start us, length us, event | category | flops | bytes accessed | tf_op | source)
XLA Modules:
  0.0 214.2 jit_solution(33290879119059991)
XLA Ops:
  8.0 2.0 collective-permute-start.3
  10.1 1.3 collective-permute-start.2
  11.4 5.3 %collective-permute-start.1 = (bf16[64,128,128]{2,1,0:T(8,128)(2,1)}, bf16[64,128,128]{2,1,0:T(8,128)(2,1)}, u32[]{:S(2)}, u32[]{:S(2)}) collective-permute-start(bf16[64,128,128]{2,1,0:T(8,128)(2,1)} %bitcast.61), channel_id=1, source_target_pairs={{0,2},{2,4},{4,6},{1,3},{3,5},{5,7},{8,10},{10,12},{12,14},{9,11},... | collective-permute-start | bytes 6291464 | tf_op jit(solution)/shard_map/ppermute | solution.py:158
  16.7 1.5 collective-permute-start.4
  18.2 31.7 %collective-permute-done.3.refs_5_.refs_4_ = bf16[56,128,128]{2,1,0:T(8,128)(2,1)} collective-permute-done((bf16[56,128,128]{2,1,0:T(8,128)(2,1)S(1)}, bf16[56,128,128]{2,1,0:T(8,128)(2,1)}, u32[]{:S(2)}, u32[]{:S(2)}) %collective-permute-start.3) | collective-permute-done | bytes 1835040 | tf_op jit(solution)/shard_map/ppermute | solution.py:120
  49.9 1.2 collective-permute-start.5
  51.2 1.3 copy-done.1
  52.5 6.0 %collective-permute-done.2 = bf16[64,128,128]{2,1,0:T(8,128)(2,1)} collective-permute-done((bf16[64,128,128]{2,1,0:T(8,128)(2,1)}, bf16[64,128,128]{2,1,0:T(8,128)(2,1)}, u32[]{:S(2)}, u32[]{:S(2)}) %collective-permute-start.2) | collective-permute-done | bytes 2097184 | tf_op jit(solution)/shard_map/ppermute | solution.py:159
  58.5 0.9 collective-permute-done.1
  60.2 0.8 collective-permute-start.6
  61.0 1.3 collective-permute-start.7
  62.3 2.2 %collective-permute-start = (s32[7,3,64]{2,0,1:T(8,128)S(1)}, s32[7,3,64]{2,0,1:T(8,128)S(1)}, u32[]{:S(2)}, u32[]{:S(2)}) collective-permute-start(s32[7,3,64]{2,0,1:T(8,128)S(1)} %bitcast.64), channel_id=1, source_target_pairs={{0,1},{1,0},{2,3},{3,2},{4,5},{5,4},{6,7},{7,6},{8,9},{9,8},{10,11... | collective-permute-start | bytes 16136 | tf_op jit(solution)/shard_map/ppermute | solution.py:101
  64.5 0.8 collective-permute-done
  66.2 11.4 %all-gather.7.cloned.1.call-done.refs_2_ = bf16[128,128,128]{2,1,0:T(8,128)(2,1)} async-done(((bf16[64,128,128]{2,1,0:T(8,128)(2,1)}), bf16[128,128,128]{2,1,0:T(8,128)(2,1)}) %all-gather.7.cloned.1.call-update) | async-done | bytes 4194320 | tf_op jit(solution)/shard_map/all_gather | solution.py:142
  77.6 16.4 %all-gather.9.cloned.1.call-done.refs_3_ = bf16[128,128,128]{2,1,0:T(8,128)(2,1)} async-done(((bf16[64,128,128]{2,1,0:T(8,128)(2,1)}), bf16[128,128,128]{2,1,0:T(8,128)(2,1)}) %all-gather.9.cloned.1.call-update) | async-done | bytes 4194320 | tf_op jit(solution)/shard_map/all_gather | solution.py:142
  94.1 17.0 %shard_map.37.refs_7_ = f32[113,128,128]{2,1,0:T(8,128)} custom-call(s32[640]{0:T(1024)} %pad_add_fusion.1.refs_0_, bf16[128,128,128]{2,1,0:T(8,128)(2,1)} %bitcast.58, bf16[128,128,128]{2,1,0:T(8,128)(2,1)} %all-gather.7.cloned.1.call-done.refs_2_, bf16[128,128,128]{2,1,0:T(8,128)(2,1)} %all-gather.9.cloned.1.call-done.refs_3_, ...), custom_call_target="tpu_custom_call" | custom-call | flops 1342177280 | bytes 33554432 | tf_op jit(solution)/shard_map/pallas_call | solution.py:80
  111.1 0.7 collective-permute-done.7
  111.9 3.1 %broadcast_select_fusion.1 = bf16[64,128,128]{2,1,0:T(8,128)(2,1)} fusion(bf16[64,128,128]{2,1,0:T(8,128)(2,1)S(1)} %collective-permute-done.6, bf16[64,128,128]{2,1,0:T(8,128)(2,1)} %collective-permute-done.7, pred[]{:T(512)S(6)} %gt.7), kind=kLoop, calls=%fused_computation.1 | loop fusion | flops 1048576 | bytes 6291457 | tf_op jit(solution)/shard_map/jit(_where)/select_n | solution.py:171
  115.1 0.8 collective-permute-start.8
  115.9 1.3 collective-permute-start.9
  117.2 43.1 %collective-permute-done.9 = bf16[64,128,128]{2,1,0:T(8,128)(2,1)S(1)} collective-permute-done((bf16[64,128,128]{2,1,0:T(8,128)(2,1)}, bf16[64,128,128]{2,1,0:T(8,128)(2,1)S(1)}, u32[]{:S(2)}, u32[]{:S(2)}) %collective-permute-start.9) | collective-permute-done | bytes 2097184 | tf_op jit(solution)/shard_map/ppermute | solution.py:170
  160.2 1.6 broadcast_select_fusion
  162.5 22.8 %all-gather.13.cloned.1.call-done.refs_2_ = bf16[128,128,128]{2,1,0:T(8,128)(2,1)} async-done(((bf16[64,128,128]{2,1,0:T(8,128)(2,1)}), bf16[128,128,128]{2,1,0:T(8,128)(2,1)}) %all-gather.13.cloned.1.call-update) | async-done | bytes 4194320 | tf_op jit(solution)/shard_map/all_gather | solution.py:142
  185.3 22.3 %shard_map.38 = bf16[112,128,128]{2,1,0:T(8,128)(2,1)} custom-call(s32[512]{0:T(512)} %pad_add_fusion.2.refs_0_, bf16[128,128,128]{2,1,0:T(8,128)(2,1)} %all-gather.11.cloned.1.call-done.refs_1_, bf16[128,128,128]{2,1,0:T(8,128)(2,1)} %all-gather.13.cloned.1.call-done.refs_2_, bf16[56,128,128]{2,1,0:T(8,128)(2,1)} %bitcast.55, ...), custom_call_target="tpu_custom_call" | custom-call | flops 1073741824 | bytes 33554432 | tf_op jit(solution)/shard_map/pallas_call | solution.py:80
  (32 shorter events, 3.9 us)
Async XLA Ops:
  6.5 1.5 copy-start
  6.5 52.8 %all-gather.15.cloned.1.call-start = ((), (), s32[]{:S(2)}) async-start(), calls=%async_computation.4 | async-start | bytes 6291456 | tf_op jit(solution)/shard_map/all_gather | solution.py:142
  7.3 70.4 %all-gather.7.cloned.1.call-start = ((), (), s32[]{:S(2)}) async-start(), calls=%async_computation | async-start | bytes 6291456 | tf_op jit(solution)/shard_map/all_gather | solution.py:142
  8.0 41.9 %collective-permute-start.3 = (bf16[56,128,128]{2,1,0:T(8,128)(2,1)S(1)}, bf16[56,128,128]{2,1,0:T(8,128)(2,1)}, u32[]{:S(2)}, u32[]{:S(2)}) collective-permute-start(bf16[56,128,128]{2,1,0:T(8,128)(2,1)S(1)} %bitcast.56), channel_id=1, source_target_pairs={{0,8},{8,0},{1,9},{9,1},{2,10},{10,2},{3,11},{11,3},{4,12},{12,4},... | collective-permute-start | bytes 5505032 | tf_op jit(solution)/shard_map/ppermute | solution.py:120
  10.1 48.4 %collective-permute-start.2 = (bf16[64,128,128]{2,1,0:T(8,128)(2,1)}, bf16[64,128,128]{2,1,0:T(8,128)(2,1)}, u32[]{:S(2)}, u32[]{:S(2)}) collective-permute-start(bf16[64,128,128]{2,1,0:T(8,128)(2,1)} %bitcast.60), channel_id=1, source_target_pairs={{2,0},{4,2},{6,4},{3,1},{5,3},{7,5},{10,8},{12,10},{14,12},{11,9},... | collective-permute-start | bytes 6291464 | tf_op jit(solution)/shard_map/ppermute | solution.py:159
  11.4 48.0 %collective-permute-start.1 = (bf16[64,128,128]{2,1,0:T(8,128)(2,1)}, bf16[64,128,128]{2,1,0:T(8,128)(2,1)}, u32[]{:S(2)}, u32[]{:S(2)}) collective-permute-start(bf16[64,128,128]{2,1,0:T(8,128)(2,1)} %bitcast.61), channel_id=1, source_target_pairs={{0,2},{2,4},{4,6},{1,3},{3,5},{5,7},{8,10},{10,12},{12,14},{9,11},... | collective-permute-start | bytes 6291464 | tf_op jit(solution)/shard_map/ppermute | solution.py:158
  16.7 34.5 %collective-permute-start.4 = (bf16[56,128,128]{2,1,0:T(8,128)(2,1)S(1)}, bf16[56,128,128]{2,1,0:T(8,128)(2,1)S(1)}, u32[]{:S(2)}, u32[]{:S(2)}) collective-permute-start(bf16[56,128,128]{2,1,0:T(8,128)(2,1)S(1)} %bitcast.57), channel_id=1, source_target_pairs={{0,1},{1,0},{2,3},{3,2},{4,5},{5,4},{6,7},{7,6},{8,9},{9,8},{10,11... | collective-permute-start | bytes 5505032 | tf_op jit(solution)/shard_map/ppermute | solution.py:101
  49.9 9.4 %collective-permute-start.5 = (bf16[56,128,128]{2,1,0:T(8,128)(2,1)}, bf16[56,128,128]{2,1,0:T(8,128)(2,1)}, u32[]{:S(2)}, u32[]{:S(2)}) collective-permute-start(bf16[56,128,128]{2,1,0:T(8,128)(2,1)} %collective-permute-done.3.refs_5_.refs_4_), channel_id=1, source_target_pairs={{0,1},{1,0},{2,3},{3,2},{4,5},{5,4},{6,7},{7,6},{8,9},{9,8},{10,11... | collective-permute-start | bytes 5505032 | tf_op jit(solution)/shard_map/ppermute | solution.py:101
  51.1 1.3 copy-start.1
  59.3 2.9 %copy-start.2 = (s32[1,1,1,7,3,64]{5,2,4,3,1,0:T(1,128)S(1)}, s32[1,1,1,7,3,64]{5,2,4,3,1,0:T(1,128)}, u32[]{:S(2)}) copy-start(s32[1,1,1,7,3,64]{5,2,4,3,1,0:T(1,128)} %param.5) | copy-start | bytes 16132
  59.4 34.7 %all-gather.9.cloned.1.call-start = ((), (), s32[]{:S(2)}) async-start(), calls=%async_computation.1 | async-start | bytes 6291456 | tf_op jit(solution)/shard_map/all_gather | solution.py:142
  60.1 102.4 %all-gather.11.cloned.1.call-start = ((), (), s32[]{:S(2)}) async-start(), calls=%async_computation.2 | async-start | bytes 6291456 | tf_op jit(solution)/shard_map/all_gather | solution.py:142
  60.2 50.9 %collective-permute-start.6 = (bf16[64,128,128]{2,1,0:T(8,128)(2,1)}, bf16[64,128,128]{2,1,0:T(8,128)(2,1)S(1)}, u32[]{:S(2)}, u32[]{:S(2)}) collective-permute-start(bf16[64,128,128]{2,1,0:T(8,128)(2,1)} %collective-permute-done.1), channel_id=1, source_target_pairs={{2,4},{4,6},{3,5},{5,7},{10,12},{12,14},{11,13},{13,15},{18,20},{2... | collective-permute-start | bytes 6291464 | tf_op jit(solution)/shard_map/ppermute | solution.py:162
  61.0 50.9 %collective-permute-start.7 = (bf16[64,128,128]{2,1,0:T(8,128)(2,1)}, bf16[64,128,128]{2,1,0:T(8,128)(2,1)}, u32[]{:S(2)}, u32[]{:S(2)}) collective-permute-start(bf16[64,128,128]{2,1,0:T(8,128)(2,1)} %collective-permute-done.2), channel_id=1, source_target_pairs={{2,0},{4,2},{3,1},{5,3},{10,8},{12,10},{11,9},{13,11},{18,16},{20,... | collective-permute-start | bytes 6291464 | tf_op jit(solution)/shard_map/ppermute | solution.py:163
  62.3 3.1 %collective-permute-start = (s32[7,3,64]{2,0,1:T(8,128)S(1)}, s32[7,3,64]{2,0,1:T(8,128)S(1)}, u32[]{:S(2)}, u32[]{:S(2)}) collective-permute-start(s32[7,3,64]{2,0,1:T(8,128)S(1)} %bitcast.64), channel_id=1, source_target_pairs={{0,1},{1,0},{2,3},{3,2},{4,5},{5,4},{6,7},{7,6},{8,9},{9,8},{10,11... | collective-permute-start | bytes 16136 | tf_op jit(solution)/shard_map/ppermute | solution.py:101
  115.0 70.3 %all-gather.13.cloned.1.call-start = ((), (), s32[]{:S(2)}) async-start(), calls=%async_computation.3 | async-start | bytes 6291456 | tf_op jit(solution)/shard_map/all_gather | solution.py:142
  115.1 2.1 collective-permute-start.8
  115.9 44.4 %collective-permute-start.9 = (bf16[64,128,128]{2,1,0:T(8,128)(2,1)}, bf16[64,128,128]{2,1,0:T(8,128)(2,1)S(1)}, u32[]{:S(2)}, u32[]{:S(2)}) collective-permute-start(bf16[64,128,128]{2,1,0:T(8,128)(2,1)} %collective-permute-done.7), channel_id=1, source_target_pairs={{2,0},{3,1},{10,8},{11,9},{18,16},{19,17},{26,24},{27,25}} | collective-permute-start | bytes 6291464 | tf_op jit(solution)/shard_map/ppermute | solution.py:170
Sparse Core Ops, SparseCore 0:
  8.9 16.1 all-gather.14
  59.5 18.0 all-gather.6
  79.2 14.8 all-gather.8
  115.1 19.6 all-gather.10
  161.9 23.3 all-gather.12

commit v3 on v2

v3 whole, which is shorter than its diff:
```python
import functools

import jax
import jax.numpy as jnp
from jax import lax
from jax.experimental import pallas as pl
from jax.experimental.pallas import tpu as pltpu
from jax.sharding import PartitionSpec as P

NBQ = 32
UNROLL = 4


def adding_kernel(shape, left_counts, right_count, given_count, *refs):
    step_count, columns, slots, rounds = shape
    packed, classes, refs = refs[0], refs[1], refs[2:]
    lefts, refs = refs[: sum(left_counts)], refs[sum(left_counts) :]
    rights, refs = refs[:right_count], refs[right_count:]
    givens, refs = refs[:given_count], refs[given_count:]
    out, work, left_all, right_all, todo, sems, out_sem = refs
    half = work.shape[0] - 1
    copies, needed = [], []
    owners = [panel for panel, pieces in enumerate(left_counts) for _ in range(pieces)]
    for group, target, panels in ((rights, right_all, [None] * right_count), (lefts, left_all, owners)):
        start = 0
        for source, panel in zip(group, panels):
            count = source.shape[0]
            copies.append(pltpu.make_async_copy(source, target.at[pl.ds(start, count)], sems.at[len(copies)]))
            needed.append(None if panel is None else classes[panel] >= 0)
            start += count
    if givens:
        copies.append(pltpu.make_async_copy(givens[0], work, sems.at[len(copies)]))
        needed.append(None)

    def each_copy(method):
        for copy, when in zip(copies, needed):
            if when is None:
                getattr(copy, method)()
            else:
                pl.when(when)(getattr(copy, method))

    each_copy("start")

    count = jnp.int32(0)
    for panel in range(len(left_counts)):
        kind = classes[panel]
        for extra in range(rounds):
            step = lax.rem(kind + step_count // 2, columns) + extra * columns
            groups = jnp.where((kind >= 0) & (step < step_count), slots // 8, 0)
            for layer in range(2):
                base = (layer * step_count + step) * slots

                def keep(group, count):
                    for lane in range(8):
                        entry = packed[base + group * 8 + lane]
                        todo[count] = entry + (panel * 2 * slots << 10)
                        count += (entry >= 0).astype(jnp.int32)
                    return count

                count = lax.fori_loop(0, groups, keep, count)
    for extra in range(UNROLL - 1):
        todo[count + extra] = jnp.int32(half)
    if not givens:
        work[...] = jnp.zeros_like(work)
    each_copy("wait")

    def several(group, carry):
        entries = [todo[group * UNROLL + lane] for lane in range(UNROLL)]
        products = [
            jnp.dot(left_all[(entry >> 10) & 1023], right_all[entry >> 20], preferred_element_type=jnp.float32)
            for entry in entries
        ]
        for entry, product in zip(entries, products):
            work[entry & 1023] += product
        return carry

    lax.fori_loop(0, (count + UNROLL - 1) // UNROLL, several, jnp.int32(0))
    if out.dtype == work.dtype:
        copy = pltpu.make_async_copy(work, out, out_sem)
        copy.start()
        copy.wait()
    else:
        out[...] = work[:half].astype(out.dtype)


def add_products(packed, classes, columns, panels, rights, givens, half, last):
    step_count, slots = packed.shape[1:]
    rounds = -(-step_count // columns)
    width = rights[0].shape[2]
    lefts = [piece for panel in panels for piece in panel]
    rows = lefts[0].shape[1]
    left_slots = sum(piece.shape[0] for piece in lefts)
    right_slots = sum(piece.shape[0] for piece in rights)
    assert left_slots <= 1024 and right_slots <= 1024 and half < 1024 and slots % 8 == 0
    anywhere = pl.BlockSpec(memory_space=pl.ANY)
    in_scalar = pl.BlockSpec(memory_space=pltpu.SMEM)
    out_shape = (
        jax.ShapeDtypeStruct((half, rows, width), jnp.bfloat16)
        if last
        else jax.ShapeDtypeStruct((half + 1, rows, width), jnp.float32)
    )
    operands = [*lefts, *rights, *givens]
    room = len(panels) * rounds * 2 * slots + UNROLL
    shape = (step_count, columns, slots, rounds)
    return pl.pallas_call(
        functools.partial(adding_kernel, shape, [len(panel) for panel in panels], len(rights), len(givens)),
        out_shape=out_shape,
        in_specs=[in_scalar, in_scalar] + [anywhere] * len(operands),
        out_specs=pl.BlockSpec(memory_space=pltpu.VMEM) if last else anywhere,
        scratch_shapes=[
            pltpu.VMEM((half + 1, rows, width), jnp.float32),
            pltpu.VMEM((left_slots, rows, width), jnp.bfloat16),
            pltpu.VMEM((right_slots, width, width), jnp.bfloat16),
            pltpu.SMEM((room,), jnp.int32),
            pltpu.SemaphoreType.DMA((len(operands),)),
            pltpu.SemaphoreType.DMA,
        ],
        compiler_params=pltpu.CompilerParams(vmem_limit_bytes=56 << 20),
        cost_estimate=pl.CostEstimate(
            flops=len(panels) * 4 * slots * rows * width**2, bytes_accessed=32 << 20, transcendentals=0
        ),
    )(packed.reshape(-1), classes, *operands)


def swapped(value):
    return lax.ppermute(value, "dep", [(0, 1), (1, 0)])


def paired(value):
    return lax.all_gather(value, "dep", axis=0, tiled=True)


def local(left_blocks, right_blocks, triples):
    own = left_blocks[0, 0, 0]
    right_own = right_blocks[0, 0, 0]
    step_lists = triples[0, 0, 0]
    slots = own.shape[0]
    part = right_own.shape[0]
    step_count = step_lists.shape[0]
    centre = step_count // 2
    columns, row_count = lax.axis_size("col"), lax.axis_size("row")
    place, layer = lax.axis_index("col"), lax.axis_index("dep")
    cyclic = columns >= step_count
    half = (2 * step_count - 2 + row_count) // row_count * NBQ // 2

    lists = paired(step_lists).reshape(2, step_count, 3, slots)
    result = lists[:, :, 2] - layer * half
    wanted = (result >= 0) & (result < half)
    layers = jnp.arange(2, dtype=jnp.int32)[:, None, None]
    given_first, given_second = lists[:, :, 0], lists[:, :, 1]
    first = layers * slots + given_first
    if row_count == 2:
        met = lax.ppermute(right_own, "row", [(0, 1), (1, 0)])
        rights = [paired(right_own), paired(met)]
        second = (((given_second // part) ^ lax.axis_index("row")) * 2 + layers) * part + given_second % part
    else:
        rights = [paired(lax.all_gather(right_own, "row", axis=0, tiled=True))]
        second = layers * (row_count * part) + given_second
    packed = jnp.where(wanted, second << 20 | first << 10 | result, -1)

    def kinds(*values):
        return jnp.stack([jnp.asarray(value, jnp.int32) for value in values])

    if cyclic:
        rising, falling, total = own, own, None
        panels, offsets = [[paired(own)]], [0]
        for distance in range(1, centre + 1):
            rising = lax.ppermute(rising, "col", [(i, (i + 1) % columns) for i in range(columns)])
            falling = lax.ppermute(falling, "col", [(i, (i - 1) % columns) for i in range(columns)])
            panels += [[paired(rising)], [paired(falling)]]
            offsets += [columns - distance, distance]
            givens = [] if total is None else [total]
            total = add_products(
                packed, kinds(*offsets), columns, panels, rights, givens, half, distance == centre
            )
            panels, offsets = [], []
        return total[None, None, None]

    assert columns == 4
    rising = lax.ppermute(own, "col", [(0, 1), (1, 2), (2, 3)])
    falling = lax.ppermute(own, "col", [(1, 0), (2, 1), (3, 2)])
    rising_two = lax.ppermute(rising, "col", [(1, 2), (2, 3)])
    falling_two = lax.ppermute(falling, "col", [(1, 0), (2, 1)])
    rising_three = lax.ppermute(rising_two, "col", [(2, 3)])
    falling_three = lax.ppermute(falling_two, "col", [(1, 0)])
    two = jnp.where(place > 1, rising_two, falling_two)
    panels = [[paired(value)] for value in (own, rising, falling, two)]
    classes = kinds(0, jnp.where(place > 0, 3, -1), jnp.where(place < 3, 1, -1), 2)
    total = add_products(packed, classes, columns, panels, rights, [], half, False)
    rising_three, falling_three, total = lax.optimization_barrier((rising_three, falling_three, total))
    three = jnp.where(place > 1, rising_three, falling_three)
    classes = kinds(jnp.where(place == 3, 1, jnp.where(place == 0, 3, -1)))
    packed_far = jnp.where(packed >= 0, packed ^ (layer * slots << 10), -1)
    total = add_products(packed_far, classes, columns, [[three, swapped(three)]], rights, [total], half, True)
    return total[None, None, None]


def solution(mesh):
    return jax.shard_map(
        local,
        mesh=mesh,
        in_specs=(
            P(("grp", "row"), "col", "dep", None, None, None),
            P(("grp", "row"), "col", "dep", None, None, None),
            P(("grp", "row"), "col", "dep", None, None, None),
        ),
        out_specs=P(("grp", "row"), "col", "dep", None, None, None),
        check_vma=False,
    )
```

time: 215 us -> 276 us (1.28); the launches traced: 214 us -> 272 us
  waiting for transfers between devices: 135 us -> 190 us
  blocking collectives: 0 us -> 5.51 us
    ppermute x1, waiting for transfers between devices: 0.74 us -> 43.7 us  [local(): falling_two = lax.ppermute(falling, 'col', [(1, 0), (2, 1)])]
    ppermute x1, waiting for transfers between devices: 43.1 us -> 1.74 us  [local(): falling_three = lax.ppermute(falling_two, 'col', [(1, 0)])]
    ppermute x1, waiting for transfers between devices: 5.96 us -> 46.6 us  [local(): falling = lax.ppermute(own, 'col', [(1, 0), (2, 1), (3, 2)])]
    ppermute x1, waiting for transfers between devices: 0.89 us -> 41.1 us  [local(): rising = lax.ppermute(own, 'col', [(0, 1), (1, 2), (2, 3)])]
    all_gather x5 -> x6, waiting for transfers between devices: 50.7 us -> 11.2 us  [paired(): return lax.all_gather(value, 'dep', axis=0, tiled=True)]
    ppermute x1, waiting for transfers between devices: 31.7 us -> 40.1 us  [local(): met = lax.ppermute(right_own, 'row', [(0, 1), (1, 0)])]
    all_gather x0 -> x1, blocking collectives: none -> 5.51 us  [paired(): return lax.all_gather(value, 'dep', axis=0, tiled=True)]
    ppermute x3 -> x1, waiting for transfers between devices: 0.83 us -> 3.92 us  [swapped(): return lax.ppermute(value, 'dep', [(0, 1), (1, 0)])]
  transfers between devices with their start and end apart: 15 -> 14, of which waited for: 9 -> 7; matrix products, arithmetic and copies ran while one was open for 1% -> 1% of each run, Pallas kernels for 8% -> 8%
where the time goes in v3:
time: 276 us; the launch traced here: 272 us
  waiting for transfers between devices  190 us (69%)
  Pallas kernels  38.2 us (14%)
  starting transfers between devices  19.6 us (7%)
  between operations  13.6 us (5%)
  blocking collectives  5.51 us (2%)
  other arithmetic  4.54 us (2%)
    ppermute x1, waiting for transfers between devices, local(): falling = lax.ppermute(own, 'col', [(1, 0), (2, 1), (3, 2)])  46.6 us
    ppermute x1, waiting for transfers between devices, local(): falling_two = lax.ppermute(falling, 'col', [(1, 0), (2, 1)])  43.7 us
    ppermute x1, waiting for transfers between devices, local(): rising = lax.ppermute(own, 'col', [(0, 1), (1, 2), (2, 3)])  41.1 us
    ppermute x1, waiting for transfers between devices, local(): met = lax.ppermute(right_own, 'row', [(0, 1), (1, 0)])  40.1 us
    pallas_call x2, Pallas kernels, add_products(): pl.pallas_call(functools.partial(adding_kernel, shape, [len(panel) for pa...  38.2 us
    all_gather x6, waiting for transfers between devices, paired(): return lax.all_gather(value, 'dep', axis=0, tiled=True)  11.2 us
  transfers between devices with their start and end apart: 14, of which 7 were waited for; matrix products, arithmetic and copies ran while one was open for 1% of the time, Pallas kernels for 8%

profile of v3, /device:TPU:1, one launch (start us, length us, event | category | flops | bytes accessed | tf_op | source)
XLA Modules:
  0.0 271.8 jit_solution(5905788689961583500)
XLA Ops:
  6.5 0.7 all-gather.20.cloned.1.call-update
  7.3 0.7 all-gather.18.cloned.1.call-update
  8.1 2.1 collective-permute-start.6
  10.2 40.1 %collective-permute-done.6 = bf16[56,128,128]{2,1,0:T(8,128)(2,1)} collective-permute-done((bf16[56,128,128]{2,1,0:T(8,128)(2,1)}, bf16[56,128,128]{2,1,0:T(8,128)(2,1)}, u32[]{:S(2)}, u32[]{:S(2)}) %collective-permute-start.6) | collective-permute-done | bytes 1835040 | tf_op jit(solution)/shard_map/ppermute | solution.py:153
  50.3 1.3 collective-permute-start.3
  51.6 46.6 %collective-permute-done.3 = bf16[64,128,128]{2,1,0:T(8,128)(2,1)} collective-permute-done((bf16[64,128,128]{2,1,0:T(8,128)(2,1)S(1)}, bf16[64,128,128]{2,1,0:T(8,128)(2,1)}, u32[]{:S(2)}, u32[]{:S(2)}) %collective-permute-start.3) | collective-permute-done | bytes 2097184 | tf_op jit(solution)/shard_map/ppermute | solution.py:181
  98.3 4.1 %collective-permute-start = (bf16[64,128,128]{2,1,0:T(8,128)(2,1)S(1)}, bf16[64,128,128]{2,1,0:T(8,128)(2,1)}, u32[]{:S(2)}, u32[]{:S(2)}) collective-permute-start(bf16[64,128,128]{2,1,0:T(8,128)(2,1)S(1)} %bitcast.25), channel_id=1, source_target_pairs={{0,2},{2,4},{4,6},{1,3},{3,5},{5,7},{8,10},{10,12},{12,14},{9,11},... | collective-permute-start | bytes 6291464 | tf_op jit(solution)/shard_map/ppermute | solution.py:180
  102.4 41.1 %collective-permute-done = bf16[64,128,128]{2,1,0:T(8,128)(2,1)} collective-permute-done((bf16[64,128,128]{2,1,0:T(8,128)(2,1)S(1)}, bf16[64,128,128]{2,1,0:T(8,128)(2,1)}, u32[]{:S(2)}, u32[]{:S(2)}) %collective-permute-start) | collective-permute-done | bytes 2097184 | tf_op jit(solution)/shard_map/ppermute | solution.py:180
  143.6 1.3 collective-permute-start.4
  144.9 2.0 collective-permute-start.1
  146.9 43.7 %collective-permute-done.4 = bf16[64,128,128]{2,1,0:T(8,128)(2,1)S(1)} collective-permute-done((bf16[64,128,128]{2,1,0:T(8,128)(2,1)}, bf16[64,128,128]{2,1,0:T(8,128)(2,1)S(1)}, u32[]{:S(2)}, u32[]{:S(2)}) %collective-permute-start.4) | collective-permute-done | bytes 2097184 | tf_op jit(solution)/shard_map/ppermute | solution.py:183
  190.6 1.5 broadcast_select_fusion.1
  192.1 1.3 collective-permute-start.5
  193.4 2.0 collective-permute-start.2
  195.6 5.5 %all-gather = s32[1,1,1,14,3,64]{5,2,4,1,0,3:T(1,128)S(1)} all-gather(s32[1,1,1,7,3,64]{5,2,4,1,0,3:T(1,128)S(1)} %bitcast.29), channel_id=2, replica_groups=mesh['grp'=2,'row'=2,'col'=4,'dep'=2] {'dep'}, dimensions={3}, use_global_device_ids=true | all-gather | bytes 16128 | tf_op jit(solution)/shard_map/all_gather | solution.py:130
  201.6 0.6 pad_add_fusion.refs_1_
  202.2 0.6 xor_select_fusion
  202.8 11.2 %all-gather.14.cloned.1.call-done.refs_5_ = bf16[128,128,128]{2,1,0:T(8,128)(2,1)} async-done(((bf16[64,128,128]{2,1,0:T(8,128)(2,1)}), bf16[128,128,128]{2,1,0:T(8,128)(2,1)}) %all-gather.14.cloned.1.call-update) | async-done | bytes 4194320 | tf_op jit(solution)/shard_map/all_gather | solution.py:130
  214.0 21.4 %shard_map.37.refs_6_ = f32[113,128,128]{2,1,0:T(8,128)} custom-call(s32[896]{0:T(1024)} %get-tuple-element.12.refs_0_, s32[4]{0:T(128)} %pad_add_fusion.refs_1_, bf16[128,128,128]{2,1,0:T(8,128)(2,1)} %bitcast.22, bf16[128,128,128]{2,1,0:T(8,128)(2,1)} %all-gather.10.cloned.1.call-done.refs_3_, ...), custom_call_target="tpu_custom_call" | custom-call | flops 2147483648 | bytes 33554432 | tf_op jit(solution)/shard_map/pallas_call | solution.py:105
  235.4 1.7 collective-permute-done.5
  237.2 1.8 broadcast_select_fusion.refs_2_
  239.0 5.3 %collective-permute-start.7 = (bf16[64,128,128]{2,1,0:T(8,128)(2,1)S(1)}, bf16[64,128,128]{2,1,0:T(8,128)(2,1)}, u32[]{:S(2)}, u32[]{:S(2)}) collective-permute-start(bf16[64,128,128]{2,1,0:T(8,128)(2,1)S(1)} %broadcast_select_fusion.refs_2_), channel_id=1, source_target_pairs={{0,1},{1,0},{2,3},{3,2},{4,5},{5,4},{6,7},{7,6},{8,9},{9,8},{10,11... | collective-permute-start | bytes 6291464 | tf_op jit(solution)/shard_map/ppermute | solution.py:126
  244.3 3.9 %collective-permute-done.7.refs_3_ = bf16[64,128,128]{2,1,0:T(8,128)(2,1)} collective-permute-done((bf16[64,128,128]{2,1,0:T(8,128)(2,1)S(1)}, bf16[64,128,128]{2,1,0:T(8,128)(2,1)}, u32[]{:S(2)}, u32[]{:S(2)}) %collective-permute-start.7) | collective-permute-done | bytes 2097184 | tf_op jit(solution)/shard_map/ppermute | solution.py:126
  248.2 16.7 %shard_map.38 = bf16[112,128,128]{2,1,0:T(8,128)(2,1)} custom-call(s32[896]{0:T(1024)} %get-tuple-element.11.refs_0_, s32[1]{0:T(128)} %bitcast.1.refs_1_, bf16[64,128,128]{2,1,0:T(8,128)(2,1)} %copy-done, bf16[64,128,128]{2,1,0:T(8,128)(2,1)} %collective-permute-done.7.refs_3_, bf16[112,128,128]{2,1,0:T(8,128)(2,1)} %bitcast.21, ...), custom_call_target="tpu_custom_call" | custom-call | flops 536870912 | bytes 33554432 | tf_op jit(solution)/shard_map/pallas_call | solution.py:105
  (37 shorter events, 1.0 us)
Async XLA Ops:
  6.5 196.2 %all-gather.20.cloned.1.call-start = ((), (), s32[]{:S(2)}) async-start(), calls=%async_computation.5 | async-start | bytes 5505024 | tf_op jit(solution)/shard_map/all_gather | solution.py:130
  7.3 43.0 %copy-start.1 = (bf16[1,1,1,64,128,128]{5,4,3,2,1,0:T(8,128)(2,1)S(1)}, bf16[1,1,1,64,128,128]{5,4,3,2,1,0:T(8,128)(2,1)}, u32[]{:S(2)}) copy-start(bf16[1,1,1,64,128,128]{5,4,3,2,1,0:T(8,128)(2,1)} %param.3) | copy-start | bytes 6291460
  7.3 195.5 %all-gather.18.cloned.1.call-start = ((), (), s32[]{:S(2)}) async-start(), calls=%async_computation.4 | async-start | bytes 6291456 | tf_op jit(solution)/shard_map/all_gather | solution.py:130
  8.0 194.8 %all-gather.16.cloned.1.call-start = ((), (), s32[]{:S(2)}) async-start(), calls=%async_computation.3 | async-start | bytes 5505024 | tf_op jit(solution)/shard_map/all_gather | solution.py:130
  8.1 42.2 %collective-permute-start.6 = (bf16[56,128,128]{2,1,0:T(8,128)(2,1)}, bf16[56,128,128]{2,1,0:T(8,128)(2,1)}, u32[]{:S(2)}, u32[]{:S(2)}) collective-permute-start(bf16[56,128,128]{2,1,0:T(8,128)(2,1)} %bitcast.27), channel_id=1, source_target_pairs={{0,8},{8,0},{1,9},{9,1},{2,10},{10,2},{3,11},{11,3},{4,12},{12,4},... | collective-permute-start | bytes 5505032 | tf_op jit(solution)/shard_map/ppermute | solution.py:153
  50.2 152.5 %all-gather.12.cloned.1.call-start = ((), (), s32[]{:S(2)}) async-start(), calls=%async_computation.1 | async-start | bytes 6291456 | tf_op jit(solution)/shard_map/all_gather | solution.py:130
  50.3 47.9 %collective-permute-start.3 = (bf16[64,128,128]{2,1,0:T(8,128)(2,1)S(1)}, bf16[64,128,128]{2,1,0:T(8,128)(2,1)}, u32[]{:S(2)}, u32[]{:S(2)}) collective-permute-start(bf16[64,128,128]{2,1,0:T(8,128)(2,1)S(1)} %bitcast.24), channel_id=1, source_target_pairs={{2,0},{4,2},{6,4},{3,1},{5,3},{7,5},{10,8},{12,10},{14,12},{11,9},... | collective-permute-start | bytes 6291464 | tf_op jit(solution)/shard_map/ppermute | solution.py:181
  98.2 104.6 %all-gather.10.cloned.1.call-start = ((), (), s32[]{:S(2)}) async-start(), calls=%async_computation | async-start | bytes 6291456 | tf_op jit(solution)/shard_map/all_gather | solution.py:130
  98.3 45.3 %collective-permute-start = (bf16[64,128,128]{2,1,0:T(8,128)(2,1)S(1)}, bf16[64,128,128]{2,1,0:T(8,128)(2,1)}, u32[]{:S(2)}, u32[]{:S(2)}) collective-permute-start(bf16[64,128,128]{2,1,0:T(8,128)(2,1)S(1)} %bitcast.25), channel_id=1, source_target_pairs={{0,2},{2,4},{4,6},{1,3},{3,5},{5,7},{8,10},{10,12},{12,14},{9,11},... | collective-permute-start | bytes 6291464 | tf_op jit(solution)/shard_map/ppermute | solution.py:180
  143.6 70.4 %all-gather.14.cloned.1.call-start = ((), (), s32[]{:S(2)}) async-start(), calls=%async_computation.2 | async-start | bytes 6291456 | tf_op jit(solution)/shard_map/all_gather | solution.py:130
  143.6 47.0 %collective-permute-start.4 = (bf16[64,128,128]{2,1,0:T(8,128)(2,1)}, bf16[64,128,128]{2,1,0:T(8,128)(2,1)S(1)}, u32[]{:S(2)}, u32[]{:S(2)}) collective-permute-start(bf16[64,128,128]{2,1,0:T(8,128)(2,1)} %collective-permute-done.3), channel_id=1, source_target_pairs={{2,0},{4,2},{3,1},{5,3},{10,8},{12,10},{11,9},{13,11},{18,16},{20,... | collective-permute-start | bytes 6291464 | tf_op jit(solution)/shard_map/ppermute | solution.py:183
  144.9 45.7 %collective-permute-start.1 = (bf16[64,128,128]{2,1,0:T(8,128)(2,1)}, bf16[64,128,128]{2,1,0:T(8,128)(2,1)}, u32[]{:S(2)}, u32[]{:S(2)}) collective-permute-start(bf16[64,128,128]{2,1,0:T(8,128)(2,1)} %collective-permute-done), channel_id=1, source_target_pairs={{2,4},{4,6},{3,5},{5,7},{10,12},{12,14},{11,13},{13,15},{18,20},{2... | collective-permute-start | bytes 6291464 | tf_op jit(solution)/shard_map/ppermute | solution.py:182
  192.1 3.5 %copy-start.2 = (s32[1,1,1,7,3,64]{5,2,4,3,1,0:T(1,128)S(1)}, s32[1,1,1,7,3,64]{5,2,4,3,1,0:T(1,128)}, u32[]{:S(2)}) copy-start(s32[1,1,1,7,3,64]{5,2,4,3,1,0:T(1,128)} %param.5) | copy-start | bytes 16132
  192.1 45.0 %collective-permute-start.5 = (bf16[64,128,128]{2,1,0:T(8,128)(2,1)S(1)}, bf16[64,128,128]{2,1,0:T(8,128)(2,1)}, u32[]{:S(2)}, u32[]{:S(2)}) collective-permute-start(bf16[64,128,128]{2,1,0:T(8,128)(2,1)S(1)} %collective-permute-done.4), channel_id=1, source_target_pairs={{2,0},{3,1},{10,8},{11,9},{18,16},{19,17},{26,24},{27,25}} | collective-permute-start | bytes 6291464 | tf_op jit(solution)/shard_map/ppermute | solution.py:185
  193.4 43.7 %collective-permute-start.2 = (bf16[64,128,128]{2,1,0:T(8,128)(2,1)}, bf16[64,128,128]{2,1,0:T(8,128)(2,1)}, u32[]{:S(2)}, u32[]{:S(2)}) collective-permute-start(bf16[64,128,128]{2,1,0:T(8,128)(2,1)} %collective-permute-done.1), channel_id=1, source_target_pairs={{4,6},{5,7},{12,14},{13,15},{20,22},{21,23},{28,30},{29,31}} | collective-permute-start | bytes 6291464 | tf_op jit(solution)/shard_map/ppermute | solution.py:184
  239.0 9.2 %copy-start = (bf16[64,128,128]{2,1,0:T(8,128)(2,1)}, bf16[64,128,128]{2,1,0:T(8,128)(2,1)S(1)}, u32[]{:S(2)}) copy-start(bf16[64,128,128]{2,1,0:T(8,128)(2,1)S(1)} %broadcast_select_fusion.refs_2_) | copy-start | bytes 6291460
  239.0 9.2 %collective-permute-start.7 = (bf16[64,128,128]{2,1,0:T(8,128)(2,1)S(1)}, bf16[64,128,128]{2,1,0:T(8,128)(2,1)}, u32[]{:S(2)}, u32[]{:S(2)}) collective-permute-start(bf16[64,128,128]{2,1,0:T(8,128)(2,1)S(1)} %broadcast_select_fusion.refs_2_), channel_id=1, source_target_pairs={{0,1},{1,0},{2,3},{3,2},{4,5},{5,4},{6,7},{7,6},{8,9},{9,8},{10,11... | collective-permute-start | bytes 6291464 | tf_op jit(solution)/shard_map/ppermute | solution.py:126
Sparse Core Ops, SparseCore 0:
  8.9 15.3 all-gather.19
  25.8 14.8 all-gather.17
  50.4 15.3 all-gather.15
  98.3 15.6 all-gather.11
  143.7 17.9 all-gather.9
  192.3 21.6 all-gather.13

commit v4 on v3

--- a/solution.py
+++ b/solution.py
@@ -8,7 +8,7 @@
 from jax.sharding import PartitionSpec as P
 
 NBQ = 32
-UNROLL = 4
+UNROLL = 8
 
 
 def adding_kernel(shape, left_counts, right_count, given_count, *refs):
@@ -151,8 +151,9 @@
     first = layers * slots + given_first
     if row_count == 2:
         met = lax.ppermute(right_own, "row", [(0, 1), (1, 0)])
-        rights = [paired(right_own), paired(met)]
-        second = (((given_second // part) ^ lax.axis_index("row")) * 2 + layers) * part + given_second % part
+        rights = [right_own, met, swapped(right_own), swapped(met)]
+        nearer = (given_second // part) ^ lax.axis_index("row")
+        second = ((layers ^ layer) * 2 + nearer) * part + given_second % part
     else:
         rights = [paired(lax.all_gather(right_own, "row", axis=0, tiled=True))]
         second = layers * (row_count * part) + given_second
@@ -179,16 +180,16 @@
     assert columns == 4
     rising = lax.ppermute(own, "col", [(0, 1), (1, 2), (2, 3)])
     falling = lax.ppermute(own, "col", [(1, 0), (2, 1), (3, 2)])
+    rising, falling, rights = lax.optimization_barrier((rising, falling, rights))
     rising_two = lax.ppermute(rising, "col", [(1, 2), (2, 3)])
     falling_two = lax.ppermute(falling, "col", [(1, 0), (2, 1)])
-    rising_three = lax.ppermute(rising_two, "col", [(2, 3)])
-    falling_three = lax.ppermute(falling_two, "col", [(1, 0)])
+    rising_two, falling_two = lax.optimization_barrier((rising_two, falling_two))
     two = jnp.where(place > 1, rising_two, falling_two)
+    three = lax.ppermute(two, "col", [(2, 3), (1, 0)])
     panels = [[paired(value)] for value in (own, rising, falling, two)]
     classes = kinds(0, jnp.where(place > 0, 3, -1), jnp.where(place < 3, 1, -1), 2)
     total = add_products(packed, classes, columns, panels, rights, [], half, False)
-    rising_three, falling_three, total = lax.optimization_barrier((rising_three, falling_three, total))
-    three = jnp.where(place > 1, rising_three, falling_three)
+    three, total = lax.optimization_barrier((three, total))
     classes = kinds(jnp.where(place == 3, 1, jnp.where(place == 0, 3, -1)))
     packed_far = jnp.where(packed >= 0, packed ^ (layer * slots << 10), -1)
     total = add_products(packed_far, classes, columns, [[three, swapped(three)]], rights, [total], half, True)

time: 276 us -> 193 us (0.70); the launches traced: 272 us -> 193 us
  waiting for transfers between devices: 190 us -> 114 us
  Pallas kernels: 38.2 us -> 31.4 us
  local copies, waits for them, and re-layouts: 0.64 us -> 5.74 us
    ppermute x1, waiting for transfers between devices: 46.6 us -> 5.96 us  [local(): falling = lax.ppermute(own, 'col', [(1, 0), (2, 1), (3, 2)])]
    ppermute x1, waiting for transfers between devices: 41.1 us -> 0.89 us  [local(): rising = lax.ppermute(own, 'col', [(0, 1), (1, 2), (2, 3)])]
    ppermute x2 -> x1, waiting for transfers between devices: 1.74 us -> 15.2 us  [local(): three = lax.ppermute(two, 'col', [(2, 3), (1, 0)])]
    ppermute x1, waiting for transfers between devices: 40.1 us -> 31.7 us  [local(): met = lax.ppermute(right_own, 'row', [(0, 1), (1, 0)])]
    pallas_call x2, Pallas kernels: 38.2 us -> 31.4 us  [add_products(): pl.pallas_call(functools.partial(adding_kernel, shape, [len(panel) for pa...]
    ppermute x1, waiting for transfers between devices: 43.7 us -> 49.5 us  [local(): falling_two = lax.ppermute(falling, 'col', [(1, 0), (2, 1)])]
    all_gather x6 -> x4, waiting for transfers between devices: 11.2 us -> 5.67 us  [paired(): return lax.all_gather(value, 'dep', axis=0, tiled=True)]
    unnamed x7 -> x11, local copies, waits for them, and re-layouts: 0.02 us -> 5.05 us
  transfers between devices with their start and end apart: 14 -> 13, of which waited for: 7 -> 7; matrix products, arithmetic and copies ran while one was open for 1% -> 3% of each run, Pallas kernels for 8% -> 9%
where the time goes in v4:
time: 193 us
  waiting for transfers between devices  114 us (59%)
  Pallas kernels  31.4 us (16%)
  starting transfers between devices  18.9 us (10%)
  between operations  13.3 us (7%)
  local copies, waits for them, and re-layouts  5.74 us (3%)
  blocking collectives  4.56 us (2%)
  other arithmetic  4.36 us (2%)
    ppermute x1, waiting for transfers between devices, local(): falling_two = lax.ppermute(falling, 'col', [(1, 0), (2, 1)])  49.5 us
    ppermute x1, waiting for transfers between devices, local(): met = lax.ppermute(right_own, 'row', [(0, 1), (1, 0)])  31.7 us
    pallas_call x2, Pallas kernels, add_products(): pl.pallas_call(functools.partial(adding_kernel, shape, [len(panel) for pa...  31.4 us
    ppermute x1, waiting for transfers between devices, local(): three = lax.ppermute(two, 'col', [(2, 3), (1, 0)])  15.2 us
    ppermute x3, starting transfers between devices, swapped(): return lax.ppermute(value, 'dep', [(0, 1), (1, 0)])  6.75 us
    ppermute x1, waiting for transfers between devices, local(): falling = lax.ppermute(own, 'col', [(1, 0), (2, 1), (3, 2)])  5.96 us
    all_gather x4, waiting for transfers between devices, paired(): return lax.all_gather(value, 'dep', axis=0, tiled=True)  5.67 us
    ppermute x1, starting transfers between devices, local(): rising = lax.ppermute(own, 'col', [(0, 1), (1, 2), (2, 3)])  5.3 us
  transfers between devices with their start and end apart: 13, of which 7 were waited for; matrix products, arithmetic and copies ran while one was open for 3% of the time, Pallas kernels for 9%

profile of v4, /device:TPU:1, one launch (start us, length us, event | category | flops | bytes accessed | tf_op | source)
XLA Modules:
  0.0 192.6 jit_solution(14693175597100095557)
XLA Ops:
  7.3 0.7 copy-done.1
  8.0 2.0 %collective-permute-start.2 = (bf16[56,128,128]{2,1,0:T(8,128)(2,1)S(1)}, bf16[56,128,128]{2,1,0:T(8,128)(2,1)}, u32[]{:S(2)}, u32[]{:S(2)}) collective-permute-start(bf16[56,128,128]{2,1,0:T(8,128)(2,1)S(1)} %bitcast.20), channel_id=1, source_target_pairs={{0,8},{8,0},{1,9},{9,1},{2,10},{10,2},{3,11},{11,3},{4,12},{12,4},... | collective-permute-start | bytes 5505032 | tf_op jit(solution)/shard_map/ppermute | solution.py:153
  10.1 1.3 collective-permute-start.1
  11.4 5.3 %collective-permute-start = (bf16[64,128,128]{2,1,0:T(8,128)(2,1)}, bf16[64,128,128]{2,1,0:T(8,128)(2,1)}, u32[]{:S(2)}, u32[]{:S(2)}) collective-permute-start(bf16[64,128,128]{2,1,0:T(8,128)(2,1)} %bitcast.25), channel_id=1, source_target_pairs={{0,2},{2,4},{4,6},{1,3},{3,5},{5,7},{8,10},{10,12},{12,14},{9,11},... | collective-permute-start | bytes 6291464 | tf_op jit(solution)/shard_map/ppermute | solution.py:181
  16.7 1.5 collective-permute-start.3
  18.2 31.7 %collective-permute-done.2.refs_7_.refs_5_ = bf16[56,128,128]{2,1,0:T(8,128)(2,1)} collective-permute-done((bf16[56,128,128]{2,1,0:T(8,128)(2,1)S(1)}, bf16[56,128,128]{2,1,0:T(8,128)(2,1)}, u32[]{:S(2)}, u32[]{:S(2)}) %collective-permute-start.2) | collective-permute-done | bytes 1835040 | tf_op jit(solution)/shard_map/ppermute | solution.py:153
  49.9 1.2 collective-permute-start.4
  51.2 1.3 copy-done.2
  52.5 6.0 %collective-permute-done.1 = bf16[64,128,128]{2,1,0:T(8,128)(2,1)} collective-permute-done((bf16[64,128,128]{2,1,0:T(8,128)(2,1)}, bf16[64,128,128]{2,1,0:T(8,128)(2,1)}, u32[]{:S(2)}, u32[]{:S(2)}) %collective-permute-start.1) | collective-permute-done | bytes 2097184 | tf_op jit(solution)/shard_map/ppermute | solution.py:182
  58.5 0.9 collective-permute-done
  60.2 0.8 collective-permute-start.5
  61.0 1.3 collective-permute-start.6
  62.3 49.5 %collective-permute-done.6 = bf16[64,128,128]{2,1,0:T(8,128)(2,1)} collective-permute-done((bf16[64,128,128]{2,1,0:T(8,128)(2,1)}, bf16[64,128,128]{2,1,0:T(8,128)(2,1)}, u32[]{:S(2)}, u32[]{:S(2)}) %collective-permute-start.6) | collective-permute-done | bytes 2097184 | tf_op jit(solution)/shard_map/ppermute | solution.py:185
  111.8 3.1 %broadcast_select_fusion = bf16[64,128,128]{2,1,0:T(8,128)(2,1)} fusion(bf16[64,128,128]{2,1,0:T(8,128)(2,1)S(1)} %collective-permute-done.5, bf16[64,128,128]{2,1,0:T(8,128)(2,1)} %collective-permute-done.6, pred[]{:T(512)S(6)} %gt.6), kind=kLoop, calls=%fused_computation | loop fusion | flops 1048576 | bytes 6291457 | tf_op jit(solution)/shard_map/jit(_where)/select_n | solution.py:187
  115.0 1.6 copy-done
  116.5 1.3 collective-permute-start.7
  118.2 4.6 %all-gather = s32[1,1,1,14,3,64]{5,2,4,1,0,3:T(1,128)S(1)} all-gather(s32[1,1,1,7,3,64]{5,2,4,1,0,3:T(1,128)S(1)} %bitcast.27), channel_id=2, replica_groups=mesh['grp'=2,'row'=2,'col'=4,'dep'=2] {'dep'}, dimensions={3}, use_global_device_ids=true | all-gather | bytes 16128 | tf_op jit(solution)/shard_map/all_gather | solution.py:130
  124.4 5.7 %all-gather.11.cloned.1.call-done.refs_5_ = bf16[128,128,128]{2,1,0:T(8,128)(2,1)} async-done(((bf16[64,128,128]{2,1,0:T(8,128)(2,1)}), bf16[128,128,128]{2,1,0:T(8,128)(2,1)}) %all-gather.11.cloned.1.call-update) | async-done | bytes 4194320 | tf_op jit(solution)/shard_map/all_gather | solution.py:130
  130.0 17.3 %shard_map.37.refs_8_ = f32[113,128,128]{2,1,0:T(8,128)} custom-call(s32[896]{0:T(1024)} %get-tuple-element.26.refs_0_, s32[4]{0:T(128)} %pad_add_fusion.refs_1_, bf16[128,128,128]{2,1,0:T(8,128)(2,1)} %bitcast.22, bf16[128,128,128]{2,1,0:T(8,128)(2,1)} %all-gather.7.cloned.1.call-done.refs_3_, bf16[128,128,128]{2,1,0:T(8,128)(2,1)} %all-gather.9.cloned.1.call-done.refs_4_, ...), custom_call_target="tpu_custom_call" | custom-call | flops 2147483648 | bytes 33554432 | tf_op jit(solution)/shard_map/pallas_call | solution.py:105
  147.4 15.2 %collective-permute-done.7.refs_2_ = bf16[64,128,128]{2,1,0:T(8,128)(2,1)} collective-permute-done((bf16[64,128,128]{2,1,0:T(8,128)(2,1)S(1)}, bf16[64,128,128]{2,1,0:T(8,128)(2,1)}, u32[]{:S(2)}, u32[]{:S(2)}) %collective-permute-start.7) | collective-permute-done | bytes 2097184 | tf_op jit(solution)/shard_map/ppermute | solution.py:188
  162.6 4.0 %collective-permute-start.8 = (bf16[64,128,128]{2,1,0:T(8,128)(2,1)}, bf16[64,128,128]{2,1,0:T(8,128)(2,1)S(1)}, u32[]{:S(2)}, u32[]{:S(2)}) collective-permute-start(bf16[64,128,128]{2,1,0:T(8,128)(2,1)} %collective-permute-done.7.refs_2_), channel_id=1, source_target_pairs={{0,1},{1,0},{2,3},{3,2},{4,5},{5,4},{6,7},{7,6},{8,9},{9,8},{10,11... | collective-permute-start | bytes 6291464 | tf_op jit(solution)/shard_map/ppermute | solution.py:126
  166.6 4.0 %collective-permute-done.8.refs_3_ = bf16[64,128,128]{2,1,0:T(8,128)(2,1)S(1)} collective-permute-done((bf16[64,128,128]{2,1,0:T(8,128)(2,1)}, bf16[64,128,128]{2,1,0:T(8,128)(2,1)S(1)}, u32[]{:S(2)}, u32[]{:S(2)}) %collective-permute-start.8) | collective-permute-done | bytes 2097184 | tf_op jit(solution)/shard_map/ppermute | solution.py:126
  170.6 1.4 copy-done.3
  172.0 14.1 %shard_map.38 = bf16[112,128,128]{2,1,0:T(8,128)(2,1)} custom-call(s32[896]{0:T(1024)} %get-tuple-element.25.refs_0_, s32[1]{0:T(128)} %bitcast.1.refs_1_, bf16[64,128,128]{2,1,0:T(8,128)(2,1)} %collective-permute-done.7.refs_2_, bf16[64,128,128]{2,1,0:T(8,128)(2,1)} %copy-done.3, bf16[56,128,128]{2,1,0:T(8,128)(2,1)} %bitcast.19, ...), custom_call_target="tpu_custom_call" | custom-call | flops 536870912 | bytes 33554432 | tf_op jit(solution)/shard_map/pallas_call | solution.py:105
  (37 shorter events, 3.5 us)
Async XLA Ops:
  6.5 1.5 copy-start.1
  6.5 117.8 %all-gather.13.cloned.1.call-start = ((), (), s32[]{:S(2)}) async-start(), calls=%async_computation.3 | async-start | bytes 6291456 | tf_op jit(solution)/shard_map/all_gather | solution.py:130
  7.3 117.1 %all-gather.7.cloned.1.call-start = ((), (), s32[]{:S(2)}) async-start(), calls=%async_computation | async-start | bytes 6291456 | tf_op jit(solution)/shard_map/all_gather | solution.py:130
  8.0 41.9 %collective-permute-start.2 = (bf16[56,128,128]{2,1,0:T(8,128)(2,1)S(1)}, bf16[56,128,128]{2,1,0:T(8,128)(2,1)}, u32[]{:S(2)}, u32[]{:S(2)}) collective-permute-start(bf16[56,128,128]{2,1,0:T(8,128)(2,1)S(1)} %bitcast.20), channel_id=1, source_target_pairs={{0,8},{8,0},{1,9},{9,1},{2,10},{10,2},{3,11},{11,3},{4,12},{12,4},... | collective-permute-start | bytes 5505032 | tf_op jit(solution)/shard_map/ppermute | solution.py:153
  10.1 48.4 %collective-permute-start.1 = (bf16[64,128,128]{2,1,0:T(8,128)(2,1)}, bf16[64,128,128]{2,1,0:T(8,128)(2,1)}, u32[]{:S(2)}, u32[]{:S(2)}) collective-permute-start(bf16[64,128,128]{2,1,0:T(8,128)(2,1)} %bitcast.24), channel_id=1, source_target_pairs={{2,0},{4,2},{6,4},{3,1},{5,3},{7,5},{10,8},{12,10},{14,12},{11,9},... | collective-permute-start | bytes 6291464 | tf_op jit(solution)/shard_map/ppermute | solution.py:182
  11.4 48.0 %collective-permute-start = (bf16[64,128,128]{2,1,0:T(8,128)(2,1)}, bf16[64,128,128]{2,1,0:T(8,128)(2,1)}, u32[]{:S(2)}, u32[]{:S(2)}) collective-permute-start(bf16[64,128,128]{2,1,0:T(8,128)(2,1)} %bitcast.25), channel_id=1, source_target_pairs={{0,2},{2,4},{4,6},{1,3},{3,5},{5,7},{8,10},{10,12},{12,14},{9,11},... | collective-permute-start | bytes 6291464 | tf_op jit(solution)/shard_map/ppermute | solution.py:181
  16.7 34.5 %collective-permute-start.3 = (bf16[56,128,128]{2,1,0:T(8,128)(2,1)S(1)}, bf16[56,128,128]{2,1,0:T(8,128)(2,1)S(1)}, u32[]{:S(2)}, u32[]{:S(2)}) collective-permute-start(bf16[56,128,128]{2,1,0:T(8,128)(2,1)S(1)} %bitcast.21), channel_id=1, source_target_pairs={{0,1},{1,0},{2,3},{3,2},{4,5},{5,4},{6,7},{7,6},{8,9},{9,8},{10,11... | collective-permute-start | bytes 5505032 | tf_op jit(solution)/shard_map/ppermute | solution.py:126
  49.9 9.4 %collective-permute-start.4 = (bf16[56,128,128]{2,1,0:T(8,128)(2,1)}, bf16[56,128,128]{2,1,0:T(8,128)(2,1)}, u32[]{:S(2)}, u32[]{:S(2)}) collective-permute-start(bf16[56,128,128]{2,1,0:T(8,128)(2,1)} %collective-permute-done.2.refs_7_.refs_5_), channel_id=1, source_target_pairs={{0,1},{1,0},{2,3},{3,2},{4,5},{5,4},{6,7},{7,6},{8,9},{9,8},{10,11... | collective-permute-start | bytes 5505032 | tf_op jit(solution)/shard_map/ppermute | solution.py:126
  51.1 1.3 copy-start.2
  59.4 65.0 %all-gather.9.cloned.1.call-start = ((), (), s32[]{:S(2)}) async-start(), calls=%async_computation.1 | async-start | bytes 6291456 | tf_op jit(solution)/shard_map/all_gather | solution.py:130
  60.1 69.9 %all-gather.11.cloned.1.call-start = ((), (), s32[]{:S(2)}) async-start(), calls=%async_computation.2 | async-start | bytes 6291456 | tf_op jit(solution)/shard_map/all_gather | solution.py:130
  60.2 2.1 %collective-permute-start.5 = (bf16[64,128,128]{2,1,0:T(8,128)(2,1)}, bf16[64,128,128]{2,1,0:T(8,128)(2,1)S(1)}, u32[]{:S(2)}, u32[]{:S(2)}) collective-permute-start(bf16[64,128,128]{2,1,0:T(8,128)(2,1)} %collective-permute-done), channel_id=1, source_target_pairs={{2,4},{4,6},{3,5},{5,7},{10,12},{12,14},{11,13},{13,15},{18,20},{2... | collective-permute-start | bytes 6291464 | tf_op jit(solution)/shard_map/ppermute | solution.py:184
  61.0 50.9 %collective-permute-start.6 = (bf16[64,128,128]{2,1,0:T(8,128)(2,1)}, bf16[64,128,128]{2,1,0:T(8,128)(2,1)}, u32[]{:S(2)}, u32[]{:S(2)}) collective-permute-start(bf16[64,128,128]{2,1,0:T(8,128)(2,1)} %collective-permute-done.1), channel_id=1, source_target_pairs={{2,0},{4,2},{3,1},{5,3},{10,8},{12,10},{11,9},{13,11},{18,16},{20,... | collective-permute-start | bytes 6291464 | tf_op jit(solution)/shard_map/ppermute | solution.py:185
  115.0 1.6 copy-start
  115.0 3.2 %copy-start.4 = (s32[1,1,1,7,3,64]{5,2,4,3,1,0:T(1,128)S(1)}, s32[1,1,1,7,3,64]{5,2,4,3,1,0:T(1,128)}, u32[]{:S(2)}) copy-start(s32[1,1,1,7,3,64]{5,2,4,3,1,0:T(1,128)} %param.5) | copy-start | bytes 16132
  116.5 46.0 %collective-permute-start.7 = (bf16[64,128,128]{2,1,0:T(8,128)(2,1)S(1)}, bf16[64,128,128]{2,1,0:T(8,128)(2,1)}, u32[]{:S(2)}, u32[]{:S(2)}) collective-permute-start(bf16[64,128,128]{2,1,0:T(8,128)(2,1)S(1)} %copy-done), channel_id=1, source_target_pairs={{4,6},{2,0},{5,7},{3,1},{12,14},{10,8},{13,15},{11,9},{20,22},{18,... | collective-permute-start | bytes 6291464 | tf_op jit(solution)/shard_map/ppermute | solution.py:188
  162.6 8.0 %collective-permute-start.8 = (bf16[64,128,128]{2,1,0:T(8,128)(2,1)}, bf16[64,128,128]{2,1,0:T(8,128)(2,1)S(1)}, u32[]{:S(2)}, u32[]{:S(2)}) collective-permute-start(bf16[64,128,128]{2,1,0:T(8,128)(2,1)} %collective-permute-done.7.refs_2_), channel_id=1, source_target_pairs={{0,1},{1,0},{2,3},{3,2},{4,5},{5,4},{6,7},{7,6},{8,9},{9,8},{10,11... | collective-permute-start | bytes 6291464 | tf_op jit(solution)/shard_map/ppermute | solution.py:126
  170.6 1.4 copy-start.3
Sparse Core Ops, SparseCore 0:
  8.9 16.1 all-gather.12
  59.5 18.0 all-gather.6
  79.1 14.8 all-gather.8
  115.1 14.8 all-gather.10

commit v5 on v0

v5 whole, which is shorter than its diff:
```python
import functools

import jax
import jax.numpy as jnp
from jax import lax
from jax.experimental import pallas as pl
from jax.experimental.pallas import tpu as pltpu
from jax.sharding import PartitionSpec as P

NBQ = 32
NEAR = 0.75
DIRECT = 0.65


def chosen_products(packed, classes, panels, todo, shape, unroll, spare):
    step_count, columns, slots = shape
    count = jnp.int32(0)
    for panel in range(panels):
        kind = classes[panel]
        for extra in range(-(-step_count // columns)):
            step = lax.rem(kind + step_count // 2, columns) + extra * columns
            groups = jnp.where((kind >= 0) & (step < step_count), slots // 8, 0)
            for layer in range(2):
                base = (layer * step_count + step) * slots

                def keep(group, count):
                    for lane in range(8):
                        entry = packed[base + group * 8 + lane]
                        todo[count] = entry + (panel * 2 * slots << 10)
                        count += (entry >= 0).astype(jnp.int32)
                    return count

                count = lax.fori_loop(0, groups, keep, count)
    for extra in range(unroll - 1):
        todo[count + extra] = jnp.int32(spare)
    return count


def add_chosen(todo, count, left, right, work, unroll):
    rows, width = work.shape[1:]

    def several(group, carry):
        entries = [todo[group * unroll + lane] for lane in range(unroll)]
        products = []
        for entry in entries:
            first = pl.multiple_of(((entry >> 10) & 1023) * rows, rows)
            second = pl.multiple_of((entry >> 20) * width, width)
            products.append(
                jnp.dot(left[pl.ds(first, rows)], right[pl.ds(second, width)], preferred_element_type=jnp.float32)
            )
        for entry, product in zip(entries, products):
            work[entry & 1023] += product
        return carry

    lax.fori_loop(0, (count + unroll - 1) // unroll, several, jnp.int32(0))


def sum_kernel(groups, right_spans, has_given, shape, half, operand_count, layer_at, *refs):
    packed, classes, refs = refs[0], refs[1], refs[2:]
    operands, refs = refs[:operand_count], refs[operand_count:]
    out, refs = refs[0], refs[1:]
    works, lefts = refs[: len(groups)], refs[len(groups) : 2 * len(groups)]
    right, todo, sems, out_sem = refs[2 * len(groups) :]
    slots = shape[2]
    other = 1 - classes[layer_at]
    copies = []

    def plan(source, target, when):
        copies.append((pltpu.make_async_copy(source, target, sems.at[len(copies)]), when))

    any_class = classes[0]
    for at in range(1, layer_at):
        any_class = jnp.maximum(any_class, classes[at])
    start = 0
    for operand, first, size in right_spans:
        plan(operands[operand].at[pl.ds(first, size)], right.at[pl.ds(start, size)], any_class >= 0)
        start += size
    class_at = 0
    for (panels, rows), left in zip(groups, lefts):
        start, size = 0, slots * rows
        for panel, pieces in enumerate(panels):
            for operand, first, gathered in pieces:
                if gathered:
                    first = pl.multiple_of(first + other * gathered, 16)
                source = operands[operand].at[pl.ds(first, size)]
                plan(source, left.at[pl.ds(start, size)], classes[class_at + panel] >= 0)
                start += size
        class_at += len(panels)
    if has_given:
        plan(operands[operand_count - 1], works[0], None)
    for copy, when in copies:
        copy.start() if when is None else pl.when(when)(copy.start)
    for index, work in enumerate(works):
        if index > 0 or not has_given:
            work[...] = jnp.zeros_like(work)

    class_at = 0
    for index, ((panels, rows), work, left) in enumerate(zip(groups, works, lefts)):
        unroll = 16 if rows <= 64 else 8
        kinds = [classes[class_at + panel] for panel in range(len(panels))]
        class_at += len(panels)
        count = chosen_products(packed, kinds, len(panels), todo, shape, unroll, half)
        if index == 0:
            for copy, when in copies:
                copy.wait() if when is None else pl.when(when)(copy.wait)
        add_chosen(todo, count, left, right, work, unroll)
    if out.dtype == works[0].dtype:
        copy = pltpu.make_async_copy(works[0], out, out_sem)
        copy.start()
        copy.wait()
    else:
        start = 0
        for (panels, rows), work in zip(groups, works):
            out[:, start : start + rows] = work[:half].astype(out.dtype)
            start += rows


def flat(value):
    return value.reshape(-1, value.shape[-1])


def product_sums(packed, classes, layer, shape, groups, rights, given, half, finished):
    step_count, columns, slots = shape
    width = rights[0][0].shape[-1]
    operands, known = [], []

    def number(value):
        for index, other in enumerate(known):
            if other is value:
                return index
        known.append(value)
        operands.append(flat(value))
        return len(operands) - 1

    right_spans = [(number(value), first, size) for value, first, size in rights]
    numbered = [
        ([[(number(value), first, gathered) for value, first, gathered in panel] for panel in panels], rows)
        for panels, rows in groups
    ]
    if given is not None:
        operands.append(given)
    right_rows = sum(size for _, _, size in rights)
    most = max(len(panels) for panels, _ in groups)
    assert right_rows <= 1024 * width and most * 2 * slots <= 1024 and half < 1024 and slots % 8 == 0
    anywhere = pl.BlockSpec(memory_space=pl.ANY)
    in_scalar = pl.BlockSpec(memory_space=pltpu.SMEM)
    all_rows = sum(rows for _, rows in groups)
    out_shape = (
        jax.ShapeDtypeStruct((half, all_rows, width), jnp.bfloat16)
        if finished
        else jax.ShapeDtypeStruct((half + 1, all_rows, width), jnp.float32)
    )
    copy_count = len(rights) + sum(len(panel) for panels, _ in groups for panel in panels) + 1
    scalars = jnp.stack([jnp.asarray(value, jnp.int32) for value in [*classes, layer]])
    return pl.pallas_call(
        functools.partial(
            sum_kernel, numbered, right_spans, given is not None, shape, half, len(operands), len(classes)
        ),
        out_shape=out_shape,
        in_specs=[in_scalar, in_scalar] + [anywhere] * len(operands),
        out_specs=pl.BlockSpec(memory_space=pltpu.VMEM) if finished else anywhere,
        scratch_shapes=[pltpu.VMEM((half + 1, rows, width), jnp.float32) for _, rows in groups]
        + [pltpu.VMEM((len(panels) * 2 * slots * rows, width), jnp.bfloat16) for panels, rows in groups]
        + [
            pltpu.VMEM((right_rows, width), jnp.bfloat16),
            pltpu.SMEM((most * 4 * slots + 16,), jnp.int32),
            pltpu.SemaphoreType.DMA((copy_count,)),
            pltpu.SemaphoreType.DMA,
        ],
        compiler_params=pltpu.CompilerParams(vmem_limit_bytes=48 << 20),
        cost_estimate=pl.CostEstimate(flops=1, bytes_accessed=1, transcendentals=0),
    )(packed, scalars, *operands)


def place_rows_kernel(first, rows, takes, block, received, out, sem):
    del block

    @pl.when(takes[0] > 0)
    def _():
        copy = pltpu.make_async_copy(received, out.at[:, pl.ds(first, rows)], sem)
        copy.start()
        copy.wait()


def place_rows(takes, block, received, first):
    anywhere = pl.BlockSpec(memory_space=pl.ANY)
    return pl.pallas_call(
        functools.partial(place_rows_kernel, first, received.shape[1]),
        out_shape=jax.ShapeDtypeStruct(block.shape, block.dtype),
        in_specs=[pl.BlockSpec(memory_space=pltpu.SMEM), anywhere, anywhere],
        out_specs=anywhere,
        scratch_shapes=[pltpu.SemaphoreType.DMA],
        input_output_aliases={1: 0},
    )(takes.astype(jnp.int32).reshape(1), block, received)


def swapped(value):
    return lax.ppermute(value, "dep", [(0, 1), (1, 0)])


def paired(value):
    return lax.all_gather(value, "dep", axis=0, tiled=True)


def packed_lists(step_lists, layer, half, right_place):
    step_count, _, slots = step_lists.shape
    both = paired(step_lists).reshape(2, step_count, 3, slots)
    both = jnp.where(layer > 0, both[::-1], both)
    result = both[:, :, 2] - layer * half
    wanted = (result >= 0) & (result < half)
    layers = jnp.arange(2, dtype=jnp.int32)[:, None, None]
    packed = right_place(both[:, :, 1], layers) << 20 | (layers * slots + both[:, :, 0]) << 10 | result
    return jnp.where(wanted, packed, -1).reshape(-1)


def ring(left_blocks, right_blocks, triples, half):
    own, right_own, step_lists = left_blocks[0, 0, 0], right_blocks[0, 0, 0], triples[0, 0, 0]
    slots, rows = own.shape[0], own.shape[1]
    columns, layer = lax.axis_size("col"), lax.axis_index("dep")
    gathered = lax.all_gather(right_own, "row", axis=0, tiled=True)
    right_slots = gathered.shape[0]
    packed = packed_lists(step_lists, layer, half, lambda slot, layers: layers * right_slots + slot)
    rights = [(value, 0, right_slots * rows) for value in (gathered, swapped(gathered))]
    shape = (step_lists.shape[0], columns, slots)
    rising, falling, total = own, own, None
    size = slots * rows
    panels, classes = [[(own, 0, 0), (paired(own), 0, size)]], [0]
    reach = step_lists.shape[0] // 2
    for distance in range(1, reach + 1):
        rising = lax.ppermute(rising, "col", [(i, (i + 1) % columns) for i in range(columns)])
        falling = lax.ppermute(falling, "col", [(i, (i - 1) % columns) for i in range(columns)])
        panels += [[(value, 0, 0), (paired(value), 0, size)] for value in (rising, falling)]
        classes += [columns - distance, distance]
        total = product_sums(
            packed, classes, layer, shape, [(panels, rows)], rights, total, half, distance == reach
        )
        panels, classes = [], []
    return total[None, None, None]


def line(left_blocks, right_blocks, triples, half):
    own, right_own, step_lists = left_blocks[0, 0, 0], right_blocks[0, 0, 0], triples[0, 0, 0]
    slots, rows, part = own.shape[0], own.shape[1], right_own.shape[0]
    columns, layer, place = lax.axis_size("col"), lax.axis_index("dep"), lax.axis_index("col")
    shape = (step_lists.shape[0], columns, slots)
    near = int(rows * NEAR) // 16 * 16
    far = rows - near
    cut = int(part * DIRECT)
    up, down = [(0, 1), (1, 2), (2, 3)], [(1, 0), (2, 1), (3, 2)]
    inward, across, outward = [(0, 1), (3, 2)], [(1, 2), (2, 1)], [(2, 3), (1, 0)]
    high, inner = place == 2, (place == 1) | (place == 2)

    own_near, own_far = own[:, :near], flat(own[:, near:])
    met = lax.ppermute(right_own, "row", [(0, 1), (1, 0)])
    rising = lax.ppermute(own_near, "col", up)
    falling = lax.ppermute(own_near, "col", down)
    near_other, far_other, right_pair = swapped(own_near), swapped(own_far), paired(right_own)

    def right_place(slot, layers):
        farther, within = (slot // part) ^ lax.axis_index("row"), slot % part
        first = jnp.where(within < cut, farther * cut + within, 2 * cut + farther * (part - cut) + within - cut)
        return layers * 2 * part + first

    packed = packed_lists(step_lists, layer, half, right_place)
    first_inward = jnp.concatenate([own_far, flat(right_own[:cut])])

    rising, falling, near_other, far_other, packed, first_inward = lax.optimization_barrier(
        (rising, falling, near_other, far_other, packed, first_inward)
    )
    rising_two = lax.ppermute(rising, "col", [(1, 2), (2, 3)])
    falling_two = lax.ppermute(falling, "col", [(2, 1), (1, 0)])
    end_far = lax.ppermute(first_inward, "col", inward)
    end_rest = lax.ppermute(jnp.concatenate([flat(right_own[cut:]), flat(met[cut:])]), "col", inward)
    end_packed = lax.ppermute(packed, "col", inward)
    met_pair, rising_pair, falling_pair = paired(met), paired(rising), paired(falling)

    rising_two, falling_two, end_far, end_packed, rising, falling = lax.optimization_barrier(
        (rising_two, falling_two, end_far, end_packed, rising, falling)
    )
    two = jnp.where(place > 1, rising_two, falling_two)
    near_size, far_size = slots * near, slots * far
    crossing = jnp.concatenate([own_far, end_far[:far_size]])
    two, crossing, end_right = lax.optimization_barrier((two, crossing, end_far[far_size:]))
    three = lax.ppermute(two, "col", outward)
    crossed = lax.ppermute(crossing, "col", across)
    end_met = lax.ppermute(end_right, "row", [(0, 1), (1, 0)])
    end_pair, two_pair = paired(end_far), paired(two)

    right_other = lax.dynamic_slice_in_dim(right_pair, (1 - layer) * part, part)
    met_other = lax.dynamic_slice_in_dim(met_pair, (1 - layer) * part, part)
    rights = []
    for nearer, farther in ((right_own, met), (right_other, met_other)):
        for first, size in ((0, cut), (cut, part - cut)):
            rights += [(nearer, first * rows, size * rows), (farther, first * rows, size * rows)]
    panels = [
        [(own_near, 0, 0), (near_other, 0, 0)],
        [(rising, 0, 0), (rising_pair, 0, near_size)],
        [(falling, 0, 0), (falling_pair, 0, near_size)],
    ]
    classes = [0, jnp.where(place > 0, 3, -1), jnp.where(place < 3, 1, -1)]
    total = product_sums(packed, classes, layer, shape, [(panels, near)], rights, None, half, False)

    crossed, end_met, end_rest, total = lax.optimization_barrier((crossed, end_met, end_rest, total))
    crossed_other, end_met_other, end_rest_other = swapped(crossed), swapped(end_met), swapped(end_rest)
    far_panels = [
        [(own_far, 0, 0), (far_other, 0, 0)],
        [(end_far, 0, 0), (end_pair, 0, end_far.shape[0])],
        [(crossed, 0, 0), (crossed_other, 0, 0)],
        [(crossed, far_size, 0), (crossed_other, far_size, 0)],
    ]
    end_other = lax.dynamic_slice_in_dim(end_pair, (1 - layer) * end_far.shape[0] + far_size, cut * rows)
    end_rights = [
        (end_far, far_size, cut * rows),
        (end_met, 0, cut * rows),
        (end_rest, 0, end_rest.shape[0]),
        (end_other, 0, cut * rows),
        (end_met_other, 0, cut * rows),
        (end_rest_other, 0, end_rest.shape[0]),
    ]
    classes = [jnp.where(high, 3, 1), 0, 2, jnp.where(high, 1, 3)]
    classes = [jnp.where(inner, kind, -1) for kind in classes]
    end_rows = product_sums(
        end_packed, classes, layer, shape, [(far_panels, far)], end_rights, None, half, True
    )

    end_rows, total, three, two_pair = lax.optimization_barrier((end_rows, total, three, two_pair))
    received = lax.ppermute(end_rows, "col", outward)
    near_panels = [
        [(two, 0, 0), (two_pair, 0, near_size)],
        [(three, 0, 0), (swapped(three), 0, 0)],
    ]
    classes = [2, jnp.where(place == 3, 1, jnp.where(place == 0, 3, -1))]
    far_classes = [0, jnp.where(high, 1, 3), jnp.where(high, 3, 1), 2]
    classes += [jnp.where(inner, kind, -1) for kind in far_classes]
    groups = [(near_panels, near), (far_panels, far)]
    block = product_sums(packed, classes, layer, shape, groups, rights, total, half, True)
    return place_rows(~inner, block, received, near)[None, None, None]


def local(left_blocks, right_blocks, triples):
    step_count = triples.shape[3]
    row_count, columns = lax.axis_size("row"), lax.axis_size("col")
    half = (2 * step_count - 2 + row_count) // row_count * NBQ // 2
    if columns >= step_count:
        return ring(left_blocks, right_blocks, triples, half)
    assert columns == 4 and row_count == 2
    return line(left_blocks, right_blocks, triples, half)


def solution(mesh):
    return jax.shard_map(
        local,
        mesh=mesh,
        in_specs=(
            P(("grp", "row"), "col", "dep", None, None, None),
            P(("grp", "row"), "col", "dep", None, None, None),
            P(("grp", "row"), "col", "dep", None, None, None),
        ),
        out_specs=P(("grp", "row"), "col", "dep", None, None, None),
        check_vma=False,
    )
```

time: 373 us -> 262 us (0.70)
  other arithmetic: 104 us -> 4.95 us
  Pallas kernels: 0 us -> 59.1 us
  local copies, waits for them, and re-layouts: 74.3 us -> 26.8 us
  matrix products: 34.2 us -> 0 us
  starting transfers between devices: 12.3 us -> 36.5 us
  waiting for transfers between devices: 133 us -> 116 us
    scatter-add x7 -> x0, other arithmetic: 96.5 us -> none  [add_products(): return accumulated.at[step_list[2]].add(products)]
    pallas_call x0 -> x4, Pallas kernels: none -> 59.1 us  [the longest x3 30.2 us: product_sums(): pl.pallas_call(functools.partial(sum_kernel, numbered, right_spans, given...]
    gather x14 -> x0, local copies, waits for them, and re-layouts: 54.2 us -> none  [the longest x7 28.1 us: add_products(): right_rows = jnp.take(gathered, step_list[1], axis=0)]
    dot_general x7 -> x0, matrix products: 34.2 us -> none  [add_products(): jnp.einsum('tij,tjk->tik', left_rows, right_rows, preferred_element_type=...]
    reduce_scatter x1 -> x0, waiting for transfers between devices: 26.6 us -> none  [local(): lax.psum_scatter(accumulated[:out_count], 'dep', scatter_dimension=0, til...]
    ppermute x6 -> x18, starting transfers between devices: 12.3 us -> 36.3 us  [the longest x6 11.4 us: swapped(): return lax.ppermute(value, 'dep', [(0, 1), (1, 0)])]
    unnamed x0 -> x33, local copies, waits for them, and re-layouts: none -> 9.1 us
    dynamic_slice x0 -> x3, local copies, waits for them, and re-layouts: none -> 8.43 us  [the longest x1 3.04 us: line(): met_other = lax.dynamic_slice_in_dim(met_pair, (1 - layer) * part, part)]
  transfers between devices with their start and end apart: 8 -> 24, of which waited for: 5 -> 9; matrix products, arithmetic and copies ran while one was open for 46% -> 9% of each run, Pallas kernels for 0% -> 12%
where the time goes in v5:
time: 262 us; the launch traced here: 260 us
  waiting for transfers between devices  116 us (44%)
  Pallas kernels  59.1 us (23%)
  starting transfers between devices  36.5 us (14%)
  local copies, waits for them, and re-layouts  26.8 us (10%)
  between operations  13.8 us (5%)
  other arithmetic  4.95 us (2%)
  blocking collectives  2.9 us (1%)
    ppermute x1, waiting for transfers between devices, line(): met = lax.ppermute(right_own, 'row', [(0, 1), (1, 0)])  39.8 us
    pallas_call x3, Pallas kernels, product_sums(): pl.pallas_call(functools.partial(sum_kernel, numbered, right_spans, given...  30.2 us
    pallas_call x1, Pallas kernels, place_rows(): pl.pallas_call(functools.partial(place_rows_kernel, first, received.shape...  28.9 us
    ppermute x1, waiting for transfers between devices, line(): end_packed = lax.ppermute(packed, 'col', inward)  27.5 us
    ppermute x1, waiting for transfers between devices, line(): rising = lax.ppermute(own_near, 'col', up)  20.2 us
    ppermute x1, waiting for transfers between devices, line(): received = lax.ppermute(end_rows, 'col', outward)  15.8 us
    ppermute x6, starting transfers between devices, swapped(): return lax.ppermute(value, 'dep', [(0, 1), (1, 0)])  11.4 us
    unnamed x33, local copies, waits for them, and re-layouts  9.1 us
  transfers between devices with their start and end apart: 24, of which 9 were waited for; matrix products, arithmetic and copies ran while one was open for 9% of the time, Pallas kernels for 12%

profile of v5, /device:TPU:1, one launch (start us, length us, event | category | flops | bytes accessed | tf_op | source)
XLA Modules:
  0.0 260.2 jit_solution(1851694276868817206)
XLA Ops:
  8.0 2.0 collective-permute-start.4
  10.1 39.8 %collective-permute-done.4 = bf16[56,128,128]{2,1,0:T(8,128)(2,1)} collective-permute-done((bf16[56,128,128]{2,1,0:T(8,128)(2,1)S(1)}, bf16[56,128,128]{2,1,0:T(8,128)(2,1)}, u32[]{:S(2)}, u32[]{:S(2)}) %collective-permute-start.4) | collective-permute-done | bytes 1835040 | tf_op jit(solution)/shard_map/ppermute | solution.py:254
  50.0 1.5 slice.42
  51.5 4.3 %collective-permute-start = (bf16[64,96,128]{2,1,0:T(8,128)(2,1)S(1)}, bf16[64,96,128]{2,1,0:T(8,128)(2,1)}, u32[]{:S(2)}, u32[]{:S(2)}) collective-permute-start(bf16[64,96,128]{2,1,0:T(8,128)(2,1)S(1)} %slice.42), channel_id=1, source_target_pairs={{0,2},{2,4},{4,6},{1,3},{3,5},{5,7},{8,10},{10,12},{12,14},{9,11},... | collective-permute-start | bytes 4718600 | tf_op jit(solution)/shard_map/ppermute | solution.py:255
  57.1 1.9 collective-permute-start.2
  60.3 2.9 %all-gather = s32[1,1,1,14,3,64]{5,2,4,1,0,3:T(1,128)S(1)} all-gather(s32[1,1,1,7,3,64]{5,2,4,1,0,3:T(1,128)S(1)} %bitcast.67), channel_id=2, replica_groups=mesh['grp'=2,'row'=2,'col'=4,'dep'=2] {'dep'}, dimensions={3}, use_global_device_ids=true | all-gather | bytes 16128 | tf_op jit(solution)/shard_map/all_gather | solution.py:202
  66.6 20.2 %collective-permute-done = bf16[64,96,128]{2,1,0:T(8,128)(2,1)} collective-permute-done((bf16[64,96,128]{2,1,0:T(8,128)(2,1)S(1)}, bf16[64,96,128]{2,1,0:T(8,128)(2,1)}, u32[]{:S(2)}, u32[]{:S(2)}) %collective-permute-start) | collective-permute-done | bytes 1572896 | tf_op jit(solution)/shard_map/ppermute | solution.py:255
  86.8 5.1 %collective-permute-done.1 = bf16[64,96,128]{2,1,0:T(8,128)(2,1)} collective-permute-done((bf16[64,96,128]{2,1,0:T(8,128)(2,1)S(1)}, bf16[64,96,128]{2,1,0:T(8,128)(2,1)}, u32[]{:S(2)}, u32[]{:S(2)}) %collective-permute-start.1) | collective-permute-done | bytes 1572896 | tf_op jit(solution)/shard_map/ppermute | solution.py:256
  92.5 2.2 collective-permute-start.7
  96.8 4.4 %collective-permute-start.8 = (s32[896]{0:T(1024)S(1)}, s32[896]{0:T(1024)S(1)}, u32[]{:S(2)}, u32[]{:S(2)}) collective-permute-start(s32[896]{0:T(1024)S(1)} %or_select_fusion.refs_0_), channel_id=1, source_target_pairs={{0,2},{6,4},{1,3},{7,5},{8,10},{14,12},{9,11},{15,13},{16,18},{22,... | collective-permute-start | bytes 10760 | tf_op jit(solution)/shard_map/ppermute | solution.py:274
  101.1 27.5 %collective-permute-done.8.refs_0_ = s32[896]{0:T(1024)S(1)} collective-permute-done((s32[896]{0:T(1024)S(1)}, s32[896]{0:T(1024)S(1)}, u32[]{:S(2)}, u32[]{:S(2)}) %collective-permute-start.8) | collective-permute-done | bytes 3616 | tf_op jit(solution)/shard_map/ppermute | solution.py:274
  134.8 2.0 slice.47
  143.0 4.2 %collective-permute-start.11 = (bf16[5120,128]{1,0:T(8,128)(2,1)}, bf16[5120,128]{1,0:T(8,128)(2,1)}, u32[]{:S(2)}, u32[]{:S(2)}) collective-permute-start(bf16[5120,128]{1,0:T(8,128)(2,1)} %pad_maximum_fusion.1), channel_id=1, source_target_pairs={{0,2},{6,4},{1,3},{7,5},{8,10},{14,12},{9,11},{15,13},{16,18},{22,... | collective-permute-start | bytes 3932168 | tf_op jit(solution)/shard_map/ppermute | solution.py:273
  150.5 3.0 %constant_dynamic-slice_fusion.2 = bf16[1,1,1,56,128,128]{5,4,2,1,0,3:T(8,128)(2,1)} fusion(bf16[1,1,1,112,128,128]{5,4,2,1,0,3:T(8,128)(2,1)} %all-gather.19.cloned.1.call-done, s32[]{:T(128)S(6)} %select_n.99), kind=kLoop, calls=%fused_computation.15 | loop fusion | bytes 3670020 | tf_op jit(solution)/shard_map/dynamic_slice | solution.py:289
  153.5 3.0 %constant_dynamic-slice_fusion.1 = bf16[56,128,128]{2,1,0:T(8,128)(2,1)} fusion(bf16[112,128,128]{2,1,0:T(8,128)(2,1)} %all-gather.9.cloned.1.call-done, s32[]{:T(128)S(6)} %select_n.99), kind=kLoop, calls=%fused_computation.14 | loop fusion | bytes 3670020 | tf_op jit(solution)/shard_map/dynamic_slice | solution.py:290
  157.9 12.9 %shard_map.37.refs_16_ = f32[113,96,128]{2,1,0:T(8,128)} custom-call(s32[896]{0:T(1024)S(1)} %or_select_fusion.refs_0_, s32[4]{0:T(128)S(1)} %pad_add_fusion.refs_1_, bf16[7168,128]{1,0:T(8,128)(2,1)} %bitcast.51, bf16[7168,128]{1,0:T(8,128)(2,1)} %bitcast.13.refs_3_, bf16[7168,128]{1,0:T(8,128)(2,1)} %bitcast.54, bf16[7168,128]{1,0:T(8,128)(2,1)} %bitcast.56, ...), custom_call_target="tpu_custom_call" | custom-call | flops 1 | bytes 1 | tf_op jit(solution)/shard_map/pallas_call | solution.py:155
  170.8 5.6 %collective-permute-start.13 = (bf16[5120,128]{1,0:T(8,128)(2,1)}, bf16[5120,128]{1,0:T(8,128)(2,1)}, u32[]{:S(2)}, u32[]{:S(2)}) collective-permute-start(bf16[5120,128]{1,0:T(8,128)(2,1)} %collective-permute-done.11.refs_4_), channel_id=1, source_target_pairs={{0,1},{1,0},{2,3},{3,2},{4,5},{5,4},{6,7},{7,6},{8,9},{9,8},{10,11... | collective-permute-start | bytes 3932168 | tf_op jit(solution)/shard_map/ppermute | solution.py:198
  177.1 2.4 constant_dynamic-slice_fusion.refs_5_
  179.5 2.8 %collective-permute-done.14.refs_12_.refs_15_ = bf16[4096,128]{1,0:T(8,128)(2,1)} collective-permute-done((bf16[4096,128]{1,0:T(8,128)(2,1)S(1)}, bf16[4096,128]{1,0:T(8,128)(2,1)}, u32[]{:S(2)}, u32[]{:S(2)}) %collective-permute-start.14) | collective-permute-done | bytes 1048608 | tf_op jit(solution)/shard_map/ppermute | solution.py:198
  184.7 3.3 %collective-permute-start.16 = (bf16[64,96,128]{2,1,0:T(8,128)(2,1)}, bf16[64,96,128]{2,1,0:T(8,128)(2,1)}, u32[]{:S(2)}, u32[]{:S(2)}) collective-permute-start(bf16[64,96,128]{2,1,0:T(8,128)(2,1)} %collective-permute-done.15), channel_id=1, source_target_pairs={{0,1},{1,0},{2,3},{3,2},{4,5},{5,4},{6,7},{7,6},{8,9},{9,8},{10,11... | collective-permute-start | bytes 4718600 | tf_op jit(solution)/shard_map/ppermute | solution.py:198
  189.4 2.0 collective-permute-done.16
  192.4 16.2 %shard_map.39.block = bf16[112,128,128]{2,1,0:T(8,128)(2,1)} custom-call(s32[896]{0:T(1024)S(1)} %or_select_fusion.refs_0_, s32[7]{0:T(128)S(1)} %stack.45.refs_1_, bf16[7168,128]{1,0:T(8,128)(2,1)} %bitcast.52, bf16[7168,128]{1,0:T(8,128)(2,1)} %bitcast.13.refs_3_, bf16[7168,128]{1,0:T(8,128)(2,1)} %bitcast.55, bf16[7168,128]{1,0:T(8,128)(2,1)} %bitcast.57, ...), custom_call_target="tpu_custom_call" | custom-call | flops 1 | bytes 1 | tf_op jit(solution)/shard_map/pallas_call | solution.py:155
  208.6 15.8 %collective-permute-done.17.received = bf16[112,32,128]{2,1,0:T(8,128)(2,1)} collective-permute-done((bf16[112,32,128]{2,1,0:T(8,128)(2,1)}, bf16[112,32,128]{2,1,0:T(8,128)(2,1)}, u32[]{:S(2)}, u32[]{:S(2)}) %collective-permute-start.17) | collective-permute-done | bytes 917536 | tf_op jit(solution)/shard_map/ppermute | solution.py:327
  224.4 28.9 %shard_map.40 = bf16[112,128,128]{2,1,0:T(8,128)(2,1)} custom-call(s32[1]{0:T(128)} %bitcast.takes, bf16[112,128,128]{2,1,0:T(8,128)(2,1)} %shard_map.39.block, bf16[112,32,128]{2,1,0:T(8,128)(2,1)} %collective-permute-done.17.received), custom_call_target="tpu_custom_call", output_to_operand_aliasing={{}: (1, {})} | custom-call | tf_op jit(solution)/shard_map/pallas_call | solution.py:187
  (101 shorter events, 32.5 us)
Async XLA Ops:
  6.5 143.9 %all-gather.19.cloned.1.call-start = ((), (), s32[]{:S(2)}) async-start(), calls=%async_computation.5 | async-start | bytes 5505024 | tf_op jit(solution)/shard_map/all_gather | solution.py:202
  7.3 146.2 %all-gather.9.cloned.1.call-start = ((), (), s32[]{:S(2)}) async-start(), calls=%async_computation | async-start | bytes 5505024 | tf_op jit(solution)/shard_map/all_gather | solution.py:202
  8.0 41.9 %collective-permute-start.4 = (bf16[56,128,128]{2,1,0:T(8,128)(2,1)S(1)}, bf16[56,128,128]{2,1,0:T(8,128)(2,1)}, u32[]{:S(2)}, u32[]{:S(2)}) collective-permute-start(bf16[56,128,128]{2,1,0:T(8,128)(2,1)S(1)} %bitcast.53), channel_id=1, source_target_pairs={{0,8},{8,0},{1,9},{9,1},{2,10},{10,2},{3,11},{11,3},{4,12},{12,4},... | collective-permute-start | bytes 5505032 | tf_op jit(solution)/shard_map/ppermute | solution.py:254
  49.9 106.6 %all-gather.11.cloned.1.call-start = ((), (), s32[]{:S(2)}) async-start(), calls=%async_computation.1 | async-start | bytes 4718592 | tf_op jit(solution)/shard_map/all_gather | solution.py:202
  51.5 35.3 %collective-permute-start = (bf16[64,96,128]{2,1,0:T(8,128)(2,1)S(1)}, bf16[64,96,128]{2,1,0:T(8,128)(2,1)}, u32[]{:S(2)}, u32[]{:S(2)}) collective-permute-start(bf16[64,96,128]{2,1,0:T(8,128)(2,1)S(1)} %slice.42), channel_id=1, source_target_pairs={{0,2},{2,4},{4,6},{1,3},{3,5},{5,7},{8,10},{10,12},{12,14},{9,11},... | collective-permute-start | bytes 4718600 | tf_op jit(solution)/shard_map/ppermute | solution.py:255
  55.8 36.0 %collective-permute-start.1 = (bf16[64,96,128]{2,1,0:T(8,128)(2,1)S(1)}, bf16[64,96,128]{2,1,0:T(8,128)(2,1)}, u32[]{:S(2)}, u32[]{:S(2)}) collective-permute-start(bf16[64,96,128]{2,1,0:T(8,128)(2,1)S(1)} %slice.42), channel_id=1, source_target_pairs={{2,0},{4,2},{6,4},{3,1},{5,3},{7,5},{10,8},{12,10},{14,12},{11,9},... | collective-permute-start | bytes 4718600 | tf_op jit(solution)/shard_map/ppermute | solution.py:256
  57.1 34.8 %collective-permute-start.2 = (bf16[64,96,128]{2,1,0:T(8,128)(2,1)S(1)}, bf16[64,96,128]{2,1,0:T(8,128)(2,1)}, u32[]{:S(2)}, u32[]{:S(2)}) collective-permute-start(bf16[64,96,128]{2,1,0:T(8,128)(2,1)S(1)} %slice.42), channel_id=1, source_target_pairs={{0,1},{1,0},{2,3},{3,2},{4,5},{5,4},{6,7},{7,6},{8,9},{9,8},{10,11... | collective-permute-start | bytes 4718600 | tf_op jit(solution)/shard_map/ppermute | solution.py:198
  60.2 6.4 %collective-permute-start.3 = (bf16[2048,128]{1,0:T(8,128)(2,1)S(1)}, bf16[2048,128]{1,0:T(8,128)(2,1)S(1)}, u32[]{:S(2)}, u32[]{:S(2)}) collective-permute-start(bf16[2048,128]{1,0:T(8,128)(2,1)S(1)} %bitcast.44), channel_id=1, source_target_pairs={{0,1},{1,0},{2,3},{3,2},{4,5},{5,4},{6,7},{7,6},{8,9},{9,8},{10,11... | collective-permute-start | bytes 1572872 | tf_op jit(solution)/shard_map/ppermute | solution.py:198
  91.9 64.6 %all-gather.13.cloned.1.call-start = ((), (), s32[]{:S(2)}) async-start(), calls=%async_computation.2 | async-start | bytes 4718592 | tf_op jit(solution)/shard_map/all_gather | solution.py:202
  92.5 84.5 %all-gather.15.cloned.1.call-start = ((), (), s32[]{:S(2)}) async-start(), calls=%async_computation.3 | async-start | bytes 5111808 | tf_op jit(solution)/shard_map/all_gather | solution.py:202
  92.5 39.7 %collective-permute-start.7 = (bf16[6656,128]{1,0:T(8,128)(2,1)}, bf16[6656,128]{1,0:T(8,128)(2,1)S(1)}, u32[]{:S(2)}, u32[]{:S(2)}) collective-permute-start(bf16[6656,128]{1,0:T(8,128)(2,1)} %pad_maximum_fusion), channel_id=1, source_target_pairs={{0,2},{6,4},{1,3},{7,5},{8,10},{14,12},{9,11},{15,13},{16,18},{22,... | collective-permute-start | bytes 5111816 | tf_op jit(solution)/shard_map/ppermute | solution.py:272
  94.7 33.9 %collective-permute-start.5 = (bf16[64,96,128]{2,1,0:T(8,128)(2,1)}, bf16[64,96,128]{2,1,0:T(8,128)(2,1)S(1)}, u32[]{:S(2)}, u32[]{:S(2)}) collective-permute-start(bf16[64,96,128]{2,1,0:T(8,128)(2,1)} %collective-permute-done), channel_id=1, source_target_pairs={{2,4},{4,6},{3,5},{5,7},{10,12},{12,14},{11,13},{13,15},{18,20},{2... | collective-permute-start | bytes 4718600 | tf_op jit(solution)/shard_map/ppermute | solution.py:270
  95.5 35.6 %collective-permute-start.6 = (bf16[64,96,128]{2,1,0:T(8,128)(2,1)}, bf16[64,96,128]{2,1,0:T(8,128)(2,1)S(1)}, u32[]{:S(2)}, u32[]{:S(2)}) collective-permute-start(bf16[64,96,128]{2,1,0:T(8,128)(2,1)} %collective-permute-done.1), channel_id=1, source_target_pairs={{4,2},{2,0},{5,3},{3,1},{12,10},{10,8},{13,11},{11,9},{20,18},{18,... | collective-permute-start | bytes 4718600 | tf_op jit(solution)/shard_map/ppermute | solution.py:271
  96.8 31.9 %collective-permute-start.8 = (s32[896]{0:T(1024)S(1)}, s32[896]{0:T(1024)S(1)}, u32[]{:S(2)}, u32[]{:S(2)}) collective-permute-start(s32[896]{0:T(1024)S(1)} %or_select_fusion.refs_0_), channel_id=1, source_target_pairs={{0,2},{6,4},{1,3},{7,5},{8,10},{14,12},{9,11},{15,13},{16,18},{22,... | collective-permute-start | bytes 10760 | tf_op jit(solution)/shard_map/ppermute | solution.py:274
  133.5 51.2 %all-gather.17.cloned.1.call-start = ((), (), s32[]{:S(2)}) async-start(), calls=%async_computation.4 | async-start | bytes 4718592 | tf_op jit(solution)/shard_map/all_gather | solution.py:202
  143.0 27.8 %collective-permute-start.11 = (bf16[5120,128]{1,0:T(8,128)(2,1)}, bf16[5120,128]{1,0:T(8,128)(2,1)}, u32[]{:S(2)}, u32[]{:S(2)}) collective-permute-start(bf16[5120,128]{1,0:T(8,128)(2,1)} %pad_maximum_fusion.1), channel_id=1, source_target_pairs={{0,2},{6,4},{1,3},{7,5},{8,10},{14,12},{9,11},{15,13},{16,18},{22,... | collective-permute-start | bytes 3932168 | tf_op jit(solution)/shard_map/ppermute | solution.py:273
  147.1 23.7 %collective-permute-start.10 = (bf16[4608,128]{1,0:T(8,128)(2,1)}, bf16[4608,128]{1,0:T(8,128)(2,1)}, u32[]{:S(2)}, u32[]{:S(2)}) collective-permute-start(bf16[4608,128]{1,0:T(8,128)(2,1)} %slice.39), channel_id=1, source_target_pairs={{0,8},{8,0},{1,9},{9,1},{2,10},{10,2},{3,11},{11,3},{4,12},{12,4},... | collective-permute-start | bytes 3538952 | tf_op jit(solution)/shard_map/ppermute | solution.py:286
  148.4 22.4 %collective-permute-start.9 = (bf16[4096,128]{1,0:T(8,128)(2,1)}, bf16[4096,128]{1,0:T(8,128)(2,1)S(1)}, u32[]{:S(2)}, u32[]{:S(2)}) collective-permute-start(bf16[4096,128]{1,0:T(8,128)(2,1)} %pad_maximum_fusion.2), channel_id=1, source_target_pairs={{2,4},{4,2},{3,5},{5,3},{10,12},{12,10},{11,13},{13,11},{18,20},{2... | collective-permute-start | bytes 3145736 | tf_op jit(solution)/shard_map/ppermute | solution.py:285
  149.2 35.5 %collective-permute-start.15 = (bf16[64,96,128]{2,1,0:T(8,128)(2,1)S(1)}, bf16[64,96,128]{2,1,0:T(8,128)(2,1)}, u32[]{:S(2)}, u32[]{:S(2)}) collective-permute-start(bf16[64,96,128]{2,1,0:T(8,128)(2,1)S(1)} %copy-done), channel_id=1, source_target_pairs={{4,6},{2,0},{5,7},{3,1},{12,14},{10,8},{13,15},{11,9},{20,22},{18,... | collective-permute-start | bytes 4718600 | tf_op jit(solution)/shard_map/ppermute | solution.py:284
  170.8 11.8 %collective-permute-start.13 = (bf16[5120,128]{1,0:T(8,128)(2,1)}, bf16[5120,128]{1,0:T(8,128)(2,1)}, u32[]{:S(2)}, u32[]{:S(2)}) collective-permute-start(bf16[5120,128]{1,0:T(8,128)(2,1)} %collective-permute-done.11.refs_4_), channel_id=1, source_target_pairs={{0,1},{1,0},{2,3},{3,2},{4,5},{5,4},{6,7},{7,6},{8,9},{9,8},{10,11... | collective-permute-start | bytes 3932168 | tf_op jit(solution)/shard_map/ppermute | solution.py:198
  176.5 6.2 %collective-permute-start.12 = (bf16[4608,128]{1,0:T(8,128)(2,1)}, bf16[4608,128]{1,0:T(8,128)(2,1)}, u32[]{:S(2)}, u32[]{:S(2)}) collective-permute-start(bf16[4608,128]{1,0:T(8,128)(2,1)} %collective-permute-done.10.refs_3_), channel_id=1, source_target_pairs={{0,1},{1,0},{2,3},{3,2},{4,5},{5,4},{6,7},{7,6},{8,9},{9,8},{10,11... | collective-permute-start | bytes 3538952 | tf_op jit(solution)/shard_map/ppermute | solution.py:198
  176.5 5.7 %collective-permute-start.14 = (bf16[4096,128]{1,0:T(8,128)(2,1)S(1)}, bf16[4096,128]{1,0:T(8,128)(2,1)}, u32[]{:S(2)}, u32[]{:S(2)}) collective-permute-start(bf16[4096,128]{1,0:T(8,128)(2,1)S(1)} %collective-permute-done.9.refs_11_.refs_14_), channel_id=1, source_target_pairs={{0,1},{1,0},{2,3},{3,2},{4,5},{5,4},{6,7},{7,6},{8,9},{9,8},{10,11... | collective-permute-start | bytes 3145736 | tf_op jit(solution)/shard_map/ppermute | solution.py:198
  184.7 6.7 %collective-permute-start.16 = (bf16[64,96,128]{2,1,0:T(8,128)(2,1)}, bf16[64,96,128]{2,1,0:T(8,128)(2,1)}, u32[]{:S(2)}, u32[]{:S(2)}) collective-permute-start(bf16[64,96,128]{2,1,0:T(8,128)(2,1)} %collective-permute-done.15), channel_id=1, source_target_pairs={{0,1},{1,0},{2,3},{3,2},{4,5},{5,4},{6,7},{7,6},{8,9},{9,8},{10,11... | collective-permute-start | bytes 4718600 | tf_op jit(solution)/shard_map/ppermute | solution.py:198
  188.0 36.5 %collective-permute-start.17 = (bf16[112,32,128]{2,1,0:T(8,128)(2,1)}, bf16[112,32,128]{2,1,0:T(8,128)(2,1)}, u32[]{:S(2)}, u32[]{:S(2)}) collective-permute-start(bf16[112,32,128]{2,1,0:T(8,128)(2,1)} %copy-done.6), channel_id=1, source_target_pairs={{4,6},{2,0},{5,7},{3,1},{12,14},{10,8},{13,15},{11,9},{20,22},{18,... | collective-permute-start | bytes 2752520 | tf_op jit(solution)/shard_map/ppermute | solution.py:327
  (16 other events, 120.7 us)
Sparse Core Ops, SparseCore 0:
  8.9 15.3 all-gather.18
  50.1 15.5 all-gather.8
  92.0 13.6 all-gather.10
  107.1 13.2 all-gather.12
  133.6 16.0 all-gather.14
  151.1 13.3 all-gather.16

commit v6 on v5

--- a/solution.py
+++ b/solution.py
@@ -72,7 +72,9 @@
     for at in range(1, layer_at):
         any_class = jnp.maximum(any_class, classes[at])
     start = 0
-    for operand, first, size in right_spans:
+    for operand, first, size, gathered in right_spans:
+        if gathered:
+            first = pl.multiple_of(first + other * gathered, 16)
         plan(operands[operand].at[pl.ds(first, size)], right.at[pl.ds(start, size)], any_class >= 0)
         start += size
     class_at = 0
@@ -132,14 +134,14 @@
         operands.append(flat(value))
         return len(operands) - 1
 
-    right_spans = [(number(value), first, size) for value, first, size in rights]
+    right_spans = [(number(value), first, size, gathered) for value, first, size, gathered in rights]
     numbered = [
         ([[(number(value), first, gathered) for value, first, gathered in panel] for panel in panels], rows)
         for panels, rows in groups
     ]
     if given is not None:
         operands.append(given)
-    right_rows = sum(size for _, _, size in rights)
+    right_rows = sum(span[2] for span in rights)
     most = max(len(panels) for panels, _ in groups)
     assert right_rows <= 1024 * width and most * 2 * slots <= 1024 and half < 1024 and slots % 8 == 0
     anywhere = pl.BlockSpec(memory_space=pl.ANY)
@@ -172,12 +174,12 @@
     )(packed, scalars, *operands)
 
 
-def place_rows_kernel(first, rows, takes, block, received, out, sem):
+def place_rows_kernel(first, takes, block, received, out, sem):
     del block
 
     @pl.when(takes[0] > 0)
     def _():
-        copy = pltpu.make_async_copy(received, out.at[:, pl.ds(first, rows)], sem)
+        copy = pltpu.make_async_copy(received, out.at[:, pl.ds(first, received.shape[1])], sem)
         copy.start()
         copy.wait()
 
@@ -185,9 +187,9 @@
 def place_rows(takes, block, received, first):
     anywhere = pl.BlockSpec(memory_space=pl.ANY)
     return pl.pallas_call(
-        functools.partial(place_rows_kernel, first, received.shape[1]),
+        functools.partial(place_rows_kernel, first),
         out_shape=jax.ShapeDtypeStruct(block.shape, block.dtype),
-        in_specs=[pl.BlockSpec(memory_space=pltpu.SMEM), anywhere, anywhere],
+        in_specs=[pl.BlockSpec(memory_space=pltpu.SMEM), anywhere, pl.BlockSpec(memory_space=pltpu.VMEM)],
         out_specs=anywhere,
         scratch_shapes=[pltpu.SemaphoreType.DMA],
         input_output_aliases={1: 0},
@@ -202,9 +204,8 @@
     return lax.all_gather(value, "dep", axis=0, tiled=True)
 
 
-def packed_lists(step_lists, layer, half, right_place):
-    step_count, _, slots = step_lists.shape
-    both = paired(step_lists).reshape(2, step_count, 3, slots)
+def packed_lists(both, layer, half, right_place):
+    step_count, _, slots = both.shape[1:]
     both = jnp.where(layer > 0, both[::-1], both)
     result = both[:, :, 2] - layer * half
     wanted = (result >= 0) & (result < half)
@@ -219,8 +220,9 @@
     columns, layer = lax.axis_size("col"), lax.axis_index("dep")
     gathered = lax.all_gather(right_own, "row", axis=0, tiled=True)
     right_slots = gathered.shape[0]
-    packed = packed_lists(step_lists, layer, half, lambda slot, layers: layers * right_slots + slot)
-    rights = [(value, 0, right_slots * rows) for value in (gathered, swapped(gathered))]
+    both = lax.all_gather(step_lists, "dep")
+    packed = packed_lists(both, layer, half, lambda slot, layers: layers * right_slots + slot)
+    rights = [(value, 0, right_slots * rows, 0) for value in (gathered, swapped(gathered))]
     shape = (step_lists.shape[0], columns, slots)
     rising, falling, total = own, own, None
     size = slots * rows
@@ -251,47 +253,51 @@
     high, inner = place == 2, (place == 1) | (place == 2)
 
     own_near, own_far = own[:, :near], flat(own[:, near:])
+    near_size, far_size = slots * near, slots * far
     met = lax.ppermute(right_own, "row", [(0, 1), (1, 0)])
     rising = lax.ppermute(own_near, "col", up)
     falling = lax.ppermute(own_near, "col", down)
-    near_other, far_other, right_pair = swapped(own_near), swapped(own_far), paired(right_own)
+    near_other, far_other = swapped(own_near), swapped(own_far)
+    lists = lax.all_gather(step_lists, ("col", "dep")).reshape(columns, 2, *step_lists.shape)
+    right_pair = paired(right_own)
 
     def right_place(slot, layers):
         farther, within = (slot // part) ^ lax.axis_index("row"), slot % part
         first = jnp.where(within < cut, farther * cut + within, 2 * cut + farther * (part - cut) + within - cut)
         return layers * 2 * part + first
 
-    packed = packed_lists(step_lists, layer, half, right_place)
-    first_inward = jnp.concatenate([own_far, flat(right_own[:cut])])
-
-    rising, falling, near_other, far_other, packed, first_inward = lax.optimization_barrier(
-        (rising, falling, near_other, far_other, packed, first_inward)
+    def lists_of(column):
+        return packed_lists(lax.dynamic_index_in_dim(lists, column, 0, False), layer, half, right_place)
+
+    packed, end_packed = lists_of(place), lists_of(jnp.where(place > 1, 3, 0))
+    end_right = right_own[:cut]
+
+    rising, falling, met, near_other, far_other, packed, end_packed, end_right = lax.optimization_barrier(
+        (rising, falling, met, near_other, far_other, packed, end_packed, end_right)
     )
     rising_two = lax.ppermute(rising, "col", [(1, 2), (2, 3)])
     falling_two = lax.ppermute(falling, "col", [(2, 1), (1, 0)])
-    end_far = lax.ppermute(first_inward, "col", inward)
-    end_rest = lax.ppermute(jnp.concatenate([flat(right_own[cut:]), flat(met[cut:])]), "col", inward)
-    end_packed = lax.ppermute(packed, "col", inward)
+    outer_far = lax.ppermute(own_far, "col", inward)
+    outer_far, end_right = lax.optimization_barrier((outer_far, end_right))
+    end_right = lax.ppermute(end_right, "col", inward)
     met_pair, rising_pair, falling_pair = paired(met), paired(rising), paired(falling)
-
-    rising_two, falling_two, end_far, end_packed, rising, falling = lax.optimization_barrier(
-        (rising_two, falling_two, end_far, end_packed, rising, falling)
-    )
-    two = jnp.where(place > 1, rising_two, falling_two)
-    near_size, far_size = slots * near, slots * far
-    crossing = jnp.concatenate([own_far, end_far[:far_size]])
-    two, crossing, end_right = lax.optimization_barrier((two, crossing, end_far[far_size:]))
-    three = lax.ppermute(two, "col", outward)
-    crossed = lax.ppermute(crossing, "col", across)
+    outer_other = swapped(outer_far)
+    end_rest = jnp.concatenate([flat(right_own[cut:]), flat(met[cut:])])
+
+    rising_two, falling_two, outer_far, outer_other, end_right, end_rest = lax.optimization_barrier(
+        (rising_two, falling_two, outer_far, outer_other, end_right, end_rest)
+    )
+    rising_three = lax.ppermute(rising_two, "col", [(2, 3)])
+    falling_three = lax.ppermute(falling_two, "col", [(1, 0)])
+    crossed = lax.ppermute(jnp.concatenate([own_far, outer_far]), "col", across)
     end_met = lax.ppermute(end_right, "row", [(0, 1), (1, 0)])
-    end_pair, two_pair = paired(end_far), paired(two)
-
-    right_other = lax.dynamic_slice_in_dim(right_pair, (1 - layer) * part, part)
-    met_other = lax.dynamic_slice_in_dim(met_pair, (1 - layer) * part, part)
+    end_rest = lax.ppermute(end_rest, "col", inward)
+    end_pair = paired(end_right)
+
     rights = []
-    for nearer, farther in ((right_own, met), (right_other, met_other)):
+    for nearer, farther, stride in ((right_own, met, 0), (right_pair, met_pair, part * rows)):
         for first, size in ((0, cut), (cut, part - cut)):
-            rights += [(nearer, first * rows, size * rows), (farther, first * rows, size * rows)]
+            rights += [(value, first * rows, size * rows, stride) for value in (nearer, farther)]
     panels = [
         [(own_near, 0, 0), (near_other, 0, 0)],
         [(rising, 0, 0), (rising_pair, 0, near_size)],
@@ -300,22 +306,24 @@
     classes = [0, jnp.where(place > 0, 3, -1), jnp.where(place < 3, 1, -1)]
     total = product_sums(packed, classes, layer, shape, [(panels, near)], rights, None, half, False)
 
-    crossed, end_met, end_rest, total = lax.optimization_barrier((crossed, end_met, end_rest, total))
+    crossed, end_met, end_rest, end_pair, total = lax.optimization_barrier(
+        (crossed, end_met, end_rest, end_pair, total)
+    )
     crossed_other, end_met_other, end_rest_other = swapped(crossed), swapped(end_met), swapped(end_rest)
     far_panels = [
         [(own_far, 0, 0), (far_other, 0, 0)],
-        [(end_far, 0, 0), (end_pair, 0, end_far.shape[0])],
+        [(outer_far, 0, 0), (outer_other, 0, 0)],
         [(crossed, 0, 0), (crossed_other, 0, 0)],
         [(crossed, far_size, 0), (crossed_other, far_size, 0)],
     ]
-    end_other = lax.dynamic_slice_in_dim(end_pair, (1 - layer) * end_far.shape[0] + far_size, cut * rows)
+    rest = 2 * (part - cut) * rows
     end_rights = [
-        (end_far, far_size, cut * rows),
-        (end_met, 0, cut * rows),
-        (end_rest, 0, end_rest.shape[0]),
-        (end_other, 0, cut * rows),
-        (end_met_other, 0, cut * rows),
-        (end_rest_other, 0, end_rest.shape[0]),
+        (end_right, 0, cut * rows, 0),
+        (end_met, 0, cut * rows, 0),
+        (end_rest, 0, rest, 0),
+        (end_pair, 0, cut * rows, cut * rows),
+        (end_met_other, 0, cut * rows, 0),
+        (end_rest_other, 0, rest, 0),
     ]
     classes = [jnp.where(high, 3, 1), 0, 2, jnp.where(high, 1, 3)]
     classes = [jnp.where(inner, kind, -1) for kind in classes]
@@ -323,8 +331,13 @@
         end_packed, classes, layer, shape, [(far_panels, far)], end_rights, None, half, True
     )
 
-    end_rows, total, three, two_pair = lax.optimization_barrier((end_rows, total, three, two_pair))
+    two = jnp.where(place > 1, rising_two, falling_two)
+    two_pair = paired(two)
+    end_rows, total, rising_three, falling_three = lax.optimization_barrier(
+        (end_rows, total, rising_three, falling_three)
+    )
     received = lax.ppermute(end_rows, "col", outward)
+    three = jnp.where(place > 1, rising_three, falling_three)
     near_panels = [
         [(two, 0, 0), (two_pair, 0, near_size)],
         [(three, 0, 0), (swapped(three), 0, 0)],

time: 262 us -> 206 us (0.79)
  the two profiles are of different devices: /device:TPU:1 before, /device:TPU:12 now
where the time goes in v6:
time: 206 us; the launch traced here: 205 us
  Pallas kernels  54.5 us (26%)
  blocking collectives  41.8 us (20%)
  waiting for transfers between devices  40.8 us (20%)
  starting transfers between devices  33.3 us (16%)
  between operations  13.8 us (7%)
  local copies, waits for them, and re-layouts  12.7 us (6%)
  other arithmetic  8.09 us (4%)
    pallas_call x3, Pallas kernels, product_sums(): pl.pallas_call(functools.partial(sum_kernel, numbered, right_spans, given...  53.3 us
    all_gather x1, blocking collectives, line(): lax.all_gather(step_lists, ('col', 'dep'))  41.8 us
    ppermute x1, waiting for transfers between devices, line(): end_right = lax.ppermute(end_right, 'col', inward)  23.4 us
    ppermute x1, waiting for transfers between devices, line(): outer_far = lax.ppermute(own_far, 'col', inward)  8.28 us
    ppermute x7, waiting for transfers between devices, swapped(): return lax.ppermute(value, 'dep', [(0, 1), (1, 0)])  5.82 us
    ppermute x1, starting transfers between devices, line(): falling_three = lax.ppermute(falling_two, 'col', [(1, 0)])  5.66 us
  transfers between devices with their start and end apart: 26, of which 6 were waited for; matrix products, arithmetic and copies ran while one was open for 8% of the time, Pallas kernels for 26%

profile of v6, /device:TPU:12, one launch (start us, length us, event | category | flops | bytes accessed | tf_op | source)
XLA Modules:
  0.0 204.9 jit_solution(10179699626628992349)
XLA Ops:
  7.3 1.5 slice.49
  8.9 2.4 %collective-permute-start.1 = (bf16[64,96,128]{2,1,0:T(8,128)(2,1)S(1)}, bf16[64,96,128]{2,1,0:T(8,128)(2,1)}, u32[]{:S(2)}, u32[]{:S(2)}) collective-permute-start(bf16[64,96,128]{2,1,0:T(8,128)(2,1)S(1)} %slice.49), channel_id=1, source_target_pairs={{2,0},{4,2},{6,4},{3,1},{5,3},{7,5},{10,8},{12,10},{14,12},{11,9},... | collective-permute-start | bytes 4718600 | tf_op jit(solution)/shard_map/ppermute | solution.py:259
  11.3 3.5 %collective-permute-start = (bf16[64,96,128]{2,1,0:T(8,128)(2,1)S(1)}, bf16[64,96,128]{2,1,0:T(8,128)(2,1)}, u32[]{:S(2)}, u32[]{:S(2)}) collective-permute-start(bf16[64,96,128]{2,1,0:T(8,128)(2,1)S(1)} %slice.49), channel_id=1, source_target_pairs={{0,2},{2,4},{4,6},{1,3},{3,5},{5,7},{8,10},{10,12},{12,14},{9,11},... | collective-permute-start | bytes 4718600 | tf_op jit(solution)/shard_map/ppermute | solution.py:258
  16.0 1.6 collective-permute-start.2
  17.5 41.8 %all-gather = s32[8,1,1,7,3,64]{5,2,4,3,1,0:T(1,128)S(1)} all-gather(s32[1,1,1,7,3,64]{5,2,4,3,1,0:T(1,128)S(1)} %copy-done.6), channel_id=2, replica_groups=mesh['grp'=2,'row'=2,'col'=4,'dep'=2] {'col','dep'}, dimensions={0}, use_global_device_ids=true | all-gather | bytes 48384 | tf_op jit(solution)/shard_map/all_gather | solution.py:261
  60.7 2.4 %slice_bitcast_fusion = bf16[36,128,128]{2,1,0:T(8,128)(2,1)} fusion(bf16[1,1,1,56,128,128]{5,4,3,2,1,0:T(8,128)(2,1)} %param.4), kind=kLoop, calls=%fused_computation.3 | loop fusion | bytes 2359296 | tf_op jit(solution)/shard_map/slice | solution.py:273
  64.6 1.3 collective-permute-start.7
  65.9 2.5 %collective-permute-start.5 = (bf16[64,96,128]{2,1,0:T(8,128)(2,1)}, bf16[64,96,128]{2,1,0:T(8,128)(2,1)}, u32[]{:S(2)}, u32[]{:S(2)}) collective-permute-start(bf16[64,96,128]{2,1,0:T(8,128)(2,1)} %collective-permute-done), channel_id=1, source_target_pairs={{2,4},{4,6},{3,5},{5,7},{10,12},{12,14},{11,13},{13,15},{18,20},{2... | collective-permute-start | bytes 4718600 | tf_op jit(solution)/shard_map/ppermute | solution.py:278
  68.4 3.9 %collective-permute-start.6 = (bf16[64,96,128]{2,1,0:T(8,128)(2,1)}, bf16[64,96,128]{2,1,0:T(8,128)(2,1)}, u32[]{:S(2)}, u32[]{:S(2)}) collective-permute-start(bf16[64,96,128]{2,1,0:T(8,128)(2,1)} %collective-permute-done.1), channel_id=1, source_target_pairs={{4,2},{2,0},{5,3},{3,1},{12,10},{10,8},{13,11},{11,9},{20,18},{18,... | collective-permute-start | bytes 4718600 | tf_op jit(solution)/shard_map/ppermute | solution.py:279
  72.4 8.3 %collective-permute-done.7.refs_10_.refs_12_ = bf16[2048,128]{1,0:T(8,128)(2,1)S(1)} collective-permute-done((bf16[2048,128]{1,0:T(8,128)(2,1)S(1)}, bf16[2048,128]{1,0:T(8,128)(2,1)S(1)}, u32[]{:S(2)}, u32[]{:S(2)}) %collective-permute-start.7) | collective-permute-done | bytes 524320 | tf_op jit(solution)/shard_map/ppermute | solution.py:280
  80.7 1.3 collective-permute-start.9
  87.0 23.4 %collective-permute-done.9 = bf16[36,128,128]{2,1,0:T(8,128)(2,1)} collective-permute-done((bf16[36,128,128]{2,1,0:T(8,128)(2,1)}, bf16[36,128,128]{2,1,0:T(8,128)(2,1)}, u32[]{:S(2)}, u32[]{:S(2)}) %collective-permute-start.9) | collective-permute-done | bytes 1179680 | tf_op jit(solution)/shard_map/ppermute | solution.py:282
  110.5 1.6 collective-permute-start.11
  114.4 2.7 %collective-permute-start.10 = (bf16[4096,128]{1,0:T(8,128)(2,1)}, bf16[4096,128]{1,0:T(8,128)(2,1)}, u32[]{:S(2)}, u32[]{:S(2)}) collective-permute-start(bf16[4096,128]{1,0:T(8,128)(2,1)} %pad_maximum_fusion.1), channel_id=1, source_target_pairs={{2,4},{4,2},{3,5},{5,3},{10,12},{12,10},{11,13},{13,11},{18,20},{2... | collective-permute-start | bytes 3145736 | tf_op jit(solution)/shard_map/ppermute | solution.py:292
  117.2 1.8 collective-permute-start.16
  119.0 5.7 %collective-permute-start.17 = (bf16[64,96,128]{2,1,0:T(8,128)(2,1)}, bf16[64,96,128]{2,1,0:T(8,128)(2,1)}, u32[]{:S(2)}, u32[]{:S(2)}) collective-permute-start(bf16[64,96,128]{2,1,0:T(8,128)(2,1)} %collective-permute-done.6), channel_id=1, source_target_pairs={{2,0},{3,1},{10,8},{11,9},{18,16},{19,17},{26,24},{27,25}} | collective-permute-start | bytes 4718600 | tf_op jit(solution)/shard_map/ppermute | solution.py:291
  124.7 17.3 %shard_map.37.refs_16_ = f32[113,96,128]{2,1,0:T(8,128)} custom-call(s32[896]{0:T(1024)S(1)} %get-tuple-element.30.refs_0_, s32[4]{0:T(128)S(1)} %pad_add_fusion.refs_1_, bf16[7168,128]{1,0:T(8,128)(2,1)} %bitcast.14.refs_2_, bf16[7168,128]{1,0:T(8,128)(2,1)} %bitcast.15.refs_3_, bf16[14336,128]{1,0:T(8,128)(2,1)} %bitcast.68, bf16[14336,128]{1,0:T(8,128)(2,1)} %bitcast.70, ...), custom_call_target="tpu_custom_call" | custom-call | flops 1 | bytes 1 | tf_op jit(solution)/shard_map/pallas_call | solution.py:157
  142.0 1.3 collective-permute-done.12.refs_4_
  143.4 2.7 %broadcast_select_fusion.1 = bf16[64,96,128]{2,1,0:T(8,128)(2,1)} fusion(bf16[64,96,128]{2,1,0:T(8,128)(2,1)} %collective-permute-done.5, bf16[64,96,128]{2,1,0:T(8,128)(2,1)} %collective-permute-done.6, pred[]{:T(512)S(6)} %gt.13), kind=kLoop, calls=%fused_computation.1 | loop fusion | flops 786432 | bytes 4718593 | tf_op jit(solution)/shard_map/jit(_where)/select_n | solution.py:334
  146.9 4.0 %collective-permute-done.15.refs_13_.refs_15_ = bf16[4096,128]{1,0:T(8,128)(2,1)S(1)} collective-permute-done((bf16[4096,128]{1,0:T(8,128)(2,1)}, bf16[4096,128]{1,0:T(8,128)(2,1)S(1)}, u32[]{:S(2)}, u32[]{:S(2)}) %collective-permute-start.15) | collective-permute-done | bytes 1048608 | tf_op jit(solution)/shard_map/ppermute | solution.py:200
  150.9 12.6 %shard_map.38 = bf16[112,32,128]{2,1,0:T(8,128)(2,1)} custom-call(s32[896]{0:T(1024)S(1)} %get-tuple-element.39.refs_0_, s32[5]{0:T(128)S(1)} %stack.46.refs_1_, bf16[4608,128]{1,0:T(8,128)(2,1)} %bitcast.23.refs_2_, bf16[4608,128]{1,0:T(8,128)(2,1)} %bitcast.32.refs_3_, bf16[5120,128]{1,0:T(8,128)(2,1)} %collective-permute-done.12.refs_4_, ...), custom_call_target="tpu_custom_call" | custom-call | flops 1 | bytes 1 | tf_op jit(solution)/shard_map/pallas_call | solution.py:157
  164.5 2.9 %broadcast_select_fusion = bf16[64,96,128]{2,1,0:T(8,128)(2,1)} fusion(bf16[64,96,128]{2,1,0:T(8,128)(2,1)} %collective-permute-done.16, bf16[64,96,128]{2,1,0:T(8,128)(2,1)} %collective-permute-done.17, pred[]{:T(512)S(6)} %gt.13), kind=kLoop, calls=%fused_computation | loop fusion | flops 786432 | bytes 4718593 | tf_op jit(solution)/shard_map/jit(_where)/select_n | solution.py:340
  167.9 2.3 %collective-permute-start.19 = (bf16[112,32,128]{2,1,0:T(8,128)(2,1)}, bf16[112,32,128]{2,1,0:T(8,128)(2,1)}, u32[]{:S(2)}, u32[]{:S(2)}) collective-permute-start(bf16[112,32,128]{2,1,0:T(8,128)(2,1)} %shard_map.38), channel_id=1, source_target_pairs={{4,6},{2,0},{5,7},{3,1},{12,14},{10,8},{13,15},{11,9},{20,22},{18,... | collective-permute-start | bytes 2752520 | tf_op jit(solution)/shard_map/ppermute | solution.py:339
  173.5 23.3 %shard_map.39.block = bf16[112,128,128]{2,1,0:T(8,128)(2,1)} custom-call(s32[896]{0:T(1024)S(1)} %get-tuple-element.30.refs_0_, s32[7]{0:T(128)S(1)} %stack.45.refs_1_, bf16[7168,128]{1,0:T(8,128)(2,1)} %bitcast.14.refs_2_, bf16[7168,128]{1,0:T(8,128)(2,1)} %bitcast.15.refs_3_, bf16[14336,128]{1,0:T(8,128)(2,1)} %bitcast.69, bf16[14336,128]{1,0:T(8,128)(2,1)} %bitcast.71, ...), custom_call_target="tpu_custom_call" | custom-call | flops 1 | bytes 1 | tf_op jit(solution)/shard_map/pallas_call | solution.py:157
  (101 shorter events, 19.0 us)
Async XLA Ops:
  6.5 118.1 %all-gather.19.cloned.1.call-start = ((), (), s32[]{:S(2)}) async-start(), calls=%async_computation.5 | async-start | bytes 5505024 | tf_op jit(solution)/shard_map/all_gather | solution.py:204
  7.3 117.4 %all-gather.15.cloned.1.call-start = ((), (), s32[]{:S(2)}) async-start(), calls=%async_computation.3 | async-start | bytes 4718592 | tf_op jit(solution)/shard_map/all_gather | solution.py:204
  8.8 54.3 %collective-permute-start.3 = (bf16[64,96,128]{2,1,0:T(8,128)(2,1)S(1)}, bf16[64,96,128]{2,1,0:T(8,128)(2,1)}, u32[]{:S(2)}, u32[]{:S(2)}) collective-permute-start(bf16[64,96,128]{2,1,0:T(8,128)(2,1)S(1)} %slice.49), channel_id=1, source_target_pairs={{0,1},{1,0},{2,3},{3,2},{4,5},{5,4},{6,7},{7,6},{8,9},{9,8},{10,11... | collective-permute-start | bytes 4718600 | tf_op jit(solution)/shard_map/ppermute | solution.py:200
  8.9 54.3 %collective-permute-start.1 = (bf16[64,96,128]{2,1,0:T(8,128)(2,1)S(1)}, bf16[64,96,128]{2,1,0:T(8,128)(2,1)}, u32[]{:S(2)}, u32[]{:S(2)}) collective-permute-start(bf16[64,96,128]{2,1,0:T(8,128)(2,1)S(1)} %slice.49), channel_id=1, source_target_pairs={{2,0},{4,2},{6,4},{3,1},{5,3},{7,5},{10,8},{12,10},{14,12},{11,9},... | collective-permute-start | bytes 4718600 | tf_op jit(solution)/shard_map/ppermute | solution.py:259
  11.3 51.9 %collective-permute-start = (bf16[64,96,128]{2,1,0:T(8,128)(2,1)S(1)}, bf16[64,96,128]{2,1,0:T(8,128)(2,1)}, u32[]{:S(2)}, u32[]{:S(2)}) collective-permute-start(bf16[64,96,128]{2,1,0:T(8,128)(2,1)S(1)} %slice.49), channel_id=1, source_target_pairs={{0,2},{2,4},{4,6},{1,3},{3,5},{5,7},{8,10},{10,12},{12,14},{9,11},... | collective-permute-start | bytes 4718600 | tf_op jit(solution)/shard_map/ppermute | solution.py:258
  15.9 47.3 %collective-permute-start.4 = (bf16[2048,128]{1,0:T(8,128)(2,1)S(1)}, bf16[2048,128]{1,0:T(8,128)(2,1)S(1)}, u32[]{:S(2)}, u32[]{:S(2)}) collective-permute-start(bf16[2048,128]{1,0:T(8,128)(2,1)S(1)} %bitcast.62), channel_id=1, source_target_pairs={{0,1},{1,0},{2,3},{3,2},{4,5},{5,4},{6,7},{7,6},{8,9},{9,8},{10,11... | collective-permute-start | bytes 1572872 | tf_op jit(solution)/shard_map/ppermute | solution.py:200
  16.0 47.2 %collective-permute-start.2 = (bf16[56,128,128]{2,1,0:T(8,128)(2,1)}, bf16[56,128,128]{2,1,0:T(8,128)(2,1)}, u32[]{:S(2)}, u32[]{:S(2)}) collective-permute-start(bf16[56,128,128]{2,1,0:T(8,128)(2,1)} %bitcast.2), channel_id=1, source_target_pairs={{0,8},{8,0},{1,9},{9,1},{2,10},{10,2},{3,11},{11,3},{4,12},{12,4},... | collective-permute-start | bytes 5505032 | tf_op jit(solution)/shard_map/ppermute | solution.py:257
  63.2 61.5 %all-gather.17.cloned.1.call-start = ((), (), s32[]{:S(2)}) async-start(), calls=%async_computation.4 | async-start | bytes 4718592 | tf_op jit(solution)/shard_map/all_gather | solution.py:204
  64.0 60.7 %all-gather.9.cloned.1.call-start = ((), (), s32[]{:S(2)}) async-start(), calls=%async_computation | async-start | bytes 5505024 | tf_op jit(solution)/shard_map/all_gather | solution.py:204
  64.5 78.8 %all-gather.13.cloned.1.call-start = ((), (), s32[]{:S(2)}) async-start(), calls=%async_computation.2 | async-start | bytes 3538944 | tf_op jit(solution)/shard_map/all_gather | solution.py:204
  64.6 16.1 %collective-permute-start.7 = (bf16[2048,128]{1,0:T(8,128)(2,1)S(1)}, bf16[2048,128]{1,0:T(8,128)(2,1)S(1)}, u32[]{:S(2)}, u32[]{:S(2)}) collective-permute-start(bf16[2048,128]{1,0:T(8,128)(2,1)S(1)} %bitcast.63), channel_id=1, source_target_pairs={{0,2},{6,4},{1,3},{7,5},{8,10},{14,12},{9,11},{15,13},{16,18},{22,... | collective-permute-start | bytes 1572872 | tf_op jit(solution)/shard_map/ppermute | solution.py:280
  65.9 44.5 %collective-permute-start.5 = (bf16[64,96,128]{2,1,0:T(8,128)(2,1)}, bf16[64,96,128]{2,1,0:T(8,128)(2,1)}, u32[]{:S(2)}, u32[]{:S(2)}) collective-permute-start(bf16[64,96,128]{2,1,0:T(8,128)(2,1)} %collective-permute-done), channel_id=1, source_target_pairs={{2,4},{4,6},{3,5},{5,7},{10,12},{12,14},{11,13},{13,15},{18,20},{2... | collective-permute-start | bytes 4718600 | tf_op jit(solution)/shard_map/ppermute | solution.py:278
  68.4 42.0 %collective-permute-start.6 = (bf16[64,96,128]{2,1,0:T(8,128)(2,1)}, bf16[64,96,128]{2,1,0:T(8,128)(2,1)}, u32[]{:S(2)}, u32[]{:S(2)}) collective-permute-start(bf16[64,96,128]{2,1,0:T(8,128)(2,1)} %collective-permute-done.1), channel_id=1, source_target_pairs={{4,2},{2,0},{5,3},{3,1},{12,10},{10,8},{13,11},{11,9},{20,18},{18,... | collective-permute-start | bytes 4718600 | tf_op jit(solution)/shard_map/ppermute | solution.py:279
  80.7 29.7 %collective-permute-start.9 = (bf16[36,128,128]{2,1,0:T(8,128)(2,1)}, bf16[36,128,128]{2,1,0:T(8,128)(2,1)}, u32[]{:S(2)}, u32[]{:S(2)}) collective-permute-start(bf16[36,128,128]{2,1,0:T(8,128)(2,1)} %slice_bitcast_fusion), channel_id=1, source_target_pairs={{0,2},{6,4},{1,3},{7,5},{8,10},{14,12},{9,11},{15,13},{16,18},{22,... | collective-permute-start | bytes 3538952 | tf_op jit(solution)/shard_map/ppermute | solution.py:282
  110.4 59.8 %all-gather.11.cloned.1.call-start = ((), (), s32[]{:S(2)}) async-start(), calls=%async_computation.1 | async-start | bytes 4718592 | tf_op jit(solution)/shard_map/all_gather | solution.py:204
  110.5 31.6 %collective-permute-start.11 = (bf16[36,128,128]{2,1,0:T(8,128)(2,1)}, bf16[36,128,128]{2,1,0:T(8,128)(2,1)}, u32[]{:S(2)}, u32[]{:S(2)}) collective-permute-start(bf16[36,128,128]{2,1,0:T(8,128)(2,1)} %collective-permute-done.9), channel_id=1, source_target_pairs={{0,8},{8,0},{1,9},{9,1},{2,10},{10,2},{3,11},{11,3},{4,12},{12,4},... | collective-permute-start | bytes 3538952 | tf_op jit(solution)/shard_map/ppermute | solution.py:293
  112.0 31.4 %collective-permute-start.12 = (bf16[5120,128]{1,0:T(8,128)(2,1)}, bf16[5120,128]{1,0:T(8,128)(2,1)}, u32[]{:S(2)}, u32[]{:S(2)}) collective-permute-start(bf16[5120,128]{1,0:T(8,128)(2,1)} %pad_maximum_fusion), channel_id=1, source_target_pairs={{0,2},{6,4},{1,3},{7,5},{8,10},{14,12},{9,11},{15,13},{16,18},{22,... | collective-permute-start | bytes 3932168 | tf_op jit(solution)/shard_map/ppermute | solution.py:294
  114.4 27.7 %collective-permute-start.10 = (bf16[4096,128]{1,0:T(8,128)(2,1)}, bf16[4096,128]{1,0:T(8,128)(2,1)}, u32[]{:S(2)}, u32[]{:S(2)}) collective-permute-start(bf16[4096,128]{1,0:T(8,128)(2,1)} %pad_maximum_fusion.1), channel_id=1, source_target_pairs={{2,4},{4,2},{3,5},{5,3},{10,12},{12,10},{11,13},{13,11},{18,20},{2... | collective-permute-start | bytes 3145736 | tf_op jit(solution)/shard_map/ppermute | solution.py:292
  117.2 47.3 %collective-permute-start.16 = (bf16[64,96,128]{2,1,0:T(8,128)(2,1)}, bf16[64,96,128]{2,1,0:T(8,128)(2,1)}, u32[]{:S(2)}, u32[]{:S(2)}) collective-permute-start(bf16[64,96,128]{2,1,0:T(8,128)(2,1)} %collective-permute-done.5), channel_id=1, source_target_pairs={{4,6},{5,7},{12,14},{13,15},{20,22},{21,23},{28,30},{29,31}} | collective-permute-start | bytes 4718600 | tf_op jit(solution)/shard_map/ppermute | solution.py:290
  119.0 45.5 %collective-permute-start.17 = (bf16[64,96,128]{2,1,0:T(8,128)(2,1)}, bf16[64,96,128]{2,1,0:T(8,128)(2,1)}, u32[]{:S(2)}, u32[]{:S(2)}) collective-permute-start(bf16[64,96,128]{2,1,0:T(8,128)(2,1)} %collective-permute-done.6), channel_id=1, source_target_pairs={{2,0},{3,1},{10,8},{11,9},{18,16},{19,17},{26,24},{27,25}} | collective-permute-start | bytes 4718600 | tf_op jit(solution)/shard_map/ppermute | solution.py:291
  143.4 7.5 %collective-permute-start.14 = (bf16[5120,128]{1,0:T(8,128)(2,1)}, bf16[5120,128]{1,0:T(8,128)(2,1)}, u32[]{:S(2)}, u32[]{:S(2)}) collective-permute-start(bf16[5120,128]{1,0:T(8,128)(2,1)} %collective-permute-done.12.refs_4_), channel_id=1, source_target_pairs={{0,1},{1,0},{2,3},{3,2},{4,5},{5,4},{6,7},{7,6},{8,9},{9,8},{10,11... | collective-permute-start | bytes 3932168 | tf_op jit(solution)/shard_map/ppermute | solution.py:200
  146.1 4.8 %collective-permute-start.13 = (bf16[36,128,128]{2,1,0:T(8,128)(2,1)}, bf16[36,128,128]{2,1,0:T(8,128)(2,1)}, u32[]{:S(2)}, u32[]{:S(2)}) collective-permute-start(bf16[36,128,128]{2,1,0:T(8,128)(2,1)} %collective-permute-done.11), channel_id=1, source_target_pairs={{0,1},{1,0},{2,3},{3,2},{4,5},{5,4},{6,7},{7,6},{8,9},{9,8},{10,11... | collective-permute-start | bytes 3538952 | tf_op jit(solution)/shard_map/ppermute | solution.py:200
  146.7 4.2 %collective-permute-start.15 = (bf16[4096,128]{1,0:T(8,128)(2,1)}, bf16[4096,128]{1,0:T(8,128)(2,1)S(1)}, u32[]{:S(2)}, u32[]{:S(2)}) collective-permute-start(bf16[4096,128]{1,0:T(8,128)(2,1)} %collective-permute-done.10.refs_12_.refs_14_), channel_id=1, source_target_pairs={{0,1},{1,0},{2,3},{3,2},{4,5},{5,4},{6,7},{7,6},{8,9},{9,8},{10,11... | collective-permute-start | bytes 3145736 | tf_op jit(solution)/shard_map/ppermute | solution.py:200
  167.9 29.0 %collective-permute-start.19 = (bf16[112,32,128]{2,1,0:T(8,128)(2,1)}, bf16[112,32,128]{2,1,0:T(8,128)(2,1)}, u32[]{:S(2)}, u32[]{:S(2)}) collective-permute-start(bf16[112,32,128]{2,1,0:T(8,128)(2,1)} %shard_map.38), channel_id=1, source_target_pairs={{4,6},{2,0},{5,7},{3,1},{12,14},{10,8},{13,15},{11,9},{20,22},{18,... | collective-permute-start | bytes 2752520 | tf_op jit(solution)/shard_map/ppermute | solution.py:339
  (9 other events, 31.6 us)
Sparse Core Ops, SparseCore 0:
  8.9 14.2 all-gather.18
  63.3 13.3 all-gather.14
  78.3 13.2 all-gather.16
  93.0 14.0 all-gather.8
  110.5 10.5 all-gather.12
  146.2 11.2 all-gather.10

commit v7 on v6

--- a/solution.py
+++ b/solution.py
@@ -153,6 +153,9 @@
         else jax.ShapeDtypeStruct((half + 1, all_rows, width), jnp.float32)
     )
     copy_count = len(rights) + sum(len(panel) for panels, _ in groups for panel in panels) + 1
+    scratch_bytes = 4 * (half + 1) * all_rows * width + 2 * right_rows * width
+    scratch_bytes += sum(4 * len(panels) * slots * rows * width for panels, rows in groups)
+    scratch_bytes += 2 * half * all_rows * width if finished else 0
     scalars = jnp.stack([jnp.asarray(value, jnp.int32) for value in [*classes, layer]])
     return pl.pallas_call(
         functools.partial(
@@ -169,7 +172,7 @@
             pltpu.SemaphoreType.DMA((copy_count,)),
             pltpu.SemaphoreType.DMA,
         ],
-        compiler_params=pltpu.CompilerParams(vmem_limit_bytes=48 << 20),
+        compiler_params=pltpu.CompilerParams(vmem_limit_bytes=scratch_bytes + (6 << 20)),
         cost_estimate=pl.CostEstimate(flops=1, bytes_accessed=1, transcendentals=0),
     )(packed, scalars, *operands)
 
@@ -258,7 +261,7 @@
     rising = lax.ppermute(own_near, "col", up)
     falling = lax.ppermute(own_near, "col", down)
     near_other, far_other = swapped(own_near), swapped(own_far)
-    lists = lax.all_gather(step_lists, ("col", "dep")).reshape(columns, 2, *step_lists.shape)
+    both = lax.all_gather(step_lists, "dep")
     right_pair = paired(right_own)
 
     def right_place(slot, layers):
@@ -266,33 +269,33 @@
         first = jnp.where(within < cut, farther * cut + within, 2 * cut + farther * (part - cut) + within - cut)
         return layers * 2 * part + first
 
-    def lists_of(column):
-        return packed_lists(lax.dynamic_index_in_dim(lists, column, 0, False), layer, half, right_place)
-
-    packed, end_packed = lists_of(place), lists_of(jnp.where(place > 1, 3, 0))
+    packed = packed_lists(both, layer, half, right_place)
     end_right = right_own[:cut]
 
-    rising, falling, met, near_other, far_other, packed, end_packed, end_right = lax.optimization_barrier(
-        (rising, falling, met, near_other, far_other, packed, end_packed, end_right)
+    rising, falling, met, near_other, far_other, packed, end_right = lax.optimization_barrier(
+        (rising, falling, met, near_other, far_other, packed, end_right)
     )
     rising_two = lax.ppermute(rising, "col", [(1, 2), (2, 3)])
     falling_two = lax.ppermute(falling, "col", [(2, 1), (1, 0)])
     outer_far = lax.ppermute(own_far, "col", inward)
-    outer_far, end_right = lax.optimization_barrier((outer_far, end_right))
     end_right = lax.ppermute(end_right, "col", inward)
-    met_pair, rising_pair, falling_pair = paired(met), paired(rising), paired(falling)
-    outer_other = swapped(outer_far)
+    end_packed = lax.ppermute(packed, "col", inward)
+    met_pair = paired(met)
+    rising, falling, token = lax.optimization_barrier((rising, falling, swapped(packed)))
+    hop_pair = paired(jnp.concatenate([flat(rising), flat(falling)]))
     end_rest = jnp.concatenate([flat(right_own[cut:]), flat(met[cut:])])
 
-    rising_two, falling_two, outer_far, outer_other, end_right, end_rest = lax.optimization_barrier(
-        (rising_two, falling_two, outer_far, outer_other, end_right, end_rest)
+    rising_two, falling_two, outer_far, end_right, end_rest, end_packed = lax.optimization_barrier(
+        (rising_two, falling_two, outer_far, end_right, end_rest, end_packed)
     )
     rising_three = lax.ppermute(rising_two, "col", [(2, 3)])
     falling_three = lax.ppermute(falling_two, "col", [(1, 0)])
-    crossed = lax.ppermute(jnp.concatenate([own_far, outer_far]), "col", across)
+    crossing = jnp.concatenate([own_far, outer_far])
+    crossing, end_right, end_rest, outer_far = lax.optimization_barrier((crossing, end_right, end_rest, outer_far))
+    crossed = lax.ppermute(crossing, "col", across)
     end_met = lax.ppermute(end_right, "row", [(0, 1), (1, 0)])
     end_rest = lax.ppermute(end_rest, "col", inward)
-    end_pair = paired(end_right)
+    outer_pair, end_pair = paired(outer_far), paired(end_right)
 
     rights = []
     for nearer, farther, stride in ((right_own, met, 0), (right_pair, met_pair, part * rows)):
@@ -300,19 +303,20 @@
             rights += [(value, first * rows, size * rows, stride) for value in (nearer, farther)]
     panels = [
         [(own_near, 0, 0), (near_other, 0, 0)],
-        [(rising, 0, 0), (rising_pair, 0, near_size)],
-        [(falling, 0, 0), (falling_pair, 0, near_size)],
+        [(rising, 0, 0), (hop_pair, 0, 2 * near_size)],
+        [(falling, 0, 0), (hop_pair, near_size, 2 * near_size)],
     ]
     classes = [0, jnp.where(place > 0, 3, -1), jnp.where(place < 3, 1, -1)]
-    total = product_sums(packed, classes, layer, shape, [(panels, near)], rights, None, half, False)
-
-    crossed, end_met, end_rest, end_pair, total = lax.optimization_barrier(
-        (crossed, end_met, end_rest, end_pair, total)
+    known_layer = jnp.where(token[0] < -1, 2, layer)
+    total = product_sums(packed, classes, known_layer, shape, [(panels, near)], rights, None, half, False)
+
+    crossed, end_met, end_rest, outer_pair, end_pair, total = lax.optimization_barrier(
+        (crossed, end_met, end_rest, outer_pair, end_pair, total)
     )
     crossed_other, end_met_other, end_rest_other = swapped(crossed), swapped(end_met), swapped(end_rest)
     far_panels = [
         [(own_far, 0, 0), (far_other, 0, 0)],
-        [(outer_far, 0, 0), (outer_other, 0, 0)],
+        [(outer_far, 0, 0), (outer_pair, 0, far_size)],
         [(crossed, 0, 0), (crossed_other, 0, 0)],
         [(crossed, far_size, 0), (crossed_other, far_size, 0)],
     ]
@@ -331,18 +335,19 @@
         end_packed, classes, layer, shape, [(far_panels, far)], end_rights, None, half, True
     )
 
-    two = jnp.where(place > 1, rising_two, falling_two)
-    two_pair = paired(two)
+    rising_pair, falling_pair = paired(rising_two), paired(falling_two)
     end_rows, total, rising_three, falling_three = lax.optimization_barrier(
         (end_rows, total, rising_three, falling_three)
     )
     received = lax.ppermute(end_rows, "col", outward)
-    three = jnp.where(place > 1, rising_three, falling_three)
     near_panels = [
-        [(two, 0, 0), (two_pair, 0, near_size)],
-        [(three, 0, 0), (swapped(three), 0, 0)],
-    ]
-    classes = [2, jnp.where(place == 3, 1, jnp.where(place == 0, 3, -1))]
+        [(rising_two, 0, 0), (rising_pair, 0, near_size)],
+        [(falling_two, 0, 0), (falling_pair, 0, near_size)],
+        [(rising_three, 0, 0), (swapped(rising_three), 0, 0)],
+        [(falling_three, 0, 0), (swapped(falling_three), 0, 0)],
+    ]
+    classes = [jnp.where(place > 1, 2, -1), jnp.where(place < 2, 2, -1)]
+    classes += [jnp.where(place == 3, 1, -1), jnp.where(place == 0, 3, -1)]
     far_classes = [0, jnp.where(high, 1, 3), jnp.where(high, 3, 1), 2]
     classes += [jnp.where(inner, kind, -1) for kind in far_classes]
     groups = [(near_panels, near), (far_panels, far)]

time: 206 us -> 210 us (1.019)
  the two profiles are of different devices: /device:TPU:12 before, /device:TPU:18 now
where the time goes in v7:
time: 210 us; the launch traced here: 209 us
  waiting for transfers between devices  74.9 us (36%)
  Pallas kernels  52.4 us (25%)
  starting transfers between devices  35.9 us (17%)
  local copies, waits for them, and re-layouts  21.6 us (10%)
  between operations  14.4 us (7%)
  other arithmetic  6.96 us (3%)
  blocking collectives  3.19 us (2%)
    pallas_call x3, Pallas kernels, product_sums(): pl.pallas_call(functools.partial(sum_kernel, numbered, right_spans, given...  51.2 us
    ppermute x1, waiting for transfers between devices, line(): outer_far = lax.ppermute(own_far, 'col', inward)  34.6 us
    ppermute x1, waiting for transfers between devices, line(): rising = lax.ppermute(own_near, 'col', up)  25.2 us
    unnamed x26, local copies, waits for them, and re-layouts  14 us
    ppermute x8, waiting for transfers between devices, swapped(): return lax.ppermute(value, 'dep', [(0, 1), (1, 0)])  9.88 us
    ppermute x1, starting transfers between devices, line(): rising_three = lax.ppermute(rising_two, 'col', [(2, 3)])  6.44 us
    ppermute x1, starting transfers between devices, line(): falling_two = lax.ppermute(falling, 'col', [(2, 1), (1, 0)])  6.29 us
    concatenate x1, other arithmetic, line(): hop_pair = paired(jnp.concatenate([flat(rising), flat(falling)]))  4.6 us
  transfers between devices with their start and end apart: 29, of which 7 were waited for; matrix products, arithmetic and copies ran while one was open for 7% of the time, Pallas kernels for 24%

profile of v7, /device:TPU:18, one launch (start us, length us, event | category | flops | bytes accessed | tf_op | source)
XLA Modules:
  0.0 209.3 jit_solution(11993885974272139681)
XLA Ops:
  8.6 2.7 %slice.41 = bf16[64,96,128]{2,1,0:T(8,128)(2,1)} slice(bf16[64,128,128]{2,1,0:T(8,128)(2,1)} %bitcast.76), slice={[0:64], [0:96], [0:128]} | slice | bytes 3145728 | tf_op jit(solution)/shard_map/slice | solution.py:258
  11.3 3.5 %collective-permute-start = (bf16[64,96,128]{2,1,0:T(8,128)(2,1)}, bf16[64,96,128]{2,1,0:T(8,128)(2,1)}, u32[]{:S(2)}, u32[]{:S(2)}) collective-permute-start(bf16[64,96,128]{2,1,0:T(8,128)(2,1)} %slice.41), channel_id=1, source_target_pairs={{0,2},{2,4},{4,6},{1,3},{3,5},{5,7},{8,10},{10,12},{12,14},{9,11},... | collective-permute-start | bytes 4718600 | tf_op jit(solution)/shard_map/ppermute | solution.py:261
  14.7 2.4 %collective-permute-start.1 = (bf16[64,96,128]{2,1,0:T(8,128)(2,1)}, bf16[64,96,128]{2,1,0:T(8,128)(2,1)}, u32[]{:S(2)}, u32[]{:S(2)}) collective-permute-start(bf16[64,96,128]{2,1,0:T(8,128)(2,1)} %slice.41), channel_id=1, source_target_pairs={{2,0},{4,2},{6,4},{3,1},{5,3},{7,5},{10,8},{12,10},{14,12},{11,9},... | collective-permute-start | bytes 4718600 | tf_op jit(solution)/shard_map/ppermute | solution.py:262
  18.9 3.2 %all-gather = s32[2,1,1,7,3,64]{5,2,4,3,1,0:T(1,128)S(1)} all-gather(s32[1,1,1,7,3,64]{5,2,4,3,1,0:T(1,128)S(1)} %copy-done.12), channel_id=2, replica_groups=mesh['grp'=2,'row'=2,'col'=4,'dep'=2] {'dep'}, dimensions={0}, use_global_device_ids=true | all-gather | bytes 16128 | tf_op jit(solution)/shard_map/all_gather | solution.py:264
  24.1 25.2 %collective-permute-done = bf16[64,96,128]{2,1,0:T(8,128)(2,1)} collective-permute-done((bf16[64,96,128]{2,1,0:T(8,128)(2,1)}, bf16[64,96,128]{2,1,0:T(8,128)(2,1)}, u32[]{:S(2)}, u32[]{:S(2)}) %collective-permute-start) | collective-permute-done | bytes 1572896 | tf_op jit(solution)/shard_map/ppermute | solution.py:261
  49.3 3.2 %collective-permute-done.1 = bf16[64,96,128]{2,1,0:T(8,128)(2,1)} collective-permute-done((bf16[64,96,128]{2,1,0:T(8,128)(2,1)}, bf16[64,96,128]{2,1,0:T(8,128)(2,1)}, u32[]{:S(2)}, u32[]{:S(2)}) %collective-permute-start.1) | collective-permute-done | bytes 1572896 | tf_op jit(solution)/shard_map/ppermute | solution.py:262
  53.8 4.6 %pad_maximum_fusion = bf16[12288,128]{1,0:T(8,128)(2,1)} fusion(bf16[6144,128]{1,0:T(8,128)(2,1)} %bitcast.34.refs_10_, bf16[6144,128]{1,0:T(8,128)(2,1)} %bitcast.33.refs_8_), kind=kLoop, calls=%fused_computation | loop fusion | flops 6291456 | bytes 6291456 | tf_op jit(solution)/shard_map/concatenate | solution.py:285
  58.5 1.9 collective-permute-start.5
  60.4 6.3 %collective-permute-start.6 = (bf16[64,96,128]{2,1,0:T(8,128)(2,1)}, bf16[64,96,128]{2,1,0:T(8,128)(2,1)}, u32[]{:S(2)}, u32[]{:S(2)}) collective-permute-start(bf16[64,96,128]{2,1,0:T(8,128)(2,1)} %collective-permute-done.1), channel_id=1, source_target_pairs={{4,2},{2,0},{5,3},{3,1},{12,10},{10,8},{13,11},{11,9},{20,18},{18,... | collective-permute-start | bytes 4718600 | tf_op jit(solution)/shard_map/ppermute | solution.py:279
  72.9 34.6 %collective-permute-done.7.refs_10_.refs_16_ = bf16[2048,128]{1,0:T(8,128)(2,1)S(1)} collective-permute-done((bf16[2048,128]{1,0:T(8,128)(2,1)S(1)}, bf16[2048,128]{1,0:T(8,128)(2,1)S(1)}, u32[]{:S(2)}, u32[]{:S(2)}) %collective-permute-start.7) | collective-permute-done | bytes 524320 | tf_op jit(solution)/shard_map/ppermute | solution.py:280
  111.2 1.6 collective-permute-start.11
  112.8 1.9 collective-permute-start.10
  114.7 6.4 %collective-permute-start.17 = (bf16[64,96,128]{2,1,0:T(8,128)(2,1)}, bf16[64,96,128]{2,1,0:T(8,128)(2,1)}, u32[]{:S(2)}, u32[]{:S(2)}) collective-permute-start(bf16[64,96,128]{2,1,0:T(8,128)(2,1)} %collective-permute-done.5), channel_id=1, source_target_pairs={{4,6},{5,7},{12,14},{13,15},{20,22},{21,23},{28,30},{29,31}} | collective-permute-start | bytes 4718600 | tf_op jit(solution)/shard_map/ppermute | solution.py:291
  121.2 1.8 collective-permute-start.18
  124.2 2.0 copy-done.2
  126.3 2.4 %copy-done.3 = bf16[112,128,128]{2,1,0:T(8,128)(2,1)S(1)} copy-done((bf16[112,128,128]{2,1,0:T(8,128)(2,1)S(1)}, bf16[112,128,128]{2,1,0:T(8,128)(2,1)}, u32[]{:S(2)}) %copy-start.3) | copy-done | bytes 3670040
  128.7 15.2 %shard_map.37.refs_20_ = f32[113,96,128]{2,1,0:T(8,128)S(1)} custom-call(s32[896]{0:T(1024)S(1)} %or_select_fusion.refs_0_, s32[4]{0:T(128)S(1)} %pad_add_fusion.refs_1_, bf16[7168,128]{1,0:T(8,128)(2,1)S(1)} %bitcast.61, bf16[7168,128]{1,0:T(8,128)(2,1)} %bitcast.16.refs_3_, bf16[14336,128]{1,0:T(8,128)(2,1)S(1)} %bitcast.63, ...), custom_call_target="tpu_custom_call" | custom-call | flops 1 | bytes 1 | tf_op jit(solution)/shard_map/pallas_call | solution.py:160
  143.8 2.4 %copy-done.1 = f32[113,96,128]{2,1,0:T(8,128)} copy-done((f32[113,96,128]{2,1,0:T(8,128)}, f32[113,96,128]{2,1,0:T(8,128)S(1)}, u32[]{:S(2)}) %copy-start.1) | copy-done | bytes 5554200
  147.1 5.6 %collective-permute-done.16.refs_13_.refs_19_ = bf16[4096,128]{1,0:T(8,128)(2,1)S(1)} collective-permute-done((bf16[4096,128]{1,0:T(8,128)(2,1)}, bf16[4096,128]{1,0:T(8,128)(2,1)S(1)}, u32[]{:S(2)}, u32[]{:S(2)}) %collective-permute-start.16) | collective-permute-done | bytes 1048608 | tf_op jit(solution)/shard_map/ppermute | solution.py:203
  156.1 1.8 copy-done.11
  157.9 12.3 %shard_map.38 = bf16[112,32,128]{2,1,0:T(8,128)(2,1)} custom-call(s32[896]{0:T(1024)S(1)} %collective-permute-done.9.refs_0_, s32[5]{0:T(128)S(1)} %stack.60.refs_1_, bf16[4608,128]{1,0:T(8,128)(2,1)} %bitcast.26.refs_2_, bf16[4608,128]{1,0:T(8,128)(2,1)} %bitcast.35.refs_3_, bf16[5120,128]{1,0:T(8,128)(2,1)} %collective-permute-done.12.refs_4_, ...), custom_call_target="tpu_custom_call" | custom-call | flops 1 | bytes 1 | tf_op jit(solution)/shard_map/pallas_call | solution.py:160
  170.8 2.2 %collective-permute-start.21 = (bf16[112,32,128]{2,1,0:T(8,128)(2,1)}, bf16[112,32,128]{2,1,0:T(8,128)(2,1)}, u32[]{:S(2)}, u32[]{:S(2)}) collective-permute-start(bf16[112,32,128]{2,1,0:T(8,128)(2,1)} %shard_map.38), channel_id=1, source_target_pairs={{4,6},{2,0},{5,7},{3,1},{12,14},{10,8},{13,15},{11,9},{20,22},{18,... | collective-permute-start | bytes 2752520 | tf_op jit(solution)/shard_map/ppermute | solution.py:342
  174.0 2.2 %collective-permute-done.20 = bf16[64,96,128]{2,1,0:T(8,128)(2,1)} collective-permute-done((bf16[64,96,128]{2,1,0:T(8,128)(2,1)}, bf16[64,96,128]{2,1,0:T(8,128)(2,1)}, u32[]{:S(2)}, u32[]{:S(2)}) %collective-permute-start.20) | collective-permute-done | bytes 1572896 | tf_op jit(solution)/shard_map/ppermute | solution.py:203
  177.5 23.8 %shard_map.39.block = bf16[112,128,128]{2,1,0:T(8,128)(2,1)} custom-call(s32[896]{0:T(1024)S(1)} %or_select_fusion.refs_0_, s32[9]{0:T(128)S(1)} %stack.59.refs_1_, bf16[7168,128]{1,0:T(8,128)(2,1)} %bitcast.59, bf16[7168,128]{1,0:T(8,128)(2,1)} %bitcast.16.refs_3_, bf16[14336,128]{1,0:T(8,128)(2,1)} %bitcast.62, bf16[14336,128]{1,0:T(8,128)(2,1)} %bitcast.64, ...), custom_call_target="tpu_custom_call" | custom-call | flops 1 | bytes 1 | tf_op jit(solution)/shard_map/pallas_call | solution.py:160
  (106 shorter events, 25.7 us)
Async XLA Ops:
  6.5 117.7 %all-gather.22.cloned.1.call-start = ((), (), s32[]{:S(2)}) async-start(), calls=%async_computation.6 | async-start | bytes 5505024 | tf_op jit(solution)/shard_map/all_gather | solution.py:207
  7.3 116.9 %all-gather.10.cloned.1.call-start = ((), (), s32[]{:S(2)}) async-start(), calls=%async_computation | async-start | bytes 5505024 | tf_op jit(solution)/shard_map/all_gather | solution.py:207
  8.0 44.5 %collective-permute-start.2 = (bf16[56,128,128]{2,1,0:T(8,128)(2,1)S(1)}, bf16[56,128,128]{2,1,0:T(8,128)(2,1)}, u32[]{:S(2)}, u32[]{:S(2)}) collective-permute-start(bf16[56,128,128]{2,1,0:T(8,128)(2,1)S(1)} %bitcast.60), channel_id=1, source_target_pairs={{0,8},{8,0},{1,9},{9,1},{2,10},{10,2},{3,11},{11,3},{4,12},{12,4},... | collective-permute-start | bytes 5505032 | tf_op jit(solution)/shard_map/ppermute | solution.py:260
  11.3 38.1 %collective-permute-start = (bf16[64,96,128]{2,1,0:T(8,128)(2,1)}, bf16[64,96,128]{2,1,0:T(8,128)(2,1)}, u32[]{:S(2)}, u32[]{:S(2)}) collective-permute-start(bf16[64,96,128]{2,1,0:T(8,128)(2,1)} %slice.41), channel_id=1, source_target_pairs={{0,2},{2,4},{4,6},{1,3},{3,5},{5,7},{8,10},{10,12},{12,14},{9,11},... | collective-permute-start | bytes 4718600 | tf_op jit(solution)/shard_map/ppermute | solution.py:261
  14.7 37.8 %collective-permute-start.1 = (bf16[64,96,128]{2,1,0:T(8,128)(2,1)}, bf16[64,96,128]{2,1,0:T(8,128)(2,1)}, u32[]{:S(2)}, u32[]{:S(2)}) collective-permute-start(bf16[64,96,128]{2,1,0:T(8,128)(2,1)} %slice.41), channel_id=1, source_target_pairs={{2,0},{4,2},{6,4},{3,1},{5,3},{7,5},{10,8},{12,10},{14,12},{11,9},... | collective-permute-start | bytes 4718600 | tf_op jit(solution)/shard_map/ppermute | solution.py:262
  17.1 35.4 %collective-permute-start.3 = (bf16[64,96,128]{2,1,0:T(8,128)(2,1)}, bf16[64,96,128]{2,1,0:T(8,128)(2,1)}, u32[]{:S(2)}, u32[]{:S(2)}) collective-permute-start(bf16[64,96,128]{2,1,0:T(8,128)(2,1)} %slice.41), channel_id=1, source_target_pairs={{0,1},{1,0},{2,3},{3,2},{4,5},{5,4},{6,7},{7,6},{8,9},{9,8},{10,11... | collective-permute-start | bytes 4718600 | tf_op jit(solution)/shard_map/ppermute | solution.py:203
  52.6 71.7 %all-gather.20.cloned.1.call-start = ((), (), s32[]{:S(2)}) async-start(), calls=%async_computation.5 | async-start | bytes 9437184 | tf_op jit(solution)/shard_map/all_gather | solution.py:207
  58.5 87.8 %all-gather.16.cloned.1.call-start = ((), (), s32[]{:S(2)}) async-start(), calls=%async_computation.3 | async-start | bytes 1572864 | tf_op jit(solution)/shard_map/all_gather | solution.py:207
  58.5 49.1 %collective-permute-start.5 = (bf16[64,96,128]{2,1,0:T(8,128)(2,1)}, bf16[64,96,128]{2,1,0:T(8,128)(2,1)}, u32[]{:S(2)}, u32[]{:S(2)}) collective-permute-start(bf16[64,96,128]{2,1,0:T(8,128)(2,1)} %collective-permute-done), channel_id=1, source_target_pairs={{2,4},{4,6},{3,5},{5,7},{10,12},{12,14},{11,13},{13,15},{18,20},{2... | collective-permute-start | bytes 4718600 | tf_op jit(solution)/shard_map/ppermute | solution.py:278
  60.4 47.2 %collective-permute-start.6 = (bf16[64,96,128]{2,1,0:T(8,128)(2,1)}, bf16[64,96,128]{2,1,0:T(8,128)(2,1)}, u32[]{:S(2)}, u32[]{:S(2)}) collective-permute-start(bf16[64,96,128]{2,1,0:T(8,128)(2,1)} %collective-permute-done.1), channel_id=1, source_target_pairs={{4,2},{2,0},{5,3},{3,1},{12,10},{10,8},{13,11},{11,9},{20,18},{18,... | collective-permute-start | bytes 4718600 | tf_op jit(solution)/shard_map/ppermute | solution.py:279
  66.7 40.9 %collective-permute-start.8 = (bf16[36,128,128]{2,1,0:T(8,128)(2,1)}, bf16[36,128,128]{2,1,0:T(8,128)(2,1)}, u32[]{:S(2)}, u32[]{:S(2)}) collective-permute-start(bf16[36,128,128]{2,1,0:T(8,128)(2,1)} %slice_bitcast_fusion), channel_id=1, source_target_pairs={{0,2},{6,4},{1,3},{7,5},{8,10},{14,12},{9,11},{15,13},{16,18},{22,... | collective-permute-start | bytes 3538952 | tf_op jit(solution)/shard_map/ppermute | solution.py:281
  68.0 39.6 %collective-permute-start.7 = (bf16[2048,128]{1,0:T(8,128)(2,1)S(1)}, bf16[2048,128]{1,0:T(8,128)(2,1)S(1)}, u32[]{:S(2)}, u32[]{:S(2)}) collective-permute-start(bf16[2048,128]{1,0:T(8,128)(2,1)S(1)} %bitcast.67), channel_id=1, source_target_pairs={{0,2},{6,4},{1,3},{7,5},{8,10},{14,12},{9,11},{15,13},{16,18},{22,... | collective-permute-start | bytes 1572872 | tf_op jit(solution)/shard_map/ppermute | solution.py:280
  69.4 38.3 %collective-permute-start.9 = (s32[896]{0:T(1024)S(1)}, s32[896]{0:T(1024)S(1)}, u32[]{:S(2)}, u32[]{:S(2)}) collective-permute-start(s32[896]{0:T(1024)S(1)} %or_select_fusion.refs_0_), channel_id=1, source_target_pairs={{0,2},{6,4},{1,3},{7,5},{8,10},{14,12},{9,11},{15,13},{16,18},{22,... | collective-permute-start | bytes 10760 | tf_op jit(solution)/shard_map/ppermute | solution.py:282
  108.7 37.6 %all-gather.18.cloned.1.call-start = ((), (), s32[]{:S(2)}) async-start(), calls=%async_computation.4 | async-start | bytes 3538944 | tf_op jit(solution)/shard_map/all_gather | solution.py:207
  109.3 63.8 %all-gather.12.cloned.1.call-start = ((), (), s32[]{:S(2)}) async-start(), calls=%async_computation.1 | async-start | bytes 4718592 | tf_op jit(solution)/shard_map/all_gather | solution.py:207
  109.9 63.2 %all-gather.14.cloned.1.call-start = ((), (), s32[]{:S(2)}) async-start(), calls=%async_computation.2 | async-start | bytes 4718592 | tf_op jit(solution)/shard_map/all_gather | solution.py:207
  109.9 36.3 %collective-permute-start.12 = (bf16[5120,128]{1,0:T(8,128)(2,1)}, bf16[5120,128]{1,0:T(8,128)(2,1)}, u32[]{:S(2)}, u32[]{:S(2)}) collective-permute-start(bf16[5120,128]{1,0:T(8,128)(2,1)} %pad_maximum_fusion.1), channel_id=1, source_target_pairs={{0,2},{6,4},{1,3},{7,5},{8,10},{14,12},{9,11},{15,13},{16,18},{22,... | collective-permute-start | bytes 3932168 | tf_op jit(solution)/shard_map/ppermute | solution.py:297
  111.2 35.0 %collective-permute-start.11 = (bf16[36,128,128]{2,1,0:T(8,128)(2,1)}, bf16[36,128,128]{2,1,0:T(8,128)(2,1)}, u32[]{:S(2)}, u32[]{:S(2)}) collective-permute-start(bf16[36,128,128]{2,1,0:T(8,128)(2,1)} %collective-permute-done.8), channel_id=1, source_target_pairs={{0,8},{8,0},{1,9},{9,1},{2,10},{10,2},{3,11},{11,3},{4,12},{12,4},... | collective-permute-start | bytes 3538952 | tf_op jit(solution)/shard_map/ppermute | solution.py:296
  112.8 33.5 %collective-permute-start.10 = (bf16[4096,128]{1,0:T(8,128)(2,1)}, bf16[4096,128]{1,0:T(8,128)(2,1)}, u32[]{:S(2)}, u32[]{:S(2)}) collective-permute-start(bf16[4096,128]{1,0:T(8,128)(2,1)} %pad_maximum_fusion.2), channel_id=1, source_target_pairs={{2,4},{4,2},{3,5},{5,3},{10,12},{12,10},{11,13},{13,11},{18,20},{2... | collective-permute-start | bytes 3145736 | tf_op jit(solution)/shard_map/ppermute | solution.py:295
  114.7 55.4 %collective-permute-start.17 = (bf16[64,96,128]{2,1,0:T(8,128)(2,1)}, bf16[64,96,128]{2,1,0:T(8,128)(2,1)}, u32[]{:S(2)}, u32[]{:S(2)}) collective-permute-start(bf16[64,96,128]{2,1,0:T(8,128)(2,1)} %collective-permute-done.5), channel_id=1, source_target_pairs={{4,6},{5,7},{12,14},{13,15},{20,22},{21,23},{28,30},{29,31}} | collective-permute-start | bytes 4718600 | tf_op jit(solution)/shard_map/ppermute | solution.py:291
  121.2 49.0 %collective-permute-start.18 = (bf16[64,96,128]{2,1,0:T(8,128)(2,1)}, bf16[64,96,128]{2,1,0:T(8,128)(2,1)}, u32[]{:S(2)}, u32[]{:S(2)}) collective-permute-start(bf16[64,96,128]{2,1,0:T(8,128)(2,1)} %collective-permute-done.6), channel_id=1, source_target_pairs={{2,0},{3,1},{10,8},{11,9},{18,16},{19,17},{26,24},{27,25}} | collective-permute-start | bytes 4718600 | tf_op jit(solution)/shard_map/ppermute | solution.py:292
  146.3 7.3 %collective-permute-start.15 = (bf16[5120,128]{1,0:T(8,128)(2,1)}, bf16[5120,128]{1,0:T(8,128)(2,1)}, u32[]{:S(2)}, u32[]{:S(2)}) collective-permute-start(bf16[5120,128]{1,0:T(8,128)(2,1)} %collective-permute-done.12.refs_4_), channel_id=1, source_target_pairs={{0,1},{1,0},{2,3},{3,2},{4,5},{5,4},{6,7},{7,6},{8,9},{9,8},{10,11... | collective-permute-start | bytes 3932168 | tf_op jit(solution)/shard_map/ppermute | solution.py:203
  146.4 7.2 %collective-permute-start.14 = (bf16[36,128,128]{2,1,0:T(8,128)(2,1)}, bf16[36,128,128]{2,1,0:T(8,128)(2,1)}, u32[]{:S(2)}, u32[]{:S(2)}) collective-permute-start(bf16[36,128,128]{2,1,0:T(8,128)(2,1)} %collective-permute-done.11), channel_id=1, source_target_pairs={{0,1},{1,0},{2,3},{3,2},{4,5},{5,4},{6,7},{7,6},{8,9},{9,8},{10,11... | collective-permute-start | bytes 3538952 | tf_op jit(solution)/shard_map/ppermute | solution.py:203
  170.8 30.5 %collective-permute-start.21 = (bf16[112,32,128]{2,1,0:T(8,128)(2,1)}, bf16[112,32,128]{2,1,0:T(8,128)(2,1)}, u32[]{:S(2)}, u32[]{:S(2)}) collective-permute-start(bf16[112,32,128]{2,1,0:T(8,128)(2,1)} %shard_map.38), channel_id=1, source_target_pairs={{4,6},{2,0},{5,7},{3,1},{12,14},{10,8},{13,15},{11,9},{20,22},{18,... | collective-permute-start | bytes 2752520 | tf_op jit(solution)/shard_map/ppermute | solution.py:342
  (18 other events, 92.0 us)
Sparse Core Ops, SparseCore 0:
  8.9 15.1 all-gather.21
  52.7 13.2 all-gather.9
  67.5 17.9 all-gather.19
  108.9 9.3 all-gather.15
  119.6 12.1 all-gather.17
  133.2 13.2 all-gather.11
  148.1 15.4 all-gather.13

commit v8 on v0

v8 whole, which is shorter than its diff:
```python
import functools

import jax
import jax.numpy as jnp
from jax import lax
from jax.experimental import pallas as pl
from jax.experimental.pallas import tpu as pltpu
from jax.sharding import PartitionSpec as P

NBQ = 32
UNROLL = 8


def chosen_products(packed, classes, panels, todo, shape, layers, spare):
    step_count, columns, slots = shape
    count = jnp.int32(0)
    for panel in range(panels):
        kind = classes[panel]
        for extra in range(-(-step_count // columns)):
            step = lax.rem(kind + step_count // 2, columns) + extra * columns
            groups = jnp.where((kind >= 0) & (step < step_count), slots // 8, 0)
            for layer in range(layers):
                base = (layer * step_count + step) * slots

                def keep(group, count):
                    for lane in range(8):
                        entry = packed[base + group * 8 + lane]
                        todo[count] = entry + (panel * layers * slots << 10)
                        count += (entry >= 0).astype(jnp.int32)
                    return count

                count = lax.fori_loop(0, groups, keep, count)
    for extra in range(UNROLL - 1):
        todo[count + extra] = jnp.int32(spare)
    return count


def add_chosen(todo, count, left, right, work):
    def several(group, carry):
        entries = [todo[group * UNROLL + lane] for lane in range(UNROLL)]
        products = [
            jnp.dot(left[(entry >> 10) & 1023], right[entry >> 20], preferred_element_type=jnp.float32)
            for entry in entries
        ]
        for entry, product in zip(entries, products):
            work[entry & 1023] += product
        return carry

    lax.fori_loop(0, (count + UNROLL - 1) // UNROLL, several, jnp.int32(0))


def sum_kernel(panels, rights, givens, saved, shape, layers, operand_count, layer_at, *refs):
    packed, classes, refs = refs[0], refs[1], refs[2:]
    operands, refs = refs[:operand_count], refs[operand_count:]
    outs, refs = refs[: max(len(saved), 1)], refs[max(len(saved), 1) :]
    work, left, right, todo, sems = refs
    spare = work.shape[0] - 1
    other = 1 - classes[layer_at]
    copies = []

    def plan(source, target, when=None):
        copies.append((pltpu.make_async_copy(source, target, sems.at[len(copies)]), when))

    start = 0
    for operand, size, gathered in rights:
        source = operands[operand]
        if gathered:
            source = source.at[pl.ds(other * size, size)]
        plan(source, right.at[pl.ds(start, size)])
        start += size
    start = 0
    for panel, pieces in enumerate(panels):
        for operand, size, gathered in pieces:
            source = operands[operand]
            if gathered:
                source = source.at[pl.ds(other * size, size)]
            plan(source, left.at[pl.ds(start, size)], classes[panel] >= 0)
            start += size
    start = 0
    for operand, size in givens:
        plan(operands[operand], work.at[pl.ds(start, size)])
        start += size
    for copy, when in copies:
        copy.start() if when is None else pl.when(when)(copy.start)
    if givens:
        work[spare] = jnp.zeros_like(work[spare])
    else:
        work[...] = jnp.zeros_like(work)
    kinds = [classes[panel] for panel in range(len(panels))]
    count = chosen_products(packed, kinds, len(panels), todo, shape, layers, spare)
    for copy, when in copies:
        copy.wait() if when is None else pl.when(when)(copy.wait)
    add_chosen(todo, count, left, right, work)
    if saved:
        start, copies = 0, []
        for out, size in zip(outs, saved):
            copies.append(pltpu.make_async_copy(work.at[pl.ds(start, size)], out, sems.at[len(copies)]))
            start += size
        for copy in copies:
            copy.start()
        for copy in copies:
            copy.wait()
    else:
        outs[0][...] = work[:spare].astype(outs[0].dtype)


def product_sums(packed, classes, layer, shape, layers, panels, rights, givens, result_slots, saved):
    step_count, columns, slots = shape
    rows, width = rights[0][0].shape[1:]
    operands = []

    def number(value):
        for index, known in enumerate(operands):
            if known is value:
                return index
        operands.append(value)
        return len(operands) - 1

    def spans(pieces):
        return [
            (number(value), value.shape[0] // 2 if gathered else value.shape[0], gathered)
            for value, gathered in pieces
        ]

    right_spans = spans(rights)
    panel_spans = [spans(pieces) for pieces in panels]
    given_spans = [(number(value), value.shape[0]) for value in givens]
    right_slots = sum(size for _, size, _ in right_spans)
    left_slots = len(panels) * layers * slots
    assert right_slots <= 1024 and left_slots <= 1024 and result_slots < 1024 and slots % 8 == 0
    assert all(sum(size for _, size, _ in pieces) == layers * slots for pieces in panel_spans)
    anywhere = pl.BlockSpec(memory_space=pl.ANY)
    in_scalar = pl.BlockSpec(memory_space=pltpu.SMEM)
    copy_count = len(rights) + sum(len(pieces) for pieces in panels) + len(givens) + len(saved)
    scalars = jnp.stack([jnp.asarray(value, jnp.int32) for value in [*classes, layer]])
    if saved:
        out_shape = [jax.ShapeDtypeStruct((size, rows, width), jnp.float32) for size in saved]
    else:
        out_shape = [jax.ShapeDtypeStruct((result_slots, rows, width), jnp.bfloat16)]
    return pl.pallas_call(
        functools.partial(
            sum_kernel, panel_spans, right_spans, given_spans, saved, shape, layers, len(operands), len(classes)
        ),
        out_shape=out_shape,
        in_specs=[in_scalar, in_scalar] + [anywhere] * len(operands),
        out_specs=[anywhere if saved else pl.BlockSpec(memory_space=pltpu.VMEM)] * len(out_shape),
        scratch_shapes=[
            pltpu.VMEM((result_slots + 1, rows, width), jnp.float32),
            pltpu.VMEM((left_slots, rows, width), jnp.bfloat16),
            pltpu.VMEM((right_slots, width, width), jnp.bfloat16),
            pltpu.SMEM((len(panels) * -(-step_count // columns) * layers * slots + UNROLL,), jnp.int32),
            pltpu.SemaphoreType.DMA((copy_count,)),
        ],
        compiler_params=pltpu.CompilerParams(vmem_limit_bytes=56 << 20),
        cost_estimate=pl.CostEstimate(flops=1, bytes_accessed=1, transcendentals=0),
    )(packed, scalars, *operands)


def swapped(value):
    return lax.ppermute(value, "dep", [(0, 1), (1, 0)])


def paired(value):
    return lax.all_gather(value, "dep", axis=0, tiled=True)


def kept_products(both, layer, half, right_slot):
    both = jnp.where(layer > 0, both[::-1], both)
    slots = both.shape[3]
    result = both[:, :, 2] - layer * half
    wanted = (result >= 0) & (result < half)
    layers = jnp.arange(2, dtype=jnp.int32)[:, None, None]
    packed = right_slot(both[:, :, 1], layers) << 20 | (layers * slots + both[:, :, 0]) << 10 | result
    return jnp.where(wanted, packed, -1).reshape(-1)


def layer_products(step_lists, layer, half, right_slot):
    result = step_lists[:, 2]
    turned = (result + layer * half) % (2 * half)
    packed = right_slot(step_lists[:, 1], 0) << 20 | step_lists[:, 0] << 10 | turned
    return jnp.where(result < 2 * half, packed, -1).reshape(-1)


def ring(left_blocks, right_blocks, triples, half):
    own, right_own, step_lists = left_blocks[0, 0, 0], right_blocks[0, 0, 0], triples[0, 0, 0]
    columns, layer = lax.axis_size("col"), lax.axis_index("dep")
    gathered = lax.all_gather(right_own, "row", axis=0, tiled=True)
    right_slots = gathered.shape[0]
    both = lax.all_gather(step_lists, "dep")
    packed = kept_products(both, layer, half, lambda slot, layers: layers * right_slots + slot)
    rights = [(gathered, False), (swapped(gathered), False)]
    shape = (step_lists.shape[0], columns, own.shape[0])
    rising, falling, total = own, own, []
    panels, classes = [[(own, False), (paired(own), True)]], [0]
    reach = step_lists.shape[0] // 2
    for distance in range(1, reach + 1):
        rising = lax.ppermute(rising, "col", [(i, (i + 1) % columns) for i in range(columns)])
        falling = lax.ppermute(falling, "col", [(i, (i - 1) % columns) for i in range(columns)])
        panels += [[(value, False), (paired(value), True)] for value in (rising, falling)]
        classes += [columns - distance, distance]
        saved = [] if distance == reach else [half]
        total = product_sums(packed, classes, layer, shape, 2, panels, rights, total, half, saved)
        panels, classes = [], []
    return total[0][None, None, None]


def line(left_blocks, right_blocks, triples, half):
    own, right_own, step_lists = left_blocks[0, 0, 0], right_blocks[0, 0, 0], triples[0, 0, 0]
    slots, part = own.shape[0], right_own.shape[0]
    columns, layer, place = lax.axis_size("col"), lax.axis_index("dep"), lax.axis_index("col")
    shape = (step_lists.shape[0], columns, slots)
    pieces = [own[: slots // 2], own[slots // 2 :]]
    fence = lax.optimization_barrier

    def hop(values, pairs):
        return [lax.ppermute(value, "col", pairs) for value in values]

    def right_slot(slot, layers):
        return (layers * 2 + ((slot // part) ^ lax.axis_index("row"))) * part + slot % part

    rising = hop(pieces, [(0, 1), (1, 2), (2, 3)])
    falling = hop(pieces, [(1, 0), (2, 1), (3, 2)])
    met = lax.ppermute(right_own, "row", [(0, 1), (1, 0)])
    both = lax.all_gather(step_lists, "dep")
    kept = kept_products(both, layer, half, right_slot)
    listed = layer_products(step_lists, layer, half, right_slot)
    right_pair = paired(right_own)

    rising[0], falling[0] = fence((rising[0], falling[0]))
    rising_two = hop(rising[:1], [(1, 2), (2, 3)])
    falling_two = hop(falling[:1], [(1, 0), (2, 1)])
    rising[1], falling[1], met, kept, listed = fence((rising[1], falling[1], met, kept, listed))
    rising_two += hop(rising[1:], [(1, 2), (2, 3)])
    falling_two += hop(falling[1:], [(1, 0), (2, 1)])
    met_pair = paired(met)
    rights = [(right_own, False), (met, False)]
    panels = [[(value, False) for value in values] for values in (pieces, rising, falling)]
    classes = [0, jnp.where(place > 0, 3, -1), jnp.where(place < 3, 1, -1)]
    sums = product_sums(listed, classes, layer, shape, 1, panels, rights, [], 2 * half, [half, half])

    rising_two[0], falling_two[0], sums = fence((rising_two[0], falling_two[0], sums))
    rising_three = hop(rising_two[:1], [(2, 3)])
    falling_three = hop(falling_two[:1], [(1, 0)])
    rising_two[1], falling_two[1] = fence((rising_two[1], falling_two[1]))
    rising_three += hop(rising_two[1:], [(2, 3)])
    falling_three += hop(falling_two[1:], [(1, 0)])
    panels = [[(value, False) for value in values] for values in (rising_two, falling_two)]
    classes = [jnp.where(place > 1, 2, -1), jnp.where(place < 2, 2, -1)]
    sums = product_sums(listed, classes, layer, shape, 1, panels, rights, sums, 2 * half, [half, half])
    total = sums[0] + swapped(sums[1])

    rising_three, falling_three, total = fence((rising_three, falling_three, total))
    panels = [
        [(value, False) for value in [*values, *[swapped(value) for value in values]]]
        for values in (rising_three, falling_three)
    ]
    classes = [jnp.where(place == 3, 1, -1), jnp.where(place == 0, 3, -1)]
    rights += [(right_pair, True), (met_pair, True)]
    return product_sums(kept, classes, layer, shape, 2, panels, rights, [total], half, [])[0][None, None, None]


def local(left_blocks, right_blocks, triples):
    step_count = triples.shape[3]
    row_count, columns = lax.axis_size("row"), lax.axis_size("col")
    half = (2 * step_count - 2 + row_count) // row_count * NBQ // 2
    if columns >= step_count:
        return ring(left_blocks, right_blocks, triples, half)
    assert columns == 4 and row_count == 2
    return line(left_blocks, right_blocks, triples, half)


def solution(mesh):
    return jax.shard_map(
        local,
        mesh=mesh,
        in_specs=(
            P(("grp", "row"), "col", "dep", None, None, None),
            P(("grp", "row"), "col", "dep", None, None, None),
            P(("grp", "row"), "col", "dep", None, None, None),
        ),
        out_specs=P(("grp", "row"), "col", "dep", None, None, None),
        check_vma=False,
    )
```

time: 373 us -> 212 us (0.57)
  other arithmetic: 104 us -> 13.7 us
  local copies, waits for them, and re-layouts: 74.3 us -> 4 us
  Pallas kernels: 0 us -> 43.8 us
  matrix products: 34.2 us -> 0 us
  waiting for transfers between devices: 133 us -> 105 us
  starting transfers between devices: 12.3 us -> 28.9 us
    scatter-add x7 -> x0, other arithmetic: 96.5 us -> none  [add_products(): return accumulated.at[step_list[2]].add(products)]
    gather x14 -> x0, local copies, waits for them, and re-layouts: 54.2 us -> none  [the longest x7 28.1 us: add_products(): right_rows = jnp.take(gathered, step_list[1], axis=0)]
    pallas_call x0 -> x3, Pallas kernels: none -> 43.8 us  [product_sums(): pl.pallas_call(functools.partial(sum_kernel, panel_spans, right_spans, gi...]
    dot_general x7 -> x0, matrix products: 34.2 us -> none  [add_products(): jnp.einsum('tij,tjk->tik', left_rows, right_rows, preferred_element_type=...]
    reduce_scatter x1 -> x0, waiting for transfers between devices: 26.6 us -> none  [local(): lax.psum_scatter(accumulated[:out_count], 'dep', scatter_dimension=0, til...]
    ppermute x6 -> x18, starting transfers between devices: 12.3 us -> 28.9 us  [the longest x12 22.5 us: hop(): return [lax.ppermute(value, 'col', pairs) for value in values]]
    add x0 -> x1, other arithmetic: none -> 10.6 us  [line(): total = sums[0] + swapped(sums[1])]
    slice x1 -> x2, local copies, waits for them, and re-layouts: 13.1 us -> 2.76 us  [the longest x1 2.76 us: line(): pieces = [own[:slots // 2], own[slots // 2:]]]
  transfers between devices with their start and end apart: 8 -> 20, of which waited for: 5 -> 11; matrix products, arithmetic and copies ran while one was open for 46% -> 8% of each run, Pallas kernels for 0% -> 7%
where the time goes in v8:
time: 212 us
  waiting for transfers between devices  105 us (50%)
  Pallas kernels  43.8 us (21%)
  starting transfers between devices  28.9 us (14%)
  other arithmetic  13.7 us (6%)
  between operations  13.7 us (6%)
  local copies, waits for them, and re-layouts  4 us (2%)
  blocking collectives  3.29 us (2%)
    ppermute x12, waiting for transfers between devices, hop(): return [lax.ppermute(value, 'col', pairs) for value in values]  92 us
    pallas_call x3, Pallas kernels, product_sums(): pl.pallas_call(functools.partial(sum_kernel, panel_spans, right_spans, gi...  43.8 us
    ppermute x12, starting transfers between devices, hop(): return [lax.ppermute(value, 'col', pairs) for value in values]  22.5 us
    ppermute x5, waiting for transfers between devices, swapped(): return lax.ppermute(value, 'dep', [(0, 1), (1, 0)])  11.8 us
    add x1, other arithmetic, line(): total = sums[0] + swapped(sums[1])  10.6 us
    ppermute x5, starting transfers between devices, swapped(): return lax.ppermute(value, 'dep', [(0, 1), (1, 0)])  4.31 us
  transfers between devices with their start and end apart: 20, of which 11 were waited for; matrix products, arithmetic and copies ran while one was open for 8% of the time, Pallas kernels for 7%

profile of v8, /device:TPU:1, one launch (start us, length us, event | category | flops | bytes accessed | tf_op | source)
XLA Modules:
  0.0 211.9 jit_solution(320808421429807869)
XLA Ops:
  6.5 2.0 collective-permute-start.2
  8.6 2.8 %slice_bitcast_fusion = (bf16[32,128,128]{2,1,0:T(8,128)(2,1)S(1)}, bf16[32,128,128]{2,1,0:T(8,128)(2,1)}) fusion(bf16[1,1,1,64,128,128]{5,4,3,2,1,0:T(8,128)(2,1)} %param.3), kind=kLoop, calls=%fused_computation | loop fusion | bytes 4194304 | tf_op jit(solution)/shard_map/slice | solution.py:212
  11.3 4.2 %collective-permute-start = (bf16[32,128,128]{2,1,0:T(8,128)(2,1)}, bf16[32,128,128]{2,1,0:T(8,128)(2,1)}, u32[]{:S(2)}, u32[]{:S(2)}) collective-permute-start(bf16[32,128,128]{2,1,0:T(8,128)(2,1)} %get-tuple-element.50.refs_5_), channel_id=1, source_target_pairs={{0,2},{2,4},{4,6},{1,3},{3,5},{5,7},{8,10},{10,12},{12,14},{9,11},... | collective-permute-start | bytes 3145736 | tf_op jit(solution)/shard_map/ppermute | solution.py:216
  16.8 5.0 %collective-permute-start.3 = (bf16[32,128,128]{2,1,0:T(8,128)(2,1)S(1)}, bf16[32,128,128]{2,1,0:T(8,128)(2,1)}, u32[]{:S(2)}, u32[]{:S(2)}) collective-permute-start(bf16[32,128,128]{2,1,0:T(8,128)(2,1)S(1)} %get-tuple-element.49.refs_4_), channel_id=1, source_target_pairs={{0,2},{2,4},{4,6},{1,3},{3,5},{5,7},{8,10},{10,12},{12,14},{9,11},... | collective-permute-start | bytes 3145736 | tf_op jit(solution)/shard_map/ppermute | solution.py:216
  23.1 3.3 %all-gather = s32[2,1,1,7,3,64]{5,2,4,3,1,0:T(1,128)S(1)} all-gather(s32[1,1,1,7,3,64]{5,2,4,3,1,0:T(1,128)S(1)} %copy-done.4), channel_id=2, replica_groups=mesh['grp'=2,'row'=2,'col'=4,'dep'=2] {'dep'}, dimensions={0}, use_global_device_ids=true | all-gather | bytes 16128 | tf_op jit(solution)/shard_map/all_gather | solution.py:224
  28.9 29.8 %collective-permute-done.3.refs_6_ = bf16[32,128,128]{2,1,0:T(8,128)(2,1)} collective-permute-done((bf16[32,128,128]{2,1,0:T(8,128)(2,1)S(1)}, bf16[32,128,128]{2,1,0:T(8,128)(2,1)}, u32[]{:S(2)}, u32[]{:S(2)}) %collective-permute-start.3) | collective-permute-done | bytes 1048608 | tf_op jit(solution)/shard_map/ppermute | solution.py:216
  58.7 4.9 %collective-permute-done.4.refs_8_ = bf16[32,128,128]{2,1,0:T(8,128)(2,1)} collective-permute-done((bf16[32,128,128]{2,1,0:T(8,128)(2,1)S(1)}, bf16[32,128,128]{2,1,0:T(8,128)(2,1)}, u32[]{:S(2)}, u32[]{:S(2)}) %collective-permute-start.4) | collective-permute-done | bytes 1048608 | tf_op jit(solution)/shard_map/ppermute | solution.py:216
  63.6 1.6 collective-permute-start.5
  66.5 1.7 collective-permute-start.8
  70.8 14.2 %shard_map.37 = (f32[112,128,128]{2,1,0:T(8,128)}, f32[112,128,128]{2,1,0:T(8,128)}) custom-call(s32[448]{0:T(512)} %fusion.14.refs_0_, s32[4]{0:T(128)} %pad_add_fusion.refs_1_, bf16[56,128,128]{2,1,0:T(8,128)(2,1)} %bitcast.46, bf16[56,128,128]{2,1,0:T(8,128)(2,1)} %copy-done, bf16[32,128,128]{2,1,0:T(8,128)(2,1)} %copy-done.1, ...), custom_call_target="tpu_custom_call" | custom-call | flops 1 | bytes 1 | tf_op jit(solution)/shard_map/pallas_call | solution.py:140
  85.0 6.3 %collective-permute-done.6.refs_6_ = bf16[32,128,128]{2,1,0:T(8,128)(2,1)} collective-permute-done((bf16[32,128,128]{2,1,0:T(8,128)(2,1)}, bf16[32,128,128]{2,1,0:T(8,128)(2,1)}, u32[]{:S(2)}, u32[]{:S(2)}) %collective-permute-start.6) | collective-permute-done | bytes 1048608 | tf_op jit(solution)/shard_map/ppermute | solution.py:216
  91.3 22.5 %collective-permute-done.9.refs_7_ = bf16[32,128,128]{2,1,0:T(8,128)(2,1)} collective-permute-done((bf16[32,128,128]{2,1,0:T(8,128)(2,1)}, bf16[32,128,128]{2,1,0:T(8,128)(2,1)}, u32[]{:S(2)}, u32[]{:S(2)}) %collective-permute-start.9) | collective-permute-done | bytes 1048608 | tf_op jit(solution)/shard_map/ppermute | solution.py:216
  113.8 15.6 %shard_map.38 = (f32[112,128,128]{2,1,0:T(8,128)}, f32[112,128,128]{2,1,0:T(8,128)}) custom-call(s32[448]{0:T(512)} %fusion.14.refs_0_, s32[3]{0:T(128)} %add_add_fusion.1.refs_1_, bf16[56,128,128]{2,1,0:T(8,128)(2,1)} %bitcast.47, bf16[56,128,128]{2,1,0:T(8,128)(2,1)} %copy-done, bf16[32,128,128]{2,1,0:T(8,128)(2,1)} %collective-permute-done.5.refs_4_, ...), custom_call_target="tpu_custom_call" | custom-call | flops 1 | bytes 1 | tf_op jit(solution)/shard_map/pallas_call | solution.py:140
  129.4 3.2 %collective-permute-start.13 = (f32[112,128,128]{2,1,0:T(8,128)}, f32[112,128,128]{2,1,0:T(8,128)}, u32[]{:S(2)}, u32[]{:S(2)}) collective-permute-start(f32[112,128,128]{2,1,0:T(8,128)} %get-tuple-element.43), channel_id=1, source_target_pairs={{0,1},{1,0},{2,3},{3,2},{4,5},{5,4},{6,7},{7,6},{8,9},{9,8},{10,11... | collective-permute-start | bytes 22020104 | tf_op jit(solution)/shard_map/ppermute | solution.py:160
  133.3 1.3 collective-permute-start.11
  135.4 1.7 collective-permute-start.10
  138.4 5.8 %collective-permute-done.13 = f32[112,128,128]{2,1,0:T(8,128)} collective-permute-done((f32[112,128,128]{2,1,0:T(8,128)}, f32[112,128,128]{2,1,0:T(8,128)}, u32[]{:S(2)}, u32[]{:S(2)}) %collective-permute-start.13) | collective-permute-done | bytes 7340064 | tf_op jit(solution)/shard_map/ppermute | solution.py:160
  144.2 10.6 %add.77.refs_14_ = f32[112,128,128]{2,1,0:T(8,128)} add(f32[112,128,128]{2,1,0:T(8,128)} %get-tuple-element.42, f32[112,128,128]{2,1,0:T(8,128)} %collective-permute-done.13) | non-fusion elementwise | flops 1835008 | bytes 22020096 | tf_op jit(solution)/shard_map/add | solution.py:250
  154.8 6.0 %collective-permute-done.11.refs_10_ = bf16[32,128,128]{2,1,0:T(8,128)(2,1)S(1)} collective-permute-done((bf16[32,128,128]{2,1,0:T(8,128)(2,1)}, bf16[32,128,128]{2,1,0:T(8,128)(2,1)S(1)}, u32[]{:S(2)}, u32[]{:S(2)}) %collective-permute-start.11) | collective-permute-done | bytes 1048608 | tf_op jit(solution)/shard_map/ppermute | solution.py:216
  160.8 22.6 %collective-permute-done.12.refs_11_ = bf16[32,128,128]{2,1,0:T(8,128)(2,1)} collective-permute-done((bf16[32,128,128]{2,1,0:T(8,128)(2,1)}, bf16[32,128,128]{2,1,0:T(8,128)(2,1)}, u32[]{:S(2)}, u32[]{:S(2)}) %collective-permute-start.12) | collective-permute-done | bytes 1048608 | tf_op jit(solution)/shard_map/ppermute | solution.py:216
  185.0 2.8 %collective-permute-done.14.refs_8_ = bf16[32,128,128]{2,1,0:T(8,128)(2,1)} collective-permute-done((bf16[32,128,128]{2,1,0:T(8,128)(2,1)S(1)}, bf16[32,128,128]{2,1,0:T(8,128)(2,1)}, u32[]{:S(2)}, u32[]{:S(2)}) %collective-permute-start.14) | collective-permute-done | bytes 1048608 | tf_op jit(solution)/shard_map/ppermute | solution.py:160
  187.8 1.6 collective-permute-done.15.refs_9_
  189.4 1.4 collective-permute-done.16.refs_12_
  191.0 14.0 %shard_map.39 = bf16[112,128,128]{2,1,0:T(8,128)(2,1)} custom-call(s32[896]{0:T(1024)} %fusion.7.refs_0_, s32[3]{0:T(128)} %add_add_fusion.refs_1_, bf16[56,128,128]{2,1,0:T(8,128)(2,1)} %bitcast.49, bf16[56,128,128]{2,1,0:T(8,128)(2,1)} %copy-done, bf16[112,128,128]{2,1,0:T(8,128)(2,1)} %bitcast.50, ...), custom_call_target="tpu_custom_call" | custom-call | flops 1 | bytes 1 | tf_op jit(solution)/shard_map/pallas_call | solution.py:140
  (69 shorter events, 13.6 us)
Async XLA Ops:
  6.5 16.5 %copy-start.4 = (s32[1,1,1,7,3,64]{5,2,4,3,1,0:T(1,128)S(1)}, s32[1,1,1,7,3,64]{5,2,4,3,1,0:T(1,128)}, u32[]{:S(2)}) copy-start(s32[1,1,1,7,3,64]{5,2,4,3,1,0:T(1,128)} %param.5) | copy-start | bytes 16132
  6.5 178.5 %all-gather.7.cloned.1.call-start = ((), (), s32[]{:S(2)}) async-start(), calls=%async_computation.1 | async-start | bytes 5505024 | tf_op jit(solution)/shard_map/all_gather | solution.py:164
  6.5 60.0 %collective-permute-start.2 = (bf16[56,128,128]{2,1,0:T(8,128)(2,1)}, bf16[56,128,128]{2,1,0:T(8,128)(2,1)S(1)}, u32[]{:S(2)}, u32[]{:S(2)}) collective-permute-start(bf16[56,128,128]{2,1,0:T(8,128)(2,1)} %bitcast.45), channel_id=1, source_target_pairs={{0,8},{8,0},{1,9},{9,1},{2,10},{10,2},{3,11},{11,3},{4,12},{12,4},... | collective-permute-start | bytes 5505032 | tf_op jit(solution)/shard_map/ppermute | solution.py:223
  11.3 59.4 %copy-start.1 = (bf16[32,128,128]{2,1,0:T(8,128)(2,1)}, bf16[32,128,128]{2,1,0:T(8,128)(2,1)S(1)}, u32[]{:S(2)}) copy-start(bf16[32,128,128]{2,1,0:T(8,128)(2,1)S(1)} %get-tuple-element.49.refs_4_) | copy-start | bytes 3145732
  11.3 55.2 %collective-permute-start = (bf16[32,128,128]{2,1,0:T(8,128)(2,1)}, bf16[32,128,128]{2,1,0:T(8,128)(2,1)}, u32[]{:S(2)}, u32[]{:S(2)}) collective-permute-start(bf16[32,128,128]{2,1,0:T(8,128)(2,1)} %get-tuple-element.50.refs_5_), channel_id=1, source_target_pairs={{0,2},{2,4},{4,6},{1,3},{3,5},{5,7},{8,10},{10,12},{12,14},{9,11},... | collective-permute-start | bytes 3145736 | tf_op jit(solution)/shard_map/ppermute | solution.py:216
  15.5 51.0 %collective-permute-start.1 = (bf16[32,128,128]{2,1,0:T(8,128)(2,1)}, bf16[32,128,128]{2,1,0:T(8,128)(2,1)}, u32[]{:S(2)}, u32[]{:S(2)}) collective-permute-start(bf16[32,128,128]{2,1,0:T(8,128)(2,1)} %get-tuple-element.50.refs_5_), channel_id=1, source_target_pairs={{2,0},{4,2},{6,4},{3,1},{5,3},{7,5},{10,8},{12,10},{14,12},{11,9},... | collective-permute-start | bytes 3145736 | tf_op jit(solution)/shard_map/ppermute | solution.py:216
  16.8 41.9 %collective-permute-start.3 = (bf16[32,128,128]{2,1,0:T(8,128)(2,1)S(1)}, bf16[32,128,128]{2,1,0:T(8,128)(2,1)}, u32[]{:S(2)}, u32[]{:S(2)}) collective-permute-start(bf16[32,128,128]{2,1,0:T(8,128)(2,1)S(1)} %get-tuple-element.49.refs_4_), channel_id=1, source_target_pairs={{0,2},{2,4},{4,6},{1,3},{3,5},{5,7},{8,10},{10,12},{12,14},{9,11},... | collective-permute-start | bytes 3145736 | tf_op jit(solution)/shard_map/ppermute | solution.py:216
  21.8 41.8 %collective-permute-start.4 = (bf16[32,128,128]{2,1,0:T(8,128)(2,1)S(1)}, bf16[32,128,128]{2,1,0:T(8,128)(2,1)}, u32[]{:S(2)}, u32[]{:S(2)}) collective-permute-start(bf16[32,128,128]{2,1,0:T(8,128)(2,1)S(1)} %get-tuple-element.49.refs_4_), channel_id=1, source_target_pairs={{2,0},{4,2},{6,4},{3,1},{5,3},{7,5},{10,8},{12,10},{14,12},{11,9},... | collective-permute-start | bytes 3145736 | tf_op jit(solution)/shard_map/ppermute | solution.py:216
  63.6 21.4 %collective-permute-start.5 = (bf16[32,128,128]{2,1,0:T(8,128)(2,1)}, bf16[32,128,128]{2,1,0:T(8,128)(2,1)}, u32[]{:S(2)}, u32[]{:S(2)}) collective-permute-start(bf16[32,128,128]{2,1,0:T(8,128)(2,1)} %collective-permute-done.3.refs_6_), channel_id=1, source_target_pairs={{2,4},{4,6},{3,5},{5,7},{10,12},{12,14},{11,13},{13,15},{18,20},{2... | collective-permute-start | bytes 3145736 | tf_op jit(solution)/shard_map/ppermute | solution.py:216
  65.2 26.1 %collective-permute-start.6 = (bf16[32,128,128]{2,1,0:T(8,128)(2,1)}, bf16[32,128,128]{2,1,0:T(8,128)(2,1)}, u32[]{:S(2)}, u32[]{:S(2)}) collective-permute-start(bf16[32,128,128]{2,1,0:T(8,128)(2,1)} %collective-permute-done.4.refs_8_), channel_id=1, source_target_pairs={{2,0},{4,2},{3,1},{5,3},{10,8},{12,10},{11,9},{13,11},{18,16},{20,... | collective-permute-start | bytes 3145736 | tf_op jit(solution)/shard_map/ppermute | solution.py:216
  66.5 24.8 %collective-permute-start.8 = (bf16[32,128,128]{2,1,0:T(8,128)(2,1)}, bf16[32,128,128]{2,1,0:T(8,128)(2,1)}, u32[]{:S(2)}, u32[]{:S(2)}) collective-permute-start(bf16[32,128,128]{2,1,0:T(8,128)(2,1)} %collective-permute-done.refs_7_), channel_id=1, source_target_pairs={{2,4},{4,6},{3,5},{5,7},{10,12},{12,14},{11,13},{13,15},{18,20},{2... | collective-permute-start | bytes 3145736 | tf_op jit(solution)/shard_map/ppermute | solution.py:216
  68.2 45.6 %collective-permute-start.9 = (bf16[32,128,128]{2,1,0:T(8,128)(2,1)}, bf16[32,128,128]{2,1,0:T(8,128)(2,1)}, u32[]{:S(2)}, u32[]{:S(2)}) collective-permute-start(bf16[32,128,128]{2,1,0:T(8,128)(2,1)} %collective-permute-done.1.refs_9_), channel_id=1, source_target_pairs={{2,0},{4,2},{3,1},{5,3},{10,8},{12,10},{11,9},{13,11},{18,16},{20,... | collective-permute-start | bytes 3145736 | tf_op jit(solution)/shard_map/ppermute | solution.py:216
  129.4 14.8 %collective-permute-start.13 = (f32[112,128,128]{2,1,0:T(8,128)}, f32[112,128,128]{2,1,0:T(8,128)}, u32[]{:S(2)}, u32[]{:S(2)}) collective-permute-start(f32[112,128,128]{2,1,0:T(8,128)} %get-tuple-element.43), channel_id=1, source_target_pairs={{0,1},{1,0},{2,3},{3,2},{4,5},{5,4},{6,7},{7,6},{8,9},{9,8},{10,11... | collective-permute-start | bytes 22020104 | tf_op jit(solution)/shard_map/ppermute | solution.py:160
  132.6 52.4 %all-gather.5.cloned.1.call-start = ((), (), s32[]{:S(2)}) async-start(), calls=%async_computation | async-start | bytes 5505024 | tf_op jit(solution)/shard_map/all_gather | solution.py:164
  133.3 27.4 %collective-permute-start.11 = (bf16[32,128,128]{2,1,0:T(8,128)(2,1)}, bf16[32,128,128]{2,1,0:T(8,128)(2,1)S(1)}, u32[]{:S(2)}, u32[]{:S(2)}) collective-permute-start(bf16[32,128,128]{2,1,0:T(8,128)(2,1)} %collective-permute-done.6.refs_6_), channel_id=1, source_target_pairs={{2,0},{3,1},{10,8},{11,9},{18,16},{19,17},{26,24},{27,25}} | collective-permute-start | bytes 3145736 | tf_op jit(solution)/shard_map/ppermute | solution.py:216
  134.6 26.1 %collective-permute-start.7 = (bf16[32,128,128]{2,1,0:T(8,128)(2,1)}, bf16[32,128,128]{2,1,0:T(8,128)(2,1)S(1)}, u32[]{:S(2)}, u32[]{:S(2)}) collective-permute-start(bf16[32,128,128]{2,1,0:T(8,128)(2,1)} %collective-permute-done.5.refs_4_), channel_id=1, source_target_pairs={{4,6},{5,7},{12,14},{13,15},{20,22},{21,23},{28,30},{29,31}} | collective-permute-start | bytes 3145736 | tf_op jit(solution)/shard_map/ppermute | solution.py:216
  135.4 25.4 %collective-permute-start.10 = (bf16[32,128,128]{2,1,0:T(8,128)(2,1)}, bf16[32,128,128]{2,1,0:T(8,128)(2,1)}, u32[]{:S(2)}, u32[]{:S(2)}) collective-permute-start(bf16[32,128,128]{2,1,0:T(8,128)(2,1)} %collective-permute-done.8.refs_5_), channel_id=1, source_target_pairs={{4,6},{5,7},{12,14},{13,15},{20,22},{21,23},{28,30},{29,31}} | collective-permute-start | bytes 3145736 | tf_op jit(solution)/shard_map/ppermute | solution.py:216
  137.1 46.2 %collective-permute-start.12 = (bf16[32,128,128]{2,1,0:T(8,128)(2,1)}, bf16[32,128,128]{2,1,0:T(8,128)(2,1)}, u32[]{:S(2)}, u32[]{:S(2)}) collective-permute-start(bf16[32,128,128]{2,1,0:T(8,128)(2,1)} %collective-permute-done.9.refs_7_), channel_id=1, source_target_pairs={{2,0},{3,1},{10,8},{11,9},{18,16},{19,17},{26,24},{27,25}} | collective-permute-start | bytes 3145736 | tf_op jit(solution)/shard_map/ppermute | solution.py:216
  160.7 30.3 %copy-start.2 = (bf16[32,128,128]{2,1,0:T(8,128)(2,1)}, bf16[32,128,128]{2,1,0:T(8,128)(2,1)S(1)}, u32[]{:S(2)}) copy-start(bf16[32,128,128]{2,1,0:T(8,128)(2,1)S(1)} %collective-permute-done.11.refs_10_) | copy-start | bytes 3145732
  160.7 30.3 %copy-start.3 = (bf16[32,128,128]{2,1,0:T(8,128)(2,1)}, bf16[32,128,128]{2,1,0:T(8,128)(2,1)S(1)}, u32[]{:S(2)}) copy-start(bf16[32,128,128]{2,1,0:T(8,128)(2,1)S(1)} %collective-permute-done.7.refs_6_) | copy-start | bytes 3145732
  183.3 4.5 %collective-permute-start.14 = (bf16[32,128,128]{2,1,0:T(8,128)(2,1)S(1)}, bf16[32,128,128]{2,1,0:T(8,128)(2,1)}, u32[]{:S(2)}, u32[]{:S(2)}) collective-permute-start(bf16[32,128,128]{2,1,0:T(8,128)(2,1)S(1)} %collective-permute-done.7.refs_6_), channel_id=1, source_target_pairs={{0,1},{1,0},{2,3},{3,2},{4,5},{5,4},{6,7},{7,6},{8,9},{9,8},{10,11... | collective-permute-start | bytes 3145736 | tf_op jit(solution)/shard_map/ppermute | solution.py:160
  183.9 5.5 %collective-permute-start.15 = (bf16[32,128,128]{2,1,0:T(8,128)(2,1)}, bf16[32,128,128]{2,1,0:T(8,128)(2,1)}, u32[]{:S(2)}, u32[]{:S(2)}) collective-permute-start(bf16[32,128,128]{2,1,0:T(8,128)(2,1)} %collective-permute-done.10.refs_7_), channel_id=1, source_target_pairs={{0,1},{1,0},{2,3},{3,2},{4,5},{5,4},{6,7},{7,6},{8,9},{9,8},{10,11... | collective-permute-start | bytes 3145736 | tf_op jit(solution)/shard_map/ppermute | solution.py:160
  183.9 6.9 %collective-permute-start.16 = (bf16[32,128,128]{2,1,0:T(8,128)(2,1)S(1)}, bf16[32,128,128]{2,1,0:T(8,128)(2,1)}, u32[]{:S(2)}, u32[]{:S(2)}) collective-permute-start(bf16[32,128,128]{2,1,0:T(8,128)(2,1)S(1)} %collective-permute-done.11.refs_10_), channel_id=1, source_target_pairs={{0,1},{1,0},{2,3},{3,2},{4,5},{5,4},{6,7},{7,6},{8,9},{9,8},{10,11... | collective-permute-start | bytes 3145736 | tf_op jit(solution)/shard_map/ppermute | solution.py:160
  184.4 6.6 %collective-permute-start.17 = (bf16[32,128,128]{2,1,0:T(8,128)(2,1)}, bf16[32,128,128]{2,1,0:T(8,128)(2,1)}, u32[]{:S(2)}, u32[]{:S(2)}) collective-permute-start(bf16[32,128,128]{2,1,0:T(8,128)(2,1)} %collective-permute-done.12.refs_11_), channel_id=1, source_target_pairs={{0,1},{1,0},{2,3},{3,2},{4,5},{5,4},{6,7},{7,6},{8,9},{9,8},{10,11... | collective-permute-start | bytes 3145736 | tf_op jit(solution)/shard_map/ppermute | solution.py:160
  (1 other events, 4.2 us)
Sparse Core Ops, SparseCore 0:
  132.7 13.9 all-gather.6
  148.3 12.1 all-gather.4

commit v9 on v8

--- a/solution.py
+++ b/solution.py
@@ -174,13 +174,6 @@
     return jnp.where(wanted, packed, -1).reshape(-1)
 
 
-def layer_products(step_lists, layer, half, right_slot):
-    result = step_lists[:, 2]
-    turned = (result + layer * half) % (2 * half)
-    packed = right_slot(step_lists[:, 1], 0) << 20 | step_lists[:, 0] << 10 | turned
-    return jnp.where(result < 2 * half, packed, -1).reshape(-1)
-
-
 def ring(left_blocks, right_blocks, triples, half):
     own, right_own, step_lists = left_blocks[0, 0, 0], right_blocks[0, 0, 0], triples[0, 0, 0]
     columns, layer = lax.axis_size("col"), lax.axis_index("dep")
@@ -209,53 +202,53 @@
     slots, part = own.shape[0], right_own.shape[0]
     columns, layer, place = lax.axis_size("col"), lax.axis_index("dep"), lax.axis_index("col")
     shape = (step_lists.shape[0], columns, slots)
-    pieces = [own[: slots // 2], own[slots // 2 :]]
+    inner = (place == 1) | (place == 2)
+    low = place < 2
+    outward, across, inward = [(2, 3), (1, 0)], [(1, 2), (2, 1)], [(0, 1), (3, 2)]
     fence = lax.optimization_barrier
 
-    def hop(values, pairs):
-        return [lax.ppermute(value, "col", pairs) for value in values]
+    def hop(value, pairs):
+        return lax.ppermute(value, "col", pairs)
 
     def right_slot(slot, layers):
         return (layers * 2 + ((slot // part) ^ lax.axis_index("row"))) * part + slot % part
 
-    rising = hop(pieces, [(0, 1), (1, 2), (2, 3)])
-    falling = hop(pieces, [(1, 0), (2, 1), (3, 2)])
+    pieces = [own[: slots // 2], own[slots // 2 :]]
+    outer_one = hop(own, outward)
+    across_one = hop(own, across)
+    inward_one = [hop(piece, inward) for piece in pieces]
     met = lax.ppermute(right_own, "row", [(0, 1), (1, 0)])
-    both = lax.all_gather(step_lists, "dep")
-    kept = kept_products(both, layer, half, right_slot)
-    listed = layer_products(step_lists, layer, half, right_slot)
-    right_pair = paired(right_own)
-
-    rising[0], falling[0] = fence((rising[0], falling[0]))
-    rising_two = hop(rising[:1], [(1, 2), (2, 3)])
-    falling_two = hop(falling[:1], [(1, 0), (2, 1)])
-    rising[1], falling[1], met, kept, listed = fence((rising[1], falling[1], met, kept, listed))
-    rising_two += hop(rising[1:], [(1, 2), (2, 3)])
-    falling_two += hop(falling[1:], [(1, 0), (2, 1)])
+    kept = kept_products(lax.all_gather(step_lists, "dep"), layer, half, right_slot)
+    right_pair, own_pair = paired(right_own), paired(own)
+
+    outer_one, across_one, inward_one, met, kept = fence((outer_one, across_one, inward_one, met, kept))
+    outer_two = hop(across_one, outward)
+    across_two = [hop(piece, across) for piece in inward_one]
     met_pair = paired(met)
-    rights = [(right_own, False), (met, False)]
-    panels = [[(value, False) for value in values] for values in (pieces, rising, falling)]
-    classes = [0, jnp.where(place > 0, 3, -1), jnp.where(place < 3, 1, -1)]
-    sums = product_sums(listed, classes, layer, shape, 1, panels, rights, [], 2 * half, [half, half])
-
-    rising_two[0], falling_two[0], sums = fence((rising_two[0], falling_two[0], sums))
-    rising_three = hop(rising_two[:1], [(2, 3)])
-    falling_three = hop(falling_two[:1], [(1, 0)])
-    rising_two[1], falling_two[1] = fence((rising_two[1], falling_two[1]))
-    rising_three += hop(rising_two[1:], [(2, 3)])
-    falling_three += hop(falling_two[1:], [(1, 0)])
-    panels = [[(value, False) for value in values] for values in (rising_two, falling_two)]
-    classes = [jnp.where(place > 1, 2, -1), jnp.where(place < 2, 2, -1)]
-    sums = product_sums(listed, classes, layer, shape, 1, panels, rights, sums, 2 * half, [half, half])
-    total = sums[0] + swapped(sums[1])
-
-    rising_three, falling_three, total = fence((rising_three, falling_three, total))
+    one = jnp.where(inner, across_one, outer_one)
+    one_pair, inward_pair = paired(one), [paired(piece) for piece in inward_one]
+
+    across_two = fence(across_two)
+    outer_three = [hop(piece, outward) for piece in across_two]
+    two = jnp.where(inner, jnp.concatenate(across_two), outer_two)
+    cuts = [0, slots * 3 // 8, slots * 3 // 4, slots]
+    two = [two[first:last] for first, last in zip(cuts, cuts[1:])]
+    rights = [(right_own, False), (met, False), (right_pair, True), (met_pair, True)]
     panels = [
-        [(value, False) for value in [*values, *[swapped(value) for value in values]]]
-        for values in (rising_three, falling_three)
+        [(own, False), (own_pair, True)],
+        [(one, False), (one_pair, True)],
+        [(piece, False) for piece in inward_one] + [(piece, True) for piece in inward_pair],
+        [(piece, False) for piece in two] + [(swapped(piece), False) for piece in two],
     ]
-    classes = [jnp.where(place == 3, 1, -1), jnp.where(place == 0, 3, -1)]
-    rights += [(right_pair, True), (met_pair, True)]
+    classes = [0, jnp.where(low, 1, 3), jnp.where(inner, jnp.where(low, 3, 1), -1), 2]
+    (total,) = product_sums(kept, classes, layer, shape, 2, panels, rights, [], half, [half])
+
+    outer_three[0], total = fence((outer_three[0], total))
+    others = [swapped(outer_three[0])]
+    outer_three[1], others[0] = fence((outer_three[1], others[0]))
+    others.append(swapped(outer_three[1]))
+    panels = [[(piece, False) for piece in [*outer_three, *others]]]
+    classes = [jnp.where(inner, -1, jnp.where(low, 3, 1))]
     return product_sums(kept, classes, layer, shape, 2, panels, rights, [total], half, [])[0][None, None, None]
 
 

time: 212 us -> 194 us (0.915)
  Pallas kernels: 43.8 us -> 31.3 us
  other arithmetic: 13.7 us -> 6.08 us
  starting transfers between devices: 28.9 us -> 33.1 us
  waiting for transfers between devices: 105 us -> 102 us
    pallas_call x3 -> x2, Pallas kernels: 43.8 us -> 31.3 us  [product_sums(): pl.pallas_call(functools.partial(sum_kernel, panel_spans, right_spans, gi...]
    add x1 -> x0, other arithmetic: 10.6 us -> none  [line(): total = sums[0] + swapped(sums[1])]
    ppermute x5, starting transfers between devices: 4.31 us -> 13.1 us  [swapped(): return lax.ppermute(value, 'dep', [(0, 1), (1, 0)])]
    ppermute x5, waiting for transfers between devices: 11.8 us -> 4.06 us  [swapped(): return lax.ppermute(value, 'dep', [(0, 1), (1, 0)])]
    ppermute x12 -> x9, starting transfers between devices: 22.5 us -> 17.7 us  [hop(): return lax.ppermute(value, 'col', pairs)]
    select_n x1 -> x2, other arithmetic: 0.59 us -> 4.78 us  [the longest x1 3.14 us: line(): one = jnp.where(inner, across_one, outer_one)]
    ppermute x12 -> x9, waiting for transfers between devices: 92 us -> 95.2 us  [hop(): return lax.ppermute(value, 'col', pairs)]
  transfers between devices with their start and end apart: 20 -> 21, of which waited for: 11 -> 6; matrix products, arithmetic and copies ran while one was open for 8% -> 5% of each run, Pallas kernels for 7% -> 9%
where the time goes in v9:
time: 194 us; the launch traced here: 193 us
  waiting for transfers between devices  102 us (53%)
  starting transfers between devices  33.1 us (17%)
  Pallas kernels  31.3 us (16%)
  between operations  13.8 us (7%)
  other arithmetic  6.08 us (3%)
  local copies, waits for them, and re-layouts  4.11 us (2%)
  blocking collectives  3 us (2%)
    ppermute x9, waiting for transfers between devices, hop(): return lax.ppermute(value, 'col', pairs)  95.2 us
    pallas_call x2, Pallas kernels, product_sums(): pl.pallas_call(functools.partial(sum_kernel, panel_spans, right_spans, gi...  31.3 us
    ppermute x9, starting transfers between devices, hop(): return lax.ppermute(value, 'col', pairs)  17.7 us
    ppermute x5, starting transfers between devices, swapped(): return lax.ppermute(value, 'dep', [(0, 1), (1, 0)])  13.1 us
    ppermute x5, waiting for transfers between devices, swapped(): return lax.ppermute(value, 'dep', [(0, 1), (1, 0)])  4.06 us
  transfers between devices with their start and end apart: 21, of which 6 were waited for; matrix products, arithmetic and copies ran while one was open for 5% of the time, Pallas kernels for 9%

profile of v9, /device:TPU:1, one launch (start us, length us, event | category | flops | bytes accessed | tf_op | source)
XLA Modules:
  0.0 193.2 jit_solution(16312675416295962096)
XLA Ops:
  8.1 2.0 %collective-permute-start.1 = (bf16[64,128,128]{2,1,0:T(8,128)(2,1)S(1)}, bf16[64,128,128]{2,1,0:T(8,128)(2,1)}, u32[]{:S(2)}, u32[]{:S(2)}) collective-permute-start(bf16[64,128,128]{2,1,0:T(8,128)(2,1)S(1)} %bitcast.32), channel_id=1, source_target_pairs={{2,4},{4,2},{3,5},{5,3},{10,12},{12,10},{11,13},{13,11},{18,20},{2... | collective-permute-start | bytes 6291464 | tf_op jit(solution)/shard_map/ppermute | solution.py:211
  10.1 1.3 collective-permute-start
  11.4 2.1 %collective-permute-start.4 = (bf16[56,128,128]{2,1,0:T(8,128)(2,1)}, bf16[56,128,128]{2,1,0:T(8,128)(2,1)}, u32[]{:S(2)}, u32[]{:S(2)}) collective-permute-start(bf16[56,128,128]{2,1,0:T(8,128)(2,1)} %bitcast.35), channel_id=1, source_target_pairs={{0,8},{8,0},{1,9},{9,1},{2,10},{10,2},{3,11},{11,3},{4,12},{12,4},... | collective-permute-start | bytes 5505032 | tf_op jit(solution)/shard_map/ppermute | solution.py:220
  13.5 1.5 slice_bitcast_fusion
  15.0 5.7 %collective-permute-start.3 = (bf16[32,128,128]{2,1,0:T(8,128)(2,1)}, bf16[32,128,128]{2,1,0:T(8,128)(2,1)S(1)}, u32[]{:S(2)}, u32[]{:S(2)}) collective-permute-start(bf16[32,128,128]{2,1,0:T(8,128)(2,1)} %get-tuple-element.31), channel_id=1, source_target_pairs={{0,2},{6,4},{1,3},{7,5},{8,10},{14,12},{9,11},{15,13},{16,18},{22,... | collective-permute-start | bytes 3145736 | tf_op jit(solution)/shard_map/ppermute | solution.py:211
  20.8 2.3 %collective-permute-start.2 = (bf16[32,128,128]{2,1,0:T(8,128)(2,1)}, bf16[32,128,128]{2,1,0:T(8,128)(2,1)}, u32[]{:S(2)}, u32[]{:S(2)}) collective-permute-start(bf16[32,128,128]{2,1,0:T(8,128)(2,1)} %get-tuple-element.32), channel_id=1, source_target_pairs={{0,2},{6,4},{1,3},{7,5},{8,10},{14,12},{9,11},{15,13},{16,18},{22,... | collective-permute-start | bytes 3145736 | tf_op jit(solution)/shard_map/ppermute | solution.py:211
  23.4 3.0 %all-gather = s32[2,1,1,7,3,64]{5,2,4,3,1,0:T(1,128)S(1)} all-gather(s32[1,1,1,7,3,64]{5,2,4,3,1,0:T(1,128)S(1)} %copy-done.10), channel_id=2, replica_groups=mesh['grp'=2,'row'=2,'col'=4,'dep'=2] {'dep'}, dimensions={0}, use_global_device_ids=true | all-gather | bytes 16128 | tf_op jit(solution)/shard_map/all_gather | solution.py:221
  27.6 14.7 %collective-permute-done.3.refs_11_ = bf16[32,128,128]{2,1,0:T(8,128)(2,1)S(1)} collective-permute-done((bf16[32,128,128]{2,1,0:T(8,128)(2,1)}, bf16[32,128,128]{2,1,0:T(8,128)(2,1)S(1)}, u32[]{:S(2)}, u32[]{:S(2)}) %collective-permute-start.3) | collective-permute-done | bytes 1048608 | tf_op jit(solution)/shard_map/ppermute | solution.py:211
  42.2 22.5 %collective-permute-done.2.refs_10_ = bf16[32,128,128]{2,1,0:T(8,128)(2,1)} collective-permute-done((bf16[32,128,128]{2,1,0:T(8,128)(2,1)}, bf16[32,128,128]{2,1,0:T(8,128)(2,1)}, u32[]{:S(2)}, u32[]{:S(2)}) %collective-permute-start.2) | collective-permute-done | bytes 1048608 | tf_op jit(solution)/shard_map/ppermute | solution.py:211
  66.0 3.1 %broadcast_select_fusion.refs_8_ = bf16[64,128,128]{2,1,0:T(8,128)(2,1)} fusion(bf16[64,128,128]{2,1,0:T(8,128)(2,1)} %collective-permute-done.1, bf16[64,128,128]{2,1,0:T(8,128)(2,1)} %collective-permute-done, pred[]{:T(512)S(6)} %or.13), kind=kLoop, calls=%fused_computation.1 | loop fusion | flops 1048576 | bytes 6291457 | tf_op jit(solution)/shard_map/jit(_where)/select_n | solution.py:228
  69.1 1.4 collective-permute-start.8
  70.5 1.6 collective-permute-start.5
  73.0 1.3 collective-permute-start.7
  74.3 42.3 %collective-permute-done.8 = bf16[64,128,128]{2,1,0:T(8,128)(2,1)S(1)} collective-permute-done((bf16[64,128,128]{2,1,0:T(8,128)(2,1)}, bf16[64,128,128]{2,1,0:T(8,128)(2,1)S(1)}, u32[]{:S(2)}, u32[]{:S(2)}) %collective-permute-start.8) | collective-permute-done | bytes 2097184 | tf_op jit(solution)/shard_map/ppermute | solution.py:211
  116.5 1.6 maximum_select_fusion
  118.3 3.0 %collective-permute-start.10 = (bf16[24,128,128]{2,1,0:T(8,128)(2,1)S(1)}, bf16[24,128,128]{2,1,0:T(8,128)(2,1)}, u32[]{:S(2)}, u32[]{:S(2)}) collective-permute-start(bf16[24,128,128]{2,1,0:T(8,128)(2,1)S(1)} %get-tuple-element.29.refs_15_), channel_id=1, source_target_pairs={{0,1},{1,0},{2,3},{3,2},{4,5},{5,4},{6,7},{7,6},{8,9},{9,8},{10,11... | collective-permute-start | bytes 2359304 | tf_op jit(solution)/shard_map/ppermute | solution.py:160
  122.5 1.3 collective-permute-start.12
  123.9 2.2 %collective-permute-done.11.refs_19_ = bf16[16,128,128]{2,1,0:T(8,128)(2,1)} collective-permute-done((bf16[16,128,128]{2,1,0:T(8,128)(2,1)S(1)}, bf16[16,128,128]{2,1,0:T(8,128)(2,1)}, u32[]{:S(2)}, u32[]{:S(2)}) %collective-permute-start.11) | collective-permute-done | bytes 524320 | tf_op jit(solution)/shard_map/ppermute | solution.py:160
  126.2 17.3 %shard_map.37.refs_10_ = f32[112,128,128]{2,1,0:T(8,128)} custom-call(s32[896]{0:T(1024)} %fusion.7.refs_0_, s32[5]{0:T(128)} %stack.24.refs_1_, bf16[56,128,128]{2,1,0:T(8,128)(2,1)} %bitcast.36, bf16[56,128,128]{2,1,0:T(8,128)(2,1)} %collective-permute-done.4.refs_3_, bf16[112,128,128]{2,1,0:T(8,128)(2,1)} %bitcast.38, ...), custom_call_target="tpu_custom_call" | custom-call | flops 1 | bytes 1 | tf_op jit(solution)/shard_map/pallas_call | solution.py:140
  143.5 5.9 %collective-permute-start.13 = (bf16[32,128,128]{2,1,0:T(8,128)(2,1)S(1)}, bf16[32,128,128]{2,1,0:T(8,128)(2,1)S(1)}, u32[]{:S(2)}, u32[]{:S(2)}) collective-permute-start(bf16[32,128,128]{2,1,0:T(8,128)(2,1)S(1)} %collective-permute-done.7.refs_6_), channel_id=1, source_target_pairs={{0,1},{1,0},{2,3},{3,2},{4,5},{5,4},{6,7},{7,6},{8,9},{9,8},{10,11... | collective-permute-start | bytes 3145736 | tf_op jit(solution)/shard_map/ppermute | solution.py:160
  149.4 15.8 %collective-permute-done.12.refs_7_ = bf16[32,128,128]{2,1,0:T(8,128)(2,1)} collective-permute-done((bf16[32,128,128]{2,1,0:T(8,128)(2,1)}, bf16[32,128,128]{2,1,0:T(8,128)(2,1)}, u32[]{:S(2)}, u32[]{:S(2)}) %collective-permute-start.12) | collective-permute-done | bytes 1048608 | tf_op jit(solution)/shard_map/ppermute | solution.py:211
  165.2 3.6 %collective-permute-start.14 = (bf16[32,128,128]{2,1,0:T(8,128)(2,1)}, bf16[32,128,128]{2,1,0:T(8,128)(2,1)S(1)}, u32[]{:S(2)}, u32[]{:S(2)}) collective-permute-start(bf16[32,128,128]{2,1,0:T(8,128)(2,1)} %collective-permute-done.12.refs_7_), channel_id=1, source_target_pairs={{0,1},{1,0},{2,3},{3,2},{4,5},{5,4},{6,7},{7,6},{8,9},{9,8},{10,11... | collective-permute-start | bytes 3145736 | tf_op jit(solution)/shard_map/ppermute | solution.py:160
  169.4 1.9 collective-permute-done.14.refs_9_
  172.3 14.0 %shard_map.38 = bf16[112,128,128]{2,1,0:T(8,128)(2,1)} custom-call(s32[896]{0:T(1024)} %fusion.7.refs_0_, s32[2]{0:T(128)} %pad_add_fusion.refs_1_, bf16[56,128,128]{2,1,0:T(8,128)(2,1)} %bitcast.37, bf16[56,128,128]{2,1,0:T(8,128)(2,1)} %collective-permute-done.4.refs_3_, bf16[112,128,128]{2,1,0:T(8,128)(2,1)} %bitcast.39, ...), custom_call_target="tpu_custom_call" | custom-call | flops 1 | bytes 1 | tf_op jit(solution)/shard_map/pallas_call | solution.py:140
  (78 shorter events, 8.0 us)
Async XLA Ops:
  6.5 117.3 %all-gather.18.cloned.1.call-start = ((), (), s32[]{:S(2)}) async-start(), calls=%async_computation.4 | async-start | bytes 5505024 | tf_op jit(solution)/shard_map/all_gather | solution.py:164
  7.3 116.6 %all-gather.20.cloned.1.call-start = ((), (), s32[]{:S(2)}) async-start(), calls=%async_computation.5 | async-start | bytes 6291456 | tf_op jit(solution)/shard_map/all_gather | solution.py:164
  8.0 115.9 %all-gather.14.cloned.1.call-start = ((), (), s32[]{:S(2)}) async-start(), calls=%async_computation.2 | async-start | bytes 3145728 | tf_op jit(solution)/shard_map/all_gather | solution.py:164
  8.1 56.6 %collective-permute-start.1 = (bf16[64,128,128]{2,1,0:T(8,128)(2,1)S(1)}, bf16[64,128,128]{2,1,0:T(8,128)(2,1)}, u32[]{:S(2)}, u32[]{:S(2)}) collective-permute-start(bf16[64,128,128]{2,1,0:T(8,128)(2,1)S(1)} %bitcast.32), channel_id=1, source_target_pairs={{2,4},{4,2},{3,5},{5,3},{10,12},{12,10},{11,13},{13,11},{18,20},{2... | collective-permute-start | bytes 6291464 | tf_op jit(solution)/shard_map/ppermute | solution.py:211
  10.1 54.6 %collective-permute-start = (bf16[64,128,128]{2,1,0:T(8,128)(2,1)S(1)}, bf16[64,128,128]{2,1,0:T(8,128)(2,1)}, u32[]{:S(2)}, u32[]{:S(2)}) collective-permute-start(bf16[64,128,128]{2,1,0:T(8,128)(2,1)S(1)} %bitcast.33), channel_id=1, source_target_pairs={{4,6},{2,0},{5,7},{3,1},{12,14},{10,8},{13,15},{11,9},{20,22},{18,... | collective-permute-start | bytes 6291464 | tf_op jit(solution)/shard_map/ppermute | solution.py:211
  11.4 53.3 %collective-permute-start.4 = (bf16[56,128,128]{2,1,0:T(8,128)(2,1)}, bf16[56,128,128]{2,1,0:T(8,128)(2,1)}, u32[]{:S(2)}, u32[]{:S(2)}) collective-permute-start(bf16[56,128,128]{2,1,0:T(8,128)(2,1)} %bitcast.35), channel_id=1, source_target_pairs={{0,8},{8,0},{1,9},{9,1},{2,10},{10,2},{3,11},{11,3},{4,12},{12,4},... | collective-permute-start | bytes 5505032 | tf_op jit(solution)/shard_map/ppermute | solution.py:220
  15.0 27.2 %collective-permute-start.3 = (bf16[32,128,128]{2,1,0:T(8,128)(2,1)}, bf16[32,128,128]{2,1,0:T(8,128)(2,1)S(1)}, u32[]{:S(2)}, u32[]{:S(2)}) collective-permute-start(bf16[32,128,128]{2,1,0:T(8,128)(2,1)} %get-tuple-element.31), channel_id=1, source_target_pairs={{0,2},{6,4},{1,3},{7,5},{8,10},{14,12},{9,11},{15,13},{16,18},{22,... | collective-permute-start | bytes 3145736 | tf_op jit(solution)/shard_map/ppermute | solution.py:211
  20.8 43.9 %collective-permute-start.2 = (bf16[32,128,128]{2,1,0:T(8,128)(2,1)}, bf16[32,128,128]{2,1,0:T(8,128)(2,1)}, u32[]{:S(2)}, u32[]{:S(2)}) collective-permute-start(bf16[32,128,128]{2,1,0:T(8,128)(2,1)} %get-tuple-element.32), channel_id=1, source_target_pairs={{0,2},{6,4},{1,3},{7,5},{8,10},{14,12},{9,11},{15,13},{16,18},{22,... | collective-permute-start | bytes 3145736 | tf_op jit(solution)/shard_map/ppermute | solution.py:211
  42.2 22.6 %copy-start.1 = (bf16[32,128,128]{2,1,0:T(8,128)(2,1)}, bf16[32,128,128]{2,1,0:T(8,128)(2,1)S(1)}, u32[]{:S(2)}) copy-start(bf16[32,128,128]{2,1,0:T(8,128)(2,1)S(1)} %collective-permute-done.3.refs_11_) | copy-start | bytes 3145732
  64.7 59.2 %all-gather.16.cloned.1.call-start = ((), (), s32[]{:S(2)}) async-start(), calls=%async_computation.3 | async-start | bytes 3145728 | tf_op jit(solution)/shard_map/all_gather | solution.py:164
  65.3 60.8 %all-gather.10.cloned.1.call-start = ((), (), s32[]{:S(2)}) async-start(), calls=%async_computation | async-start | bytes 5505024 | tf_op jit(solution)/shard_map/all_gather | solution.py:164
  65.9 60.3 %all-gather.12.cloned.1.call-start = ((), (), s32[]{:S(2)}) async-start(), calls=%async_computation.1 | async-start | bytes 6291456 | tf_op jit(solution)/shard_map/all_gather | solution.py:164
  69.1 47.4 %collective-permute-start.8 = (bf16[64,128,128]{2,1,0:T(8,128)(2,1)}, bf16[64,128,128]{2,1,0:T(8,128)(2,1)S(1)}, u32[]{:S(2)}, u32[]{:S(2)}) collective-permute-start(bf16[64,128,128]{2,1,0:T(8,128)(2,1)} %collective-permute-done.1), channel_id=1, source_target_pairs={{4,6},{2,0},{5,7},{3,1},{12,14},{10,8},{13,15},{11,9},{20,22},{18,... | collective-permute-start | bytes 6291464 | tf_op jit(solution)/shard_map/ppermute | solution.py:211
  70.5 2.4 %collective-permute-start.5 = (bf16[32,128,128]{2,1,0:T(8,128)(2,1)}, bf16[32,128,128]{2,1,0:T(8,128)(2,1)}, u32[]{:S(2)}, u32[]{:S(2)}) collective-permute-start(bf16[32,128,128]{2,1,0:T(8,128)(2,1)} %collective-permute-done.2.refs_10_), channel_id=1, source_target_pairs={{2,4},{4,2},{3,5},{5,3},{10,12},{12,10},{11,13},{13,11},{18,20},{2... | collective-permute-start | bytes 3145736 | tf_op jit(solution)/shard_map/ppermute | solution.py:211
  72.2 0.7 collective-permute-start.6
  72.9 48.5 %copy-start.7 = (bf16[32,128,128]{2,1,0:T(8,128)(2,1)}, bf16[32,128,128]{2,1,0:T(8,128)(2,1)S(1)}, u32[]{:S(2)}) copy-start(bf16[32,128,128]{2,1,0:T(8,128)(2,1)S(1)} %collective-permute-done.6) | copy-start | bytes 3145732
  73.0 70.5 %collective-permute-start.7 = (bf16[32,128,128]{2,1,0:T(8,128)(2,1)}, bf16[32,128,128]{2,1,0:T(8,128)(2,1)S(1)}, u32[]{:S(2)}, u32[]{:S(2)}) collective-permute-start(bf16[32,128,128]{2,1,0:T(8,128)(2,1)} %collective-permute-done.5), channel_id=1, source_target_pairs={{4,6},{2,0},{5,7},{3,1},{12,14},{10,8},{13,15},{11,9},{20,22},{18,... | collective-permute-start | bytes 3145736 | tf_op jit(solution)/shard_map/ppermute | solution.py:211
  118.3 7.8 %collective-permute-start.10 = (bf16[24,128,128]{2,1,0:T(8,128)(2,1)S(1)}, bf16[24,128,128]{2,1,0:T(8,128)(2,1)}, u32[]{:S(2)}, u32[]{:S(2)}) collective-permute-start(bf16[24,128,128]{2,1,0:T(8,128)(2,1)S(1)} %get-tuple-element.29.refs_15_), channel_id=1, source_target_pairs={{0,1},{1,0},{2,3},{3,2},{4,5},{5,4},{6,7},{7,6},{8,9},{9,8},{10,11... | collective-permute-start | bytes 2359304 | tf_op jit(solution)/shard_map/ppermute | solution.py:160
  121.3 4.8 %collective-permute-start.9 = (bf16[24,128,128]{2,1,0:T(8,128)(2,1)S(1)}, bf16[24,128,128]{2,1,0:T(8,128)(2,1)}, u32[]{:S(2)}, u32[]{:S(2)}) collective-permute-start(bf16[24,128,128]{2,1,0:T(8,128)(2,1)S(1)} %get-tuple-element.30.refs_14_), channel_id=1, source_target_pairs={{0,1},{1,0},{2,3},{3,2},{4,5},{5,4},{6,7},{7,6},{8,9},{9,8},{10,11... | collective-permute-start | bytes 2359304 | tf_op jit(solution)/shard_map/ppermute | solution.py:160
  121.4 4.7 %collective-permute-start.11 = (bf16[16,128,128]{2,1,0:T(8,128)(2,1)S(1)}, bf16[16,128,128]{2,1,0:T(8,128)(2,1)}, u32[]{:S(2)}, u32[]{:S(2)}) collective-permute-start(bf16[16,128,128]{2,1,0:T(8,128)(2,1)S(1)} %slice.45.refs_16_), channel_id=1, source_target_pairs={{0,1},{1,0},{2,3},{3,2},{4,5},{5,4},{6,7},{7,6},{8,9},{9,8},{10,11... | collective-permute-start | bytes 1572872 | tf_op jit(solution)/shard_map/ppermute | solution.py:160
  122.5 42.6 %collective-permute-start.12 = (bf16[32,128,128]{2,1,0:T(8,128)(2,1)}, bf16[32,128,128]{2,1,0:T(8,128)(2,1)}, u32[]{:S(2)}, u32[]{:S(2)}) collective-permute-start(bf16[32,128,128]{2,1,0:T(8,128)(2,1)} %copy-done.7), channel_id=1, source_target_pairs={{4,6},{2,0},{5,7},{3,1},{12,14},{10,8},{13,15},{11,9},{20,22},{18,... | collective-permute-start | bytes 3145736 | tf_op jit(solution)/shard_map/ppermute | solution.py:211
  143.5 27.8 %copy-start.6 = (bf16[32,128,128]{2,1,0:T(8,128)(2,1)}, bf16[32,128,128]{2,1,0:T(8,128)(2,1)S(1)}, u32[]{:S(2)}) copy-start(bf16[32,128,128]{2,1,0:T(8,128)(2,1)S(1)} %collective-permute-done.7.refs_6_) | copy-start | bytes 3145732
  143.5 21.6 %collective-permute-start.13 = (bf16[32,128,128]{2,1,0:T(8,128)(2,1)S(1)}, bf16[32,128,128]{2,1,0:T(8,128)(2,1)S(1)}, u32[]{:S(2)}, u32[]{:S(2)}) collective-permute-start(bf16[32,128,128]{2,1,0:T(8,128)(2,1)S(1)} %collective-permute-done.7.refs_6_), channel_id=1, source_target_pairs={{0,1},{1,0},{2,3},{3,2},{4,5},{5,4},{6,7},{7,6},{8,9},{9,8},{10,11... | collective-permute-start | bytes 3145736 | tf_op jit(solution)/shard_map/ppermute | solution.py:160
  165.2 6.1 %collective-permute-start.14 = (bf16[32,128,128]{2,1,0:T(8,128)(2,1)}, bf16[32,128,128]{2,1,0:T(8,128)(2,1)S(1)}, u32[]{:S(2)}, u32[]{:S(2)}) collective-permute-start(bf16[32,128,128]{2,1,0:T(8,128)(2,1)} %collective-permute-done.12.refs_7_), channel_id=1, source_target_pairs={{0,1},{1,0},{2,3},{3,2},{4,5},{5,4},{6,7},{7,6},{8,9},{9,8},{10,11... | collective-permute-start | bytes 3145736 | tf_op jit(solution)/shard_map/ppermute | solution.py:160
  (8 other events, 44.4 us)
Sparse Core Ops, SparseCore 0:
  8.9 15.3 all-gather.17
  25.8 14.8 all-gather.19
  64.8 13.3 all-gather.13
  79.6 11.7 all-gather.15
  92.8 14.0 all-gather.9
  108.3 15.8 all-gather.11

commit v10 on v9

--- a/solution.py
+++ b/solution.py
@@ -11,7 +11,7 @@
 UNROLL = 8
 
 
-def chosen_products(packed, classes, panels, todo, shape, layers, spare):
+def chosen_products(packed, classes, panels, todo, shape, layers, spare, first_left=0):
     step_count, columns, slots = shape
     count = jnp.int32(0)
     for panel in range(panels):
@@ -31,15 +31,19 @@
 
                 count = lax.fori_loop(0, groups, keep, count)
     for extra in range(UNROLL - 1):
-        todo[count + extra] = jnp.int32(spare)
+        todo[count + extra] = jnp.int32(first_left << 10 | spare)
     return count
 
 
-def add_chosen(todo, count, left, right, work):
+def add_chosen(todo, count, left, right, work, first_left=0):
     def several(group, carry):
         entries = [todo[group * UNROLL + lane] for lane in range(UNROLL)]
         products = [
-            jnp.dot(left[(entry >> 10) & 1023], right[entry >> 20], preferred_element_type=jnp.float32)
+            jnp.dot(
+                left[((entry >> 10) & 1023) - first_left],
+                right[entry >> 20],
+                preferred_element_type=jnp.float32,
+            )
             for entry in entries
         ]
         for entry, product in zip(entries, products):
@@ -49,11 +53,14 @@
     lax.fori_loop(0, (count + UNROLL - 1) // UNROLL, several, jnp.int32(0))
 
 
-def sum_kernel(panels, rights, givens, saved, shape, layers, operand_count, layer_at, *refs):
+def sum_kernel(panels, rights, givens, saved, resident, shape, layers, operand_count, layer_at, *refs):
     packed, classes, refs = refs[0], refs[1], refs[2:]
     operands, refs = refs[:operand_count], refs[operand_count:]
-    outs, refs = refs[: max(len(saved), 1)], refs[max(len(saved), 1) :]
-    work, left, right, todo, sems = refs
+    if resident:
+        (work, right), (left, todo, sems) = refs[:2], refs[2:]
+    else:
+        out_count = max(len(saved), 1)
+        outs, (work, left, right, todo, sems) = refs[:out_count], refs[out_count:]
     spare = work.shape[0] - 1
     other = 1 - classes[layer_at]
     copies = []
@@ -91,6 +98,8 @@
     for copy, when in copies:
         copy.wait() if when is None else pl.when(when)(copy.wait)
     add_chosen(todo, count, left, right, work)
+    if resident:
+        return
     if saved:
         start, copies = 0, []
         for out, size in zip(outs, saved):
@@ -104,7 +113,7 @@
         outs[0][...] = work[:spare].astype(outs[0].dtype)
 
 
-def product_sums(packed, classes, layer, shape, layers, panels, rights, givens, result_slots, saved):
+def product_sums(packed, classes, layer, shape, layers, panels, rights, givens, result_slots, saved, resident=False):
     step_count, columns, slots = shape
     rows, width = rights[0][0].shape[1:]
     operands = []
@@ -131,29 +140,74 @@
     assert all(sum(size for _, size, _ in pieces) == layers * slots for pieces in panel_spans)
     anywhere = pl.BlockSpec(memory_space=pl.ANY)
     in_scalar = pl.BlockSpec(memory_space=pltpu.SMEM)
-    copy_count = len(rights) + sum(len(pieces) for pieces in panels) + len(givens) + len(saved)
+    copy_count = len(rights) + sum(len(pieces) for pieces in panels) + len(givens) + len(saved) + 1
     scalars = jnp.stack([jnp.asarray(value, jnp.int32) for value in [*classes, layer]])
     if saved:
         out_shape = [jax.ShapeDtypeStruct((size, rows, width), jnp.float32) for size in saved]
     else:
         out_shape = [jax.ShapeDtypeStruct((result_slots, rows, width), jnp.bfloat16)]
+    scratch = [
+        pltpu.VMEM((result_slots + 1, rows, width), jnp.float32),
+        pltpu.VMEM((left_slots, rows, width), jnp.bfloat16),
+        pltpu.VMEM((right_slots, width, width), jnp.bfloat16),
+    ]
+    if resident:
+        out_shape, scratch = [scratch[0], scratch[2]], [scratch[1]]
     return pl.pallas_call(
         functools.partial(
-            sum_kernel, panel_spans, right_spans, given_spans, saved, shape, layers, len(operands), len(classes)
+            sum_kernel,
+            panel_spans,
+            right_spans,
+            given_spans,
+            saved,
+            resident,
+            shape,
+            layers,
+            len(operands),
+            len(classes),
         ),
         out_shape=out_shape,
         in_specs=[in_scalar, in_scalar] + [anywhere] * len(operands),
         out_specs=[anywhere if saved else pl.BlockSpec(memory_space=pltpu.VMEM)] * len(out_shape),
-        scratch_shapes=[
-            pltpu.VMEM((result_slots + 1, rows, width), jnp.float32),
-            pltpu.VMEM((left_slots, rows, width), jnp.bfloat16),
-            pltpu.VMEM((right_slots, width, width), jnp.bfloat16),
+        scratch_shapes=scratch
+        + [
             pltpu.SMEM((len(panels) * -(-step_count // columns) * layers * slots + UNROLL,), jnp.int32),
             pltpu.SemaphoreType.DMA((copy_count,)),
         ],
-        compiler_params=pltpu.CompilerParams(vmem_limit_bytes=56 << 20),
+        compiler_params=pltpu.CompilerParams(vmem_limit_bytes=(40 if resident else 56) << 20),
         cost_estimate=pl.CostEstimate(flops=1, bytes_accessed=1, transcendentals=0),
     )(packed, scalars, *operands)
+
+
+def last_kernel(shape, packed, classes, right, given, own, other, out, work, todo):
+    del given
+    step_count, columns, slots = shape
+    spare = work.shape[0] - 1
+    for layer, left in enumerate((own, other)):
+        base = layer * step_count * slots
+        part = packed.at[pl.ds(base, step_count * slots)]
+        count = chosen_products(part, [classes[0]], 1, todo, shape, 1, spare, layer * slots)
+        add_chosen(todo, count, left, right, work, layer * slots)
+    out[...] = work[:spare].astype(out.dtype)
+
+
+def last_sums(packed, kind, shape, own, other, right, given):
+    step_count, columns, slots = shape
+    result_slots, rows, width = given.shape[0] - 1, *given.shape[1:]
+    in_scalar, in_vector = pl.BlockSpec(memory_space=pltpu.SMEM), pl.BlockSpec(memory_space=pltpu.VMEM)
+    return pl.pallas_call(
+        functools.partial(last_kernel, shape),
+        out_shape=[
+            jax.ShapeDtypeStruct((result_slots, rows, width), jnp.bfloat16),
+            pltpu.VMEM(given.shape, given.dtype),
+        ],
+        in_specs=[in_scalar] * 2 + [in_vector] * 4,
+        out_specs=[in_vector] * 2,
+        scratch_shapes=[pltpu.SMEM((-(-step_count // columns) * slots + UNROLL,), jnp.int32)],
+        input_output_aliases={3: 1},
+        compiler_params=pltpu.CompilerParams(vmem_limit_bytes=20 << 20),
+        cost_estimate=pl.CostEstimate(flops=1, bytes_accessed=1, transcendentals=0),
+    )(packed, kind.astype(jnp.int32).reshape(1), right, given, own, other)[0]
 
 
 def swapped(value):
@@ -213,43 +267,37 @@
     def right_slot(slot, layers):
         return (layers * 2 + ((slot // part) ^ lax.axis_index("row"))) * part + slot % part
 
-    pieces = [own[: slots // 2], own[slots // 2 :]]
-    outer_one = hop(own, outward)
-    across_one = hop(own, across)
-    inward_one = [hop(piece, inward) for piece in pieces]
+    across_one, inward_one, outer_one = hop(own, across), hop(own, inward), hop(own, outward)
     met = lax.ppermute(right_own, "row", [(0, 1), (1, 0)])
     kept = kept_products(lax.all_gather(step_lists, "dep"), layer, half, right_slot)
     right_pair, own_pair = paired(right_own), paired(own)
 
-    outer_one, across_one, inward_one, met, kept = fence((outer_one, across_one, inward_one, met, kept))
-    outer_two = hop(across_one, outward)
-    across_two = [hop(piece, across) for piece in inward_one]
-    met_pair = paired(met)
-    one = jnp.where(inner, across_one, outer_one)
-    one_pair, inward_pair = paired(one), [paired(piece) for piece in inward_one]
+    across_one, inward_one, outer_one, met, kept = fence((across_one, inward_one, outer_one, met, kept))
+    outer_two, across_two = hop(across_one, outward), hop(inward_one, across)
+    met_pair, inward_pair, across_pair, outer_pair = [
+        paired(value) for value in (met, inward_one, across_one, outer_one)
+    ]
 
     across_two = fence(across_two)
-    outer_three = [hop(piece, outward) for piece in across_two]
-    two = jnp.where(inner, jnp.concatenate(across_two), outer_two)
-    cuts = [0, slots * 3 // 8, slots * 3 // 4, slots]
-    two = [two[first:last] for first, last in zip(cuts, cuts[1:])]
+    outer_three = hop(across_two, outward)
+    two = jnp.where(inner, across_two, outer_two)
+    two = [two[: slots // 2], two[slots // 2 :]]
     rights = [(right_own, False), (met, False), (right_pair, True), (met_pair, True)]
     panels = [
         [(own, False), (own_pair, True)],
-        [(one, False), (one_pair, True)],
-        [(piece, False) for piece in inward_one] + [(piece, True) for piece in inward_pair],
+        [(across_one, False), (across_pair, True)],
+        [(inward_one, False), (inward_pair, True)],
+        [(outer_one, False), (outer_pair, True)],
         [(piece, False) for piece in two] + [(swapped(piece), False) for piece in two],
     ]
-    classes = [0, jnp.where(low, 1, 3), jnp.where(inner, jnp.where(low, 3, 1), -1), 2]
-    (total,) = product_sums(kept, classes, layer, shape, 2, panels, rights, [], half, [half])
-
-    outer_three[0], total = fence((outer_three[0], total))
-    others = [swapped(outer_three[0])]
-    outer_three[1], others[0] = fence((outer_three[1], others[0]))
-    others.append(swapped(outer_three[1]))
-    panels = [[(piece, False) for piece in [*outer_three, *others]]]
-    classes = [jnp.where(inner, -1, jnp.where(low, 3, 1))]
-    return product_sums(kept, classes, layer, shape, 2, panels, rights, [total], half, [])[0][None, None, None]
+    classes = [0, jnp.where(inner, jnp.where(low, 1, 3), -1), jnp.where(inner, jnp.where(low, 3, 1), -1)]
+    classes += [jnp.where(inner, -1, jnp.where(low, 1, 3)), 2]
+    total, right = product_sums(kept, classes, layer, shape, 2, panels, rights, [], half, [], True)
+
+    outer_three, total, right = fence((outer_three, total, right))
+    kind = jnp.where(inner, -1, jnp.where(low, 3, 1))
+    block = last_sums(kept, kind, shape, outer_three, swapped(outer_three), right, total)
+    return block[None, None, None]
 
 
 def local(left_blocks, right_blocks, triples):

time: 194 us -> 189 us (0.974)
  local copies, waits for them, and re-layouts: 4.11 us -> 14.7 us
  starting transfers between devices: 33.1 us -> 22.7 us
  Pallas kernels: 31.3 us -> 24 us
  waiting for transfers between devices: 102 us -> 108 us
  other arithmetic: 6.08 us -> 2.48 us
    ppermute x9 -> x6, waiting for transfers between devices: 95.2 us -> 59.8 us  [hop(): return lax.ppermute(value, 'col', pairs)]
    ppermute x1, waiting for transfers between devices: 0.01 us -> 34.9 us  [line(): met = lax.ppermute(right_own, 'row', [(0, 1), (1, 0)])]
    pallas_call x2 -> x1, Pallas kernels: 31.3 us -> 14.6 us  [product_sums(): pl.pallas_call(functools.partial(sum_kernel, panel_spans, right_spans, gi...]
    unnamed x22 -> x16, local copies, waits for them, and re-layouts: 1.13 us -> 12.2 us
    pallas_call x0 -> x1, Pallas kernels: none -> 9.37 us  [last_sums(): pl.pallas_call(functools.partial(last_kernel, shape), out_shape=[jax.Shap...]
    ppermute x5 -> x3, starting transfers between devices: 13.1 us -> 5.89 us  [swapped(): return lax.ppermute(value, 'dep', [(0, 1), (1, 0)])]
    ppermute x5 -> x3, waiting for transfers between devices: 4.06 us -> 7.45 us  [swapped(): return lax.ppermute(value, 'dep', [(0, 1), (1, 0)])]
    ppermute x9 -> x6, starting transfers between devices: 17.7 us -> 14.6 us  [hop(): return lax.ppermute(value, 'col', pairs)]
  transfers between devices with their start and end apart: 21 -> 16, of which waited for: 6 -> 7; matrix products, arithmetic and copies ran while one was open for 5% -> 3% of each run, Pallas kernels for 9% -> 8%
where the time goes in v10:
time: 189 us
  waiting for transfers between devices  108 us (57%)
  Pallas kernels  24 us (13%)
  starting transfers between devices  22.7 us (12%)
  local copies, waits for them, and re-layouts  14.7 us (8%)
  between operations  13.6 us (7%)
  blocking collectives  3 us (2%)
  other arithmetic  2.48 us (1%)
    ppermute x6, waiting for transfers between devices, hop(): return lax.ppermute(value, 'col', pairs)  59.8 us
    ppermute x1, waiting for transfers between devices, line(): met = lax.ppermute(right_own, 'row', [(0, 1), (1, 0)])  34.9 us
    pallas_call x1, Pallas kernels, product_sums(): pl.pallas_call(functools.partial(sum_kernel, panel_spans, right_spans, gi...  14.6 us
    ppermute x6, starting transfers between devices, hop(): return lax.ppermute(value, 'col', pairs)  14.6 us
    unnamed x16, local copies, waits for them, and re-layouts  12.2 us
    pallas_call x1, Pallas kernels, last_sums(): pl.pallas_call(functools.partial(last_kernel, shape), out_shape=[jax.Shap...  9.37 us
    ppermute x3, waiting for transfers between devices, swapped(): return lax.ppermute(value, 'dep', [(0, 1), (1, 0)])  7.45 us
    ppermute x3, starting transfers between devices, swapped(): return lax.ppermute(value, 'dep', [(0, 1), (1, 0)])  5.89 us
  transfers between devices with their start and end apart: 16, of which 7 were waited for; matrix products, arithmetic and copies ran while one was open for 3% of the time, Pallas kernels for 8%

profile of v10, /device:TPU:1, one launch (start us, length us, event | category | flops | bytes accessed | tf_op | source)
XLA Modules:
  0.0 188.5 jit_solution(946265760177499421)
XLA Ops:
  8.1 1.3 collective-permute-start.2
  9.4 6.7 %collective-permute-start.1 = (bf16[64,128,128]{2,1,0:T(8,128)(2,1)S(1)}, bf16[64,128,128]{2,1,0:T(8,128)(2,1)}, u32[]{:S(2)}, u32[]{:S(2)}) collective-permute-start(bf16[64,128,128]{2,1,0:T(8,128)(2,1)S(1)} %bitcast.30), channel_id=1, source_target_pairs={{0,2},{6,4},{1,3},{7,5},{8,10},{14,12},{9,11},{15,13},{16,18},{22,... | collective-permute-start | bytes 6291464 | tf_op jit(solution)/shard_map/ppermute | solution.py:265
  16.1 2.0 %collective-permute-start = (bf16[64,128,128]{2,1,0:T(8,128)(2,1)S(1)}, bf16[64,128,128]{2,1,0:T(8,128)(2,1)}, u32[]{:S(2)}, u32[]{:S(2)}) collective-permute-start(bf16[64,128,128]{2,1,0:T(8,128)(2,1)S(1)} %bitcast.31), channel_id=1, source_target_pairs={{2,4},{4,2},{3,5},{5,3},{10,12},{12,10},{11,13},{13,11},{18,20},{2... | collective-permute-start | bytes 6291464 | tf_op jit(solution)/shard_map/ppermute | solution.py:265
  18.1 2.0 %collective-permute-start.3 = (bf16[56,128,128]{2,1,0:T(8,128)(2,1)}, bf16[56,128,128]{2,1,0:T(8,128)(2,1)}, u32[]{:S(2)}, u32[]{:S(2)}) collective-permute-start(bf16[56,128,128]{2,1,0:T(8,128)(2,1)} %bitcast.33), channel_id=1, source_target_pairs={{0,8},{8,0},{1,9},{9,1},{2,10},{10,2},{3,11},{11,3},{4,12},{12,4},... | collective-permute-start | bytes 5505032 | tf_op jit(solution)/shard_map/ppermute | solution.py:271
  20.4 3.0 %all-gather = s32[2,1,1,7,3,64]{5,2,4,3,1,0:T(1,128)S(1)} all-gather(s32[1,1,1,7,3,64]{5,2,4,3,1,0:T(1,128)S(1)} %copy-done.7), channel_id=2, replica_groups=mesh['grp'=2,'row'=2,'col'=4,'dep'=2] {'dep'}, dimensions={0}, use_global_device_ids=true | all-gather | bytes 16128 | tf_op jit(solution)/shard_map/all_gather | solution.py:272
  24.5 34.9 %collective-permute-done.3.refs_3_ = bf16[56,128,128]{2,1,0:T(8,128)(2,1)} collective-permute-done((bf16[56,128,128]{2,1,0:T(8,128)(2,1)}, bf16[56,128,128]{2,1,0:T(8,128)(2,1)}, u32[]{:S(2)}, u32[]{:S(2)}) %collective-permute-start.3) | collective-permute-done | bytes 1835040 | tf_op jit(solution)/shard_map/ppermute | solution.py:271
  61.3 2.1 %collective-permute-start.4 = (bf16[64,128,128]{2,1,0:T(8,128)(2,1)}, bf16[64,128,128]{2,1,0:T(8,128)(2,1)}, u32[]{:S(2)}, u32[]{:S(2)}) collective-permute-start(bf16[64,128,128]{2,1,0:T(8,128)(2,1)} %collective-permute-done.1.refs_10_), channel_id=1, source_target_pairs={{2,4},{4,2},{3,5},{5,3},{10,12},{12,10},{11,13},{13,11},{18,20},{2... | collective-permute-start | bytes 6291464 | tf_op jit(solution)/shard_map/ppermute | solution.py:265
  63.3 1.3 collective-permute-start.6
  64.6 1.3 collective-permute-start.5
  65.9 48.7 %collective-permute-done.6 = bf16[64,128,128]{2,1,0:T(8,128)(2,1)} collective-permute-done((bf16[64,128,128]{2,1,0:T(8,128)(2,1)}, bf16[64,128,128]{2,1,0:T(8,128)(2,1)}, u32[]{:S(2)}, u32[]{:S(2)}) %collective-permute-start.6) | collective-permute-done | bytes 2097184 | tf_op jit(solution)/shard_map/ppermute | solution.py:265
  114.6 1.8 broadcast_select_fusion
  116.4 1.2 fusion.8
  117.6 3.0 %collective-permute-start.8 = (bf16[32,128,128]{2,1,0:T(8,128)(2,1)S(1)}, bf16[32,128,128]{2,1,0:T(8,128)(2,1)}, u32[]{:S(2)}, u32[]{:S(2)}) collective-permute-start(bf16[32,128,128]{2,1,0:T(8,128)(2,1)S(1)} %get-tuple-element.27.refs_15_), channel_id=1, source_target_pairs={{0,1},{1,0},{2,3},{3,2},{4,5},{5,4},{6,7},{7,6},{8,9},{9,8},{10,11... | collective-permute-start | bytes 3145736 | tf_op jit(solution)/shard_map/ppermute | solution.py:214
  121.2 3.3 %collective-permute-done.8.refs_17_ = bf16[32,128,128]{2,1,0:T(8,128)(2,1)} collective-permute-done((bf16[32,128,128]{2,1,0:T(8,128)(2,1)S(1)}, bf16[32,128,128]{2,1,0:T(8,128)(2,1)}, u32[]{:S(2)}, u32[]{:S(2)}) %collective-permute-start.8) | collective-permute-done | bytes 1048608 | tf_op jit(solution)/shard_map/ppermute | solution.py:214
  124.7 2.8 %all-gather.12.cloned.1.call-done.refs_9_ = bf16[128,128,128]{2,1,0:T(8,128)(2,1)} async-done(((bf16[64,128,128]{2,1,0:T(8,128)(2,1)}), bf16[128,128,128]{2,1,0:T(8,128)(2,1)}) %all-gather.12.cloned.1.call-update) | async-done | bytes 4194320 | tf_op jit(solution)/shard_map/all_gather | solution.py:218
  127.6 14.6 %shard_map.37 = (f32[113,128,128]{2,1,0:T(8,128)S(1)}, bf16[224,128,128]{2,1,0:T(8,128)(2,1)S(1)}) custom-call(s32[896]{0:T(1024)} %fusion.7.refs_0_.packed, s32[6]{0:T(128)} %stack.19.refs_1_, bf16[56,128,128]{2,1,0:T(8,128)(2,1)} %bitcast.34, bf16[56,128,128]{2,1,0:T(8,128)(2,1)} %collective-permute-done.3.refs_3_, bf16[112,128,128]{2,1,0:T(8,128)(2,1)} %bitcast.36, ...), custom_call_target="tpu_custom_call" | custom-call | flops 1 | bytes 1 | tf_op jit(solution)/shard_map/pallas_call | solution.py:156
  142.2 2.9 %copy-done = f32[113,128,128]{2,1,0:T(8,128)} copy-done((f32[113,128,128]{2,1,0:T(8,128)}, f32[113,128,128]{2,1,0:T(8,128)S(1)}, u32[]{:S(2)}) %copy-start) | copy-done | bytes 7405592
  145.1 3.0 %copy-done.2 = bf16[224,128,128]{2,1,0:T(8,128)(2,1)} copy-done((bf16[224,128,128]{2,1,0:T(8,128)(2,1)}, bf16[224,128,128]{2,1,0:T(8,128)(2,1)S(1)}, u32[]{:S(2)}) %copy-start.2) | copy-done | bytes 7340056
  148.2 11.2 %collective-permute-done.5.own = bf16[64,128,128]{2,1,0:T(8,128)(2,1)S(1)} collective-permute-done((bf16[64,128,128]{2,1,0:T(8,128)(2,1)}, bf16[64,128,128]{2,1,0:T(8,128)(2,1)S(1)}, u32[]{:S(2)}, u32[]{:S(2)}) %collective-permute-start.5) | collective-permute-done | bytes 2097184 | tf_op jit(solution)/shard_map/ppermute | solution.py:265
  159.3 2.9 %collective-permute-start.9 = (bf16[64,128,128]{2,1,0:T(8,128)(2,1)S(1)}, bf16[64,128,128]{2,1,0:T(8,128)(2,1)}, u32[]{:S(2)}, u32[]{:S(2)}) collective-permute-start(bf16[64,128,128]{2,1,0:T(8,128)(2,1)S(1)} %collective-permute-done.5.own), channel_id=1, source_target_pairs={{0,1},{1,0},{2,3},{3,2},{4,5},{5,4},{6,7},{7,6},{8,9},{9,8},{10,11... | collective-permute-start | bytes 6291464 | tf_op jit(solution)/shard_map/ppermute | solution.py:214
  162.2 3.9 %collective-permute-done.9.other = bf16[64,128,128]{2,1,0:T(8,128)(2,1)} collective-permute-done((bf16[64,128,128]{2,1,0:T(8,128)(2,1)S(1)}, bf16[64,128,128]{2,1,0:T(8,128)(2,1)}, u32[]{:S(2)}, u32[]{:S(2)}) %collective-permute-start.9) | collective-permute-done | bytes 2097184 | tf_op jit(solution)/shard_map/ppermute | solution.py:214
  166.1 3.1 %copy-done.1 = f32[113,128,128]{2,1,0:T(8,128)S(1)} copy-done((f32[113,128,128]{2,1,0:T(8,128)S(1)}, f32[113,128,128]{2,1,0:T(8,128)}, u32[]{:S(2)}) %copy-start.1) | copy-done | bytes 7405592
  169.3 3.1 %copy-done.3 = bf16[224,128,128]{2,1,0:T(8,128)(2,1)S(1)} copy-done((bf16[224,128,128]{2,1,0:T(8,128)(2,1)S(1)}, bf16[224,128,128]{2,1,0:T(8,128)(2,1)}, u32[]{:S(2)}) %copy-start.3) | copy-done | bytes 7340056
  172.3 9.4 %shard_map.38 = (bf16[112,128,128]{2,1,0:T(8,128)(2,1)}, f32[113,128,128]{2,1,0:T(8,128)S(1)}) custom-call(s32[896]{0:T(1024)S(1)} %copy-done.4, s32[1]{0:T(128)} %bitcast.3.classes, bf16[224,128,128]{2,1,0:T(8,128)(2,1)S(1)} %copy-done.3, f32[113,128,128]{2,1,0:T(8,128)S(1)} %copy-done.1, ...), custom_call_target="tpu_custom_call", output_to_operand_aliasing={{1}: (3, {})} | custom-call | flops 1 | bytes 1 | tf_op jit(solution)/shard_map/pallas_call | solution.py:198
  (58 shorter events, 5.6 us)
Async XLA Ops:
  6.5 1.6 copy-start.5
  6.5 13.9 %copy-start.7 = (s32[1,1,1,7,3,64]{5,2,4,3,1,0:T(1,128)S(1)}, s32[1,1,1,7,3,64]{5,2,4,3,1,0:T(1,128)}, u32[]{:S(2)}) copy-start(s32[1,1,1,7,3,64]{5,2,4,3,1,0:T(1,128)} %param.5) | copy-start | bytes 16132
  6.5 114.7 %all-gather.18.cloned.1.call-start = ((), (), s32[]{:S(2)}) async-start(), calls=%async_computation.4 | async-start | bytes 5505024 | tf_op jit(solution)/shard_map/all_gather | solution.py:218
  7.3 113.9 %all-gather.20.cloned.1.call-start = ((), (), s32[]{:S(2)}) async-start(), calls=%async_computation.5 | async-start | bytes 6291456 | tf_op jit(solution)/shard_map/all_gather | solution.py:218
  8.0 116.7 %all-gather.10.cloned.1.call-start = ((), (), s32[]{:S(2)}) async-start(), calls=%async_computation | async-start | bytes 5505024 | tf_op jit(solution)/shard_map/all_gather | solution.py:218
  8.1 51.4 %collective-permute-start.2 = (bf16[64,128,128]{2,1,0:T(8,128)(2,1)S(1)}, bf16[64,128,128]{2,1,0:T(8,128)(2,1)}, u32[]{:S(2)}, u32[]{:S(2)}) collective-permute-start(bf16[64,128,128]{2,1,0:T(8,128)(2,1)S(1)} %bitcast.29), channel_id=1, source_target_pairs={{4,6},{2,0},{5,7},{3,1},{12,14},{10,8},{13,15},{11,9},{20,22},{18,... | collective-permute-start | bytes 6291464 | tf_op jit(solution)/shard_map/ppermute | solution.py:265
  9.4 50.1 %collective-permute-start.1 = (bf16[64,128,128]{2,1,0:T(8,128)(2,1)S(1)}, bf16[64,128,128]{2,1,0:T(8,128)(2,1)}, u32[]{:S(2)}, u32[]{:S(2)}) collective-permute-start(bf16[64,128,128]{2,1,0:T(8,128)(2,1)S(1)} %bitcast.30), channel_id=1, source_target_pairs={{0,2},{6,4},{1,3},{7,5},{8,10},{14,12},{9,11},{15,13},{16,18},{22,... | collective-permute-start | bytes 6291464 | tf_op jit(solution)/shard_map/ppermute | solution.py:265
  16.1 43.4 %collective-permute-start = (bf16[64,128,128]{2,1,0:T(8,128)(2,1)S(1)}, bf16[64,128,128]{2,1,0:T(8,128)(2,1)}, u32[]{:S(2)}, u32[]{:S(2)}) collective-permute-start(bf16[64,128,128]{2,1,0:T(8,128)(2,1)S(1)} %bitcast.31), channel_id=1, source_target_pairs={{2,4},{4,2},{3,5},{5,3},{10,12},{12,10},{11,13},{13,11},{18,20},{2... | collective-permute-start | bytes 6291464 | tf_op jit(solution)/shard_map/ppermute | solution.py:265
  18.1 41.4 %collective-permute-start.3 = (bf16[56,128,128]{2,1,0:T(8,128)(2,1)}, bf16[56,128,128]{2,1,0:T(8,128)(2,1)}, u32[]{:S(2)}, u32[]{:S(2)}) collective-permute-start(bf16[56,128,128]{2,1,0:T(8,128)(2,1)} %bitcast.33), channel_id=1, source_target_pairs={{0,8},{8,0},{1,9},{9,1},{2,10},{10,2},{3,11},{11,3},{4,12},{12,4},... | collective-permute-start | bytes 5505032 | tf_op jit(solution)/shard_map/ppermute | solution.py:271
  59.5 65.2 %all-gather.16.cloned.1.call-start = ((), (), s32[]{:S(2)}) async-start(), calls=%async_computation.3 | async-start | bytes 6291456 | tf_op jit(solution)/shard_map/all_gather | solution.py:218
  60.1 64.6 %all-gather.14.cloned.1.call-start = ((), (), s32[]{:S(2)}) async-start(), calls=%async_computation.2 | async-start | bytes 6291456 | tf_op jit(solution)/shard_map/all_gather | solution.py:218
  60.7 66.9 %all-gather.12.cloned.1.call-start = ((), (), s32[]{:S(2)}) async-start(), calls=%async_computation.1 | async-start | bytes 6291456 | tf_op jit(solution)/shard_map/all_gather | solution.py:218
  61.3 3.4 %collective-permute-start.4 = (bf16[64,128,128]{2,1,0:T(8,128)(2,1)}, bf16[64,128,128]{2,1,0:T(8,128)(2,1)}, u32[]{:S(2)}, u32[]{:S(2)}) collective-permute-start(bf16[64,128,128]{2,1,0:T(8,128)(2,1)} %collective-permute-done.1.refs_10_), channel_id=1, source_target_pairs={{2,4},{4,2},{3,5},{5,3},{10,12},{12,10},{11,13},{13,11},{18,20},{2... | collective-permute-start | bytes 6291464 | tf_op jit(solution)/shard_map/ppermute | solution.py:265
  63.3 51.3 %collective-permute-start.6 = (bf16[64,128,128]{2,1,0:T(8,128)(2,1)}, bf16[64,128,128]{2,1,0:T(8,128)(2,1)}, u32[]{:S(2)}, u32[]{:S(2)}) collective-permute-start(bf16[64,128,128]{2,1,0:T(8,128)(2,1)} %collective-permute-done.refs_8_), channel_id=1, source_target_pairs={{4,6},{2,0},{5,7},{3,1},{12,14},{10,8},{13,15},{11,9},{20,22},{18,... | collective-permute-start | bytes 6291464 | tf_op jit(solution)/shard_map/ppermute | solution.py:265
  64.6 94.7 %collective-permute-start.5 = (bf16[64,128,128]{2,1,0:T(8,128)(2,1)}, bf16[64,128,128]{2,1,0:T(8,128)(2,1)S(1)}, u32[]{:S(2)}, u32[]{:S(2)}) collective-permute-start(bf16[64,128,128]{2,1,0:T(8,128)(2,1)} %collective-permute-done.4), channel_id=1, source_target_pairs={{4,6},{2,0},{5,7},{3,1},{12,14},{10,8},{13,15},{11,9},{20,22},{18,... | collective-permute-start | bytes 6291464 | tf_op jit(solution)/shard_map/ppermute | solution.py:265
  117.6 10.0 %copy-start.6 = (bf16[32,128,128]{2,1,0:T(8,128)(2,1)}, bf16[32,128,128]{2,1,0:T(8,128)(2,1)S(1)}, u32[]{:S(2)}) copy-start(bf16[32,128,128]{2,1,0:T(8,128)(2,1)S(1)} %get-tuple-element.27.refs_15_) | copy-start | bytes 3145732
  117.6 6.9 %collective-permute-start.8 = (bf16[32,128,128]{2,1,0:T(8,128)(2,1)S(1)}, bf16[32,128,128]{2,1,0:T(8,128)(2,1)}, u32[]{:S(2)}, u32[]{:S(2)}) collective-permute-start(bf16[32,128,128]{2,1,0:T(8,128)(2,1)S(1)} %get-tuple-element.27.refs_15_), channel_id=1, source_target_pairs={{0,1},{1,0},{2,3},{3,2},{4,5},{5,4},{6,7},{7,6},{8,9},{9,8},{10,11... | collective-permute-start | bytes 3145736 | tf_op jit(solution)/shard_map/ppermute | solution.py:214
  120.6 4.2 %collective-permute-start.7 = (bf16[32,128,128]{2,1,0:T(8,128)(2,1)}, bf16[32,128,128]{2,1,0:T(8,128)(2,1)}, u32[]{:S(2)}, u32[]{:S(2)}) collective-permute-start(bf16[32,128,128]{2,1,0:T(8,128)(2,1)} %get-tuple-element.28.refs_14_), channel_id=1, source_target_pairs={{0,1},{1,0},{2,3},{3,2},{4,5},{5,4},{6,7},{7,6},{8,9},{9,8},{10,11... | collective-permute-start | bytes 3145736 | tf_op jit(solution)/shard_map/ppermute | solution.py:214
  127.6 38.5 %copy-start.4 = (s32[896]{0:T(1024)S(1)}, s32[896]{0:T(1024)}, u32[]{:S(2)}) copy-start(s32[896]{0:T(1024)} %fusion.7.refs_0_.packed) | copy-start | bytes 10756
  142.2 2.9 %copy-start = (f32[113,128,128]{2,1,0:T(8,128)}, f32[113,128,128]{2,1,0:T(8,128)S(1)}, u32[]{:S(2)}) copy-start(f32[113,128,128]{2,1,0:T(8,128)S(1)} %get-tuple-element.24.given) | copy-start | bytes 22216708
  145.1 3.0 %copy-start.2 = (bf16[224,128,128]{2,1,0:T(8,128)(2,1)}, bf16[224,128,128]{2,1,0:T(8,128)(2,1)S(1)}, u32[]{:S(2)}) copy-start(bf16[224,128,128]{2,1,0:T(8,128)(2,1)S(1)} %get-tuple-element.23.right) | copy-start | bytes 22020100
  159.3 6.8 %collective-permute-start.9 = (bf16[64,128,128]{2,1,0:T(8,128)(2,1)S(1)}, bf16[64,128,128]{2,1,0:T(8,128)(2,1)}, u32[]{:S(2)}, u32[]{:S(2)}) collective-permute-start(bf16[64,128,128]{2,1,0:T(8,128)(2,1)S(1)} %collective-permute-done.5.own), channel_id=1, source_target_pairs={{0,1},{1,0},{2,3},{3,2},{4,5},{5,4},{6,7},{7,6},{8,9},{9,8},{10,11... | collective-permute-start | bytes 6291464 | tf_op jit(solution)/shard_map/ppermute | solution.py:214
  166.1 3.1 %copy-start.1 = (f32[113,128,128]{2,1,0:T(8,128)S(1)}, f32[113,128,128]{2,1,0:T(8,128)}, u32[]{:S(2)}) copy-start(f32[113,128,128]{2,1,0:T(8,128)} %copy-done) | copy-start | bytes 22216708
  169.2 3.1 %copy-start.3 = (bf16[224,128,128]{2,1,0:T(8,128)(2,1)S(1)}, bf16[224,128,128]{2,1,0:T(8,128)(2,1)}, u32[]{:S(2)}) copy-start(bf16[224,128,128]{2,1,0:T(8,128)(2,1)} %copy-done.2) | copy-start | bytes 22020100
Sparse Core Ops, SparseCore 0:
  8.9 15.3 all-gather.17
  25.9 14.8 all-gather.19
  59.7 18.1 all-gather.9
  79.2 14.8 all-gather.15
  95.5 14.8 all-gather.13
  111.8 15.7 all-gather.11

commit v11 on v10

--- a/solution.py
+++ b/solution.py
@@ -9,6 +9,7 @@
 
 NBQ = 32
 UNROLL = 8
+PARTS = 4
 
 
 def chosen_products(packed, classes, panels, todo, shape, layers, spare, first_left=0):
@@ -113,7 +114,7 @@
         outs[0][...] = work[:spare].astype(outs[0].dtype)
 
 
-def product_sums(packed, classes, layer, shape, layers, panels, rights, givens, result_slots, saved, resident=False):
+def product_sums(packed, scalars, shape, layers, panels, rights, givens, result_slots, saved, resident=False):
     step_count, columns, slots = shape
     rows, width = rights[0][0].shape[1:]
     operands = []
@@ -141,7 +142,6 @@
     anywhere = pl.BlockSpec(memory_space=pl.ANY)
     in_scalar = pl.BlockSpec(memory_space=pltpu.SMEM)
     copy_count = len(rights) + sum(len(pieces) for pieces in panels) + len(givens) + len(saved) + 1
-    scalars = jnp.stack([jnp.asarray(value, jnp.int32) for value in [*classes, layer]])
     if saved:
         out_shape = [jax.ShapeDtypeStruct((size, rows, width), jnp.float32) for size in saved]
     else:
@@ -164,7 +164,7 @@
             shape,
             layers,
             len(operands),
-            len(classes),
+            len(panels),
         ),
         out_shape=out_shape,
         in_specs=[in_scalar, in_scalar] + [anywhere] * len(operands),
@@ -179,35 +179,52 @@
     )(packed, scalars, *operands)
 
 
-def last_kernel(shape, packed, classes, right, given, own, other, out, work, todo):
+def panel_kernel(shape, layer, kind_at, finish, packed, scalars, right, given, left, *refs):
     del given
     step_count, columns, slots = shape
-    spare = work.shape[0] - 1
-    for layer, left in enumerate((own, other)):
-        base = layer * step_count * slots
-        part = packed.at[pl.ds(base, step_count * slots)]
-        count = chosen_products(part, [classes[0]], 1, todo, shape, 1, spare, layer * slots)
-        add_chosen(todo, count, left, right, work, layer * slots)
-    out[...] = work[:spare].astype(out.dtype)
-
-
-def last_sums(packed, kind, shape, own, other, right, given):
+    work, todo = (refs[1], refs[2]) if finish else (refs[0], refs[1])
+    spare, first = work.shape[0] - 1, layer * slots
+    part = packed.at[pl.ds(layer * step_count * slots, step_count * slots)]
+    count = chosen_products(part, [scalars[kind_at]], 1, todo, shape, 1, spare, first)
+    add_chosen(todo, count, left, right, work, first)
+    if finish:
+        out, rounded, sems = refs[0], refs[3], refs[4]
+        size = spare // PARTS
+        copies = []
+        for index in range(PARTS):
+            span = pl.ds(index * size, size if index < PARTS - 1 else spare - index * size)
+            rounded[span] = work[span].astype(rounded.dtype)
+            copies.append(pltpu.make_async_copy(rounded.at[span], out.at[span], sems.at[index]))
+            copies[-1].start()
+        for copy in copies:
+            copy.wait()
+
+
+def add_panel(packed, scalars, kind_at, shape, layer, panel, right, given, finish):
     step_count, columns, slots = shape
     result_slots, rows, width = given.shape[0] - 1, *given.shape[1:]
     in_scalar, in_vector = pl.BlockSpec(memory_space=pltpu.SMEM), pl.BlockSpec(memory_space=pltpu.VMEM)
+    out_shape, out_specs = [pltpu.VMEM(given.shape, given.dtype)], [in_vector]
+    scratch = [pltpu.SMEM((-(-step_count // columns) * slots + UNROLL,), jnp.int32)]
+    if finish:
+        out_shape.insert(0, jax.ShapeDtypeStruct((result_slots, rows, width), jnp.bfloat16))
+        out_specs.insert(0, pl.BlockSpec(memory_space=pl.ANY))
+        scratch.append(pltpu.VMEM((result_slots, rows, width), jnp.bfloat16))
+        scratch.append(pltpu.SemaphoreType.DMA((PARTS,)))
     return pl.pallas_call(
-        functools.partial(last_kernel, shape),
-        out_shape=[
-            jax.ShapeDtypeStruct((result_slots, rows, width), jnp.bfloat16),
-            pltpu.VMEM(given.shape, given.dtype),
-        ],
-        in_specs=[in_scalar] * 2 + [in_vector] * 4,
-        out_specs=[in_vector] * 2,
-        scratch_shapes=[pltpu.SMEM((-(-step_count // columns) * slots + UNROLL,), jnp.int32)],
-        input_output_aliases={3: 1},
-        compiler_params=pltpu.CompilerParams(vmem_limit_bytes=20 << 20),
+        functools.partial(panel_kernel, shape, layer, kind_at, finish),
+        out_shape=out_shape,
+        in_specs=[in_scalar] * 2 + [in_vector] * 3,
+        out_specs=out_specs,
+        scratch_shapes=scratch,
+        input_output_aliases={3: len(out_shape) - 1},
+        compiler_params=pltpu.CompilerParams(vmem_limit_bytes=12 << 20),
         cost_estimate=pl.CostEstimate(flops=1, bytes_accessed=1, transcendentals=0),
-    )(packed, kind.astype(jnp.int32).reshape(1), right, given, own, other)[0]
+    )(packed, scalars, right, given, panel)[0]
+
+
+def scalar_list(*values):
+    return jnp.stack([jnp.asarray(value, jnp.int32) for value in values])
 
 
 def swapped(value):
@@ -246,7 +263,8 @@
         panels += [[(value, False), (paired(value), True)] for value in (rising, falling)]
         classes += [columns - distance, distance]
         saved = [] if distance == reach else [half]
-        total = product_sums(packed, classes, layer, shape, 2, panels, rights, total, half, saved)
+        scalars = scalar_list(*classes, layer)
+        total = product_sums(packed, scalars, shape, 2, panels, rights, total, half, saved)
         panels, classes = [], []
     return total[0][None, None, None]
 
@@ -267,7 +285,7 @@
     def right_slot(slot, layers):
         return (layers * 2 + ((slot // part) ^ lax.axis_index("row"))) * part + slot % part
 
-    across_one, inward_one, outer_one = hop(own, across), hop(own, inward), hop(own, outward)
+    outer_one, inward_one, across_one = hop(own, outward), hop(own, inward), hop(own, across)
     met = lax.ppermute(right_own, "row", [(0, 1), (1, 0)])
     kept = kept_products(lax.all_gather(step_lists, "dep"), layer, half, right_slot)
     right_pair, own_pair = paired(right_own), paired(own)
@@ -285,18 +303,20 @@
     rights = [(right_own, False), (met, False), (right_pair, True), (met_pair, True)]
     panels = [
         [(own, False), (own_pair, True)],
+        [(outer_one, False), (outer_pair, True)],
+        [(inward_one, False), (inward_pair, True)],
         [(across_one, False), (across_pair, True)],
-        [(inward_one, False), (inward_pair, True)],
-        [(outer_one, False), (outer_pair, True)],
         [(piece, False) for piece in two] + [(swapped(piece), False) for piece in two],
     ]
-    classes = [0, jnp.where(inner, jnp.where(low, 1, 3), -1), jnp.where(inner, jnp.where(low, 3, 1), -1)]
-    classes += [jnp.where(inner, -1, jnp.where(low, 1, 3)), 2]
-    total, right = product_sums(kept, classes, layer, shape, 2, panels, rights, [], half, [], True)
+    classes = [0, jnp.where(inner, -1, jnp.where(low, 1, 3)), jnp.where(inner, jnp.where(low, 3, 1), -1)]
+    classes += [jnp.where(inner, jnp.where(low, 1, 3), -1), 2]
+    scalars = scalar_list(*classes, layer, jnp.where(inner, -1, jnp.where(low, 3, 1)))
+    total, right = product_sums(kept, scalars, shape, 2, panels, rights, [], half, [], True)
 
     outer_three, total, right = fence((outer_three, total, right))
-    kind = jnp.where(inner, -1, jnp.where(low, 3, 1))
-    block = last_sums(kept, kind, shape, outer_three, swapped(outer_three), right, total)
+    kind_at = len(classes) + 1
+    total = add_panel(kept, scalars, kind_at, shape, 0, outer_three, right, total, False)
+    block = add_panel(kept, scalars, kind_at, shape, 1, swapped(outer_three), right, total, True)
     return block[None, None, None]
 
 

time: 189 us -> 179 us (0.947)
  local copies, waits for them, and re-layouts: 14.7 us -> 2.68 us
  waiting for transfers between devices: 108 us -> 110 us
    unnamed x16 -> x10, local copies, waits for them, and re-layouts: 12.2 us -> 0.09 us
    ppermute x6, waiting for transfers between devices: 59.8 us -> 65.5 us  [hop(): return lax.ppermute(value, 'col', pairs)]
    ppermute x3, waiting for transfers between devices: 7.45 us -> 3.78 us  [swapped(): return lax.ppermute(value, 'dep', [(0, 1), (1, 0)])]
    pallas_call x1 -> x2, Pallas kernels: 9.37 us -> 8.82 us  [add_panel(): pl.pallas_call(functools.partial(panel_kernel, shape, layer, kind_at, fin...]
  transfers between devices with their start and end apart: 16 -> 16, of which waited for: 7 -> 7; matrix products, arithmetic and copies ran while one was open for 3% -> 3% of each run, Pallas kernels for 8% -> 10%
where the time goes in v11:
time: 179 us; the launch traced here: 178 us
  waiting for transfers between devices  110 us (61%)
  Pallas kernels  23.6 us (13%)
  starting transfers between devices  22.7 us (13%)
  between operations  13.6 us (8%)
  blocking collectives  3 us (2%)
  local copies, waits for them, and re-layouts  2.68 us (1%)
  other arithmetic  2.48 us (1%)
    ppermute x6, waiting for transfers between devices, hop(): return lax.ppermute(value, 'col', pairs)  65.5 us
    ppermute x1, waiting for transfers between devices, line(): met = lax.ppermute(right_own, 'row', [(0, 1), (1, 0)])  34.9 us
    pallas_call x1, Pallas kernels, product_sums(): pl.pallas_call(functools.partial(sum_kernel, panel_spans, right_spans, gi...  14.8 us
    ppermute x6, starting transfers between devices, hop(): return lax.ppermute(value, 'col', pairs)  14.7 us
    pallas_call x2, Pallas kernels, add_panel(): pl.pallas_call(functools.partial(panel_kernel, shape, layer, kind_at, fin...  8.82 us
    ppermute x3, starting transfers between devices, swapped(): return lax.ppermute(value, 'dep', [(0, 1), (1, 0)])  5.89 us
    ppermute x3, waiting for transfers between devices, swapped(): return lax.ppermute(value, 'dep', [(0, 1), (1, 0)])  3.78 us
  transfers between devices with their start and end apart: 16, of which 7 were waited for; matrix products, arithmetic and copies ran while one was open for 3% of the time, Pallas kernels for 10%

profile of v11, /device:TPU:1, one launch (start us, length us, event | category | flops | bytes accessed | tf_op | source)
XLA Modules:
  0.0 178.2 jit_solution(6593054454171738502)
XLA Ops:
  6.5 0.7 all-gather.18.cloned.1.call-update
  7.3 0.7 all-gather.20.cloned.1.call-update
  8.1 1.3 collective-permute-start.2
  9.4 6.7 %collective-permute-start.1 = (bf16[64,128,128]{2,1,0:T(8,128)(2,1)S(1)}, bf16[64,128,128]{2,1,0:T(8,128)(2,1)}, u32[]{:S(2)}, u32[]{:S(2)}) collective-permute-start(bf16[64,128,128]{2,1,0:T(8,128)(2,1)S(1)} %bitcast.30), channel_id=1, source_target_pairs={{0,2},{6,4},{1,3},{7,5},{8,10},{14,12},{9,11},{15,13},{16,18},{22,... | collective-permute-start | bytes 6291464 | tf_op jit(solution)/shard_map/ppermute | solution.py:283
  16.2 2.0 %collective-permute-start = (bf16[64,128,128]{2,1,0:T(8,128)(2,1)S(1)}, bf16[64,128,128]{2,1,0:T(8,128)(2,1)}, u32[]{:S(2)}, u32[]{:S(2)}) collective-permute-start(bf16[64,128,128]{2,1,0:T(8,128)(2,1)S(1)} %bitcast.31), channel_id=1, source_target_pairs={{2,4},{4,2},{3,5},{5,3},{10,12},{12,10},{11,13},{13,11},{18,20},{2... | collective-permute-start | bytes 6291464 | tf_op jit(solution)/shard_map/ppermute | solution.py:283
  18.1 2.0 %collective-permute-start.3 = (bf16[56,128,128]{2,1,0:T(8,128)(2,1)}, bf16[56,128,128]{2,1,0:T(8,128)(2,1)}, u32[]{:S(2)}, u32[]{:S(2)}) collective-permute-start(bf16[56,128,128]{2,1,0:T(8,128)(2,1)} %bitcast.33), channel_id=1, source_target_pairs={{0,8},{8,0},{1,9},{9,1},{2,10},{10,2},{3,11},{11,3},{4,12},{12,4},... | collective-permute-start | bytes 5505032 | tf_op jit(solution)/shard_map/ppermute | solution.py:289
  20.4 3.0 %all-gather = s32[2,1,1,7,3,64]{5,2,4,3,1,0:T(1,128)S(1)} all-gather(s32[1,1,1,7,3,64]{5,2,4,3,1,0:T(1,128)S(1)} %copy-done.4), channel_id=2, replica_groups=mesh['grp'=2,'row'=2,'col'=4,'dep'=2] {'dep'}, dimensions={0}, use_global_device_ids=true | all-gather | bytes 16128 | tf_op jit(solution)/shard_map/all_gather | solution.py:290
  24.0 0.6 fusion.7.refs_0_.packed
  24.6 34.9 %collective-permute-done.3.refs_3_ = bf16[56,128,128]{2,1,0:T(8,128)(2,1)} collective-permute-done((bf16[56,128,128]{2,1,0:T(8,128)(2,1)}, bf16[56,128,128]{2,1,0:T(8,128)(2,1)}, u32[]{:S(2)}, u32[]{:S(2)}) %collective-permute-start.3) | collective-permute-done | bytes 1835040 | tf_op jit(solution)/shard_map/ppermute | solution.py:289
  61.3 2.1 %collective-permute-start.4 = (bf16[64,128,128]{2,1,0:T(8,128)(2,1)}, bf16[64,128,128]{2,1,0:T(8,128)(2,1)}, u32[]{:S(2)}, u32[]{:S(2)}) collective-permute-start(bf16[64,128,128]{2,1,0:T(8,128)(2,1)} %collective-permute-done.1.refs_10_), channel_id=1, source_target_pairs={{2,4},{4,2},{3,5},{5,3},{10,12},{12,10},{11,13},{13,11},{18,20},{2... | collective-permute-start | bytes 6291464 | tf_op jit(solution)/shard_map/ppermute | solution.py:283
  63.4 1.3 collective-permute-start.6
  64.7 1.3 collective-permute-start.5
  66.0 48.6 %collective-permute-done.6 = bf16[64,128,128]{2,1,0:T(8,128)(2,1)} collective-permute-done((bf16[64,128,128]{2,1,0:T(8,128)(2,1)}, bf16[64,128,128]{2,1,0:T(8,128)(2,1)}, u32[]{:S(2)}, u32[]{:S(2)}) %collective-permute-start.6) | collective-permute-done | bytes 2097184 | tf_op jit(solution)/shard_map/ppermute | solution.py:283
  114.6 1.8 %broadcast_select_fusion = bf16[64,128,128]{2,1,0:T(8,128)(2,1)S(1)} fusion(bf16[64,128,128]{2,1,0:T(8,128)(2,1)} %collective-permute-done.4, bf16[64,128,128]{2,1,0:T(8,128)(2,1)} %collective-permute-done.6, pred[]{:T(512)S(6)} %or.13), kind=kLoop, calls=%fused_computation | loop fusion | flops 1048576 | bytes 6291457 | tf_op jit(solution)/shard_map/jit(_where)/select_n | solution.py:301
  116.4 1.2 fusion.8
  117.6 3.0 %collective-permute-start.8 = (bf16[32,128,128]{2,1,0:T(8,128)(2,1)S(1)}, bf16[32,128,128]{2,1,0:T(8,128)(2,1)}, u32[]{:S(2)}, u32[]{:S(2)}) collective-permute-start(bf16[32,128,128]{2,1,0:T(8,128)(2,1)S(1)} %get-tuple-element.27.refs_15_), channel_id=1, source_target_pairs={{0,1},{1,0},{2,3},{3,2},{4,5},{5,4},{6,7},{7,6},{8,9},{9,8},{10,11... | collective-permute-start | bytes 3145736 | tf_op jit(solution)/shard_map/ppermute | solution.py:231
  120.6 0.7 stack.23.refs_1_.scalars
  121.3 3.2 %collective-permute-done.8.refs_17_ = bf16[32,128,128]{2,1,0:T(8,128)(2,1)} collective-permute-done((bf16[32,128,128]{2,1,0:T(8,128)(2,1)S(1)}, bf16[32,128,128]{2,1,0:T(8,128)(2,1)}, u32[]{:S(2)}, u32[]{:S(2)}) %collective-permute-start.8) | collective-permute-done | bytes 1048608 | tf_op jit(solution)/shard_map/ppermute | solution.py:231
  124.8 2.8 %all-gather.16.cloned.1.call-done.refs_13_ = bf16[128,128,128]{2,1,0:T(8,128)(2,1)} async-done(((bf16[64,128,128]{2,1,0:T(8,128)(2,1)}), bf16[128,128,128]{2,1,0:T(8,128)(2,1)}) %all-gather.16.cloned.1.call-update) | async-done | bytes 4194320 | tf_op jit(solution)/shard_map/all_gather | solution.py:235
  127.6 14.8 %shard_map.37 = (f32[113,128,128]{2,1,0:T(8,128)S(1)}, bf16[224,128,128]{2,1,0:T(8,128)(2,1)S(1)}) custom-call(s32[896]{0:T(1024)} %fusion.7.refs_0_.packed, s32[7]{0:T(128)} %stack.23.refs_1_.scalars, bf16[56,128,128]{2,1,0:T(8,128)(2,1)} %bitcast.34, bf16[56,128,128]{2,1,0:T(8,128)(2,1)} %collective-permute-done.3.refs_3_, ...), custom_call_target="tpu_custom_call" | custom-call | flops 1 | bytes 1 | tf_op jit(solution)/shard_map/pallas_call | solution.py:156
  142.4 16.9 %collective-permute-done.5.left = bf16[64,128,128]{2,1,0:T(8,128)(2,1)S(1)} collective-permute-done((bf16[64,128,128]{2,1,0:T(8,128)(2,1)}, bf16[64,128,128]{2,1,0:T(8,128)(2,1)S(1)}, u32[]{:S(2)}, u32[]{:S(2)}) %collective-permute-start.5) | collective-permute-done | bytes 2097184 | tf_op jit(solution)/shard_map/ppermute | solution.py:283
  159.3 2.9 %collective-permute-start.9 = (bf16[64,128,128]{2,1,0:T(8,128)(2,1)S(1)}, bf16[64,128,128]{2,1,0:T(8,128)(2,1)S(1)}, u32[]{:S(2)}, u32[]{:S(2)}) collective-permute-start(bf16[64,128,128]{2,1,0:T(8,128)(2,1)S(1)} %collective-permute-done.5.left), channel_id=1, source_target_pairs={{0,1},{1,0},{2,3},{3,2},{4,5},{5,4},{6,7},{7,6},{8,9},{9,8},{10,11... | collective-permute-start | bytes 6291464 | tf_op jit(solution)/shard_map/ppermute | solution.py:231
  162.2 3.5 %shard_map.38.given = f32[113,128,128]{2,1,0:T(8,128)S(1)} custom-call(s32[896]{0:T(1024)S(1)} %copy-done, s32[7]{0:T(128)S(1)} %copy-done.1, bf16[224,128,128]{2,1,0:T(8,128)(2,1)S(1)} %get-tuple-element.23.right, f32[113,128,128]{2,1,0:T(8,128)S(1)} %get-tuple-element.24.given, ...), custom_call_target="tpu_custom_call", output_to_operand_aliasing={{}: (3, {})} | custom-call | flops 1 | bytes 1 | tf_op jit(solution)/shard_map/pallas_call | solution.py:214
  166.0 5.4 %shard_map.39 = (bf16[112,128,128]{2,1,0:T(8,128)(2,1)}, f32[113,128,128]{2,1,0:T(8,128)S(1)}) custom-call(s32[896]{0:T(1024)S(1)} %copy-done, s32[7]{0:T(128)S(1)} %copy-done.1, bf16[224,128,128]{2,1,0:T(8,128)(2,1)S(1)} %get-tuple-element.23.right, f32[113,128,128]{2,1,0:T(8,128)S(1)} %shard_map.38.given, ...), custom_call_target="tpu_custom_call", output_to_operand_aliasing={{1}: (3, {})} | custom-call | flops 1 | bytes 1 | tf_op jit(solution)/shard_map/pallas_call | solution.py:214
  (53 shorter events, 3.3 us)
Async XLA Ops:
  6.5 1.6 copy-start.2
  6.5 13.9 %copy-start.4 = (s32[1,1,1,7,3,64]{5,2,4,3,1,0:T(1,128)S(1)}, s32[1,1,1,7,3,64]{5,2,4,3,1,0:T(1,128)}, u32[]{:S(2)}) copy-start(s32[1,1,1,7,3,64]{5,2,4,3,1,0:T(1,128)} %param.5) | copy-start | bytes 16132
  6.5 114.7 %all-gather.18.cloned.1.call-start = ((), (), s32[]{:S(2)}) async-start(), calls=%async_computation.4 | async-start | bytes 5505024 | tf_op jit(solution)/shard_map/all_gather | solution.py:235
  7.3 114.0 %all-gather.20.cloned.1.call-start = ((), (), s32[]{:S(2)}) async-start(), calls=%async_computation.5 | async-start | bytes 6291456 | tf_op jit(solution)/shard_map/all_gather | solution.py:235
  8.0 116.7 %all-gather.10.cloned.1.call-start = ((), (), s32[]{:S(2)}) async-start(), calls=%async_computation | async-start | bytes 5505024 | tf_op jit(solution)/shard_map/all_gather | solution.py:235
  8.1 51.4 %collective-permute-start.2 = (bf16[64,128,128]{2,1,0:T(8,128)(2,1)S(1)}, bf16[64,128,128]{2,1,0:T(8,128)(2,1)}, u32[]{:S(2)}, u32[]{:S(2)}) collective-permute-start(bf16[64,128,128]{2,1,0:T(8,128)(2,1)S(1)} %bitcast.29), channel_id=1, source_target_pairs={{4,6},{2,0},{5,7},{3,1},{12,14},{10,8},{13,15},{11,9},{20,22},{18,... | collective-permute-start | bytes 6291464 | tf_op jit(solution)/shard_map/ppermute | solution.py:283
  9.4 50.1 %collective-permute-start.1 = (bf16[64,128,128]{2,1,0:T(8,128)(2,1)S(1)}, bf16[64,128,128]{2,1,0:T(8,128)(2,1)}, u32[]{:S(2)}, u32[]{:S(2)}) collective-permute-start(bf16[64,128,128]{2,1,0:T(8,128)(2,1)S(1)} %bitcast.30), channel_id=1, source_target_pairs={{0,2},{6,4},{1,3},{7,5},{8,10},{14,12},{9,11},{15,13},{16,18},{22,... | collective-permute-start | bytes 6291464 | tf_op jit(solution)/shard_map/ppermute | solution.py:283
  16.2 43.4 %collective-permute-start = (bf16[64,128,128]{2,1,0:T(8,128)(2,1)S(1)}, bf16[64,128,128]{2,1,0:T(8,128)(2,1)}, u32[]{:S(2)}, u32[]{:S(2)}) collective-permute-start(bf16[64,128,128]{2,1,0:T(8,128)(2,1)S(1)} %bitcast.31), channel_id=1, source_target_pairs={{2,4},{4,2},{3,5},{5,3},{10,12},{12,10},{11,13},{13,11},{18,20},{2... | collective-permute-start | bytes 6291464 | tf_op jit(solution)/shard_map/ppermute | solution.py:283
  18.1 41.4 %collective-permute-start.3 = (bf16[56,128,128]{2,1,0:T(8,128)(2,1)}, bf16[56,128,128]{2,1,0:T(8,128)(2,1)}, u32[]{:S(2)}, u32[]{:S(2)}) collective-permute-start(bf16[56,128,128]{2,1,0:T(8,128)(2,1)} %bitcast.33), channel_id=1, source_target_pairs={{0,8},{8,0},{1,9},{9,1},{2,10},{10,2},{3,11},{11,3},{4,12},{12,4},... | collective-permute-start | bytes 5505032 | tf_op jit(solution)/shard_map/ppermute | solution.py:289
  59.6 65.2 %all-gather.12.cloned.1.call-start = ((), (), s32[]{:S(2)}) async-start(), calls=%async_computation.1 | async-start | bytes 6291456 | tf_op jit(solution)/shard_map/all_gather | solution.py:235
  60.2 64.6 %all-gather.14.cloned.1.call-start = ((), (), s32[]{:S(2)}) async-start(), calls=%async_computation.2 | async-start | bytes 6291456 | tf_op jit(solution)/shard_map/all_gather | solution.py:235
  60.8 66.8 %all-gather.16.cloned.1.call-start = ((), (), s32[]{:S(2)}) async-start(), calls=%async_computation.3 | async-start | bytes 6291456 | tf_op jit(solution)/shard_map/all_gather | solution.py:235
  61.3 3.4 %collective-permute-start.4 = (bf16[64,128,128]{2,1,0:T(8,128)(2,1)}, bf16[64,128,128]{2,1,0:T(8,128)(2,1)}, u32[]{:S(2)}, u32[]{:S(2)}) collective-permute-start(bf16[64,128,128]{2,1,0:T(8,128)(2,1)} %collective-permute-done.1.refs_10_), channel_id=1, source_target_pairs={{2,4},{4,2},{3,5},{5,3},{10,12},{12,10},{11,13},{13,11},{18,20},{2... | collective-permute-start | bytes 6291464 | tf_op jit(solution)/shard_map/ppermute | solution.py:283
  63.4 51.2 %collective-permute-start.6 = (bf16[64,128,128]{2,1,0:T(8,128)(2,1)}, bf16[64,128,128]{2,1,0:T(8,128)(2,1)}, u32[]{:S(2)}, u32[]{:S(2)}) collective-permute-start(bf16[64,128,128]{2,1,0:T(8,128)(2,1)} %collective-permute-done.refs_12_), channel_id=1, source_target_pairs={{4,6},{2,0},{5,7},{3,1},{12,14},{10,8},{13,15},{11,9},{20,22},{18,... | collective-permute-start | bytes 6291464 | tf_op jit(solution)/shard_map/ppermute | solution.py:283
  64.7 94.6 %collective-permute-start.5 = (bf16[64,128,128]{2,1,0:T(8,128)(2,1)}, bf16[64,128,128]{2,1,0:T(8,128)(2,1)S(1)}, u32[]{:S(2)}, u32[]{:S(2)}) collective-permute-start(bf16[64,128,128]{2,1,0:T(8,128)(2,1)} %collective-permute-done.4), channel_id=1, source_target_pairs={{4,6},{2,0},{5,7},{3,1},{12,14},{10,8},{13,15},{11,9},{20,22},{18,... | collective-permute-start | bytes 6291464 | tf_op jit(solution)/shard_map/ppermute | solution.py:283
  117.6 10.0 %copy-start.3 = (bf16[32,128,128]{2,1,0:T(8,128)(2,1)}, bf16[32,128,128]{2,1,0:T(8,128)(2,1)S(1)}, u32[]{:S(2)}) copy-start(bf16[32,128,128]{2,1,0:T(8,128)(2,1)S(1)} %get-tuple-element.27.refs_15_) | copy-start | bytes 3145732
  117.6 6.9 %collective-permute-start.8 = (bf16[32,128,128]{2,1,0:T(8,128)(2,1)S(1)}, bf16[32,128,128]{2,1,0:T(8,128)(2,1)}, u32[]{:S(2)}, u32[]{:S(2)}) collective-permute-start(bf16[32,128,128]{2,1,0:T(8,128)(2,1)S(1)} %get-tuple-element.27.refs_15_), channel_id=1, source_target_pairs={{0,1},{1,0},{2,3},{3,2},{4,5},{5,4},{6,7},{7,6},{8,9},{9,8},{10,11... | collective-permute-start | bytes 3145736 | tf_op jit(solution)/shard_map/ppermute | solution.py:231
  120.6 4.2 %collective-permute-start.7 = (bf16[32,128,128]{2,1,0:T(8,128)(2,1)}, bf16[32,128,128]{2,1,0:T(8,128)(2,1)}, u32[]{:S(2)}, u32[]{:S(2)}) collective-permute-start(bf16[32,128,128]{2,1,0:T(8,128)(2,1)} %get-tuple-element.28.refs_14_), channel_id=1, source_target_pairs={{0,1},{1,0},{2,3},{3,2},{4,5},{5,4},{6,7},{7,6},{8,9},{9,8},{10,11... | collective-permute-start | bytes 3145736 | tf_op jit(solution)/shard_map/ppermute | solution.py:231
  127.6 34.6 %copy-start = (s32[896]{0:T(1024)S(1)}, s32[896]{0:T(1024)}, u32[]{:S(2)}) copy-start(s32[896]{0:T(1024)} %fusion.7.refs_0_.packed) | copy-start | bytes 10756
  127.6 34.6 %copy-start.1 = (s32[7]{0:T(128)S(1)}, s32[7]{0:T(128)}, u32[]{:S(2)}) copy-start(s32[7]{0:T(128)} %stack.23.refs_1_.scalars) | copy-start | bytes 88
  159.3 6.7 %collective-permute-start.9 = (bf16[64,128,128]{2,1,0:T(8,128)(2,1)S(1)}, bf16[64,128,128]{2,1,0:T(8,128)(2,1)S(1)}, u32[]{:S(2)}, u32[]{:S(2)}) collective-permute-start(bf16[64,128,128]{2,1,0:T(8,128)(2,1)S(1)} %collective-permute-done.5.left), channel_id=1, source_target_pairs={{0,1},{1,0},{2,3},{3,2},{4,5},{5,4},{6,7},{7,6},{8,9},{9,8},{10,11... | collective-permute-start | bytes 6291464 | tf_op jit(solution)/shard_map/ppermute | solution.py:231
Sparse Core Ops, SparseCore 0:
  8.9 15.3 all-gather.17
  25.9 14.8 all-gather.19
  59.7 18.0 all-gather.9
  79.2 14.8 all-gather.11
  95.5 14.8 all-gather.13
  111.8 15.7 all-gather.15

commit v12 on v11

--- a/solution.py
+++ b/solution.py
@@ -290,7 +290,7 @@
     kept = kept_products(lax.all_gather(step_lists, "dep"), layer, half, right_slot)
     right_pair, own_pair = paired(right_own), paired(own)
 
-    across_one, inward_one, outer_one, met, kept = fence((across_one, inward_one, outer_one, met, kept))
+    outer_one, inward_one, across_one, met, kept = fence((outer_one, inward_one, across_one, met, kept))
     outer_two, across_two = hop(across_one, outward), hop(inward_one, across)
     met_pair, inward_pair, across_pair, outer_pair = [
         paired(value) for value in (met, inward_one, across_one, outer_one)

time: 179 us -> 180 us (level)
  starting transfers between devices: 22.7 us -> 25.3 us
    ppermute x3, starting transfers between devices: 5.89 us -> 9.22 us  [swapped(): return lax.ppermute(value, 'dep', [(0, 1), (1, 0)])]
    all_gather x6, waiting for transfers between devices: 2.86 us -> 0.02 us  [paired(): return lax.all_gather(value, 'dep', axis=0, tiled=True)]
  transfers between devices with their start and end apart: 16 -> 16, of which waited for: 7 -> 8; matrix products, arithmetic and copies ran while one was open for 3% -> 3% of each run, Pallas kernels for 10% -> 10%
where the time goes in v12:
time: 180 us
  waiting for transfers between devices  109 us (61%)
  starting transfers between devices  25.3 us (14%)
  Pallas kernels  23.3 us (13%)
  between operations  13.6 us (8%)
  blocking collectives  3 us (2%)
  local copies, waits for them, and re-layouts  2.68 us (1%)
  other arithmetic  2.48 us (1%)
    ppermute x6, waiting for transfers between devices, hop(): return lax.ppermute(value, 'col', pairs)  65.7 us
    ppermute x1, waiting for transfers between devices, line(): met = lax.ppermute(right_own, 'row', [(0, 1), (1, 0)])  34.9 us
    pallas_call x1, Pallas kernels, product_sums(): pl.pallas_call(functools.partial(sum_kernel, panel_spans, right_spans, gi...  14.7 us
    ppermute x6, starting transfers between devices, hop(): return lax.ppermute(value, 'col', pairs)  14.6 us
    ppermute x3, starting transfers between devices, swapped(): return lax.ppermute(value, 'dep', [(0, 1), (1, 0)])  9.22 us
    pallas_call x2, Pallas kernels, add_panel(): pl.pallas_call(functools.partial(panel_kernel, shape, layer, kind_at, fin...  8.64 us
    ppermute x3, waiting for transfers between devices, swapped(): return lax.ppermute(value, 'dep', [(0, 1), (1, 0)])  5.54 us
  transfers between devices with their start and end apart: 16, of which 8 were waited for; matrix products, arithmetic and copies ran while one was open for 3% of the time, Pallas kernels for 10%

profile of v12, /device:TPU:1, one launch (start us, length us, event | category | flops | bytes accessed | tf_op | source)
XLA Modules:
  0.0 179.6 jit_solution(16555486457869953980)
XLA Ops:
  6.5 0.7 all-gather.18.cloned.1.call-update
  7.3 0.7 all-gather.20.cloned.1.call-update
  8.1 2.0 %collective-permute-start.2 = (bf16[64,128,128]{2,1,0:T(8,128)(2,1)S(1)}, bf16[64,128,128]{2,1,0:T(8,128)(2,1)}, u32[]{:S(2)}, u32[]{:S(2)}) collective-permute-start(bf16[64,128,128]{2,1,0:T(8,128)(2,1)S(1)} %bitcast.29), channel_id=1, source_target_pairs={{2,4},{4,2},{3,5},{5,3},{10,12},{12,10},{11,13},{13,11},{18,20},{2... | collective-permute-start | bytes 6291464 | tf_op jit(solution)/shard_map/ppermute | solution.py:283
  10.1 6.7 %collective-permute-start.1 = (bf16[64,128,128]{2,1,0:T(8,128)(2,1)S(1)}, bf16[64,128,128]{2,1,0:T(8,128)(2,1)}, u32[]{:S(2)}, u32[]{:S(2)}) collective-permute-start(bf16[64,128,128]{2,1,0:T(8,128)(2,1)S(1)} %bitcast.30), channel_id=1, source_target_pairs={{0,2},{6,4},{1,3},{7,5},{8,10},{14,12},{9,11},{15,13},{16,18},{22,... | collective-permute-start | bytes 6291464 | tf_op jit(solution)/shard_map/ppermute | solution.py:283
  16.8 1.3 collective-permute-start
  18.1 1.3 collective-permute-start.3
  19.6 3.0 %all-gather = s32[2,1,1,7,3,64]{5,2,4,3,1,0:T(1,128)S(1)} all-gather(s32[1,1,1,7,3,64]{5,2,4,3,1,0:T(1,128)S(1)} %copy-done.4), channel_id=2, replica_groups=mesh['grp'=2,'row'=2,'col'=4,'dep'=2] {'dep'}, dimensions={0}, use_global_device_ids=true | all-gather | bytes 16128 | tf_op jit(solution)/shard_map/all_gather | solution.py:290
  23.8 34.9 %collective-permute-done.3.refs_3_ = bf16[56,128,128]{2,1,0:T(8,128)(2,1)} collective-permute-done((bf16[56,128,128]{2,1,0:T(8,128)(2,1)}, bf16[56,128,128]{2,1,0:T(8,128)(2,1)}, u32[]{:S(2)}, u32[]{:S(2)}) %collective-permute-start.3) | collective-permute-done | bytes 1835040 | tf_op jit(solution)/shard_map/ppermute | solution.py:289
  58.7 0.6 collective-permute-done.1.refs_10_
  59.3 5.3 %collective-permute-done.refs_8_ = bf16[64,128,128]{2,1,0:T(8,128)(2,1)} collective-permute-done((bf16[64,128,128]{2,1,0:T(8,128)(2,1)S(1)}, bf16[64,128,128]{2,1,0:T(8,128)(2,1)}, u32[]{:S(2)}, u32[]{:S(2)}) %collective-permute-start) | collective-permute-done | bytes 2097184 | tf_op jit(solution)/shard_map/ppermute | solution.py:283
  66.4 2.1 %collective-permute-start.4 = (bf16[64,128,128]{2,1,0:T(8,128)(2,1)}, bf16[64,128,128]{2,1,0:T(8,128)(2,1)}, u32[]{:S(2)}, u32[]{:S(2)}) collective-permute-start(bf16[64,128,128]{2,1,0:T(8,128)(2,1)} %collective-permute-done.1.refs_10_), channel_id=1, source_target_pairs={{2,4},{4,2},{3,5},{5,3},{10,12},{12,10},{11,13},{13,11},{18,20},{2... | collective-permute-start | bytes 6291464 | tf_op jit(solution)/shard_map/ppermute | solution.py:283
  68.5 1.3 collective-permute-start.6
  69.8 1.3 collective-permute-start.5
  71.1 44.6 %collective-permute-done.6 = bf16[64,128,128]{2,1,0:T(8,128)(2,1)} collective-permute-done((bf16[64,128,128]{2,1,0:T(8,128)(2,1)}, bf16[64,128,128]{2,1,0:T(8,128)(2,1)}, u32[]{:S(2)}, u32[]{:S(2)}) %collective-permute-start.6) | collective-permute-done | bytes 2097184 | tf_op jit(solution)/shard_map/ppermute | solution.py:283
  115.6 1.8 %broadcast_select_fusion = bf16[64,128,128]{2,1,0:T(8,128)(2,1)S(1)} fusion(bf16[64,128,128]{2,1,0:T(8,128)(2,1)} %collective-permute-done.4, bf16[64,128,128]{2,1,0:T(8,128)(2,1)} %collective-permute-done.6, pred[]{:T(512)S(6)} %or.13), kind=kLoop, calls=%fused_computation | loop fusion | flops 1048576 | bytes 6291457 | tf_op jit(solution)/shard_map/jit(_where)/select_n | solution.py:301
  117.5 1.2 fusion.8
  118.6 6.1 %collective-permute-start.8 = (bf16[32,128,128]{2,1,0:T(8,128)(2,1)S(1)}, bf16[32,128,128]{2,1,0:T(8,128)(2,1)}, u32[]{:S(2)}, u32[]{:S(2)}) collective-permute-start(bf16[32,128,128]{2,1,0:T(8,128)(2,1)S(1)} %get-tuple-element.27.refs_15_), channel_id=1, source_target_pairs={{0,1},{1,0},{2,3},{3,2},{4,5},{5,4},{6,7},{7,6},{8,9},{9,8},{10,11... | collective-permute-start | bytes 3145736 | tf_op jit(solution)/shard_map/ppermute | solution.py:231
  124.8 0.7 stack.23.refs_1_.scalars
  125.4 4.7 %collective-permute-done.8.refs_17_ = bf16[32,128,128]{2,1,0:T(8,128)(2,1)} collective-permute-done((bf16[32,128,128]{2,1,0:T(8,128)(2,1)S(1)}, bf16[32,128,128]{2,1,0:T(8,128)(2,1)}, u32[]{:S(2)}, u32[]{:S(2)}) %collective-permute-start.8) | collective-permute-done | bytes 1048608 | tf_op jit(solution)/shard_map/ppermute | solution.py:231
  130.6 14.7 %shard_map.37 = (f32[113,128,128]{2,1,0:T(8,128)S(1)}, bf16[224,128,128]{2,1,0:T(8,128)(2,1)S(1)}) custom-call(s32[896]{0:T(1024)} %fusion.7.refs_0_.packed, s32[7]{0:T(128)} %stack.23.refs_1_.scalars, bf16[56,128,128]{2,1,0:T(8,128)(2,1)} %bitcast.34, bf16[56,128,128]{2,1,0:T(8,128)(2,1)} %collective-permute-done.3.refs_3_, ...), custom_call_target="tpu_custom_call" | custom-call | flops 1 | bytes 1 | tf_op jit(solution)/shard_map/pallas_call | solution.py:156
  145.3 15.2 %collective-permute-done.5.left = bf16[64,128,128]{2,1,0:T(8,128)(2,1)S(1)} collective-permute-done((bf16[64,128,128]{2,1,0:T(8,128)(2,1)}, bf16[64,128,128]{2,1,0:T(8,128)(2,1)S(1)}, u32[]{:S(2)}, u32[]{:S(2)}) %collective-permute-start.5) | collective-permute-done | bytes 2097184 | tf_op jit(solution)/shard_map/ppermute | solution.py:283
  160.5 3.1 %collective-permute-start.9 = (bf16[64,128,128]{2,1,0:T(8,128)(2,1)S(1)}, bf16[64,128,128]{2,1,0:T(8,128)(2,1)S(1)}, u32[]{:S(2)}, u32[]{:S(2)}) collective-permute-start(bf16[64,128,128]{2,1,0:T(8,128)(2,1)S(1)} %collective-permute-done.5.left), channel_id=1, source_target_pairs={{0,1},{1,0},{2,3},{3,2},{4,5},{5,4},{6,7},{7,6},{8,9},{9,8},{10,11... | collective-permute-start | bytes 6291464 | tf_op jit(solution)/shard_map/ppermute | solution.py:231
  163.6 3.3 %shard_map.38.given = f32[113,128,128]{2,1,0:T(8,128)S(1)} custom-call(s32[896]{0:T(1024)S(1)} %copy-done, s32[7]{0:T(128)S(1)} %copy-done.1, bf16[224,128,128]{2,1,0:T(8,128)(2,1)S(1)} %get-tuple-element.23.right, f32[113,128,128]{2,1,0:T(8,128)S(1)} %get-tuple-element.24.given, ...), custom_call_target="tpu_custom_call", output_to_operand_aliasing={{}: (3, {})} | custom-call | flops 1 | bytes 1 | tf_op jit(solution)/shard_map/pallas_call | solution.py:214
  167.3 5.3 %shard_map.39 = (bf16[112,128,128]{2,1,0:T(8,128)(2,1)}, f32[113,128,128]{2,1,0:T(8,128)S(1)}) custom-call(s32[896]{0:T(1024)S(1)} %copy-done, s32[7]{0:T(128)S(1)} %copy-done.1, bf16[224,128,128]{2,1,0:T(8,128)(2,1)S(1)} %get-tuple-element.23.right, f32[113,128,128]{2,1,0:T(8,128)S(1)} %shard_map.38.given, ...), custom_call_target="tpu_custom_call", output_to_operand_aliasing={{1}: (3, {})} | custom-call | flops 1 | bytes 1 | tf_op jit(solution)/shard_map/pallas_call | solution.py:214
  (53 shorter events, 4.1 us)
Async XLA Ops:
  6.5 1.6 copy-start.2
  6.5 13.1 %copy-start.4 = (s32[1,1,1,7,3,64]{5,2,4,3,1,0:T(1,128)S(1)}, s32[1,1,1,7,3,64]{5,2,4,3,1,0:T(1,128)}, u32[]{:S(2)}) copy-start(s32[1,1,1,7,3,64]{5,2,4,3,1,0:T(1,128)} %param.5) | copy-start | bytes 16132
  6.5 118.9 %all-gather.18.cloned.1.call-start = ((), (), s32[]{:S(2)}) async-start(), calls=%async_computation.4 | async-start | bytes 5505024 | tf_op jit(solution)/shard_map/all_gather | solution.py:235
  7.3 118.2 %all-gather.20.cloned.1.call-start = ((), (), s32[]{:S(2)}) async-start(), calls=%async_computation.5 | async-start | bytes 6291456 | tf_op jit(solution)/shard_map/all_gather | solution.py:235
  8.0 122.5 %all-gather.10.cloned.1.call-start = ((), (), s32[]{:S(2)}) async-start(), calls=%async_computation | async-start | bytes 5505024 | tf_op jit(solution)/shard_map/all_gather | solution.py:235
  8.1 50.6 %collective-permute-start.2 = (bf16[64,128,128]{2,1,0:T(8,128)(2,1)S(1)}, bf16[64,128,128]{2,1,0:T(8,128)(2,1)}, u32[]{:S(2)}, u32[]{:S(2)}) collective-permute-start(bf16[64,128,128]{2,1,0:T(8,128)(2,1)S(1)} %bitcast.29), channel_id=1, source_target_pairs={{2,4},{4,2},{3,5},{5,3},{10,12},{12,10},{11,13},{13,11},{18,20},{2... | collective-permute-start | bytes 6291464 | tf_op jit(solution)/shard_map/ppermute | solution.py:283
  10.1 49.2 %collective-permute-start.1 = (bf16[64,128,128]{2,1,0:T(8,128)(2,1)S(1)}, bf16[64,128,128]{2,1,0:T(8,128)(2,1)}, u32[]{:S(2)}, u32[]{:S(2)}) collective-permute-start(bf16[64,128,128]{2,1,0:T(8,128)(2,1)S(1)} %bitcast.30), channel_id=1, source_target_pairs={{0,2},{6,4},{1,3},{7,5},{8,10},{14,12},{9,11},{15,13},{16,18},{22,... | collective-permute-start | bytes 6291464 | tf_op jit(solution)/shard_map/ppermute | solution.py:283
  16.8 47.9 %collective-permute-start = (bf16[64,128,128]{2,1,0:T(8,128)(2,1)S(1)}, bf16[64,128,128]{2,1,0:T(8,128)(2,1)}, u32[]{:S(2)}, u32[]{:S(2)}) collective-permute-start(bf16[64,128,128]{2,1,0:T(8,128)(2,1)S(1)} %bitcast.31), channel_id=1, source_target_pairs={{4,6},{2,0},{5,7},{3,1},{12,14},{10,8},{13,15},{11,9},{20,22},{18,... | collective-permute-start | bytes 6291464 | tf_op jit(solution)/shard_map/ppermute | solution.py:283
  18.1 40.6 %collective-permute-start.3 = (bf16[56,128,128]{2,1,0:T(8,128)(2,1)}, bf16[56,128,128]{2,1,0:T(8,128)(2,1)}, u32[]{:S(2)}, u32[]{:S(2)}) collective-permute-start(bf16[56,128,128]{2,1,0:T(8,128)(2,1)} %bitcast.33), channel_id=1, source_target_pairs={{0,8},{8,0},{1,9},{9,1},{2,10},{10,2},{3,11},{11,3},{4,12},{12,4},... | collective-permute-start | bytes 5505032 | tf_op jit(solution)/shard_map/ppermute | solution.py:289
  64.7 65.8 %all-gather.12.cloned.1.call-start = ((), (), s32[]{:S(2)}) async-start(), calls=%async_computation.1 | async-start | bytes 6291456 | tf_op jit(solution)/shard_map/all_gather | solution.py:235
  65.2 65.3 %all-gather.14.cloned.1.call-start = ((), (), s32[]{:S(2)}) async-start(), calls=%async_computation.2 | async-start | bytes 6291456 | tf_op jit(solution)/shard_map/all_gather | solution.py:235
  65.8 64.7 %all-gather.16.cloned.1.call-start = ((), (), s32[]{:S(2)}) async-start(), calls=%async_computation.3 | async-start | bytes 6291456 | tf_op jit(solution)/shard_map/all_gather | solution.py:235
  66.4 3.4 %collective-permute-start.4 = (bf16[64,128,128]{2,1,0:T(8,128)(2,1)}, bf16[64,128,128]{2,1,0:T(8,128)(2,1)}, u32[]{:S(2)}, u32[]{:S(2)}) collective-permute-start(bf16[64,128,128]{2,1,0:T(8,128)(2,1)} %collective-permute-done.1.refs_10_), channel_id=1, source_target_pairs={{2,4},{4,2},{3,5},{5,3},{10,12},{12,10},{11,13},{13,11},{18,20},{2... | collective-permute-start | bytes 6291464 | tf_op jit(solution)/shard_map/ppermute | solution.py:283
  68.5 47.2 %collective-permute-start.6 = (bf16[64,128,128]{2,1,0:T(8,128)(2,1)}, bf16[64,128,128]{2,1,0:T(8,128)(2,1)}, u32[]{:S(2)}, u32[]{:S(2)}) collective-permute-start(bf16[64,128,128]{2,1,0:T(8,128)(2,1)} %collective-permute-done.2.refs_12_), channel_id=1, source_target_pairs={{4,6},{2,0},{5,7},{3,1},{12,14},{10,8},{13,15},{11,9},{20,22},{18,... | collective-permute-start | bytes 6291464 | tf_op jit(solution)/shard_map/ppermute | solution.py:283
  69.8 90.7 %collective-permute-start.5 = (bf16[64,128,128]{2,1,0:T(8,128)(2,1)}, bf16[64,128,128]{2,1,0:T(8,128)(2,1)S(1)}, u32[]{:S(2)}, u32[]{:S(2)}) collective-permute-start(bf16[64,128,128]{2,1,0:T(8,128)(2,1)} %collective-permute-done.4), channel_id=1, source_target_pairs={{4,6},{2,0},{5,7},{3,1},{12,14},{10,8},{13,15},{11,9},{20,22},{18,... | collective-permute-start | bytes 6291464 | tf_op jit(solution)/shard_map/ppermute | solution.py:283
  118.6 11.9 %copy-start.3 = (bf16[32,128,128]{2,1,0:T(8,128)(2,1)}, bf16[32,128,128]{2,1,0:T(8,128)(2,1)S(1)}, u32[]{:S(2)}) copy-start(bf16[32,128,128]{2,1,0:T(8,128)(2,1)S(1)} %get-tuple-element.27.refs_15_) | copy-start | bytes 3145732
  118.6 11.5 %collective-permute-start.8 = (bf16[32,128,128]{2,1,0:T(8,128)(2,1)S(1)}, bf16[32,128,128]{2,1,0:T(8,128)(2,1)}, u32[]{:S(2)}, u32[]{:S(2)}) collective-permute-start(bf16[32,128,128]{2,1,0:T(8,128)(2,1)S(1)} %get-tuple-element.27.refs_15_), channel_id=1, source_target_pairs={{0,1},{1,0},{2,3},{3,2},{4,5},{5,4},{6,7},{7,6},{8,9},{9,8},{10,11... | collective-permute-start | bytes 3145736 | tf_op jit(solution)/shard_map/ppermute | solution.py:231
  124.8 5.7 %collective-permute-start.7 = (bf16[32,128,128]{2,1,0:T(8,128)(2,1)}, bf16[32,128,128]{2,1,0:T(8,128)(2,1)}, u32[]{:S(2)}, u32[]{:S(2)}) collective-permute-start(bf16[32,128,128]{2,1,0:T(8,128)(2,1)} %get-tuple-element.28.refs_14_), channel_id=1, source_target_pairs={{0,1},{1,0},{2,3},{3,2},{4,5},{5,4},{6,7},{7,6},{8,9},{9,8},{10,11... | collective-permute-start | bytes 3145736 | tf_op jit(solution)/shard_map/ppermute | solution.py:231
  130.5 33.0 %copy-start = (s32[896]{0:T(1024)S(1)}, s32[896]{0:T(1024)}, u32[]{:S(2)}) copy-start(s32[896]{0:T(1024)} %fusion.7.refs_0_.packed) | copy-start | bytes 10756
  130.6 33.0 %copy-start.1 = (s32[7]{0:T(128)S(1)}, s32[7]{0:T(128)}, u32[]{:S(2)}) copy-start(s32[7]{0:T(128)} %stack.23.refs_1_.scalars) | copy-start | bytes 88
  160.5 6.9 %collective-permute-start.9 = (bf16[64,128,128]{2,1,0:T(8,128)(2,1)S(1)}, bf16[64,128,128]{2,1,0:T(8,128)(2,1)S(1)}, u32[]{:S(2)}, u32[]{:S(2)}) collective-permute-start(bf16[64,128,128]{2,1,0:T(8,128)(2,1)S(1)} %collective-permute-done.5.left), channel_id=1, source_target_pairs={{0,1},{1,0},{2,3},{3,2},{4,5},{5,4},{6,7},{7,6},{8,9},{9,8},{10,11... | collective-permute-start | bytes 6291464 | tf_op jit(solution)/shard_map/ppermute | solution.py:231
Sparse Core Ops, SparseCore 0:
  8.9 15.3 all-gather.17
  25.9 14.8 all-gather.19
  64.8 13.7 all-gather.9
  80.0 14.8 all-gather.11
  96.2 14.8 all-gather.13
  112.5 17.8 all-gather.15

commit v13 on v12

--- a/solution.py
+++ b/solution.py
@@ -54,14 +54,15 @@
     lax.fori_loop(0, (count + UNROLL - 1) // UNROLL, several, jnp.int32(0))
 
 
-def sum_kernel(panels, rights, givens, saved, resident, shape, layers, operand_count, layer_at, *refs):
+def sum_kernel(panels, rights, givens, saved, mode, shape, layers, operand_count, layer_at, *refs):
     packed, classes, refs = refs[0], refs[1], refs[2:]
     operands, refs = refs[:operand_count], refs[operand_count:]
-    if resident:
-        (work, right), (left, todo, sems) = refs[:2], refs[2:]
+    out_count = max(len(saved), 1)
+    outs, refs = refs[:out_count], refs[out_count:]
+    if mode == "split":
+        (right, kept), (work, left, todo, sems) = refs[:2], refs[2:]
     else:
-        out_count = max(len(saved), 1)
-        outs, (work, left, right, todo, sems) = refs[:out_count], refs[out_count:]
+        work, left, right, todo, sems = refs
     spare = work.shape[0] - 1
     other = 1 - classes[layer_at]
     copies = []
@@ -99,22 +100,24 @@
     for copy, when in copies:
         copy.wait() if when is None else pl.when(when)(copy.wait)
     add_chosen(todo, count, left, right, work)
-    if resident:
+    if not saved:
+        outs[0][...] = work[:spare].astype(outs[0].dtype)
         return
-    if saved:
-        start, copies = 0, []
-        for out, size in zip(outs, saved):
-            copies.append(pltpu.make_async_copy(work.at[pl.ds(start, size)], out, sems.at[len(copies)]))
-            start += size
-        for copy in copies:
-            copy.start()
-        for copy in copies:
-            copy.wait()
-    else:
-        outs[0][...] = work[:spare].astype(outs[0].dtype)
-
-
-def product_sums(packed, scalars, shape, layers, panels, rights, givens, result_slots, saved, resident=False):
+    start, copies, targets = 0, [], list(outs)
+    if mode == "split":
+        kept[kept.shape[0] - 1] = jnp.zeros(kept.shape[1:], kept.dtype)
+        targets.insert(0, kept.at[pl.ds(0, kept.shape[0] - 1)])
+    for out in targets:
+        size = out.shape[0]
+        copies.append(pltpu.make_async_copy(work.at[pl.ds(start, size)], out, sems.at[len(copies)]))
+        start += size
+    for copy in copies:
+        copy.start()
+    for copy in copies:
+        copy.wait()
+
+
+def product_sums(packed, scalars, shape, layers, panels, rights, givens, result_slots, saved, mode="whole"):
     step_count, columns, slots = shape
     rows, width = rights[0][0].shape[1:]
     operands = []
@@ -140,19 +143,21 @@
     assert right_slots <= 1024 and left_slots <= 1024 and result_slots < 1024 and slots % 8 == 0
     assert all(sum(size for _, size, _ in pieces) == layers * slots for pieces in panel_spans)
     anywhere = pl.BlockSpec(memory_space=pl.ANY)
-    in_scalar = pl.BlockSpec(memory_space=pltpu.SMEM)
+    in_scalar, in_vector = pl.BlockSpec(memory_space=pltpu.SMEM), pl.BlockSpec(memory_space=pltpu.VMEM)
     copy_count = len(rights) + sum(len(pieces) for pieces in panels) + len(givens) + len(saved) + 1
-    if saved:
-        out_shape = [jax.ShapeDtypeStruct((size, rows, width), jnp.float32) for size in saved]
-    else:
-        out_shape = [jax.ShapeDtypeStruct((result_slots, rows, width), jnp.bfloat16)]
     scratch = [
         pltpu.VMEM((result_slots + 1, rows, width), jnp.float32),
         pltpu.VMEM((left_slots, rows, width), jnp.bfloat16),
         pltpu.VMEM((right_slots, width, width), jnp.bfloat16),
     ]
-    if resident:
-        out_shape, scratch = [scratch[0], scratch[2]], [scratch[1]]
+    if saved:
+        out_shape = [jax.ShapeDtypeStruct((size, rows, width), jnp.float32) for size in saved]
+    else:
+        out_shape = [jax.ShapeDtypeStruct((result_slots, rows, width), jnp.bfloat16)]
+    out_specs = [anywhere if saved else in_vector] * len(out_shape)
+    if mode == "split":
+        out_shape += [scratch.pop(), pltpu.VMEM((result_slots - sum(saved) + 1, rows, width), jnp.float32)]
+        out_specs += [in_vector] * 2
     return pl.pallas_call(
         functools.partial(
             sum_kernel,
@@ -160,7 +165,7 @@
             right_spans,
             given_spans,
             saved,
-            resident,
+            mode,
             shape,
             layers,
             len(operands),
@@ -168,15 +173,37 @@
         ),
         out_shape=out_shape,
         in_specs=[in_scalar, in_scalar] + [anywhere] * len(operands),
-        out_specs=[anywhere if saved else pl.BlockSpec(memory_space=pltpu.VMEM)] * len(out_shape),
+        out_specs=out_specs,
         scratch_shapes=scratch
         + [
             pltpu.SMEM((len(panels) * -(-step_count // columns) * layers * slots + UNROLL,), jnp.int32),
             pltpu.SemaphoreType.DMA((copy_count,)),
         ],
-        compiler_params=pltpu.CompilerParams(vmem_limit_bytes=(40 if resident else 56) << 20),
+        compiler_params=pltpu.CompilerParams(vmem_limit_bytes=(34 if mode == "split" else 56) << 20),
         cost_estimate=pl.CostEstimate(flops=1, bytes_accessed=1, transcendentals=0),
     )(packed, scalars, *operands)
+
+
+def received_kernel(given, *refs):
+    del given
+    work, start = refs[-1], 0
+    for piece in refs[:-1]:
+        span = pl.ds(start, piece.shape[0])
+        work[span] += piece[...]
+        start += piece.shape[0]
+
+
+def add_received(given, pieces):
+    in_vector = pl.BlockSpec(memory_space=pltpu.VMEM)
+    return pl.pallas_call(
+        received_kernel,
+        out_shape=pltpu.VMEM(given.shape, given.dtype),
+        in_specs=[in_vector] * (1 + len(pieces)),
+        out_specs=in_vector,
+        input_output_aliases={0: 0},
+        compiler_params=pltpu.CompilerParams(vmem_limit_bytes=12 << 20),
+        cost_estimate=pl.CostEstimate(flops=1, bytes_accessed=1, transcendentals=0),
+    )(given, *pieces)
 
 
 def panel_kernel(shape, layer, kind_at, finish, packed, scalars, right, given, left, *refs):
@@ -236,7 +263,6 @@
 
 
 def kept_products(both, layer, half, right_slot):
-    both = jnp.where(layer > 0, both[::-1], both)
     slots = both.shape[3]
     result = both[:, :, 2] - layer * half
     wanted = (result >= 0) & (result < half)
@@ -245,12 +271,19 @@
     return jnp.where(wanted, packed, -1).reshape(-1)
 
 
+def layer_products(step_lists, layer, half, right_slot):
+    result = step_lists[:, 2]
+    turned = jnp.where(result < half, result + layer * half, result - layer * half)
+    packed = right_slot(step_lists[:, 1], 0) << 20 | step_lists[:, 0] << 10 | turned
+    return jnp.where(result < 2 * half, packed, -1).reshape(-1)
+
+
 def ring(left_blocks, right_blocks, triples, half):
     own, right_own, step_lists = left_blocks[0, 0, 0], right_blocks[0, 0, 0], triples[0, 0, 0]
     columns, layer = lax.axis_size("col"), lax.axis_index("dep")
     gathered = lax.all_gather(right_own, "row", axis=0, tiled=True)
     right_slots = gathered.shape[0]
-    both = lax.all_gather(step_lists, "dep")
+    both = jnp.stack([step_lists, swapped(step_lists)])
     packed = kept_products(both, layer, half, lambda slot, layers: layers * right_slots + slot)
     rights = [(gathered, False), (swapped(gathered), False)]
     shape = (step_lists.shape[0], columns, own.shape[0])
@@ -287,31 +320,28 @@
 
     outer_one, inward_one, across_one = hop(own, outward), hop(own, inward), hop(own, across)
     met = lax.ppermute(right_own, "row", [(0, 1), (1, 0)])
-    kept = kept_products(lax.all_gather(step_lists, "dep"), layer, half, right_slot)
-    right_pair, own_pair = paired(right_own), paired(own)
-
-    outer_one, inward_one, across_one, met, kept = fence((outer_one, inward_one, across_one, met, kept))
+    listed = layer_products(step_lists, layer, half, right_slot)
+    classes = [0, jnp.where(inner, jnp.where(low, 1, 3), -1), jnp.where(inner, jnp.where(low, 3, 1), -1)]
+    classes += [jnp.where(inner, -1, jnp.where(low, 1, 3)), jnp.where(inner, 2, -1), jnp.where(inner, -1, 2)]
+    scalars = scalar_list(*classes, layer, jnp.where(inner, -1, jnp.where(low, 3, 1)))
+
+    across_one, inward_one, outer_one, met, listed, scalars = fence(
+        (across_one, inward_one, outer_one, met, listed, scalars)
+    )
     outer_two, across_two = hop(across_one, outward), hop(inward_one, across)
-    met_pair, inward_pair, across_pair, outer_pair = [
-        paired(value) for value in (met, inward_one, across_one, outer_one)
-    ]
-
-    across_two = fence(across_two)
+    right_other, met_other = swapped(right_own), swapped(met)
+    both = jnp.stack([step_lists, swapped(step_lists)])
+    kept = kept_products(both, layer, half, right_slot)
+
+    across_two, right_other, met_other, kept = fence((across_two, right_other, met_other, kept))
     outer_three = hop(across_two, outward)
-    two = jnp.where(inner, across_two, outer_two)
-    two = [two[: slots // 2], two[slots // 2 :]]
-    rights = [(right_own, False), (met, False), (right_pair, True), (met_pair, True)]
-    panels = [
-        [(own, False), (own_pair, True)],
-        [(outer_one, False), (outer_pair, True)],
-        [(inward_one, False), (inward_pair, True)],
-        [(across_one, False), (across_pair, True)],
-        [(piece, False) for piece in two] + [(swapped(piece), False) for piece in two],
-    ]
-    classes = [0, jnp.where(inner, -1, jnp.where(low, 1, 3)), jnp.where(inner, jnp.where(low, 3, 1), -1)]
-    classes += [jnp.where(inner, jnp.where(low, 1, 3), -1), 2]
-    scalars = scalar_list(*classes, layer, jnp.where(inner, -1, jnp.where(low, 3, 1)))
-    total, right = product_sums(kept, scalars, shape, 2, panels, rights, [], half, [], True)
+    panels = [[(value, False)] for value in (own, across_one, inward_one, outer_one, across_two, outer_two)]
+    rights = [(value, False) for value in (right_own, met, right_other, met_other)]
+    saved = [half // PARTS] * (PARTS - 1) + [half - half // PARTS * (PARTS - 1)]
+    *parts, right, total = product_sums(
+        listed, scalars, shape, 1, panels, rights, [], 2 * half, saved, "split"
+    )
+    total = add_received(total, [swapped(part) for part in parts])
 
     outer_three, total, right = fence((outer_three, total, right))
     kind_at = len(classes) + 1

time: 180 us -> 163 us (0.906)
  between operations: 13.6 us -> 0.09 us
  blocking collectives: 3 us -> 0 us
  other arithmetic: 2.48 us -> 0.08 us
  starting transfers between devices: 25.3 us -> 27.2 us
  Pallas kernels: 23.3 us -> 25.1 us
    ppermute x6, waiting for transfers between devices: 65.7 us -> 53.9 us  [hop(): return lax.ppermute(value, 'col', pairs)]
    ppermute x3 -> x8, waiting for transfers between devices: 5.54 us -> 16.4 us  [swapped(): return lax.ppermute(value, 'dep', [(0, 1), (1, 0)])]
    ppermute x1, waiting for transfers between devices: 34.9 us -> 38.1 us  [line(): met = lax.ppermute(right_own, 'row', [(0, 1), (1, 0)])]
    unnamed x6 -> x0, waiting for transfers between devices: 3 us -> none
    all_gather x1 -> x0, blocking collectives: 3 us -> none  [line(): lax.all_gather(step_lists, 'dep')]
    ppermute x3 -> x8, starting transfers between devices: 9.22 us -> 11.5 us  [swapped(): return lax.ppermute(value, 'dep', [(0, 1), (1, 0)])]
    select_n x2 -> x1, other arithmetic: 1.83 us -> 0.01 us  [layer_products(): return jnp.where(result < 2 * half, packed, -1).reshape(-1)]
  transfers between devices with their start and end apart: 16 -> 15, of which waited for: 8 -> 11; matrix products, arithmetic and copies ran while one was open for 3% -> 1% of each run, Pallas kernels for 10% -> 12%
where the time goes in v13:
time: 163 us
  waiting for transfers between devices  108 us (66%)
  starting transfers between devices  27.2 us (17%)
  Pallas kernels  25.1 us (15%)
  local copies, waits for them, and re-layouts  1.92 us (1%)
    ppermute x6, waiting for transfers between devices, hop(): return lax.ppermute(value, 'col', pairs)  53.9 us
    ppermute x1, waiting for transfers between devices, line(): met = lax.ppermute(right_own, 'row', [(0, 1), (1, 0)])  38.1 us
    ppermute x8, waiting for transfers between devices, swapped(): return lax.ppermute(value, 'dep', [(0, 1), (1, 0)])  16.4 us
    pallas_call x1, Pallas kernels, product_sums(): pl.pallas_call(functools.partial(sum_kernel, panel_spans, right_spans, gi...  15.7 us
    ppermute x6, starting transfers between devices, hop(): return lax.ppermute(value, 'col', pairs)  14.4 us
    ppermute x8, starting transfers between devices, swapped(): return lax.ppermute(value, 'dep', [(0, 1), (1, 0)])  11.5 us
    pallas_call x2, Pallas kernels, add_panel(): pl.pallas_call(functools.partial(panel_kernel, shape, layer, kind_at, fin...  8.66 us
  transfers between devices with their start and end apart: 15, of which 11 were waited for; matrix products, arithmetic and copies ran while one was open for 1% of the time, Pallas kernels for 12%

profile of v13, /device:TPU:1, one launch (start us, length us, event | category | flops | bytes accessed | tf_op | source)
XLA Modules:
  0.0 162.8 jit_solution(3309862053357858304)
XLA Ops:
  0.0 0.8 collective-permute-start
  0.8 7.8 %collective-permute-start.1 = (bf16[64,128,128]{2,1,0:T(8,128)(2,1)}, bf16[64,128,128]{2,1,0:T(8,128)(2,1)}, u32[]{:S(2)}, u32[]{:S(2)}) collective-permute-start(bf16[64,128,128]{2,1,0:T(8,128)(2,1)} %bitcast.39), channel_id=1, source_target_pairs={{0,2},{6,4},{1,3},{7,5},{8,10},{14,12},{9,11},{15,13},{16,18},{22,... | collective-permute-start | bytes 6291464 | tf_op jit(solution)/shard_map/ppermute | solution.py:316
  8.6 1.3 collective-permute-start.2
  9.9 1.3 collective-permute-start.3
  12.5 38.1 %collective-permute-done.3.refs_3_ = bf16[56,128,128]{2,1,0:T(8,128)(2,1)} collective-permute-done((bf16[56,128,128]{2,1,0:T(8,128)(2,1)}, bf16[56,128,128]{2,1,0:T(8,128)(2,1)}, u32[]{:S(2)}, u32[]{:S(2)}) %collective-permute-start.3) | collective-permute-done | bytes 1835040 | tf_op jit(solution)/shard_map/ppermute | solution.py:322
  50.5 1.0 collective-permute-done.1.refs_8_
  51.5 5.1 %collective-permute-done.2.refs_9_ = bf16[64,128,128]{2,1,0:T(8,128)(2,1)} collective-permute-done((bf16[64,128,128]{2,1,0:T(8,128)(2,1)}, bf16[64,128,128]{2,1,0:T(8,128)(2,1)}, u32[]{:S(2)}, u32[]{:S(2)}) %collective-permute-start.2) | collective-permute-done | bytes 2097184 | tf_op jit(solution)/shard_map/ppermute | solution.py:316
  56.7 2.0 %collective-permute-start.4 = (bf16[64,128,128]{2,1,0:T(8,128)(2,1)}, bf16[64,128,128]{2,1,0:T(8,128)(2,1)}, u32[]{:S(2)}, u32[]{:S(2)}) collective-permute-start(bf16[64,128,128]{2,1,0:T(8,128)(2,1)} %collective-permute-done.1.refs_8_), channel_id=1, source_target_pairs={{2,4},{4,2},{3,5},{5,3},{10,12},{12,10},{11,13},{13,11},{18,20},{2... | collective-permute-start | bytes 6291464 | tf_op jit(solution)/shard_map/ppermute | solution.py:316
  58.7 1.3 collective-permute-start.9
  60.0 2.2 %collective-permute-start.5 = (bf16[56,128,128]{2,1,0:T(8,128)(2,1)}, bf16[56,128,128]{2,1,0:T(8,128)(2,1)}, u32[]{:S(2)}, u32[]{:S(2)}) collective-permute-start(bf16[56,128,128]{2,1,0:T(8,128)(2,1)} %bitcast.43), channel_id=1, source_target_pairs={{0,1},{1,0},{2,3},{3,2},{4,5},{5,4},{6,7},{7,6},{8,9},{9,8},{10,11... | collective-permute-start | bytes 5505032 | tf_op jit(solution)/shard_map/ppermute | solution.py:258
  63.0 2.6 %collective-permute-done.7 = s32[7,3,64]{2,0,1:T(8,128)S(1)} collective-permute-done((s32[7,3,64]{2,0,1:T(8,128)S(1)}, s32[7,3,64]{2,0,1:T(8,128)S(1)}, u32[]{:S(2)}, u32[]{:S(2)}) %collective-permute-start.7) | collective-permute-done | bytes 5408 | tf_op jit(solution)/shard_map/ppermute | solution.py:258
  66.1 2.5 %collective-permute-done.6.refs_5_ = bf16[56,128,128]{2,1,0:T(8,128)(2,1)} collective-permute-done((bf16[56,128,128]{2,1,0:T(8,128)(2,1)}, bf16[56,128,128]{2,1,0:T(8,128)(2,1)}, u32[]{:S(2)}, u32[]{:S(2)}) %collective-permute-start.6) | collective-permute-done | bytes 1835040 | tf_op jit(solution)/shard_map/ppermute | solution.py:258
  68.6 1.3 collective-permute-start.8
  69.9 35.7 %collective-permute-done.9.refs_11_ = bf16[64,128,128]{2,1,0:T(8,128)(2,1)} collective-permute-done((bf16[64,128,128]{2,1,0:T(8,128)(2,1)S(1)}, bf16[64,128,128]{2,1,0:T(8,128)(2,1)}, u32[]{:S(2)}, u32[]{:S(2)}) %collective-permute-start.9) | collective-permute-done | bytes 2097184 | tf_op jit(solution)/shard_map/ppermute | solution.py:316
  105.6 15.7 %shard_map.37 = (f32[28,128,128]{2,1,0:T(8,128)S(1)}, f32[28,128,128]{2,1,0:T(8,128)S(1)}, f32[28,128,128]{2,1,0:T(8,128)S(1)}, f32[28,128,128]{2,1,0:T(8,128)},...) custom-call(s32[448]{0:T(512)S(1)} %fusion.17.refs_0_, s32[8]{0:T(128)S(1)} %stack.37.refs_1_.scalars, ...), custom_call_target="tpu_custom_call" | custom-call | flops 1 | bytes 1 | tf_op jit(solution)/shard_map/pallas_call | solution.py:161
  121.3 5.5 %collective-permute-start.10 = (f32[28,128,128]{2,1,0:T(8,128)S(1)}, f32[28,128,128]{2,1,0:T(8,128)S(1)}, u32[]{:S(2)}, u32[]{:S(2)}) collective-permute-start(f32[28,128,128]{2,1,0:T(8,128)S(1)} %get-tuple-element.36), channel_id=1, source_target_pairs={{0,1},{1,0},{2,3},{3,2},{4,5},{5,4},{6,7},{7,6},{8,9},{9,8},{10,11... | collective-permute-start | bytes 5505032 | tf_op jit(solution)/shard_map/ppermute | solution.py:258
  127.4 2.8 %collective-permute-done.10.refs_0_ = f32[28,128,128]{2,1,0:T(8,128)S(1)} collective-permute-done((f32[28,128,128]{2,1,0:T(8,128)S(1)}, f32[28,128,128]{2,1,0:T(8,128)S(1)}, u32[]{:S(2)}, u32[]{:S(2)}) %collective-permute-start.10) | collective-permute-done | bytes 1835040 | tf_op jit(solution)/shard_map/ppermute | solution.py:258
  130.2 5.2 %collective-permute-done.11.refs_1_ = f32[28,128,128]{2,1,0:T(8,128)S(1)} collective-permute-done((f32[28,128,128]{2,1,0:T(8,128)S(1)}, f32[28,128,128]{2,1,0:T(8,128)S(1)}, u32[]{:S(2)}, u32[]{:S(2)}) %collective-permute-start.11) | collective-permute-done | bytes 1835040 | tf_op jit(solution)/shard_map/ppermute | solution.py:258
  135.5 2.6 %collective-permute-done.12.refs_2_ = f32[28,128,128]{2,1,0:T(8,128)S(1)} collective-permute-done((f32[28,128,128]{2,1,0:T(8,128)S(1)}, f32[28,128,128]{2,1,0:T(8,128)S(1)}, u32[]{:S(2)}, u32[]{:S(2)}) %collective-permute-start.12) | collective-permute-done | bytes 1835040 | tf_op jit(solution)/shard_map/ppermute | solution.py:258
  138.1 0.7 shard_map.38.given
  138.8 12.0 %collective-permute-done.8.left = bf16[64,128,128]{2,1,0:T(8,128)(2,1)S(1)} collective-permute-done((bf16[64,128,128]{2,1,0:T(8,128)(2,1)}, bf16[64,128,128]{2,1,0:T(8,128)(2,1)S(1)}, u32[]{:S(2)}, u32[]{:S(2)}) %collective-permute-start.8) | collective-permute-done | bytes 2097184 | tf_op jit(solution)/shard_map/ppermute | solution.py:316
  150.8 2.7 %collective-permute-start.14 = (bf16[64,128,128]{2,1,0:T(8,128)(2,1)S(1)}, bf16[64,128,128]{2,1,0:T(8,128)(2,1)S(1)}, u32[]{:S(2)}, u32[]{:S(2)}) collective-permute-start(bf16[64,128,128]{2,1,0:T(8,128)(2,1)S(1)} %collective-permute-done.8.left), channel_id=1, source_target_pairs={{0,1},{1,0},{2,3},{3,2},{4,5},{5,4},{6,7},{7,6},{8,9},{9,8},{10,11... | collective-permute-start | bytes 6291464 | tf_op jit(solution)/shard_map/ppermute | solution.py:258
  153.5 3.2 %shard_map.39.given = f32[113,128,128]{2,1,0:T(8,128)S(1)} custom-call(s32[896]{0:T(1024)S(1)} %fusion.10.packed, s32[8]{0:T(128)S(1)} %stack.37.refs_1_.scalars, bf16[224,128,128]{2,1,0:T(8,128)(2,1)S(1)} %get-tuple-element.41.right, f32[113,128,128]{2,1,0:T(8,128)S(1)} %shard_map.38.given, ...), custom_call_target="tpu_custom_call", output_to_operand_aliasing={{}: (3, {})} | custom-call | flops 1 | bytes 1 | tf_op jit(solution)/shard_map/pallas_call | solution.py:241
  157.3 5.4 %shard_map.40 = (bf16[112,128,128]{2,1,0:T(8,128)(2,1)}, f32[113,128,128]{2,1,0:T(8,128)S(1)}) custom-call(s32[896]{0:T(1024)S(1)} %fusion.10.packed, s32[8]{0:T(128)S(1)} %stack.37.refs_1_.scalars, bf16[224,128,128]{2,1,0:T(8,128)(2,1)S(1)} %get-tuple-element.41.right, f32[113,128,128]{2,1,0:T(8,128)S(1)} %shard_map.39.given, ...), custom_call_target="tpu_custom_call", output_to_operand_aliasing={{1}: (3, {})} | custom-call | flops 1 | bytes 1 | tf_op jit(solution)/shard_map/pallas_call | solution.py:241
  (37 shorter events, 3.6 us)
Async XLA Ops:
  0.0 50.5 %collective-permute-start = (bf16[64,128,128]{2,1,0:T(8,128)(2,1)}, bf16[64,128,128]{2,1,0:T(8,128)(2,1)S(1)}, u32[]{:S(2)}, u32[]{:S(2)}) collective-permute-start(bf16[64,128,128]{2,1,0:T(8,128)(2,1)} %bitcast.38), channel_id=1, source_target_pairs={{2,4},{4,2},{3,5},{5,3},{10,12},{12,10},{11,13},{13,11},{18,20},{2... | collective-permute-start | bytes 6291464 | tf_op jit(solution)/shard_map/ppermute | solution.py:316
  0.8 50.7 %collective-permute-start.1 = (bf16[64,128,128]{2,1,0:T(8,128)(2,1)}, bf16[64,128,128]{2,1,0:T(8,128)(2,1)}, u32[]{:S(2)}, u32[]{:S(2)}) collective-permute-start(bf16[64,128,128]{2,1,0:T(8,128)(2,1)} %bitcast.39), channel_id=1, source_target_pairs={{0,2},{6,4},{1,3},{7,5},{8,10},{14,12},{9,11},{15,13},{16,18},{22,... | collective-permute-start | bytes 6291464 | tf_op jit(solution)/shard_map/ppermute | solution.py:316
  8.6 48.1 %collective-permute-start.2 = (bf16[64,128,128]{2,1,0:T(8,128)(2,1)}, bf16[64,128,128]{2,1,0:T(8,128)(2,1)}, u32[]{:S(2)}, u32[]{:S(2)}) collective-permute-start(bf16[64,128,128]{2,1,0:T(8,128)(2,1)} %bitcast.40), channel_id=1, source_target_pairs={{4,6},{2,0},{5,7},{3,1},{12,14},{10,8},{13,15},{11,9},{20,22},{18,... | collective-permute-start | bytes 6291464 | tf_op jit(solution)/shard_map/ppermute | solution.py:316
  9.9 40.6 %collective-permute-start.3 = (bf16[56,128,128]{2,1,0:T(8,128)(2,1)}, bf16[56,128,128]{2,1,0:T(8,128)(2,1)}, u32[]{:S(2)}, u32[]{:S(2)}) collective-permute-start(bf16[56,128,128]{2,1,0:T(8,128)(2,1)} %bitcast.42), channel_id=1, source_target_pairs={{0,8},{8,0},{1,9},{9,1},{2,10},{10,2},{3,11},{11,3},{4,12},{12,4},... | collective-permute-start | bytes 5505032 | tf_op jit(solution)/shard_map/ppermute | solution.py:322
  50.5 55.1 %copy-start = (bf16[64,128,128]{2,1,0:T(8,128)(2,1)}, bf16[64,128,128]{2,1,0:T(8,128)(2,1)S(1)}, u32[]{:S(2)}) copy-start(bf16[64,128,128]{2,1,0:T(8,128)(2,1)S(1)} %collective-permute-done.refs_7_) | copy-start | bytes 6291460
  56.7 11.9 %collective-permute-start.4 = (bf16[64,128,128]{2,1,0:T(8,128)(2,1)}, bf16[64,128,128]{2,1,0:T(8,128)(2,1)}, u32[]{:S(2)}, u32[]{:S(2)}) collective-permute-start(bf16[64,128,128]{2,1,0:T(8,128)(2,1)} %collective-permute-done.1.refs_8_), channel_id=1, source_target_pairs={{2,4},{4,2},{3,5},{5,3},{10,12},{12,10},{11,13},{13,11},{18,20},{2... | collective-permute-start | bytes 6291464 | tf_op jit(solution)/shard_map/ppermute | solution.py:316
  58.7 47.0 %collective-permute-start.9 = (bf16[64,128,128]{2,1,0:T(8,128)(2,1)S(1)}, bf16[64,128,128]{2,1,0:T(8,128)(2,1)}, u32[]{:S(2)}, u32[]{:S(2)}) collective-permute-start(bf16[64,128,128]{2,1,0:T(8,128)(2,1)S(1)} %collective-permute-done.refs_7_), channel_id=1, source_target_pairs={{4,6},{2,0},{5,7},{3,1},{12,14},{10,8},{13,15},{11,9},{20,22},{18,... | collective-permute-start | bytes 6291464 | tf_op jit(solution)/shard_map/ppermute | solution.py:316
  60.0 6.1 %collective-permute-start.5 = (bf16[56,128,128]{2,1,0:T(8,128)(2,1)}, bf16[56,128,128]{2,1,0:T(8,128)(2,1)}, u32[]{:S(2)}, u32[]{:S(2)}) collective-permute-start(bf16[56,128,128]{2,1,0:T(8,128)(2,1)} %bitcast.43), channel_id=1, source_target_pairs={{0,1},{1,0},{2,3},{3,2},{4,5},{5,4},{6,7},{7,6},{8,9},{9,8},{10,11... | collective-permute-start | bytes 5505032 | tf_op jit(solution)/shard_map/ppermute | solution.py:258
  62.2 6.4 %collective-permute-start.6 = (bf16[56,128,128]{2,1,0:T(8,128)(2,1)}, bf16[56,128,128]{2,1,0:T(8,128)(2,1)}, u32[]{:S(2)}, u32[]{:S(2)}) collective-permute-start(bf16[56,128,128]{2,1,0:T(8,128)(2,1)} %collective-permute-done.3.refs_3_), channel_id=1, source_target_pairs={{0,1},{1,0},{2,3},{3,2},{4,5},{5,4},{6,7},{7,6},{8,9},{9,8},{10,11... | collective-permute-start | bytes 5505032 | tf_op jit(solution)/shard_map/ppermute | solution.py:258
  62.3 3.4 %collective-permute-start.7 = (s32[7,3,64]{2,0,1:T(8,128)S(1)}, s32[7,3,64]{2,0,1:T(8,128)S(1)}, u32[]{:S(2)}, u32[]{:S(2)}) collective-permute-start(s32[7,3,64]{2,0,1:T(8,128)S(1)} %bitcast.47), channel_id=1, source_target_pairs={{0,1},{1,0},{2,3},{3,2},{4,5},{5,4},{6,7},{7,6},{8,9},{9,8},{10,11... | collective-permute-start | bytes 16136 | tf_op jit(solution)/shard_map/ppermute | solution.py:258
  68.6 82.2 %collective-permute-start.8 = (bf16[64,128,128]{2,1,0:T(8,128)(2,1)}, bf16[64,128,128]{2,1,0:T(8,128)(2,1)S(1)}, u32[]{:S(2)}, u32[]{:S(2)}) collective-permute-start(bf16[64,128,128]{2,1,0:T(8,128)(2,1)} %collective-permute-done.4.refs_10_), channel_id=1, source_target_pairs={{4,6},{2,0},{5,7},{3,1},{12,14},{10,8},{13,15},{11,9},{20,22},{18,... | collective-permute-start | bytes 6291464 | tf_op jit(solution)/shard_map/ppermute | solution.py:316
  121.3 8.9 %collective-permute-start.10 = (f32[28,128,128]{2,1,0:T(8,128)S(1)}, f32[28,128,128]{2,1,0:T(8,128)S(1)}, u32[]{:S(2)}, u32[]{:S(2)}) collective-permute-start(f32[28,128,128]{2,1,0:T(8,128)S(1)} %get-tuple-element.36), channel_id=1, source_target_pairs={{0,1},{1,0},{2,3},{3,2},{4,5},{5,4},{6,7},{7,6},{8,9},{9,8},{10,11... | collective-permute-start | bytes 5505032 | tf_op jit(solution)/shard_map/ppermute | solution.py:258
  126.8 8.7 %collective-permute-start.11 = (f32[28,128,128]{2,1,0:T(8,128)S(1)}, f32[28,128,128]{2,1,0:T(8,128)S(1)}, u32[]{:S(2)}, u32[]{:S(2)}) collective-permute-start(f32[28,128,128]{2,1,0:T(8,128)S(1)} %get-tuple-element.37), channel_id=1, source_target_pairs={{0,1},{1,0},{2,3},{3,2},{4,5},{5,4},{6,7},{7,6},{8,9},{9,8},{10,11... | collective-permute-start | bytes 5505032 | tf_op jit(solution)/shard_map/ppermute | solution.py:258
  126.9 11.2 %collective-permute-start.12 = (f32[28,128,128]{2,1,0:T(8,128)S(1)}, f32[28,128,128]{2,1,0:T(8,128)S(1)}, u32[]{:S(2)}, u32[]{:S(2)}) collective-permute-start(f32[28,128,128]{2,1,0:T(8,128)S(1)} %get-tuple-element.38), channel_id=1, source_target_pairs={{0,1},{1,0},{2,3},{3,2},{4,5},{5,4},{6,7},{7,6},{8,9},{9,8},{10,11... | collective-permute-start | bytes 5505032 | tf_op jit(solution)/shard_map/ppermute | solution.py:258
  127.3 10.8 %collective-permute-start.13 = (f32[28,128,128]{2,1,0:T(8,128)}, f32[28,128,128]{2,1,0:T(8,128)S(1)}, u32[]{:S(2)}, u32[]{:S(2)}) collective-permute-start(f32[28,128,128]{2,1,0:T(8,128)} %get-tuple-element.39), channel_id=1, source_target_pairs={{0,1},{1,0},{2,3},{3,2},{4,5},{5,4},{6,7},{7,6},{8,9},{9,8},{10,11... | collective-permute-start | bytes 5505032 | tf_op jit(solution)/shard_map/ppermute | solution.py:258
  150.8 6.5 %collective-permute-start.14 = (bf16[64,128,128]{2,1,0:T(8,128)(2,1)S(1)}, bf16[64,128,128]{2,1,0:T(8,128)(2,1)S(1)}, u32[]{:S(2)}, u32[]{:S(2)}) collective-permute-start(bf16[64,128,128]{2,1,0:T(8,128)(2,1)S(1)} %collective-permute-done.8.left), channel_id=1, source_target_pairs={{0,1},{1,0},{2,3},{3,2},{4,5},{5,4},{6,7},{7,6},{8,9},{9,8},{10,11... | collective-permute-start | bytes 6291464 | tf_op jit(solution)/shard_map/ppermute | solution.py:258

commit v14 on v13

--- a/solution.py
+++ b/solution.py
@@ -325,10 +325,10 @@
     classes += [jnp.where(inner, -1, jnp.where(low, 1, 3)), jnp.where(inner, 2, -1), jnp.where(inner, -1, 2)]
     scalars = scalar_list(*classes, layer, jnp.where(inner, -1, jnp.where(low, 3, 1)))
 
-    across_one, inward_one, outer_one, met, listed, scalars = fence(
-        (across_one, inward_one, outer_one, met, listed, scalars)
+    outer_two, across_two = hop(across_one, outward), hop(inward_one, across)
+    inward_one, across_one, outer_one, met, listed, scalars = fence(
+        (inward_one, across_one, outer_one, met, listed, scalars)
     )
-    outer_two, across_two = hop(across_one, outward), hop(inward_one, across)
     right_other, met_other = swapped(right_own), swapped(met)
     both = jnp.stack([step_lists, swapped(step_lists)])
     kept = kept_products(both, layer, half, right_slot)

time: 163 us -> 157 us (0.963)
  starting transfers between devices: 27.2 us -> 22.5 us
    ppermute x6, waiting for transfers between devices: 53.9 us -> 92.4 us  [hop(): return lax.ppermute(value, 'col', pairs)]
    ppermute x1, waiting for transfers between devices: 38.1 us -> 0.01 us  [line(): met = lax.ppermute(right_own, 'row', [(0, 1), (1, 0)])]
    ppermute x6, starting transfers between devices: 14.4 us -> 12 us  [hop(): return lax.ppermute(value, 'col', pairs)]
    ppermute x8, starting transfers between devices: 11.5 us -> 9.27 us  [swapped(): return lax.ppermute(value, 'dep', [(0, 1), (1, 0)])]
    ppermute x8, waiting for transfers between devices: 16.4 us -> 14.3 us  [swapped(): return lax.ppermute(value, 'dep', [(0, 1), (1, 0)])]
  transfers between devices with their start and end apart: 15 -> 15, of which waited for: 11 -> 9; matrix products, arithmetic and copies ran while one was open for 1% -> 1% of each run, Pallas kernels for 12% -> 13%
where the time goes in v14:
time: 157 us
  waiting for transfers between devices  107 us (68%)
  Pallas kernels  25.6 us (16%)
  starting transfers between devices  22.5 us (14%)
  local copies, waits for them, and re-layouts  1.93 us (1%)
    ppermute x6, waiting for transfers between devices, hop(): return lax.ppermute(value, 'col', pairs)  92.4 us
    pallas_call x1, Pallas kernels, product_sums(): pl.pallas_call(functools.partial(sum_kernel, panel_spans, right_spans, gi...  15.9 us
    ppermute x8, waiting for transfers between devices, swapped(): return lax.ppermute(value, 'dep', [(0, 1), (1, 0)])  14.3 us
    ppermute x6, starting transfers between devices, hop(): return lax.ppermute(value, 'col', pairs)  12 us
    ppermute x8, starting transfers between devices, swapped(): return lax.ppermute(value, 'dep', [(0, 1), (1, 0)])  9.27 us
    pallas_call x2, Pallas kernels, add_panel(): pl.pallas_call(functools.partial(panel_kernel, shape, layer, kind_at, fin...  8.73 us
  transfers between devices with their start and end apart: 15, of which 9 were waited for; matrix products, arithmetic and copies ran while one was open for 1% of the time, Pallas kernels for 13%

profile of v14, /device:TPU:1, one launch (start us, length us, event | category | flops | bytes accessed | tf_op | source)
XLA Modules:
  0.0 156.9 jit_solution(12264821975392337987)
XLA Ops:
  0.0 5.3 %collective-permute-start = (bf16[64,128,128]{2,1,0:T(8,128)(2,1)}, bf16[64,128,128]{2,1,0:T(8,128)(2,1)}, u32[]{:S(2)}, u32[]{:S(2)}) collective-permute-start(bf16[64,128,128]{2,1,0:T(8,128)(2,1)} %bitcast.38), channel_id=1, source_target_pairs={{0,2},{6,4},{1,3},{7,5},{8,10},{14,12},{9,11},{15,13},{16,18},{22,... | collective-permute-start | bytes 6291464 | tf_op jit(solution)/shard_map/ppermute | solution.py:316
  5.3 2.0 %collective-permute-start.3 = (bf16[64,128,128]{2,1,0:T(8,128)(2,1)}, bf16[64,128,128]{2,1,0:T(8,128)(2,1)}, u32[]{:S(2)}, u32[]{:S(2)}) collective-permute-start(bf16[64,128,128]{2,1,0:T(8,128)(2,1)} %bitcast.39), channel_id=1, source_target_pairs={{2,4},{4,2},{3,5},{5,3},{10,12},{12,10},{11,13},{13,11},{18,20},{2... | collective-permute-start | bytes 6291464 | tf_op jit(solution)/shard_map/ppermute | solution.py:316
  7.3 1.3 collective-permute-start.4
  8.6 1.3 collective-permute-start.5
  9.9 1.2 collective-permute-start.2
  11.1 0.7 copy.13
  11.9 36.8 %collective-permute-done.refs_8_ = bf16[64,128,128]{2,1,0:T(8,128)(2,1)} collective-permute-done((bf16[64,128,128]{2,1,0:T(8,128)(2,1)}, bf16[64,128,128]{2,1,0:T(8,128)(2,1)}, u32[]{:S(2)}, u32[]{:S(2)}) %collective-permute-start) | collective-permute-done | bytes 2097184 | tf_op jit(solution)/shard_map/ppermute | solution.py:316
  48.6 0.8 collective-permute-start.1
  50.0 1.3 collective-permute-start.9
  51.4 4.4 %collective-permute-done.4.refs_9_ = bf16[64,128,128]{2,1,0:T(8,128)(2,1)} collective-permute-done((bf16[64,128,128]{2,1,0:T(8,128)(2,1)}, bf16[64,128,128]{2,1,0:T(8,128)(2,1)}, u32[]{:S(2)}, u32[]{:S(2)}) %collective-permute-start.4) | collective-permute-done | bytes 2097184 | tf_op jit(solution)/shard_map/ppermute | solution.py:316
  55.7 1.9 %collective-permute-start.6 = (bf16[56,128,128]{2,1,0:T(8,128)(2,1)}, bf16[56,128,128]{2,1,0:T(8,128)(2,1)}, u32[]{:S(2)}, u32[]{:S(2)}) collective-permute-start(bf16[56,128,128]{2,1,0:T(8,128)(2,1)} %collective-permute-done.5.refs_3_), channel_id=1, source_target_pairs={{0,1},{1,0},{2,3},{3,2},{4,5},{5,4},{6,7},{7,6},{8,9},{9,8},{10,11... | collective-permute-start | bytes 5505032 | tf_op jit(solution)/shard_map/ppermute | solution.py:258
  57.9 3.0 %collective-permute-done.7 = s32[7,3,64]{2,0,1:T(8,128)S(1)} collective-permute-done((s32[7,3,64]{2,0,1:T(8,128)S(1)}, s32[7,3,64]{2,0,1:T(8,128)S(1)}, u32[]{:S(2)}, u32[]{:S(2)}) %collective-permute-start.7) | collective-permute-done | bytes 5408 | tf_op jit(solution)/shard_map/ppermute | solution.py:258
  61.4 1.3 collective-permute-start.8
  62.6 37.6 %collective-permute-done.9.refs_11_ = bf16[64,128,128]{2,1,0:T(8,128)(2,1)} collective-permute-done((bf16[64,128,128]{2,1,0:T(8,128)(2,1)}, bf16[64,128,128]{2,1,0:T(8,128)(2,1)}, u32[]{:S(2)}, u32[]{:S(2)}) %collective-permute-start.9) | collective-permute-done | bytes 2097184 | tf_op jit(solution)/shard_map/ppermute | solution.py:316
  100.3 15.9 %shard_map.37 = (f32[28,128,128]{2,1,0:T(8,128)S(1)}, f32[28,128,128]{2,1,0:T(8,128)S(1)}, f32[28,128,128]{2,1,0:T(8,128)S(1)}, f32[28,128,128]{2,1,0:T(8,128)},...) custom-call(s32[448]{0:T(512)S(1)} %fusion.17.refs_0_, s32[8]{0:T(128)S(1)} %stack.37.refs_1_.scalars, ...), custom_call_target="tpu_custom_call" | custom-call | flops 1 | bytes 1 | tf_op jit(solution)/shard_map/pallas_call | solution.py:161
  116.2 3.7 %collective-permute-start.10 = (f32[28,128,128]{2,1,0:T(8,128)S(1)}, f32[28,128,128]{2,1,0:T(8,128)S(1)}, u32[]{:S(2)}, u32[]{:S(2)}) collective-permute-start(f32[28,128,128]{2,1,0:T(8,128)S(1)} %get-tuple-element.36), channel_id=1, source_target_pairs={{0,1},{1,0},{2,3},{3,2},{4,5},{5,4},{6,7},{7,6},{8,9},{9,8},{10,11... | collective-permute-start | bytes 5505032 | tf_op jit(solution)/shard_map/ppermute | solution.py:258
  120.5 2.8 %collective-permute-done.10.refs_0_ = f32[28,128,128]{2,1,0:T(8,128)S(1)} collective-permute-done((f32[28,128,128]{2,1,0:T(8,128)S(1)}, f32[28,128,128]{2,1,0:T(8,128)S(1)}, u32[]{:S(2)}, u32[]{:S(2)}) %collective-permute-start.10) | collective-permute-done | bytes 1835040 | tf_op jit(solution)/shard_map/ppermute | solution.py:258
  123.3 5.2 %collective-permute-done.11.refs_1_ = f32[28,128,128]{2,1,0:T(8,128)S(1)} collective-permute-done((f32[28,128,128]{2,1,0:T(8,128)S(1)}, f32[28,128,128]{2,1,0:T(8,128)S(1)}, u32[]{:S(2)}, u32[]{:S(2)}) %collective-permute-start.11) | collective-permute-done | bytes 1835040 | tf_op jit(solution)/shard_map/ppermute | solution.py:258
  128.5 2.6 %collective-permute-done.12.refs_2_ = f32[28,128,128]{2,1,0:T(8,128)S(1)} collective-permute-done((f32[28,128,128]{2,1,0:T(8,128)S(1)}, f32[28,128,128]{2,1,0:T(8,128)S(1)}, u32[]{:S(2)}, u32[]{:S(2)}) %collective-permute-start.12) | collective-permute-done | bytes 1835040 | tf_op jit(solution)/shard_map/ppermute | solution.py:258
  131.2 0.9 shard_map.38.given
  132.1 13.6 %collective-permute-done.8.left = bf16[64,128,128]{2,1,0:T(8,128)(2,1)S(1)} collective-permute-done((bf16[64,128,128]{2,1,0:T(8,128)(2,1)S(1)}, bf16[64,128,128]{2,1,0:T(8,128)(2,1)S(1)}, u32[]{:S(2)}, u32[]{:S(2)}) %collective-permute-start.8) | collective-permute-done | bytes 2097184 | tf_op jit(solution)/shard_map/ppermute | solution.py:316
  145.7 1.9 %collective-permute-start.14 = (bf16[64,128,128]{2,1,0:T(8,128)(2,1)S(1)}, bf16[64,128,128]{2,1,0:T(8,128)(2,1)S(1)}, u32[]{:S(2)}, u32[]{:S(2)}) collective-permute-start(bf16[64,128,128]{2,1,0:T(8,128)(2,1)S(1)} %collective-permute-done.8.left), channel_id=1, source_target_pairs={{0,1},{1,0},{2,3},{3,2},{4,5},{5,4},{6,7},{7,6},{8,9},{9,8},{10,11... | collective-permute-start | bytes 6291464 | tf_op jit(solution)/shard_map/ppermute | solution.py:258
  147.6 3.2 %shard_map.39.given = f32[113,128,128]{2,1,0:T(8,128)S(1)} custom-call(s32[896]{0:T(1024)S(1)} %fusion.10.packed, s32[8]{0:T(128)S(1)} %stack.37.refs_1_.scalars, bf16[224,128,128]{2,1,0:T(8,128)(2,1)S(1)} %get-tuple-element.41.right, f32[113,128,128]{2,1,0:T(8,128)S(1)} %shard_map.38.given, ...), custom_call_target="tpu_custom_call", output_to_operand_aliasing={{}: (3, {})} | custom-call | flops 1 | bytes 1 | tf_op jit(solution)/shard_map/pallas_call | solution.py:241
  151.4 5.5 %shard_map.40 = (bf16[112,128,128]{2,1,0:T(8,128)(2,1)}, f32[113,128,128]{2,1,0:T(8,128)S(1)}) custom-call(s32[896]{0:T(1024)S(1)} %fusion.10.packed, s32[8]{0:T(128)S(1)} %stack.37.refs_1_.scalars, bf16[224,128,128]{2,1,0:T(8,128)(2,1)S(1)} %get-tuple-element.41.right, f32[113,128,128]{2,1,0:T(8,128)S(1)} %shard_map.39.given, ...), custom_call_target="tpu_custom_call", output_to_operand_aliasing={{1}: (3, {})} | custom-call | flops 1 | bytes 1 | tf_op jit(solution)/shard_map/pallas_call | solution.py:241
  (37 shorter events, 2.5 us)
Async XLA Ops:
  0.0 48.6 %collective-permute-start = (bf16[64,128,128]{2,1,0:T(8,128)(2,1)}, bf16[64,128,128]{2,1,0:T(8,128)(2,1)}, u32[]{:S(2)}, u32[]{:S(2)}) collective-permute-start(bf16[64,128,128]{2,1,0:T(8,128)(2,1)} %bitcast.38), channel_id=1, source_target_pairs={{0,2},{6,4},{1,3},{7,5},{8,10},{14,12},{9,11},{15,13},{16,18},{22,... | collective-permute-start | bytes 6291464 | tf_op jit(solution)/shard_map/ppermute | solution.py:316
  5.3 44.6 %collective-permute-start.3 = (bf16[64,128,128]{2,1,0:T(8,128)(2,1)}, bf16[64,128,128]{2,1,0:T(8,128)(2,1)}, u32[]{:S(2)}, u32[]{:S(2)}) collective-permute-start(bf16[64,128,128]{2,1,0:T(8,128)(2,1)} %bitcast.39), channel_id=1, source_target_pairs={{2,4},{4,2},{3,5},{5,3},{10,12},{12,10},{11,13},{13,11},{18,20},{2... | collective-permute-start | bytes 6291464 | tf_op jit(solution)/shard_map/ppermute | solution.py:316
  7.3 48.4 %collective-permute-start.4 = (bf16[64,128,128]{2,1,0:T(8,128)(2,1)}, bf16[64,128,128]{2,1,0:T(8,128)(2,1)}, u32[]{:S(2)}, u32[]{:S(2)}) collective-permute-start(bf16[64,128,128]{2,1,0:T(8,128)(2,1)} %bitcast.40), channel_id=1, source_target_pairs={{4,6},{2,0},{5,7},{3,1},{12,14},{10,8},{13,15},{11,9},{20,22},{18,... | collective-permute-start | bytes 6291464 | tf_op jit(solution)/shard_map/ppermute | solution.py:316
  8.6 42.7 %collective-permute-start.5 = (bf16[56,128,128]{2,1,0:T(8,128)(2,1)}, bf16[56,128,128]{2,1,0:T(8,128)(2,1)}, u32[]{:S(2)}, u32[]{:S(2)}) collective-permute-start(bf16[56,128,128]{2,1,0:T(8,128)(2,1)} %bitcast.42), channel_id=1, source_target_pairs={{0,8},{8,0},{1,9},{9,1},{2,10},{10,2},{3,11},{11,3},{4,12},{12,4},... | collective-permute-start | bytes 5505032 | tf_op jit(solution)/shard_map/ppermute | solution.py:322
  9.9 51.4 %collective-permute-start.2 = (bf16[56,128,128]{2,1,0:T(8,128)(2,1)}, bf16[56,128,128]{2,1,0:T(8,128)(2,1)}, u32[]{:S(2)}, u32[]{:S(2)}) collective-permute-start(bf16[56,128,128]{2,1,0:T(8,128)(2,1)} %bitcast.43), channel_id=1, source_target_pairs={{0,1},{1,0},{2,3},{3,2},{4,5},{5,4},{6,7},{7,6},{8,9},{9,8},{10,11... | collective-permute-start | bytes 5505032 | tf_op jit(solution)/shard_map/ppermute | solution.py:258
  48.6 12.7 %collective-permute-start.1 = (bf16[64,128,128]{2,1,0:T(8,128)(2,1)}, bf16[64,128,128]{2,1,0:T(8,128)(2,1)S(1)}, u32[]{:S(2)}, u32[]{:S(2)}) collective-permute-start(bf16[64,128,128]{2,1,0:T(8,128)(2,1)} %collective-permute-done.refs_8_), channel_id=1, source_target_pairs={{2,4},{4,2},{3,5},{5,3},{10,12},{12,10},{11,13},{13,11},{18,20},{2... | collective-permute-start | bytes 6291464 | tf_op jit(solution)/shard_map/ppermute | solution.py:316
  50.0 50.3 %collective-permute-start.9 = (bf16[64,128,128]{2,1,0:T(8,128)(2,1)}, bf16[64,128,128]{2,1,0:T(8,128)(2,1)}, u32[]{:S(2)}, u32[]{:S(2)}) collective-permute-start(bf16[64,128,128]{2,1,0:T(8,128)(2,1)} %collective-permute-done.3.refs_7_), channel_id=1, source_target_pairs={{4,6},{2,0},{5,7},{3,1},{12,14},{10,8},{13,15},{11,9},{20,22},{18,... | collective-permute-start | bytes 6291464 | tf_op jit(solution)/shard_map/ppermute | solution.py:316
  55.7 5.6 %collective-permute-start.6 = (bf16[56,128,128]{2,1,0:T(8,128)(2,1)}, bf16[56,128,128]{2,1,0:T(8,128)(2,1)}, u32[]{:S(2)}, u32[]{:S(2)}) collective-permute-start(bf16[56,128,128]{2,1,0:T(8,128)(2,1)} %collective-permute-done.5.refs_3_), channel_id=1, source_target_pairs={{0,1},{1,0},{2,3},{3,2},{4,5},{5,4},{6,7},{7,6},{8,9},{9,8},{10,11... | collective-permute-start | bytes 5505032 | tf_op jit(solution)/shard_map/ppermute | solution.py:258
  57.6 3.3 %collective-permute-start.7 = (s32[7,3,64]{2,0,1:T(8,128)S(1)}, s32[7,3,64]{2,0,1:T(8,128)S(1)}, u32[]{:S(2)}, u32[]{:S(2)}) collective-permute-start(s32[7,3,64]{2,0,1:T(8,128)S(1)} %bitcast.47), channel_id=1, source_target_pairs={{0,1},{1,0},{2,3},{3,2},{4,5},{5,4},{6,7},{7,6},{8,9},{9,8},{10,11... | collective-permute-start | bytes 16136 | tf_op jit(solution)/shard_map/ppermute | solution.py:258
  61.4 38.9 %copy-start = (bf16[64,128,128]{2,1,0:T(8,128)(2,1)}, bf16[64,128,128]{2,1,0:T(8,128)(2,1)S(1)}, u32[]{:S(2)}) copy-start(bf16[64,128,128]{2,1,0:T(8,128)(2,1)S(1)} %collective-permute-done.1.refs_10_) | copy-start | bytes 6291460
  61.4 84.3 %collective-permute-start.8 = (bf16[64,128,128]{2,1,0:T(8,128)(2,1)S(1)}, bf16[64,128,128]{2,1,0:T(8,128)(2,1)S(1)}, u32[]{:S(2)}, u32[]{:S(2)}) collective-permute-start(bf16[64,128,128]{2,1,0:T(8,128)(2,1)S(1)} %collective-permute-done.1.refs_10_), channel_id=1, source_target_pairs={{4,6},{2,0},{5,7},{3,1},{12,14},{10,8},{13,15},{11,9},{20,22},{18,... | collective-permute-start | bytes 6291464 | tf_op jit(solution)/shard_map/ppermute | solution.py:316
  116.2 7.1 %collective-permute-start.10 = (f32[28,128,128]{2,1,0:T(8,128)S(1)}, f32[28,128,128]{2,1,0:T(8,128)S(1)}, u32[]{:S(2)}, u32[]{:S(2)}) collective-permute-start(f32[28,128,128]{2,1,0:T(8,128)S(1)} %get-tuple-element.36), channel_id=1, source_target_pairs={{0,1},{1,0},{2,3},{3,2},{4,5},{5,4},{6,7},{7,6},{8,9},{9,8},{10,11... | collective-permute-start | bytes 5505032 | tf_op jit(solution)/shard_map/ppermute | solution.py:258
  119.9 8.7 %collective-permute-start.11 = (f32[28,128,128]{2,1,0:T(8,128)S(1)}, f32[28,128,128]{2,1,0:T(8,128)S(1)}, u32[]{:S(2)}, u32[]{:S(2)}) collective-permute-start(f32[28,128,128]{2,1,0:T(8,128)S(1)} %get-tuple-element.37), channel_id=1, source_target_pairs={{0,1},{1,0},{2,3},{3,2},{4,5},{5,4},{6,7},{7,6},{8,9},{9,8},{10,11... | collective-permute-start | bytes 5505032 | tf_op jit(solution)/shard_map/ppermute | solution.py:258
  119.9 11.2 %collective-permute-start.12 = (f32[28,128,128]{2,1,0:T(8,128)S(1)}, f32[28,128,128]{2,1,0:T(8,128)S(1)}, u32[]{:S(2)}, u32[]{:S(2)}) collective-permute-start(f32[28,128,128]{2,1,0:T(8,128)S(1)} %get-tuple-element.38), channel_id=1, source_target_pairs={{0,1},{1,0},{2,3},{3,2},{4,5},{5,4},{6,7},{7,6},{8,9},{9,8},{10,11... | collective-permute-start | bytes 5505032 | tf_op jit(solution)/shard_map/ppermute | solution.py:258
  120.4 10.8 %collective-permute-start.13 = (f32[28,128,128]{2,1,0:T(8,128)}, f32[28,128,128]{2,1,0:T(8,128)S(1)}, u32[]{:S(2)}, u32[]{:S(2)}) collective-permute-start(f32[28,128,128]{2,1,0:T(8,128)} %get-tuple-element.39), channel_id=1, source_target_pairs={{0,1},{1,0},{2,3},{3,2},{4,5},{5,4},{6,7},{7,6},{8,9},{9,8},{10,11... | collective-permute-start | bytes 5505032 | tf_op jit(solution)/shard_map/ppermute | solution.py:258
  145.7 5.7 %collective-permute-start.14 = (bf16[64,128,128]{2,1,0:T(8,128)(2,1)S(1)}, bf16[64,128,128]{2,1,0:T(8,128)(2,1)S(1)}, u32[]{:S(2)}, u32[]{:S(2)}) collective-permute-start(bf16[64,128,128]{2,1,0:T(8,128)(2,1)S(1)} %collective-permute-done.8.left), channel_id=1, source_target_pairs={{0,1},{1,0},{2,3},{3,2},{4,5},{5,4},{6,7},{7,6},{8,9},{9,8},{10,11... | collective-permute-start | bytes 6291464 | tf_op jit(solution)/shard_map/ppermute | solution.py:258

commit v15 on v14

--- a/solution.py
+++ b/solution.py
@@ -309,7 +309,7 @@
     shape = (step_lists.shape[0], columns, slots)
     inner = (place == 1) | (place == 2)
     low = place < 2
-    outward, across, inward = [(2, 3), (1, 0)], [(1, 2), (2, 1)], [(0, 1), (3, 2)]
+    outward, across, beside = [(2, 3), (1, 0)], [(1, 2), (2, 1)], [(0, 1), (1, 0), (2, 3), (3, 2)]
     fence = lax.optimization_barrier
 
     def hop(value, pairs):
@@ -318,24 +318,22 @@
     def right_slot(slot, layers):
         return (layers * 2 + ((slot // part) ^ lax.axis_index("row"))) * part + slot % part
 
-    outer_one, inward_one, across_one = hop(own, outward), hop(own, inward), hop(own, across)
+    beside_one, across_one = hop(own, beside), hop(own, across)
     met = lax.ppermute(right_own, "row", [(0, 1), (1, 0)])
     listed = layer_products(step_lists, layer, half, right_slot)
-    classes = [0, jnp.where(inner, jnp.where(low, 1, 3), -1), jnp.where(inner, jnp.where(low, 3, 1), -1)]
-    classes += [jnp.where(inner, -1, jnp.where(low, 1, 3)), jnp.where(inner, 2, -1), jnp.where(inner, -1, 2)]
+    classes = [0, jnp.where(place % 2 == 0, 1, 3), jnp.where(inner, jnp.where(low, 1, 3), -1)]
+    classes += [jnp.where(inner, 2, -1), jnp.where(inner, -1, 2)]
     scalars = scalar_list(*classes, layer, jnp.where(inner, -1, jnp.where(low, 3, 1)))
 
-    outer_two, across_two = hop(across_one, outward), hop(inward_one, across)
-    inward_one, across_one, outer_one, met, listed, scalars = fence(
-        (inward_one, across_one, outer_one, met, listed, scalars)
-    )
+    outer_two, across_two = hop(across_one, outward), hop(beside_one, across)
+    beside_one, across_one, met, listed, scalars = fence((beside_one, across_one, met, listed, scalars))
     right_other, met_other = swapped(right_own), swapped(met)
     both = jnp.stack([step_lists, swapped(step_lists)])
     kept = kept_products(both, layer, half, right_slot)
 
     across_two, right_other, met_other, kept = fence((across_two, right_other, met_other, kept))
     outer_three = hop(across_two, outward)
-    panels = [[(value, False)] for value in (own, across_one, inward_one, outer_one, across_two, outer_two)]
+    panels = [[(value, False)] for value in (own, beside_one, across_one, across_two, outer_two)]
     rights = [(value, False) for value in (right_own, met, right_other, met_other)]
     saved = [half // PARTS] * (PARTS - 1) + [half - half // PARTS * (PARTS - 1)]
     *parts, right, total = product_sums(

time: 157 us -> 155 us (0.987)
  starting transfers between devices: 22.5 us -> 17.4 us
  waiting for transfers between devices: 107 us -> 110 us
    ppermute x6 -> x5, starting transfers between devices: 12 us -> 7.46 us  [hop(): return lax.ppermute(value, 'col', pairs)]
    ppermute x6 -> x5, waiting for transfers between devices: 92.4 us -> 95.6 us  [hop(): return lax.ppermute(value, 'col', pairs)]
  transfers between devices with their start and end apart: 15 -> 14, of which waited for: 9 -> 9; matrix products, arithmetic and copies ran while one was open for 1% -> 1% of each run, Pallas kernels for 13% -> 13%
where the time goes in v15:
time: 155 us
  waiting for transfers between devices  110 us (71%)
  Pallas kernels  25.6 us (17%)
  starting transfers between devices  17.4 us (11%)
  local copies, waits for them, and re-layouts  1.93 us (1%)
    ppermute x5, waiting for transfers between devices, hop(): return lax.ppermute(value, 'col', pairs)  95.6 us
    pallas_call x1, Pallas kernels, product_sums(): pl.pallas_call(functools.partial(sum_kernel, panel_spans, right_spans, gi...  16 us
    ppermute x8, waiting for transfers between devices, swapped(): return lax.ppermute(value, 'dep', [(0, 1), (1, 0)])  14 us
    ppermute x8, starting transfers between devices, swapped(): return lax.ppermute(value, 'dep', [(0, 1), (1, 0)])  8.75 us
    pallas_call x2, Pallas kernels, add_panel(): pl.pallas_call(functools.partial(panel_kernel, shape, layer, kind_at, fin...  8.66 us
    ppermute x5, starting transfers between devices, hop(): return lax.ppermute(value, 'col', pairs)  7.46 us
  transfers between devices with their start and end apart: 14, of which 9 were waited for; matrix products, arithmetic and copies ran while one was open for 1% of the time, Pallas kernels for 13%

profile of v15, /device:TPU:1, one launch (start us, length us, event | category | flops | bytes accessed | tf_op | source)
XLA Modules:
  0.0 154.7 jit_solution(18052037760020312547)
XLA Ops:
  0.0 2.1 %collective-permute-start = (bf16[64,128,128]{2,1,0:T(8,128)(2,1)}, bf16[64,128,128]{2,1,0:T(8,128)(2,1)}, u32[]{:S(2)}, u32[]{:S(2)}) collective-permute-start(bf16[64,128,128]{2,1,0:T(8,128)(2,1)} %bitcast.37), channel_id=1, source_target_pairs={{0,2},{2,0},{4,6},{6,4},{1,3},{3,1},{5,7},{7,5},{8,10},{10,8},{12,... | collective-permute-start | bytes 6291464 | tf_op jit(solution)/shard_map/ppermute | solution.py:316
  2.1 2.0 %collective-permute-start.3 = (bf16[64,128,128]{2,1,0:T(8,128)(2,1)}, bf16[64,128,128]{2,1,0:T(8,128)(2,1)}, u32[]{:S(2)}, u32[]{:S(2)}) collective-permute-start(bf16[64,128,128]{2,1,0:T(8,128)(2,1)} %bitcast.38), channel_id=1, source_target_pairs={{2,4},{4,2},{3,5},{5,3},{10,12},{12,10},{11,13},{13,11},{18,20},{2... | collective-permute-start | bytes 6291464 | tf_op jit(solution)/shard_map/ppermute | solution.py:316
  4.1 1.2 collective-permute-start.4
  5.3 1.2 collective-permute-start.2
  6.5 0.7 copy.13
  7.3 40.5 %collective-permute-done.refs_7_ = bf16[64,128,128]{2,1,0:T(8,128)(2,1)} collective-permute-done((bf16[64,128,128]{2,1,0:T(8,128)(2,1)}, bf16[64,128,128]{2,1,0:T(8,128)(2,1)}, u32[]{:S(2)}, u32[]{:S(2)}) %collective-permute-start) | collective-permute-done | bytes 2097184 | tf_op jit(solution)/shard_map/ppermute | solution.py:316
  47.8 0.8 collective-permute-start.1
  49.1 1.3 collective-permute-start.8
  50.5 1.3 collective-permute-start.5
  52.2 2.9 %collective-permute-done.6 = s32[7,3,64]{2,0,1:T(8,128)S(1)} collective-permute-done((s32[7,3,64]{2,0,1:T(8,128)S(1)}, s32[7,3,64]{2,0,1:T(8,128)S(1)}, u32[]{:S(2)}, u32[]{:S(2)}) %collective-permute-start.6) | collective-permute-done | bytes 5408 | tf_op jit(solution)/shard_map/ppermute | solution.py:258
  55.6 1.3 collective-permute-start.7
  56.9 41.5 %collective-permute-done.8.refs_10_ = bf16[64,128,128]{2,1,0:T(8,128)(2,1)} collective-permute-done((bf16[64,128,128]{2,1,0:T(8,128)(2,1)}, bf16[64,128,128]{2,1,0:T(8,128)(2,1)}, u32[]{:S(2)}, u32[]{:S(2)}) %collective-permute-start.8) | collective-permute-done | bytes 2097184 | tf_op jit(solution)/shard_map/ppermute | solution.py:316
  98.4 16.0 %shard_map.37 = (f32[28,128,128]{2,1,0:T(8,128)S(1)}, f32[28,128,128]{2,1,0:T(8,128)S(1)}, f32[28,128,128]{2,1,0:T(8,128)S(1)}, f32[28,128,128]{2,1,0:T(8,128)},...) custom-call(s32[448]{0:T(512)S(1)} %fusion.17.refs_0_, s32[7]{0:T(128)S(1)} %stack.33.refs_1_.scalars, ...), custom_call_target="tpu_custom_call" | custom-call | flops 1 | bytes 1 | tf_op jit(solution)/shard_map/pallas_call | solution.py:161
  114.4 3.7 %collective-permute-start.10 = (f32[28,128,128]{2,1,0:T(8,128)S(1)}, f32[28,128,128]{2,1,0:T(8,128)S(1)}, u32[]{:S(2)}, u32[]{:S(2)}) collective-permute-start(f32[28,128,128]{2,1,0:T(8,128)S(1)} %get-tuple-element.35), channel_id=1, source_target_pairs={{0,1},{1,0},{2,3},{3,2},{4,5},{5,4},{6,7},{7,6},{8,9},{9,8},{10,11... | collective-permute-start | bytes 5505032 | tf_op jit(solution)/shard_map/ppermute | solution.py:258
  118.2 0.4 collective-permute-start.12
  118.7 2.8 %collective-permute-done.10.refs_1_ = f32[28,128,128]{2,1,0:T(8,128)S(1)} collective-permute-done((f32[28,128,128]{2,1,0:T(8,128)S(1)}, f32[28,128,128]{2,1,0:T(8,128)S(1)}, u32[]{:S(2)}, u32[]{:S(2)}) %collective-permute-start.10) | collective-permute-done | bytes 1835040 | tf_op jit(solution)/shard_map/ppermute | solution.py:258
  121.5 5.2 %collective-permute-done.11.refs_2_ = f32[28,128,128]{2,1,0:T(8,128)S(1)} collective-permute-done((f32[28,128,128]{2,1,0:T(8,128)S(1)}, f32[28,128,128]{2,1,0:T(8,128)S(1)}, u32[]{:S(2)}, u32[]{:S(2)}) %collective-permute-start.11) | collective-permute-done | bytes 1835040 | tf_op jit(solution)/shard_map/ppermute | solution.py:258
  126.9 2.4 %collective-permute-done.9.refs_0_ = f32[28,128,128]{2,1,0:T(8,128)S(1)} collective-permute-done((f32[28,128,128]{2,1,0:T(8,128)S(1)}, f32[28,128,128]{2,1,0:T(8,128)S(1)}, u32[]{:S(2)}, u32[]{:S(2)}) %collective-permute-start.9) | collective-permute-done | bytes 1835040 | tf_op jit(solution)/shard_map/ppermute | solution.py:258
  129.4 0.9 shard_map.38.given
  130.3 13.5 %collective-permute-done.7.left = bf16[64,128,128]{2,1,0:T(8,128)(2,1)S(1)} collective-permute-done((bf16[64,128,128]{2,1,0:T(8,128)(2,1)S(1)}, bf16[64,128,128]{2,1,0:T(8,128)(2,1)S(1)}, u32[]{:S(2)}, u32[]{:S(2)}) %collective-permute-start.7) | collective-permute-done | bytes 2097184 | tf_op jit(solution)/shard_map/ppermute | solution.py:316
  143.8 1.9 %collective-permute-start.13 = (bf16[64,128,128]{2,1,0:T(8,128)(2,1)S(1)}, bf16[64,128,128]{2,1,0:T(8,128)(2,1)S(1)}, u32[]{:S(2)}, u32[]{:S(2)}) collective-permute-start(bf16[64,128,128]{2,1,0:T(8,128)(2,1)S(1)} %collective-permute-done.7.left), channel_id=1, source_target_pairs={{0,1},{1,0},{2,3},{3,2},{4,5},{5,4},{6,7},{7,6},{8,9},{9,8},{10,11... | collective-permute-start | bytes 6291464 | tf_op jit(solution)/shard_map/ppermute | solution.py:258
  145.7 3.5 %shard_map.39.given = f32[113,128,128]{2,1,0:T(8,128)S(1)} custom-call(s32[896]{0:T(1024)S(1)} %fusion.10.packed, s32[7]{0:T(128)S(1)} %stack.33.refs_1_.scalars, bf16[224,128,128]{2,1,0:T(8,128)(2,1)S(1)} %get-tuple-element.39.right, f32[113,128,128]{2,1,0:T(8,128)S(1)} %shard_map.38.given, ...), custom_call_target="tpu_custom_call", output_to_operand_aliasing={{}: (3, {})} | custom-call | flops 1 | bytes 1 | tf_op jit(solution)/shard_map/pallas_call | solution.py:241
  149.2 0.3 collective-permute-done.13.left
  149.5 5.2 %shard_map.40 = (bf16[112,128,128]{2,1,0:T(8,128)(2,1)}, f32[113,128,128]{2,1,0:T(8,128)S(1)}) custom-call(s32[896]{0:T(1024)S(1)} %fusion.10.packed, s32[7]{0:T(128)S(1)} %stack.33.refs_1_.scalars, bf16[224,128,128]{2,1,0:T(8,128)(2,1)S(1)} %get-tuple-element.39.right, f32[113,128,128]{2,1,0:T(8,128)S(1)} %shard_map.39.given, ...), custom_call_target="tpu_custom_call", output_to_operand_aliasing={{1}: (3, {})} | custom-call | flops 1 | bytes 1 | tf_op jit(solution)/shard_map/pallas_call | solution.py:241
  (35 shorter events, 1.8 us)
Async XLA Ops:
  0.0 47.8 %collective-permute-start = (bf16[64,128,128]{2,1,0:T(8,128)(2,1)}, bf16[64,128,128]{2,1,0:T(8,128)(2,1)}, u32[]{:S(2)}, u32[]{:S(2)}) collective-permute-start(bf16[64,128,128]{2,1,0:T(8,128)(2,1)} %bitcast.37), channel_id=1, source_target_pairs={{0,2},{2,0},{4,6},{6,4},{1,3},{3,1},{5,7},{7,5},{8,10},{10,8},{12,... | collective-permute-start | bytes 6291464 | tf_op jit(solution)/shard_map/ppermute | solution.py:316
  2.1 47.0 %collective-permute-start.3 = (bf16[64,128,128]{2,1,0:T(8,128)(2,1)}, bf16[64,128,128]{2,1,0:T(8,128)(2,1)}, u32[]{:S(2)}, u32[]{:S(2)}) collective-permute-start(bf16[64,128,128]{2,1,0:T(8,128)(2,1)} %bitcast.38), channel_id=1, source_target_pairs={{2,4},{4,2},{3,5},{5,3},{10,12},{12,10},{11,13},{13,11},{18,20},{2... | collective-permute-start | bytes 6291464 | tf_op jit(solution)/shard_map/ppermute | solution.py:316
  4.1 46.4 %collective-permute-start.4 = (bf16[56,128,128]{2,1,0:T(8,128)(2,1)}, bf16[56,128,128]{2,1,0:T(8,128)(2,1)}, u32[]{:S(2)}, u32[]{:S(2)}) collective-permute-start(bf16[56,128,128]{2,1,0:T(8,128)(2,1)} %bitcast.40), channel_id=1, source_target_pairs={{0,8},{8,0},{1,9},{9,1},{2,10},{10,2},{3,11},{11,3},{4,12},{12,4},... | collective-permute-start | bytes 5505032 | tf_op jit(solution)/shard_map/ppermute | solution.py:322
  5.3 50.2 %collective-permute-start.2 = (bf16[56,128,128]{2,1,0:T(8,128)(2,1)}, bf16[56,128,128]{2,1,0:T(8,128)(2,1)}, u32[]{:S(2)}, u32[]{:S(2)}) collective-permute-start(bf16[56,128,128]{2,1,0:T(8,128)(2,1)} %bitcast.41), channel_id=1, source_target_pairs={{0,1},{1,0},{2,3},{3,2},{4,5},{5,4},{6,7},{7,6},{8,9},{9,8},{10,11... | collective-permute-start | bytes 5505032 | tf_op jit(solution)/shard_map/ppermute | solution.py:258
  47.8 7.8 %collective-permute-start.1 = (bf16[64,128,128]{2,1,0:T(8,128)(2,1)}, bf16[64,128,128]{2,1,0:T(8,128)(2,1)S(1)}, u32[]{:S(2)}, u32[]{:S(2)}) collective-permute-start(bf16[64,128,128]{2,1,0:T(8,128)(2,1)} %collective-permute-done.refs_7_), channel_id=1, source_target_pairs={{2,4},{4,2},{3,5},{5,3},{10,12},{12,10},{11,13},{13,11},{18,20},{2... | collective-permute-start | bytes 6291464 | tf_op jit(solution)/shard_map/ppermute | solution.py:316
  49.1 49.3 %collective-permute-start.8 = (bf16[64,128,128]{2,1,0:T(8,128)(2,1)}, bf16[64,128,128]{2,1,0:T(8,128)(2,1)}, u32[]{:S(2)}, u32[]{:S(2)}) collective-permute-start(bf16[64,128,128]{2,1,0:T(8,128)(2,1)} %collective-permute-done.3.refs_8_), channel_id=1, source_target_pairs={{4,6},{2,0},{5,7},{3,1},{12,14},{10,8},{13,15},{11,9},{20,22},{18,... | collective-permute-start | bytes 6291464 | tf_op jit(solution)/shard_map/ppermute | solution.py:316
  50.5 5.0 %collective-permute-start.5 = (bf16[56,128,128]{2,1,0:T(8,128)(2,1)}, bf16[56,128,128]{2,1,0:T(8,128)(2,1)}, u32[]{:S(2)}, u32[]{:S(2)}) collective-permute-start(bf16[56,128,128]{2,1,0:T(8,128)(2,1)} %collective-permute-done.4.refs_3_), channel_id=1, source_target_pairs={{0,1},{1,0},{2,3},{3,2},{4,5},{5,4},{6,7},{7,6},{8,9},{9,8},{10,11... | collective-permute-start | bytes 5505032 | tf_op jit(solution)/shard_map/ppermute | solution.py:258
  51.8 3.3 %collective-permute-start.6 = (s32[7,3,64]{2,0,1:T(8,128)S(1)}, s32[7,3,64]{2,0,1:T(8,128)S(1)}, u32[]{:S(2)}, u32[]{:S(2)}) collective-permute-start(s32[7,3,64]{2,0,1:T(8,128)S(1)} %bitcast.45), channel_id=1, source_target_pairs={{0,1},{1,0},{2,3},{3,2},{4,5},{5,4},{6,7},{7,6},{8,9},{9,8},{10,11... | collective-permute-start | bytes 16136 | tf_op jit(solution)/shard_map/ppermute | solution.py:258
  55.6 42.8 %copy-start = (bf16[64,128,128]{2,1,0:T(8,128)(2,1)}, bf16[64,128,128]{2,1,0:T(8,128)(2,1)S(1)}, u32[]{:S(2)}) copy-start(bf16[64,128,128]{2,1,0:T(8,128)(2,1)S(1)} %collective-permute-done.1.refs_9_) | copy-start | bytes 6291460
  55.6 88.2 %collective-permute-start.7 = (bf16[64,128,128]{2,1,0:T(8,128)(2,1)S(1)}, bf16[64,128,128]{2,1,0:T(8,128)(2,1)S(1)}, u32[]{:S(2)}, u32[]{:S(2)}) collective-permute-start(bf16[64,128,128]{2,1,0:T(8,128)(2,1)S(1)} %collective-permute-done.1.refs_9_), channel_id=1, source_target_pairs={{4,6},{2,0},{5,7},{3,1},{12,14},{10,8},{13,15},{11,9},{20,22},{18,... | collective-permute-start | bytes 6291464 | tf_op jit(solution)/shard_map/ppermute | solution.py:316
  114.4 7.1 %collective-permute-start.10 = (f32[28,128,128]{2,1,0:T(8,128)S(1)}, f32[28,128,128]{2,1,0:T(8,128)S(1)}, u32[]{:S(2)}, u32[]{:S(2)}) collective-permute-start(f32[28,128,128]{2,1,0:T(8,128)S(1)} %get-tuple-element.35), channel_id=1, source_target_pairs={{0,1},{1,0},{2,3},{3,2},{4,5},{5,4},{6,7},{7,6},{8,9},{9,8},{10,11... | collective-permute-start | bytes 5505032 | tf_op jit(solution)/shard_map/ppermute | solution.py:258
  118.1 8.7 %collective-permute-start.11 = (f32[28,128,128]{2,1,0:T(8,128)S(1)}, f32[28,128,128]{2,1,0:T(8,128)S(1)}, u32[]{:S(2)}, u32[]{:S(2)}) collective-permute-start(f32[28,128,128]{2,1,0:T(8,128)S(1)} %get-tuple-element.36), channel_id=1, source_target_pairs={{0,1},{1,0},{2,3},{3,2},{4,5},{5,4},{6,7},{7,6},{8,9},{9,8},{10,11... | collective-permute-start | bytes 5505032 | tf_op jit(solution)/shard_map/ppermute | solution.py:258
  118.2 8.8 %collective-permute-start.12 = (f32[28,128,128]{2,1,0:T(8,128)}, f32[28,128,128]{2,1,0:T(8,128)S(1)}, u32[]{:S(2)}, u32[]{:S(2)}) collective-permute-start(f32[28,128,128]{2,1,0:T(8,128)} %get-tuple-element.37), channel_id=1, source_target_pairs={{0,1},{1,0},{2,3},{3,2},{4,5},{5,4},{6,7},{7,6},{8,9},{9,8},{10,11... | collective-permute-start | bytes 5505032 | tf_op jit(solution)/shard_map/ppermute | solution.py:258
  118.6 10.8 %collective-permute-start.9 = (f32[28,128,128]{2,1,0:T(8,128)S(1)}, f32[28,128,128]{2,1,0:T(8,128)S(1)}, u32[]{:S(2)}, u32[]{:S(2)}) collective-permute-start(f32[28,128,128]{2,1,0:T(8,128)S(1)} %get-tuple-element.34), channel_id=1, source_target_pairs={{0,1},{1,0},{2,3},{3,2},{4,5},{5,4},{6,7},{7,6},{8,9},{9,8},{10,11... | collective-permute-start | bytes 5505032 | tf_op jit(solution)/shard_map/ppermute | solution.py:258
  143.8 5.7 %collective-permute-start.13 = (bf16[64,128,128]{2,1,0:T(8,128)(2,1)S(1)}, bf16[64,128,128]{2,1,0:T(8,128)(2,1)S(1)}, u32[]{:S(2)}, u32[]{:S(2)}) collective-permute-start(bf16[64,128,128]{2,1,0:T(8,128)(2,1)S(1)} %collective-permute-done.7.left), channel_id=1, source_target_pairs={{0,1},{1,0},{2,3},{3,2},{4,5},{5,4},{6,7},{7,6},{8,9},{9,8},{10,11... | collective-permute-start | bytes 6291464 | tf_op jit(solution)/shard_map/ppermute | solution.py:258

commit v16 on v15

--- a/solution.py
+++ b/solution.py
@@ -318,14 +318,14 @@
     def right_slot(slot, layers):
         return (layers * 2 + ((slot // part) ^ lax.axis_index("row"))) * part + slot % part
 
-    beside_one, across_one = hop(own, beside), hop(own, across)
+    beside_one, across_one, across_two = hop(own, beside), hop(own, across), hop(own, [(0, 2), (3, 1)])
     met = lax.ppermute(right_own, "row", [(0, 1), (1, 0)])
     listed = layer_products(step_lists, layer, half, right_slot)
     classes = [0, jnp.where(place % 2 == 0, 1, 3), jnp.where(inner, jnp.where(low, 1, 3), -1)]
     classes += [jnp.where(inner, 2, -1), jnp.where(inner, -1, 2)]
     scalars = scalar_list(*classes, layer, jnp.where(inner, -1, jnp.where(low, 3, 1)))
 
-    outer_two, across_two = hop(across_one, outward), hop(beside_one, across)
+    outer_two = hop(across_one, outward)
     beside_one, across_one, met, listed, scalars = fence((beside_one, across_one, met, listed, scalars))
     right_other, met_other = swapped(right_own), swapped(met)
     both = jnp.stack([step_lists, swapped(step_lists)])

time: 155 us -> 154 us (level)
  waiting for transfers between devices: 110 us -> 104 us
  starting transfers between devices: 17.4 us -> 21.9 us
    ppermute x5, waiting for transfers between devices: 95.6 us -> 57.9 us  [hop(): return lax.ppermute(value, 'col', pairs)]
    ppermute x1, waiting for transfers between devices: 0.01 us -> 32.1 us  [line(): met = lax.ppermute(right_own, 'row', [(0, 1), (1, 0)])]
    ppermute x5, starting transfers between devices: 7.46 us -> 11 us  [hop(): return lax.ppermute(value, 'col', pairs)]
  transfers between devices with their start and end apart: 14 -> 14, of which waited for: 9 -> 11; matrix products, arithmetic and copies ran while one was open for 1% -> 1% of each run, Pallas kernels for 13% -> 13%
where the time goes in v16:
time: 154 us
  waiting for transfers between devices  104 us (68%)
  Pallas kernels  25.6 us (17%)
  starting transfers between devices  21.9 us (14%)
  local copies, waits for them, and re-layouts  1.93 us (1%)
    ppermute x5, waiting for transfers between devices, hop(): return lax.ppermute(value, 'col', pairs)  57.9 us
    ppermute x1, waiting for transfers between devices, line(): met = lax.ppermute(right_own, 'row', [(0, 1), (1, 0)])  32.1 us
    pallas_call x1, Pallas kernels, product_sums(): pl.pallas_call(functools.partial(sum_kernel, panel_spans, right_spans, gi...  16 us
    ppermute x8, waiting for transfers between devices, swapped(): return lax.ppermute(value, 'dep', [(0, 1), (1, 0)])  14 us
    ppermute x5, starting transfers between devices, hop(): return lax.ppermute(value, 'col', pairs)  11 us
    ppermute x8, starting transfers between devices, swapped(): return lax.ppermute(value, 'dep', [(0, 1), (1, 0)])  9.66 us
    pallas_call x2, Pallas kernels, add_panel(): pl.pallas_call(functools.partial(panel_kernel, shape, layer, kind_at, fin...  8.67 us
  transfers between devices with their start and end apart: 14, of which 11 were waited for; matrix products, arithmetic and copies ran while one was open for 1% of the time, Pallas kernels for 13%

profile of v16, /device:TPU:1, one launch (start us, length us, event | category | flops | bytes accessed | tf_op | source)
XLA Modules:
  0.0 153.6 jit_solution(13223614782526217180)
XLA Ops:
  0.0 2.0 %collective-permute-start.3 = (bf16[64,128,128]{2,1,0:T(8,128)(2,1)}, bf16[64,128,128]{2,1,0:T(8,128)(2,1)}, u32[]{:S(2)}, u32[]{:S(2)}) collective-permute-start(bf16[64,128,128]{2,1,0:T(8,128)(2,1)} %bitcast.37), channel_id=1, source_target_pairs={{2,4},{4,2},{3,5},{5,3},{10,12},{12,10},{11,13},{13,11},{18,20},{2... | collective-permute-start | bytes 6291464 | tf_op jit(solution)/shard_map/ppermute | solution.py:316
  2.0 3.4 %collective-permute-start.2 = (bf16[64,128,128]{2,1,0:T(8,128)(2,1)}, bf16[64,128,128]{2,1,0:T(8,128)(2,1)}, u32[]{:S(2)}, u32[]{:S(2)}) collective-permute-start(bf16[64,128,128]{2,1,0:T(8,128)(2,1)} %bitcast.38), channel_id=1, source_target_pairs={{0,2},{2,0},{4,6},{6,4},{1,3},{3,1},{5,7},{7,5},{8,10},{10,8},{12,... | collective-permute-start | bytes 6291464 | tf_op jit(solution)/shard_map/ppermute | solution.py:316
  5.4 1.2 collective-permute-start.4
  6.6 3.0 %collective-permute-start = (bf16[64,128,128]{2,1,0:T(8,128)(2,1)}, bf16[64,128,128]{2,1,0:T(8,128)(2,1)S(1)}, u32[]{:S(2)}, u32[]{:S(2)}) collective-permute-start(bf16[64,128,128]{2,1,0:T(8,128)(2,1)} %bitcast.39), channel_id=1, source_target_pairs={{0,4},{6,2},{1,5},{7,3},{8,12},{14,10},{9,13},{15,11},{16,20},{22,... | collective-permute-start | bytes 6291464 | tf_op jit(solution)/shard_map/ppermute | solution.py:316
  9.7 1.6 %collective-permute-start.1 = (bf16[56,128,128]{2,1,0:T(8,128)(2,1)}, bf16[56,128,128]{2,1,0:T(8,128)(2,1)}, u32[]{:S(2)}, u32[]{:S(2)}) collective-permute-start(bf16[56,128,128]{2,1,0:T(8,128)(2,1)} %bitcast.42), channel_id=1, source_target_pairs={{0,1},{1,0},{2,3},{3,2},{4,5},{5,4},{6,7},{7,6},{8,9},{9,8},{10,11... | collective-permute-start | bytes 5505032 | tf_op jit(solution)/shard_map/ppermute | solution.py:258
  11.2 0.7 copy.13
  12.5 1.3 collective-permute-start.8
  13.9 32.1 %collective-permute-done.4.refs_3_ = bf16[56,128,128]{2,1,0:T(8,128)(2,1)} collective-permute-done((bf16[56,128,128]{2,1,0:T(8,128)(2,1)}, bf16[56,128,128]{2,1,0:T(8,128)(2,1)}, u32[]{:S(2)}, u32[]{:S(2)}) %collective-permute-start.4) | collective-permute-done | bytes 1835040 | tf_op jit(solution)/shard_map/ppermute | solution.py:322
  46.0 4.8 %collective-permute-done.2.refs_7_ = bf16[64,128,128]{2,1,0:T(8,128)(2,1)} collective-permute-done((bf16[64,128,128]{2,1,0:T(8,128)(2,1)}, bf16[64,128,128]{2,1,0:T(8,128)(2,1)}, u32[]{:S(2)}, u32[]{:S(2)}) %collective-permute-start.2) | collective-permute-done | bytes 2097184 | tf_op jit(solution)/shard_map/ppermute | solution.py:316
  50.8 2.3 %collective-permute-start.5 = (bf16[56,128,128]{2,1,0:T(8,128)(2,1)}, bf16[56,128,128]{2,1,0:T(8,128)(2,1)}, u32[]{:S(2)}, u32[]{:S(2)}) collective-permute-start(bf16[56,128,128]{2,1,0:T(8,128)(2,1)} %collective-permute-done.4.refs_3_), channel_id=1, source_target_pairs={{0,1},{1,0},{2,3},{3,2},{4,5},{5,4},{6,7},{7,6},{8,9},{9,8},{10,11... | collective-permute-start | bytes 5505032 | tf_op jit(solution)/shard_map/ppermute | solution.py:258
  53.3 3.0 %collective-permute-done.6 = s32[7,3,64]{2,0,1:T(8,128)S(1)} collective-permute-done((s32[7,3,64]{2,0,1:T(8,128)S(1)}, s32[7,3,64]{2,0,1:T(8,128)S(1)}, u32[]{:S(2)}, u32[]{:S(2)}) %collective-permute-start.6) | collective-permute-done | bytes 5408 | tf_op jit(solution)/shard_map/ppermute | solution.py:258
  56.7 37.9 %collective-permute-done.refs_9_ = bf16[64,128,128]{2,1,0:T(8,128)(2,1)S(1)} collective-permute-done((bf16[64,128,128]{2,1,0:T(8,128)(2,1)}, bf16[64,128,128]{2,1,0:T(8,128)(2,1)S(1)}, u32[]{:S(2)}, u32[]{:S(2)}) %collective-permute-start) | collective-permute-done | bytes 2097184 | tf_op jit(solution)/shard_map/ppermute | solution.py:316
  94.6 1.3 collective-permute-start.7
  95.9 0.7 collective-permute-done.8.refs_10_
  96.6 16.0 %shard_map.37 = (f32[28,128,128]{2,1,0:T(8,128)S(1)}, f32[28,128,128]{2,1,0:T(8,128)S(1)}, f32[28,128,128]{2,1,0:T(8,128)S(1)}, f32[28,128,128]{2,1,0:T(8,128)},...) custom-call(s32[448]{0:T(512)S(1)} %fusion.17.refs_0_, s32[7]{0:T(128)S(1)} %stack.33.refs_1_.scalars, ...), custom_call_target="tpu_custom_call" | custom-call | flops 1 | bytes 1 | tf_op jit(solution)/shard_map/pallas_call | solution.py:161
  112.6 2.4 %collective-permute-start.10 = (f32[28,128,128]{2,1,0:T(8,128)S(1)}, f32[28,128,128]{2,1,0:T(8,128)S(1)}, u32[]{:S(2)}, u32[]{:S(2)}) collective-permute-start(f32[28,128,128]{2,1,0:T(8,128)S(1)} %get-tuple-element.35), channel_id=1, source_target_pairs={{0,1},{1,0},{2,3},{3,2},{4,5},{5,4},{6,7},{7,6},{8,9},{9,8},{10,11... | collective-permute-start | bytes 5505032 | tf_op jit(solution)/shard_map/ppermute | solution.py:258
  115.6 2.8 %collective-permute-done.10.refs_1_ = f32[28,128,128]{2,1,0:T(8,128)S(1)} collective-permute-done((f32[28,128,128]{2,1,0:T(8,128)S(1)}, f32[28,128,128]{2,1,0:T(8,128)S(1)}, u32[]{:S(2)}, u32[]{:S(2)}) %collective-permute-start.10) | collective-permute-done | bytes 1835040 | tf_op jit(solution)/shard_map/ppermute | solution.py:258
  118.4 5.2 %collective-permute-done.11.refs_2_ = f32[28,128,128]{2,1,0:T(8,128)S(1)} collective-permute-done((f32[28,128,128]{2,1,0:T(8,128)S(1)}, f32[28,128,128]{2,1,0:T(8,128)S(1)}, u32[]{:S(2)}, u32[]{:S(2)}) %collective-permute-start.11) | collective-permute-done | bytes 1835040 | tf_op jit(solution)/shard_map/ppermute | solution.py:258
  123.9 2.4 %collective-permute-done.9.refs_0_ = f32[28,128,128]{2,1,0:T(8,128)S(1)} collective-permute-done((f32[28,128,128]{2,1,0:T(8,128)S(1)}, f32[28,128,128]{2,1,0:T(8,128)S(1)}, u32[]{:S(2)}, u32[]{:S(2)}) %collective-permute-start.9) | collective-permute-done | bytes 1835040 | tf_op jit(solution)/shard_map/ppermute | solution.py:258
  126.3 0.9 shard_map.38.given
  127.3 14.5 %collective-permute-done.7.left = bf16[64,128,128]{2,1,0:T(8,128)(2,1)S(1)} collective-permute-done((bf16[64,128,128]{2,1,0:T(8,128)(2,1)S(1)}, bf16[64,128,128]{2,1,0:T(8,128)(2,1)S(1)}, u32[]{:S(2)}, u32[]{:S(2)}) %collective-permute-start.7) | collective-permute-done | bytes 2097184 | tf_op jit(solution)/shard_map/ppermute | solution.py:316
  141.8 2.8 %collective-permute-start.13 = (bf16[64,128,128]{2,1,0:T(8,128)(2,1)S(1)}, bf16[64,128,128]{2,1,0:T(8,128)(2,1)S(1)}, u32[]{:S(2)}, u32[]{:S(2)}) collective-permute-start(bf16[64,128,128]{2,1,0:T(8,128)(2,1)S(1)} %collective-permute-done.7.left), channel_id=1, source_target_pairs={{0,1},{1,0},{2,3},{3,2},{4,5},{5,4},{6,7},{7,6},{8,9},{9,8},{10,11... | collective-permute-start | bytes 6291464 | tf_op jit(solution)/shard_map/ppermute | solution.py:258
  144.6 3.5 %shard_map.39.given = f32[113,128,128]{2,1,0:T(8,128)S(1)} custom-call(s32[896]{0:T(1024)S(1)} %fusion.10.packed, s32[7]{0:T(128)S(1)} %stack.33.refs_1_.scalars, bf16[224,128,128]{2,1,0:T(8,128)(2,1)S(1)} %get-tuple-element.39.right, f32[113,128,128]{2,1,0:T(8,128)S(1)} %shard_map.38.given, ...), custom_call_target="tpu_custom_call", output_to_operand_aliasing={{}: (3, {})} | custom-call | flops 1 | bytes 1 | tf_op jit(solution)/shard_map/pallas_call | solution.py:241
  148.4 5.2 %shard_map.40 = (bf16[112,128,128]{2,1,0:T(8,128)(2,1)}, f32[113,128,128]{2,1,0:T(8,128)S(1)}) custom-call(s32[896]{0:T(1024)S(1)} %fusion.10.packed, s32[7]{0:T(128)S(1)} %stack.33.refs_1_.scalars, bf16[224,128,128]{2,1,0:T(8,128)(2,1)S(1)} %get-tuple-element.39.right, f32[113,128,128]{2,1,0:T(8,128)S(1)} %shard_map.39.given, ...), custom_call_target="tpu_custom_call", output_to_operand_aliasing={{1}: (3, {})} | custom-call | flops 1 | bytes 1 | tf_op jit(solution)/shard_map/pallas_call | solution.py:241
  (35 shorter events, 2.4 us)
Async XLA Ops:
  0.0 12.5 %collective-permute-start.3 = (bf16[64,128,128]{2,1,0:T(8,128)(2,1)}, bf16[64,128,128]{2,1,0:T(8,128)(2,1)}, u32[]{:S(2)}, u32[]{:S(2)}) collective-permute-start(bf16[64,128,128]{2,1,0:T(8,128)(2,1)} %bitcast.37), channel_id=1, source_target_pairs={{2,4},{4,2},{3,5},{5,3},{10,12},{12,10},{11,13},{13,11},{18,20},{2... | collective-permute-start | bytes 6291464 | tf_op jit(solution)/shard_map/ppermute | solution.py:316
  2.0 48.8 %collective-permute-start.2 = (bf16[64,128,128]{2,1,0:T(8,128)(2,1)}, bf16[64,128,128]{2,1,0:T(8,128)(2,1)}, u32[]{:S(2)}, u32[]{:S(2)}) collective-permute-start(bf16[64,128,128]{2,1,0:T(8,128)(2,1)} %bitcast.38), channel_id=1, source_target_pairs={{0,2},{2,0},{4,6},{6,4},{1,3},{3,1},{5,7},{7,5},{8,10},{10,8},{12,... | collective-permute-start | bytes 6291464 | tf_op jit(solution)/shard_map/ppermute | solution.py:316
  5.4 40.6 %collective-permute-start.4 = (bf16[56,128,128]{2,1,0:T(8,128)(2,1)}, bf16[56,128,128]{2,1,0:T(8,128)(2,1)}, u32[]{:S(2)}, u32[]{:S(2)}) collective-permute-start(bf16[56,128,128]{2,1,0:T(8,128)(2,1)} %bitcast.41), channel_id=1, source_target_pairs={{0,8},{8,0},{1,9},{9,1},{2,10},{10,2},{3,11},{11,3},{4,12},{12,4},... | collective-permute-start | bytes 5505032 | tf_op jit(solution)/shard_map/ppermute | solution.py:322
  6.6 88.0 %collective-permute-start = (bf16[64,128,128]{2,1,0:T(8,128)(2,1)}, bf16[64,128,128]{2,1,0:T(8,128)(2,1)S(1)}, u32[]{:S(2)}, u32[]{:S(2)}) collective-permute-start(bf16[64,128,128]{2,1,0:T(8,128)(2,1)} %bitcast.39), channel_id=1, source_target_pairs={{0,4},{6,2},{1,5},{7,3},{8,12},{14,10},{9,13},{15,11},{16,20},{22,... | collective-permute-start | bytes 6291464 | tf_op jit(solution)/shard_map/ppermute | solution.py:316
  9.7 47.1 %collective-permute-start.1 = (bf16[56,128,128]{2,1,0:T(8,128)(2,1)}, bf16[56,128,128]{2,1,0:T(8,128)(2,1)}, u32[]{:S(2)}, u32[]{:S(2)}) collective-permute-start(bf16[56,128,128]{2,1,0:T(8,128)(2,1)} %bitcast.42), channel_id=1, source_target_pairs={{0,1},{1,0},{2,3},{3,2},{4,5},{5,4},{6,7},{7,6},{8,9},{9,8},{10,11... | collective-permute-start | bytes 5505032 | tf_op jit(solution)/shard_map/ppermute | solution.py:258
  12.5 84.1 %collective-permute-start.8 = (bf16[64,128,128]{2,1,0:T(8,128)(2,1)}, bf16[64,128,128]{2,1,0:T(8,128)(2,1)}, u32[]{:S(2)}, u32[]{:S(2)}) collective-permute-start(bf16[64,128,128]{2,1,0:T(8,128)(2,1)} %collective-permute-done.3.refs_8_), channel_id=1, source_target_pairs={{4,6},{2,0},{5,7},{3,1},{12,14},{10,8},{13,15},{11,9},{20,22},{18,... | collective-permute-start | bytes 6291464 | tf_op jit(solution)/shard_map/ppermute | solution.py:316
  50.8 43.9 %collective-permute-start.5 = (bf16[56,128,128]{2,1,0:T(8,128)(2,1)}, bf16[56,128,128]{2,1,0:T(8,128)(2,1)}, u32[]{:S(2)}, u32[]{:S(2)}) collective-permute-start(bf16[56,128,128]{2,1,0:T(8,128)(2,1)} %collective-permute-done.4.refs_3_), channel_id=1, source_target_pairs={{0,1},{1,0},{2,3},{3,2},{4,5},{5,4},{6,7},{7,6},{8,9},{9,8},{10,11... | collective-permute-start | bytes 5505032 | tf_op jit(solution)/shard_map/ppermute | solution.py:258
  53.0 3.3 %collective-permute-start.6 = (s32[7,3,64]{2,0,1:T(8,128)S(1)}, s32[7,3,64]{2,0,1:T(8,128)S(1)}, u32[]{:S(2)}, u32[]{:S(2)}) collective-permute-start(s32[7,3,64]{2,0,1:T(8,128)S(1)} %bitcast.46), channel_id=1, source_target_pairs={{0,1},{1,0},{2,3},{3,2},{4,5},{5,4},{6,7},{7,6},{8,9},{9,8},{10,11... | collective-permute-start | bytes 16136 | tf_op jit(solution)/shard_map/ppermute | solution.py:258
  94.6 2.0 %copy-start = (bf16[64,128,128]{2,1,0:T(8,128)(2,1)}, bf16[64,128,128]{2,1,0:T(8,128)(2,1)S(1)}, u32[]{:S(2)}) copy-start(bf16[64,128,128]{2,1,0:T(8,128)(2,1)S(1)} %collective-permute-done.refs_9_) | copy-start | bytes 6291460
  94.6 47.1 %collective-permute-start.7 = (bf16[64,128,128]{2,1,0:T(8,128)(2,1)S(1)}, bf16[64,128,128]{2,1,0:T(8,128)(2,1)S(1)}, u32[]{:S(2)}, u32[]{:S(2)}) collective-permute-start(bf16[64,128,128]{2,1,0:T(8,128)(2,1)S(1)} %collective-permute-done.refs_9_), channel_id=1, source_target_pairs={{4,6},{2,0},{5,7},{3,1},{12,14},{10,8},{13,15},{11,9},{20,22},{18,... | collective-permute-start | bytes 6291464 | tf_op jit(solution)/shard_map/ppermute | solution.py:316
  112.6 5.9 %collective-permute-start.10 = (f32[28,128,128]{2,1,0:T(8,128)S(1)}, f32[28,128,128]{2,1,0:T(8,128)S(1)}, u32[]{:S(2)}, u32[]{:S(2)}) collective-permute-start(f32[28,128,128]{2,1,0:T(8,128)S(1)} %get-tuple-element.35), channel_id=1, source_target_pairs={{0,1},{1,0},{2,3},{3,2},{4,5},{5,4},{6,7},{7,6},{8,9},{9,8},{10,11... | collective-permute-start | bytes 5505032 | tf_op jit(solution)/shard_map/ppermute | solution.py:258
  115.0 8.7 %collective-permute-start.11 = (f32[28,128,128]{2,1,0:T(8,128)S(1)}, f32[28,128,128]{2,1,0:T(8,128)S(1)}, u32[]{:S(2)}, u32[]{:S(2)}) collective-permute-start(f32[28,128,128]{2,1,0:T(8,128)S(1)} %get-tuple-element.36), channel_id=1, source_target_pairs={{0,1},{1,0},{2,3},{3,2},{4,5},{5,4},{6,7},{7,6},{8,9},{9,8},{10,11... | collective-permute-start | bytes 5505032 | tf_op jit(solution)/shard_map/ppermute | solution.py:258
  115.1 8.8 %collective-permute-start.12 = (f32[28,128,128]{2,1,0:T(8,128)}, f32[28,128,128]{2,1,0:T(8,128)S(1)}, u32[]{:S(2)}, u32[]{:S(2)}) collective-permute-start(f32[28,128,128]{2,1,0:T(8,128)} %get-tuple-element.37), channel_id=1, source_target_pairs={{0,1},{1,0},{2,3},{3,2},{4,5},{5,4},{6,7},{7,6},{8,9},{9,8},{10,11... | collective-permute-start | bytes 5505032 | tf_op jit(solution)/shard_map/ppermute | solution.py:258
  115.5 10.8 %collective-permute-start.9 = (f32[28,128,128]{2,1,0:T(8,128)S(1)}, f32[28,128,128]{2,1,0:T(8,128)S(1)}, u32[]{:S(2)}, u32[]{:S(2)}) collective-permute-start(f32[28,128,128]{2,1,0:T(8,128)S(1)} %get-tuple-element.34), channel_id=1, source_target_pairs={{0,1},{1,0},{2,3},{3,2},{4,5},{5,4},{6,7},{7,6},{8,9},{9,8},{10,11... | collective-permute-start | bytes 5505032 | tf_op jit(solution)/shard_map/ppermute | solution.py:258
  141.8 6.6 %collective-permute-start.13 = (bf16[64,128,128]{2,1,0:T(8,128)(2,1)S(1)}, bf16[64,128,128]{2,1,0:T(8,128)(2,1)S(1)}, u32[]{:S(2)}, u32[]{:S(2)}) collective-permute-start(bf16[64,128,128]{2,1,0:T(8,128)(2,1)S(1)} %collective-permute-done.7.left), channel_id=1, source_target_pairs={{0,1},{1,0},{2,3},{3,2},{4,5},{5,4},{6,7},{7,6},{8,9},{9,8},{10,11... | collective-permute-start | bytes 6291464 | tf_op jit(solution)/shard_map/ppermute | solution.py:258

commit v17 on v16

--- a/solution.py
+++ b/solution.py
@@ -318,8 +318,10 @@
     def right_slot(slot, layers):
         return (layers * 2 + ((slot // part) ^ lax.axis_index("row"))) * part + slot % part
 
-    beside_one, across_one, across_two = hop(own, beside), hop(own, across), hop(own, [(0, 2), (3, 1)])
+    beside_one, across_one = hop(own, beside), hop(own, across)
     met = lax.ppermute(right_own, "row", [(0, 1), (1, 0)])
+    sent_late, met = fence((own, met))
+    across_two = hop(sent_late, [(0, 2), (3, 1)])
     listed = layer_products(step_lists, layer, half, right_slot)
     classes = [0, jnp.where(place % 2 == 0, 1, 3), jnp.where(inner, jnp.where(low, 1, 3), -1)]
     classes += [jnp.where(inner, 2, -1), jnp.where(inner, -1, 2)]

time: 154 us -> 155 us (level)
  starting transfers between devices: 21.9 us -> 24.6 us
  waiting for transfers between devices: 104 us -> 102 us
    ppermute x5, waiting for transfers between devices: 57.9 us -> 54.9 us  [hop(): return lax.ppermute(value, 'col', pairs)]
  transfers between devices with their start and end apart: 14 -> 14, of which waited for: 11 -> 10; matrix products, arithmetic and copies ran while one was open for 1% -> 1% of each run, Pallas kernels for 13% -> 13%
where the time goes in v17:
time: 155 us
  waiting for transfers between devices  102 us (66%)
  Pallas kernels  25.6 us (17%)
  starting transfers between devices  24.6 us (16%)
  local copies, waits for them, and re-layouts  1.93 us (1%)
    ppermute x5, waiting for transfers between devices, hop(): return lax.ppermute(value, 'col', pairs)  54.9 us
    ppermute x1, waiting for transfers between devices, line(): met = lax.ppermute(right_own, 'row', [(0, 1), (1, 0)])  33.2 us
    pallas_call x1, Pallas kernels, product_sums(): pl.pallas_call(functools.partial(sum_kernel, panel_spans, right_spans, gi...  16 us
    ppermute x8, waiting for transfers between devices, swapped(): return lax.ppermute(value, 'dep', [(0, 1), (1, 0)])  14.2 us
    ppermute x5, starting transfers between devices, hop(): return lax.ppermute(value, 'col', pairs)  11.4 us
    ppermute x8, starting transfers between devices, swapped(): return lax.ppermute(value, 'dep', [(0, 1), (1, 0)])  11.1 us
    pallas_call x2, Pallas kernels, add_panel(): pl.pallas_call(functools.partial(panel_kernel, shape, layer, kind_at, fin...  8.73 us
  transfers between devices with their start and end apart: 14, of which 10 were waited for; matrix products, arithmetic and copies ran while one was open for 1% of the time, Pallas kernels for 13%

profile of v17, /device:TPU:1, one launch (start us, length us, event | category | flops | bytes accessed | tf_op | source)
XLA Modules:
  0.0 154.7 jit_solution(2497998607676475147)
XLA Ops:
  0.0 2.0 %collective-permute-start = (bf16[56,128,128]{2,1,0:T(8,128)(2,1)}, bf16[56,128,128]{2,1,0:T(8,128)(2,1)}, u32[]{:S(2)}, u32[]{:S(2)}) collective-permute-start(bf16[56,128,128]{2,1,0:T(8,128)(2,1)} %bitcast.41), channel_id=1, source_target_pairs={{0,8},{8,0},{1,9},{9,1},{2,10},{10,2},{3,11},{11,3},{4,12},{12,4},... | collective-permute-start | bytes 5505032 | tf_op jit(solution)/shard_map/ppermute | solution.py:322
  2.0 2.0 %collective-permute-start.4 = (bf16[64,128,128]{2,1,0:T(8,128)(2,1)}, bf16[64,128,128]{2,1,0:T(8,128)(2,1)}, u32[]{:S(2)}, u32[]{:S(2)}) collective-permute-start(bf16[64,128,128]{2,1,0:T(8,128)(2,1)} %bitcast.37), channel_id=1, source_target_pairs={{2,4},{4,2},{3,5},{5,3},{10,12},{12,10},{11,13},{13,11},{18,20},{2... | collective-permute-start | bytes 6291464 | tf_op jit(solution)/shard_map/ppermute | solution.py:316
  4.0 2.6 %collective-permute-start.3 = (bf16[64,128,128]{2,1,0:T(8,128)(2,1)}, bf16[64,128,128]{2,1,0:T(8,128)(2,1)}, u32[]{:S(2)}, u32[]{:S(2)}) collective-permute-start(bf16[64,128,128]{2,1,0:T(8,128)(2,1)} %bitcast.38), channel_id=1, source_target_pairs={{0,2},{2,0},{4,6},{6,4},{1,3},{3,1},{5,7},{7,5},{8,10},{10,8},{12,... | collective-permute-start | bytes 6291464 | tf_op jit(solution)/shard_map/ppermute | solution.py:316
  6.6 1.5 collective-permute-start.2
  8.1 0.7 copy.13
  8.8 33.2 %collective-permute-done.refs_3_ = bf16[56,128,128]{2,1,0:T(8,128)(2,1)} collective-permute-done((bf16[56,128,128]{2,1,0:T(8,128)(2,1)}, bf16[56,128,128]{2,1,0:T(8,128)(2,1)}, u32[]{:S(2)}, u32[]{:S(2)}) %collective-permute-start) | collective-permute-done | bytes 1835040 | tf_op jit(solution)/shard_map/ppermute | solution.py:322
  42.1 4.3 %collective-permute-start.1 = (bf16[64,128,128]{2,1,0:T(8,128)(2,1)}, bf16[64,128,128]{2,1,0:T(8,128)(2,1)S(1)}, u32[]{:S(2)}, u32[]{:S(2)}) collective-permute-start(bf16[64,128,128]{2,1,0:T(8,128)(2,1)} %bitcast.39), channel_id=1, source_target_pairs={{0,4},{6,2},{1,5},{7,3},{8,12},{14,10},{9,13},{15,11},{16,20},{22,... | collective-permute-start | bytes 6291464 | tf_op jit(solution)/shard_map/ppermute | solution.py:316
  46.9 1.3 collective-permute-start.8
  48.3 3.3 %collective-permute-done.3.refs_7_ = bf16[64,128,128]{2,1,0:T(8,128)(2,1)} collective-permute-done((bf16[64,128,128]{2,1,0:T(8,128)(2,1)}, bf16[64,128,128]{2,1,0:T(8,128)(2,1)}, u32[]{:S(2)}, u32[]{:S(2)}) %collective-permute-start.3) | collective-permute-done | bytes 2097184 | tf_op jit(solution)/shard_map/ppermute | solution.py:316
  51.6 2.9 %collective-permute-start.5 = (bf16[56,128,128]{2,1,0:T(8,128)(2,1)}, bf16[56,128,128]{2,1,0:T(8,128)(2,1)}, u32[]{:S(2)}, u32[]{:S(2)}) collective-permute-start(bf16[56,128,128]{2,1,0:T(8,128)(2,1)} %collective-permute-done.refs_3_), channel_id=1, source_target_pairs={{0,1},{1,0},{2,3},{3,2},{4,5},{5,4},{6,7},{7,6},{8,9},{9,8},{10,11... | collective-permute-start | bytes 5505032 | tf_op jit(solution)/shard_map/ppermute | solution.py:258
  54.8 3.0 %collective-permute-done.6 = s32[7,3,64]{2,0,1:T(8,128)S(1)} collective-permute-done((s32[7,3,64]{2,0,1:T(8,128)S(1)}, s32[7,3,64]{2,0,1:T(8,128)S(1)}, u32[]{:S(2)}, u32[]{:S(2)}) %collective-permute-start.6) | collective-permute-done | bytes 5408 | tf_op jit(solution)/shard_map/ppermute | solution.py:258
  58.3 37.2 %collective-permute-done.1.refs_9_ = bf16[64,128,128]{2,1,0:T(8,128)(2,1)S(1)} collective-permute-done((bf16[64,128,128]{2,1,0:T(8,128)(2,1)}, bf16[64,128,128]{2,1,0:T(8,128)(2,1)S(1)}, u32[]{:S(2)}, u32[]{:S(2)}) %collective-permute-start.1) | collective-permute-done | bytes 2097184 | tf_op jit(solution)/shard_map/ppermute | solution.py:316
  95.6 1.3 collective-permute-start.7
  96.9 16.0 %shard_map.37 = (f32[28,128,128]{2,1,0:T(8,128)S(1)}, f32[28,128,128]{2,1,0:T(8,128)S(1)}, f32[28,128,128]{2,1,0:T(8,128)S(1)}, f32[28,128,128]{2,1,0:T(8,128)},...) custom-call(s32[448]{0:T(512)S(1)} %fusion.17.refs_0_, s32[7]{0:T(128)S(1)} %stack.33.refs_1_.scalars, ...), custom_call_target="tpu_custom_call" | custom-call | flops 1 | bytes 1 | tf_op jit(solution)/shard_map/pallas_call | solution.py:161
  112.9 3.1 %collective-permute-start.10 = (f32[28,128,128]{2,1,0:T(8,128)S(1)}, f32[28,128,128]{2,1,0:T(8,128)S(1)}, u32[]{:S(2)}, u32[]{:S(2)}) collective-permute-start(f32[28,128,128]{2,1,0:T(8,128)S(1)} %get-tuple-element.39), channel_id=1, source_target_pairs={{0,1},{1,0},{2,3},{3,2},{4,5},{5,4},{6,7},{7,6},{8,9},{9,8},{10,11... | collective-permute-start | bytes 5505032 | tf_op jit(solution)/shard_map/ppermute | solution.py:258
  116.5 2.8 %collective-permute-done.10.refs_1_ = f32[28,128,128]{2,1,0:T(8,128)S(1)} collective-permute-done((f32[28,128,128]{2,1,0:T(8,128)S(1)}, f32[28,128,128]{2,1,0:T(8,128)S(1)}, u32[]{:S(2)}, u32[]{:S(2)}) %collective-permute-start.10) | collective-permute-done | bytes 1835040 | tf_op jit(solution)/shard_map/ppermute | solution.py:258
  119.3 5.2 %collective-permute-done.11.refs_2_ = f32[28,128,128]{2,1,0:T(8,128)S(1)} collective-permute-done((f32[28,128,128]{2,1,0:T(8,128)S(1)}, f32[28,128,128]{2,1,0:T(8,128)S(1)}, u32[]{:S(2)}, u32[]{:S(2)}) %collective-permute-start.11) | collective-permute-done | bytes 1835040 | tf_op jit(solution)/shard_map/ppermute | solution.py:258
  124.8 2.4 %collective-permute-done.9.refs_0_ = f32[28,128,128]{2,1,0:T(8,128)S(1)} collective-permute-done((f32[28,128,128]{2,1,0:T(8,128)S(1)}, f32[28,128,128]{2,1,0:T(8,128)S(1)}, u32[]{:S(2)}, u32[]{:S(2)}) %collective-permute-start.9) | collective-permute-done | bytes 1835040 | tf_op jit(solution)/shard_map/ppermute | solution.py:258
  127.2 0.9 shard_map.38.given
  128.1 14.2 %collective-permute-done.7.left = bf16[64,128,128]{2,1,0:T(8,128)(2,1)S(1)} collective-permute-done((bf16[64,128,128]{2,1,0:T(8,128)(2,1)S(1)}, bf16[64,128,128]{2,1,0:T(8,128)(2,1)S(1)}, u32[]{:S(2)}, u32[]{:S(2)}) %collective-permute-start.7) | collective-permute-done | bytes 2097184 | tf_op jit(solution)/shard_map/ppermute | solution.py:316
  142.4 3.1 %collective-permute-start.13 = (bf16[64,128,128]{2,1,0:T(8,128)(2,1)S(1)}, bf16[64,128,128]{2,1,0:T(8,128)(2,1)S(1)}, u32[]{:S(2)}, u32[]{:S(2)}) collective-permute-start(bf16[64,128,128]{2,1,0:T(8,128)(2,1)S(1)} %collective-permute-done.7.left), channel_id=1, source_target_pairs={{0,1},{1,0},{2,3},{3,2},{4,5},{5,4},{6,7},{7,6},{8,9},{9,8},{10,11... | collective-permute-start | bytes 6291464 | tf_op jit(solution)/shard_map/ppermute | solution.py:258
  145.5 3.3 %shard_map.39.given = f32[113,128,128]{2,1,0:T(8,128)S(1)} custom-call(s32[896]{0:T(1024)S(1)} %fusion.10.packed, s32[7]{0:T(128)S(1)} %stack.33.refs_1_.scalars, bf16[224,128,128]{2,1,0:T(8,128)(2,1)S(1)} %get-tuple-element.43.right, f32[113,128,128]{2,1,0:T(8,128)S(1)} %shard_map.38.given, ...), custom_call_target="tpu_custom_call", output_to_operand_aliasing={{}: (3, {})} | custom-call | flops 1 | bytes 1 | tf_op jit(solution)/shard_map/pallas_call | solution.py:241
  148.8 0.5 collective-permute-done.13.left
  149.3 5.4 %shard_map.40 = (bf16[112,128,128]{2,1,0:T(8,128)(2,1)}, f32[113,128,128]{2,1,0:T(8,128)S(1)}) custom-call(s32[896]{0:T(1024)S(1)} %fusion.10.packed, s32[7]{0:T(128)S(1)} %stack.33.refs_1_.scalars, bf16[224,128,128]{2,1,0:T(8,128)(2,1)S(1)} %get-tuple-element.43.right, f32[113,128,128]{2,1,0:T(8,128)S(1)} %shard_map.39.given, ...), custom_call_target="tpu_custom_call", output_to_operand_aliasing={{1}: (3, {})} | custom-call | flops 1 | bytes 1 | tf_op jit(solution)/shard_map/pallas_call | solution.py:241
  (35 shorter events, 2.2 us)
Async XLA Ops:
  0.0 42.1 %collective-permute-start = (bf16[56,128,128]{2,1,0:T(8,128)(2,1)}, bf16[56,128,128]{2,1,0:T(8,128)(2,1)}, u32[]{:S(2)}, u32[]{:S(2)}) collective-permute-start(bf16[56,128,128]{2,1,0:T(8,128)(2,1)} %bitcast.41), channel_id=1, source_target_pairs={{0,8},{8,0},{1,9},{9,1},{2,10},{10,2},{3,11},{11,3},{4,12},{12,4},... | collective-permute-start | bytes 5505032 | tf_op jit(solution)/shard_map/ppermute | solution.py:322
  2.0 44.9 %collective-permute-start.4 = (bf16[64,128,128]{2,1,0:T(8,128)(2,1)}, bf16[64,128,128]{2,1,0:T(8,128)(2,1)}, u32[]{:S(2)}, u32[]{:S(2)}) collective-permute-start(bf16[64,128,128]{2,1,0:T(8,128)(2,1)} %bitcast.37), channel_id=1, source_target_pairs={{2,4},{4,2},{3,5},{5,3},{10,12},{12,10},{11,13},{13,11},{18,20},{2... | collective-permute-start | bytes 6291464 | tf_op jit(solution)/shard_map/ppermute | solution.py:316
  4.0 47.6 %collective-permute-start.3 = (bf16[64,128,128]{2,1,0:T(8,128)(2,1)}, bf16[64,128,128]{2,1,0:T(8,128)(2,1)}, u32[]{:S(2)}, u32[]{:S(2)}) collective-permute-start(bf16[64,128,128]{2,1,0:T(8,128)(2,1)} %bitcast.38), channel_id=1, source_target_pairs={{0,2},{2,0},{4,6},{6,4},{1,3},{3,1},{5,7},{7,5},{8,10},{10,8},{12,... | collective-permute-start | bytes 6291464 | tf_op jit(solution)/shard_map/ppermute | solution.py:316
  6.6 51.6 %collective-permute-start.2 = (bf16[56,128,128]{2,1,0:T(8,128)(2,1)}, bf16[56,128,128]{2,1,0:T(8,128)(2,1)}, u32[]{:S(2)}, u32[]{:S(2)}) collective-permute-start(bf16[56,128,128]{2,1,0:T(8,128)(2,1)} %bitcast.42), channel_id=1, source_target_pairs={{0,1},{1,0},{2,3},{3,2},{4,5},{5,4},{6,7},{7,6},{8,9},{9,8},{10,11... | collective-permute-start | bytes 5505032 | tf_op jit(solution)/shard_map/ppermute | solution.py:258
  42.1 53.5 %collective-permute-start.1 = (bf16[64,128,128]{2,1,0:T(8,128)(2,1)}, bf16[64,128,128]{2,1,0:T(8,128)(2,1)S(1)}, u32[]{:S(2)}, u32[]{:S(2)}) collective-permute-start(bf16[64,128,128]{2,1,0:T(8,128)(2,1)} %bitcast.39), channel_id=1, source_target_pairs={{0,4},{6,2},{1,5},{7,3},{8,12},{14,10},{9,13},{15,11},{16,20},{22,... | collective-permute-start | bytes 6291464 | tf_op jit(solution)/shard_map/ppermute | solution.py:316
  46.9 50.0 %collective-permute-start.8 = (bf16[64,128,128]{2,1,0:T(8,128)(2,1)}, bf16[64,128,128]{2,1,0:T(8,128)(2,1)}, u32[]{:S(2)}, u32[]{:S(2)}) collective-permute-start(bf16[64,128,128]{2,1,0:T(8,128)(2,1)} %collective-permute-done.4.refs_8_), channel_id=1, source_target_pairs={{4,6},{2,0},{5,7},{3,1},{12,14},{10,8},{13,15},{11,9},{20,22},{18,... | collective-permute-start | bytes 6291464 | tf_op jit(solution)/shard_map/ppermute | solution.py:316
  51.6 6.7 %collective-permute-start.5 = (bf16[56,128,128]{2,1,0:T(8,128)(2,1)}, bf16[56,128,128]{2,1,0:T(8,128)(2,1)}, u32[]{:S(2)}, u32[]{:S(2)}) collective-permute-start(bf16[56,128,128]{2,1,0:T(8,128)(2,1)} %collective-permute-done.refs_3_), channel_id=1, source_target_pairs={{0,1},{1,0},{2,3},{3,2},{4,5},{5,4},{6,7},{7,6},{8,9},{9,8},{10,11... | collective-permute-start | bytes 5505032 | tf_op jit(solution)/shard_map/ppermute | solution.py:258
  54.5 3.3 %collective-permute-start.6 = (s32[7,3,64]{2,0,1:T(8,128)S(1)}, s32[7,3,64]{2,0,1:T(8,128)S(1)}, u32[]{:S(2)}, u32[]{:S(2)}) collective-permute-start(s32[7,3,64]{2,0,1:T(8,128)S(1)} %bitcast.46), channel_id=1, source_target_pairs={{0,1},{1,0},{2,3},{3,2},{4,5},{5,4},{6,7},{7,6},{8,9},{9,8},{10,11... | collective-permute-start | bytes 16136 | tf_op jit(solution)/shard_map/ppermute | solution.py:258
  95.5 1.3 copy-start
  95.6 46.8 %collective-permute-start.7 = (bf16[64,128,128]{2,1,0:T(8,128)(2,1)S(1)}, bf16[64,128,128]{2,1,0:T(8,128)(2,1)S(1)}, u32[]{:S(2)}, u32[]{:S(2)}) collective-permute-start(bf16[64,128,128]{2,1,0:T(8,128)(2,1)S(1)} %collective-permute-done.1.refs_9_), channel_id=1, source_target_pairs={{4,6},{2,0},{5,7},{3,1},{12,14},{10,8},{13,15},{11,9},{20,22},{18,... | collective-permute-start | bytes 6291464 | tf_op jit(solution)/shard_map/ppermute | solution.py:316
  112.9 6.5 %collective-permute-start.10 = (f32[28,128,128]{2,1,0:T(8,128)S(1)}, f32[28,128,128]{2,1,0:T(8,128)S(1)}, u32[]{:S(2)}, u32[]{:S(2)}) collective-permute-start(f32[28,128,128]{2,1,0:T(8,128)S(1)} %get-tuple-element.39), channel_id=1, source_target_pairs={{0,1},{1,0},{2,3},{3,2},{4,5},{5,4},{6,7},{7,6},{8,9},{9,8},{10,11... | collective-permute-start | bytes 5505032 | tf_op jit(solution)/shard_map/ppermute | solution.py:258
  115.9 8.7 %collective-permute-start.11 = (f32[28,128,128]{2,1,0:T(8,128)S(1)}, f32[28,128,128]{2,1,0:T(8,128)S(1)}, u32[]{:S(2)}, u32[]{:S(2)}) collective-permute-start(f32[28,128,128]{2,1,0:T(8,128)S(1)} %get-tuple-element.40), channel_id=1, source_target_pairs={{0,1},{1,0},{2,3},{3,2},{4,5},{5,4},{6,7},{7,6},{8,9},{9,8},{10,11... | collective-permute-start | bytes 5505032 | tf_op jit(solution)/shard_map/ppermute | solution.py:258
  116.0 8.8 %collective-permute-start.12 = (f32[28,128,128]{2,1,0:T(8,128)}, f32[28,128,128]{2,1,0:T(8,128)S(1)}, u32[]{:S(2)}, u32[]{:S(2)}) collective-permute-start(f32[28,128,128]{2,1,0:T(8,128)} %get-tuple-element.41), channel_id=1, source_target_pairs={{0,1},{1,0},{2,3},{3,2},{4,5},{5,4},{6,7},{7,6},{8,9},{9,8},{10,11... | collective-permute-start | bytes 5505032 | tf_op jit(solution)/shard_map/ppermute | solution.py:258
  116.4 10.8 %collective-permute-start.9 = (f32[28,128,128]{2,1,0:T(8,128)S(1)}, f32[28,128,128]{2,1,0:T(8,128)S(1)}, u32[]{:S(2)}, u32[]{:S(2)}) collective-permute-start(f32[28,128,128]{2,1,0:T(8,128)S(1)} %get-tuple-element.38), channel_id=1, source_target_pairs={{0,1},{1,0},{2,3},{3,2},{4,5},{5,4},{6,7},{7,6},{8,9},{9,8},{10,11... | collective-permute-start | bytes 5505032 | tf_op jit(solution)/shard_map/ppermute | solution.py:258
  142.4 6.9 %collective-permute-start.13 = (bf16[64,128,128]{2,1,0:T(8,128)(2,1)S(1)}, bf16[64,128,128]{2,1,0:T(8,128)(2,1)S(1)}, u32[]{:S(2)}, u32[]{:S(2)}) collective-permute-start(bf16[64,128,128]{2,1,0:T(8,128)(2,1)S(1)} %collective-permute-done.7.left), channel_id=1, source_target_pairs={{0,1},{1,0},{2,3},{3,2},{4,5},{5,4},{6,7},{7,6},{8,9},{9,8},{10,11... | collective-permute-start | bytes 6291464 | tf_op jit(solution)/shard_map/ppermute | solution.py:258

commit v18 on v16

--- a/solution.py
+++ b/solution.py
@@ -8,8 +8,9 @@
 from jax.sharding import PartitionSpec as P
 
 NBQ = 32
-UNROLL = 8
+UNROLL = 16
 PARTS = 4
+OUT_PARTS = 8
 
 
 def chosen_products(packed, classes, panels, todo, shape, layers, spare, first_left=0):
@@ -216,10 +217,10 @@
     add_chosen(todo, count, left, right, work, first)
     if finish:
         out, rounded, sems = refs[0], refs[3], refs[4]
-        size = spare // PARTS
+        size = spare // OUT_PARTS
         copies = []
-        for index in range(PARTS):
-            span = pl.ds(index * size, size if index < PARTS - 1 else spare - index * size)
+        for index in range(OUT_PARTS):
+            span = pl.ds(index * size, size if index < OUT_PARTS - 1 else spare - index * size)
             rounded[span] = work[span].astype(rounded.dtype)
             copies.append(pltpu.make_async_copy(rounded.at[span], out.at[span], sems.at[index]))
             copies[-1].start()
@@ -237,7 +238,7 @@
         out_shape.insert(0, jax.ShapeDtypeStruct((result_slots, rows, width), jnp.bfloat16))
         out_specs.insert(0, pl.BlockSpec(memory_space=pl.ANY))
         scratch.append(pltpu.VMEM((result_slots, rows, width), jnp.bfloat16))
-        scratch.append(pltpu.SemaphoreType.DMA((PARTS,)))
+        scratch.append(pltpu.SemaphoreType.DMA((OUT_PARTS,)))
     return pl.pallas_call(
         functools.partial(panel_kernel, shape, layer, kind_at, finish),
         out_shape=out_shape,

time: 154 us -> 153 us (level)
  Pallas kernels: 25.6 us -> 21.3 us
  waiting for transfers between devices: 104 us -> 107 us
    pallas_call x1, Pallas kernels: 16 us -> 13.1 us  [product_sums(): pl.pallas_call(functools.partial(sum_kernel, panel_spans, right_spans, gi...]
    ppermute x5, waiting for transfers between devices: 57.9 us -> 60.7 us  [hop(): return lax.ppermute(value, 'col', pairs)]
  transfers between devices with their start and end apart: 14 -> 14, of which waited for: 11 -> 11; matrix products, arithmetic and copies ran while one was open for 1% -> 1% of each run, Pallas kernels for 13% -> 11%
where the time goes in v18:
time: 153 us
  waiting for transfers between devices  107 us (70%)
  starting transfers between devices  21.9 us (14%)
  Pallas kernels  21.3 us (14%)
  local copies, waits for them, and re-layouts  1.93 us (1%)
    ppermute x5, waiting for transfers between devices, hop(): return lax.ppermute(value, 'col', pairs)  60.7 us
    ppermute x1, waiting for transfers between devices, line(): met = lax.ppermute(right_own, 'row', [(0, 1), (1, 0)])  32.1 us
    ppermute x8, waiting for transfers between devices, swapped(): return lax.ppermute(value, 'dep', [(0, 1), (1, 0)])  14.7 us
    pallas_call x1, Pallas kernels, product_sums(): pl.pallas_call(functools.partial(sum_kernel, panel_spans, right_spans, gi...  13.1 us
    ppermute x5, starting transfers between devices, hop(): return lax.ppermute(value, 'col', pairs)  11 us
    ppermute x8, starting transfers between devices, swapped(): return lax.ppermute(value, 'dep', [(0, 1), (1, 0)])  9.67 us
    pallas_call x2, Pallas kernels, add_panel(): pl.pallas_call(functools.partial(panel_kernel, shape, layer, kind_at, fin...  7.21 us
  transfers between devices with their start and end apart: 14, of which 11 were waited for; matrix products, arithmetic and copies ran while one was open for 1% of the time, Pallas kernels for 11%

profile of v18, /device:TPU:1, one launch (start us, length us, event | category | flops | bytes accessed | tf_op | source)
XLA Modules:
  0.0 152.8 jit_solution(14449640873575874842)
XLA Ops:
  0.0 2.0 %collective-permute-start.3 = (bf16[64,128,128]{2,1,0:T(8,128)(2,1)}, bf16[64,128,128]{2,1,0:T(8,128)(2,1)}, u32[]{:S(2)}, u32[]{:S(2)}) collective-permute-start(bf16[64,128,128]{2,1,0:T(8,128)(2,1)} %bitcast.37), channel_id=1, source_target_pairs={{2,4},{4,2},{3,5},{5,3},{10,12},{12,10},{11,13},{13,11},{18,20},{2... | collective-permute-start | bytes 6291464 | tf_op jit(solution)/shard_map/ppermute | solution.py:317
  2.0 3.4 %collective-permute-start.2 = (bf16[64,128,128]{2,1,0:T(8,128)(2,1)}, bf16[64,128,128]{2,1,0:T(8,128)(2,1)}, u32[]{:S(2)}, u32[]{:S(2)}) collective-permute-start(bf16[64,128,128]{2,1,0:T(8,128)(2,1)} %bitcast.38), channel_id=1, source_target_pairs={{0,2},{2,0},{4,6},{6,4},{1,3},{3,1},{5,7},{7,5},{8,10},{10,8},{12,... | collective-permute-start | bytes 6291464 | tf_op jit(solution)/shard_map/ppermute | solution.py:317
  5.4 1.2 collective-permute-start.4
  6.6 3.0 %collective-permute-start = (bf16[64,128,128]{2,1,0:T(8,128)(2,1)}, bf16[64,128,128]{2,1,0:T(8,128)(2,1)S(1)}, u32[]{:S(2)}, u32[]{:S(2)}) collective-permute-start(bf16[64,128,128]{2,1,0:T(8,128)(2,1)} %bitcast.39), channel_id=1, source_target_pairs={{0,4},{6,2},{1,5},{7,3},{8,12},{14,10},{9,13},{15,11},{16,20},{22,... | collective-permute-start | bytes 6291464 | tf_op jit(solution)/shard_map/ppermute | solution.py:317
  9.7 1.6 %collective-permute-start.1 = (bf16[56,128,128]{2,1,0:T(8,128)(2,1)}, bf16[56,128,128]{2,1,0:T(8,128)(2,1)}, u32[]{:S(2)}, u32[]{:S(2)}) collective-permute-start(bf16[56,128,128]{2,1,0:T(8,128)(2,1)} %bitcast.42), channel_id=1, source_target_pairs={{0,1},{1,0},{2,3},{3,2},{4,5},{5,4},{6,7},{7,6},{8,9},{9,8},{10,11... | collective-permute-start | bytes 5505032 | tf_op jit(solution)/shard_map/ppermute | solution.py:259
  11.2 0.7 copy.13
  12.5 1.3 collective-permute-start.8
  13.9 32.1 %collective-permute-done.4.refs_3_ = bf16[56,128,128]{2,1,0:T(8,128)(2,1)} collective-permute-done((bf16[56,128,128]{2,1,0:T(8,128)(2,1)}, bf16[56,128,128]{2,1,0:T(8,128)(2,1)}, u32[]{:S(2)}, u32[]{:S(2)}) %collective-permute-start.4) | collective-permute-done | bytes 1835040 | tf_op jit(solution)/shard_map/ppermute | solution.py:323
  46.0 4.8 %collective-permute-done.2.refs_7_ = bf16[64,128,128]{2,1,0:T(8,128)(2,1)} collective-permute-done((bf16[64,128,128]{2,1,0:T(8,128)(2,1)}, bf16[64,128,128]{2,1,0:T(8,128)(2,1)}, u32[]{:S(2)}, u32[]{:S(2)}) %collective-permute-start.2) | collective-permute-done | bytes 2097184 | tf_op jit(solution)/shard_map/ppermute | solution.py:317
  50.8 2.3 %collective-permute-start.5 = (bf16[56,128,128]{2,1,0:T(8,128)(2,1)}, bf16[56,128,128]{2,1,0:T(8,128)(2,1)}, u32[]{:S(2)}, u32[]{:S(2)}) collective-permute-start(bf16[56,128,128]{2,1,0:T(8,128)(2,1)} %collective-permute-done.4.refs_3_), channel_id=1, source_target_pairs={{0,1},{1,0},{2,3},{3,2},{4,5},{5,4},{6,7},{7,6},{8,9},{9,8},{10,11... | collective-permute-start | bytes 5505032 | tf_op jit(solution)/shard_map/ppermute | solution.py:259
  53.3 3.0 %collective-permute-done.6 = s32[7,3,64]{2,0,1:T(8,128)S(1)} collective-permute-done((s32[7,3,64]{2,0,1:T(8,128)S(1)}, s32[7,3,64]{2,0,1:T(8,128)S(1)}, u32[]{:S(2)}, u32[]{:S(2)}) %collective-permute-start.6) | collective-permute-done | bytes 5408 | tf_op jit(solution)/shard_map/ppermute | solution.py:259
  56.7 37.9 %collective-permute-done.refs_9_ = bf16[64,128,128]{2,1,0:T(8,128)(2,1)S(1)} collective-permute-done((bf16[64,128,128]{2,1,0:T(8,128)(2,1)}, bf16[64,128,128]{2,1,0:T(8,128)(2,1)S(1)}, u32[]{:S(2)}, u32[]{:S(2)}) %collective-permute-start) | collective-permute-done | bytes 2097184 | tf_op jit(solution)/shard_map/ppermute | solution.py:317
  94.6 1.3 collective-permute-start.7
  96.6 13.1 %shard_map.37 = (f32[28,128,128]{2,1,0:T(8,128)S(1)}, f32[28,128,128]{2,1,0:T(8,128)S(1)}, f32[28,128,128]{2,1,0:T(8,128)S(1)}, f32[28,128,128]{2,1,0:T(8,128)},...) custom-call(s32[448]{0:T(512)S(1)} %fusion.17.refs_0_, s32[7]{0:T(128)S(1)} %stack.33.refs_1_.scalars, ...), custom_call_target="tpu_custom_call" | custom-call | flops 1 | bytes 1 | tf_op jit(solution)/shard_map/pallas_call | solution.py:162
  109.8 2.4 %collective-permute-start.10 = (f32[28,128,128]{2,1,0:T(8,128)S(1)}, f32[28,128,128]{2,1,0:T(8,128)S(1)}, u32[]{:S(2)}, u32[]{:S(2)}) collective-permute-start(f32[28,128,128]{2,1,0:T(8,128)S(1)} %get-tuple-element.35), channel_id=1, source_target_pairs={{0,1},{1,0},{2,3},{3,2},{4,5},{5,4},{6,7},{7,6},{8,9},{9,8},{10,11... | collective-permute-start | bytes 5505032 | tf_op jit(solution)/shard_map/ppermute | solution.py:259
  112.8 2.8 %collective-permute-done.10.refs_1_ = f32[28,128,128]{2,1,0:T(8,128)S(1)} collective-permute-done((f32[28,128,128]{2,1,0:T(8,128)S(1)}, f32[28,128,128]{2,1,0:T(8,128)S(1)}, u32[]{:S(2)}, u32[]{:S(2)}) %collective-permute-start.10) | collective-permute-done | bytes 1835040 | tf_op jit(solution)/shard_map/ppermute | solution.py:259
  115.6 5.2 %collective-permute-done.11.refs_2_ = f32[28,128,128]{2,1,0:T(8,128)S(1)} collective-permute-done((f32[28,128,128]{2,1,0:T(8,128)S(1)}, f32[28,128,128]{2,1,0:T(8,128)S(1)}, u32[]{:S(2)}, u32[]{:S(2)}) %collective-permute-start.11) | collective-permute-done | bytes 1835040 | tf_op jit(solution)/shard_map/ppermute | solution.py:259
  121.1 2.4 %collective-permute-done.9.refs_0_ = f32[28,128,128]{2,1,0:T(8,128)S(1)} collective-permute-done((f32[28,128,128]{2,1,0:T(8,128)S(1)}, f32[28,128,128]{2,1,0:T(8,128)S(1)}, u32[]{:S(2)}, u32[]{:S(2)}) %collective-permute-start.9) | collective-permute-done | bytes 1835040 | tf_op jit(solution)/shard_map/ppermute | solution.py:259
  123.5 0.9 shard_map.38.given
  124.4 17.3 %collective-permute-done.7.left = bf16[64,128,128]{2,1,0:T(8,128)(2,1)S(1)} collective-permute-done((bf16[64,128,128]{2,1,0:T(8,128)(2,1)S(1)}, bf16[64,128,128]{2,1,0:T(8,128)(2,1)S(1)}, u32[]{:S(2)}, u32[]{:S(2)}) %collective-permute-start.7) | collective-permute-done | bytes 2097184 | tf_op jit(solution)/shard_map/ppermute | solution.py:317
  141.8 2.8 %collective-permute-start.13 = (bf16[64,128,128]{2,1,0:T(8,128)(2,1)S(1)}, bf16[64,128,128]{2,1,0:T(8,128)(2,1)S(1)}, u32[]{:S(2)}, u32[]{:S(2)}) collective-permute-start(bf16[64,128,128]{2,1,0:T(8,128)(2,1)S(1)} %collective-permute-done.7.left), channel_id=1, source_target_pairs={{0,1},{1,0},{2,3},{3,2},{4,5},{5,4},{6,7},{7,6},{8,9},{9,8},{10,11... | collective-permute-start | bytes 6291464 | tf_op jit(solution)/shard_map/ppermute | solution.py:259
  144.6 2.8 %shard_map.39.given = f32[113,128,128]{2,1,0:T(8,128)S(1)} custom-call(s32[896]{0:T(1024)S(1)} %fusion.10.packed, s32[7]{0:T(128)S(1)} %stack.33.refs_1_.scalars, bf16[224,128,128]{2,1,0:T(8,128)(2,1)S(1)} %get-tuple-element.39.right, f32[113,128,128]{2,1,0:T(8,128)S(1)} %shard_map.38.given, ...), custom_call_target="tpu_custom_call", output_to_operand_aliasing={{}: (3, {})} | custom-call | flops 1 | bytes 1 | tf_op jit(solution)/shard_map/pallas_call | solution.py:242
  147.4 1.0 collective-permute-done.13.left
  148.4 4.4 %shard_map.40 = (bf16[112,128,128]{2,1,0:T(8,128)(2,1)}, f32[113,128,128]{2,1,0:T(8,128)S(1)}) custom-call(s32[896]{0:T(1024)S(1)} %fusion.10.packed, s32[7]{0:T(128)S(1)} %stack.33.refs_1_.scalars, bf16[224,128,128]{2,1,0:T(8,128)(2,1)S(1)} %get-tuple-element.39.right, f32[113,128,128]{2,1,0:T(8,128)S(1)} %shard_map.39.given, ...), custom_call_target="tpu_custom_call", output_to_operand_aliasing={{1}: (3, {})} | custom-call | flops 1 | bytes 1 | tf_op jit(solution)/shard_map/pallas_call | solution.py:242
  (35 shorter events, 2.8 us)
Async XLA Ops:
  0.0 12.5 %collective-permute-start.3 = (bf16[64,128,128]{2,1,0:T(8,128)(2,1)}, bf16[64,128,128]{2,1,0:T(8,128)(2,1)}, u32[]{:S(2)}, u32[]{:S(2)}) collective-permute-start(bf16[64,128,128]{2,1,0:T(8,128)(2,1)} %bitcast.37), channel_id=1, source_target_pairs={{2,4},{4,2},{3,5},{5,3},{10,12},{12,10},{11,13},{13,11},{18,20},{2... | collective-permute-start | bytes 6291464 | tf_op jit(solution)/shard_map/ppermute | solution.py:317
  2.0 48.8 %collective-permute-start.2 = (bf16[64,128,128]{2,1,0:T(8,128)(2,1)}, bf16[64,128,128]{2,1,0:T(8,128)(2,1)}, u32[]{:S(2)}, u32[]{:S(2)}) collective-permute-start(bf16[64,128,128]{2,1,0:T(8,128)(2,1)} %bitcast.38), channel_id=1, source_target_pairs={{0,2},{2,0},{4,6},{6,4},{1,3},{3,1},{5,7},{7,5},{8,10},{10,8},{12,... | collective-permute-start | bytes 6291464 | tf_op jit(solution)/shard_map/ppermute | solution.py:317
  5.4 40.6 %collective-permute-start.4 = (bf16[56,128,128]{2,1,0:T(8,128)(2,1)}, bf16[56,128,128]{2,1,0:T(8,128)(2,1)}, u32[]{:S(2)}, u32[]{:S(2)}) collective-permute-start(bf16[56,128,128]{2,1,0:T(8,128)(2,1)} %bitcast.41), channel_id=1, source_target_pairs={{0,8},{8,0},{1,9},{9,1},{2,10},{10,2},{3,11},{11,3},{4,12},{12,4},... | collective-permute-start | bytes 5505032 | tf_op jit(solution)/shard_map/ppermute | solution.py:323
  6.6 88.0 %collective-permute-start = (bf16[64,128,128]{2,1,0:T(8,128)(2,1)}, bf16[64,128,128]{2,1,0:T(8,128)(2,1)S(1)}, u32[]{:S(2)}, u32[]{:S(2)}) collective-permute-start(bf16[64,128,128]{2,1,0:T(8,128)(2,1)} %bitcast.39), channel_id=1, source_target_pairs={{0,4},{6,2},{1,5},{7,3},{8,12},{14,10},{9,13},{15,11},{16,20},{22,... | collective-permute-start | bytes 6291464 | tf_op jit(solution)/shard_map/ppermute | solution.py:317
  9.7 47.1 %collective-permute-start.1 = (bf16[56,128,128]{2,1,0:T(8,128)(2,1)}, bf16[56,128,128]{2,1,0:T(8,128)(2,1)}, u32[]{:S(2)}, u32[]{:S(2)}) collective-permute-start(bf16[56,128,128]{2,1,0:T(8,128)(2,1)} %bitcast.42), channel_id=1, source_target_pairs={{0,1},{1,0},{2,3},{3,2},{4,5},{5,4},{6,7},{7,6},{8,9},{9,8},{10,11... | collective-permute-start | bytes 5505032 | tf_op jit(solution)/shard_map/ppermute | solution.py:259
  12.5 84.1 %collective-permute-start.8 = (bf16[64,128,128]{2,1,0:T(8,128)(2,1)}, bf16[64,128,128]{2,1,0:T(8,128)(2,1)}, u32[]{:S(2)}, u32[]{:S(2)}) collective-permute-start(bf16[64,128,128]{2,1,0:T(8,128)(2,1)} %collective-permute-done.3.refs_8_), channel_id=1, source_target_pairs={{4,6},{2,0},{5,7},{3,1},{12,14},{10,8},{13,15},{11,9},{20,22},{18,... | collective-permute-start | bytes 6291464 | tf_op jit(solution)/shard_map/ppermute | solution.py:317
  50.8 43.9 %collective-permute-start.5 = (bf16[56,128,128]{2,1,0:T(8,128)(2,1)}, bf16[56,128,128]{2,1,0:T(8,128)(2,1)}, u32[]{:S(2)}, u32[]{:S(2)}) collective-permute-start(bf16[56,128,128]{2,1,0:T(8,128)(2,1)} %collective-permute-done.4.refs_3_), channel_id=1, source_target_pairs={{0,1},{1,0},{2,3},{3,2},{4,5},{5,4},{6,7},{7,6},{8,9},{9,8},{10,11... | collective-permute-start | bytes 5505032 | tf_op jit(solution)/shard_map/ppermute | solution.py:259
  53.0 3.3 %collective-permute-start.6 = (s32[7,3,64]{2,0,1:T(8,128)S(1)}, s32[7,3,64]{2,0,1:T(8,128)S(1)}, u32[]{:S(2)}, u32[]{:S(2)}) collective-permute-start(s32[7,3,64]{2,0,1:T(8,128)S(1)} %bitcast.46), channel_id=1, source_target_pairs={{0,1},{1,0},{2,3},{3,2},{4,5},{5,4},{6,7},{7,6},{8,9},{9,8},{10,11... | collective-permute-start | bytes 16136 | tf_op jit(solution)/shard_map/ppermute | solution.py:259
  94.6 2.0 %copy-start = (bf16[64,128,128]{2,1,0:T(8,128)(2,1)}, bf16[64,128,128]{2,1,0:T(8,128)(2,1)S(1)}, u32[]{:S(2)}) copy-start(bf16[64,128,128]{2,1,0:T(8,128)(2,1)S(1)} %collective-permute-done.refs_9_) | copy-start | bytes 6291460
  94.6 47.1 %collective-permute-start.7 = (bf16[64,128,128]{2,1,0:T(8,128)(2,1)S(1)}, bf16[64,128,128]{2,1,0:T(8,128)(2,1)S(1)}, u32[]{:S(2)}, u32[]{:S(2)}) collective-permute-start(bf16[64,128,128]{2,1,0:T(8,128)(2,1)S(1)} %collective-permute-done.refs_9_), channel_id=1, source_target_pairs={{4,6},{2,0},{5,7},{3,1},{12,14},{10,8},{13,15},{11,9},{20,22},{18,... | collective-permute-start | bytes 6291464 | tf_op jit(solution)/shard_map/ppermute | solution.py:317
  109.8 5.9 %collective-permute-start.10 = (f32[28,128,128]{2,1,0:T(8,128)S(1)}, f32[28,128,128]{2,1,0:T(8,128)S(1)}, u32[]{:S(2)}, u32[]{:S(2)}) collective-permute-start(f32[28,128,128]{2,1,0:T(8,128)S(1)} %get-tuple-element.35), channel_id=1, source_target_pairs={{0,1},{1,0},{2,3},{3,2},{4,5},{5,4},{6,7},{7,6},{8,9},{9,8},{10,11... | collective-permute-start | bytes 5505032 | tf_op jit(solution)/shard_map/ppermute | solution.py:259
  112.2 8.7 %collective-permute-start.11 = (f32[28,128,128]{2,1,0:T(8,128)S(1)}, f32[28,128,128]{2,1,0:T(8,128)S(1)}, u32[]{:S(2)}, u32[]{:S(2)}) collective-permute-start(f32[28,128,128]{2,1,0:T(8,128)S(1)} %get-tuple-element.36), channel_id=1, source_target_pairs={{0,1},{1,0},{2,3},{3,2},{4,5},{5,4},{6,7},{7,6},{8,9},{9,8},{10,11... | collective-permute-start | bytes 5505032 | tf_op jit(solution)/shard_map/ppermute | solution.py:259
  112.3 8.8 %collective-permute-start.12 = (f32[28,128,128]{2,1,0:T(8,128)}, f32[28,128,128]{2,1,0:T(8,128)S(1)}, u32[]{:S(2)}, u32[]{:S(2)}) collective-permute-start(f32[28,128,128]{2,1,0:T(8,128)} %get-tuple-element.37), channel_id=1, source_target_pairs={{0,1},{1,0},{2,3},{3,2},{4,5},{5,4},{6,7},{7,6},{8,9},{9,8},{10,11... | collective-permute-start | bytes 5505032 | tf_op jit(solution)/shard_map/ppermute | solution.py:259
  112.7 10.8 %collective-permute-start.9 = (f32[28,128,128]{2,1,0:T(8,128)S(1)}, f32[28,128,128]{2,1,0:T(8,128)S(1)}, u32[]{:S(2)}, u32[]{:S(2)}) collective-permute-start(f32[28,128,128]{2,1,0:T(8,128)S(1)} %get-tuple-element.34), channel_id=1, source_target_pairs={{0,1},{1,0},{2,3},{3,2},{4,5},{5,4},{6,7},{7,6},{8,9},{9,8},{10,11... | collective-permute-start | bytes 5505032 | tf_op jit(solution)/shard_map/ppermute | solution.py:259
  141.8 6.6 %collective-permute-start.13 = (bf16[64,128,128]{2,1,0:T(8,128)(2,1)S(1)}, bf16[64,128,128]{2,1,0:T(8,128)(2,1)S(1)}, u32[]{:S(2)}, u32[]{:S(2)}) collective-permute-start(bf16[64,128,128]{2,1,0:T(8,128)(2,1)S(1)} %collective-permute-done.7.left), channel_id=1, source_target_pairs={{0,1},{1,0},{2,3},{3,2},{4,5},{5,4},{6,7},{7,6},{8,9},{9,8},{10,11... | collective-permute-start | bytes 6291464 | tf_op jit(solution)/shard_map/ppermute | solution.py:259

commit v19 on v18

--- a/solution.py
+++ b/solution.py
@@ -320,7 +320,10 @@
         return (layers * 2 + ((slot // part) ^ lax.axis_index("row"))) * part + slot % part
 
     beside_one, across_one, across_two = hop(own, beside), hop(own, across), hop(own, [(0, 2), (3, 1)])
-    met = lax.ppermute(right_own, "row", [(0, 1), (1, 0)])
+    middle = part // 2
+    met = [lax.ppermute(right_own[:middle], "row", [(0, 1), (1, 0)])]
+    across_one, sent_late = fence((across_one, right_own[middle:]))
+    late_met = lax.ppermute(sent_late, "row", [(0, 1), (1, 0)])
     listed = layer_products(step_lists, layer, half, right_slot)
     classes = [0, jnp.where(place % 2 == 0, 1, 3), jnp.where(inner, jnp.where(low, 1, 3), -1)]
     classes += [jnp.where(inner, 2, -1), jnp.where(inner, -1, 2)]
@@ -328,14 +331,15 @@
 
     outer_two = hop(across_one, outward)
     beside_one, across_one, met, listed, scalars = fence((beside_one, across_one, met, listed, scalars))
-    right_other, met_other = swapped(right_own), swapped(met)
+    met.append(late_met)
+    right_other, met_other = swapped(right_own), [swapped(value) for value in met]
     both = jnp.stack([step_lists, swapped(step_lists)])
     kept = kept_products(both, layer, half, right_slot)
 
     across_two, right_other, met_other, kept = fence((across_two, right_other, met_other, kept))
     outer_three = hop(across_two, outward)
     panels = [[(value, False)] for value in (own, beside_one, across_one, across_two, outer_two)]
-    rights = [(value, False) for value in (right_own, met, right_other, met_other)]
+    rights = [(value, False) for value in (right_own, *met, right_other, *met_other)]
     saved = [half // PARTS] * (PARTS - 1) + [half - half // PARTS * (PARTS - 1)]
     *parts, right, total = product_sums(
         listed, scalars, shape, 1, panels, rights, [], 2 * half, saved, "split"

time: 153 us -> 154 us (level)
  waiting for transfers between devices: 107 us -> 103 us
  starting transfers between devices: 21.9 us -> 25 us
  local copies, waits for them, and re-layouts: 1.93 us -> 3.77 us
    ppermute x1 -> x2, waiting for transfers between devices: 32.1 us -> 12.4 us  [the longest x1 12.3 us: line(): met = [lax.ppermute(right_own[:middle], 'row', [(0, 1), (1, 0)])]]
    ppermute x5, waiting for transfers between devices: 60.7 us -> 77.7 us  [hop(): return lax.ppermute(value, 'col', pairs)]
    slice x0 -> x1, local copies, waits for them, and re-layouts: none -> 2.54 us  [line(): met = [lax.ppermute(right_own[:middle], 'row', [(0, 1), (1, 0)])]]
    ppermute x8 -> x9, waiting for transfers between devices: 14.7 us -> 12.9 us  [swapped(): return lax.ppermute(value, 'dep', [(0, 1), (1, 0)])]
    ppermute x8 -> x9, starting transfers between devices: 9.67 us -> 10.2 us  [swapped(): return lax.ppermute(value, 'dep', [(0, 1), (1, 0)])]
  transfers between devices with their start and end apart: 14 -> 16, of which waited for: 11 -> 11; matrix products, arithmetic and copies ran while one was open for 1% -> 3% of each run, Pallas kernels for 11% -> 11%
where the time goes in v19:
time: 154 us; the launch traced here: 153 us
  waiting for transfers between devices  103 us (67%)
  starting transfers between devices  25 us (16%)
  Pallas kernels  21.6 us (14%)
  local copies, waits for them, and re-layouts  3.77 us (2%)
    ppermute x5, waiting for transfers between devices, hop(): return lax.ppermute(value, 'col', pairs)  77.7 us
    pallas_call x1, Pallas kernels, product_sums(): pl.pallas_call(functools.partial(sum_kernel, panel_spans, right_spans, gi...  13.4 us
    ppermute x9, waiting for transfers between devices, swapped(): return lax.ppermute(value, 'dep', [(0, 1), (1, 0)])  12.9 us
    ppermute x5, starting transfers between devices, hop(): return lax.ppermute(value, 'col', pairs)  12.4 us
    ppermute x1, waiting for transfers between devices, line(): met = [lax.ppermute(right_own[:middle], 'row', [(0, 1), (1, 0)])]  12.3 us
    ppermute x9, starting transfers between devices, swapped(): return lax.ppermute(value, 'dep', [(0, 1), (1, 0)])  10.2 us
    pallas_call x2, Pallas kernels, add_panel(): pl.pallas_call(functools.partial(panel_kernel, shape, layer, kind_at, fin...  7.21 us
  transfers between devices with their start and end apart: 16, of which 11 were waited for; matrix products, arithmetic and copies ran while one was open for 3% of the time, Pallas kernels for 11%

profile of v19, /device:TPU:1, one launch (start us, length us, event | category | flops | bytes accessed | tf_op | source)
XLA Modules:
  0.0 153.4 jit_solution(16122264623915085698)
XLA Ops:
  0.0 2.1 %collective-permute-start.3 = (bf16[64,128,128]{2,1,0:T(8,128)(2,1)}, bf16[64,128,128]{2,1,0:T(8,128)(2,1)}, u32[]{:S(2)}, u32[]{:S(2)}) collective-permute-start(bf16[64,128,128]{2,1,0:T(8,128)(2,1)} %bitcast.refs_8_), channel_id=1, source_target_pairs={{2,4},{4,2},{3,5},{5,3},{10,12},{12,10},{11,13},{13,11},{18,20},{2... | collective-permute-start | bytes 6291464 | tf_op jit(solution)/shard_map/ppermute | solution.py:317
  2.1 3.4 %collective-permute-start.2 = (bf16[64,128,128]{2,1,0:T(8,128)(2,1)}, bf16[64,128,128]{2,1,0:T(8,128)(2,1)}, u32[]{:S(2)}, u32[]{:S(2)}) collective-permute-start(bf16[64,128,128]{2,1,0:T(8,128)(2,1)} %bitcast.refs_8_), channel_id=1, source_target_pairs={{0,2},{2,0},{4,6},{6,4},{1,3},{3,1},{5,7},{7,5},{8,10},{10,8},{12,... | collective-permute-start | bytes 6291464 | tf_op jit(solution)/shard_map/ppermute | solution.py:317
  5.5 2.5 %slice_bitcast_fusion = (bf16[28,128,128]{2,1,0:T(8,128)(2,1)S(1)}, bf16[28,128,128]{2,1,0:T(8,128)(2,1)}) fusion(bf16[1,1,1,56,128,128]{5,4,3,2,1,0:T(8,128)(2,1)} %param.4), kind=kLoop, calls=%fused_computation | loop fusion | bytes 3670016 | tf_op jit(solution)/shard_map/slice | solution.py:324
  8.1 1.2 collective-permute-start.4
  9.3 4.3 %collective-permute-start = (bf16[64,128,128]{2,1,0:T(8,128)(2,1)}, bf16[64,128,128]{2,1,0:T(8,128)(2,1)}, u32[]{:S(2)}, u32[]{:S(2)}) collective-permute-start(bf16[64,128,128]{2,1,0:T(8,128)(2,1)} %bitcast.refs_8_), channel_id=1, source_target_pairs={{0,4},{6,2},{1,5},{7,3},{8,12},{14,10},{9,13},{15,11},{16,20},{22,... | collective-permute-start | bytes 6291464 | tf_op jit(solution)/shard_map/ppermute | solution.py:317
  13.6 1.3 collective-permute-start.10
  14.9 1.6 %collective-permute-start.1 = (bf16[56,128,128]{2,1,0:T(8,128)(2,1)}, bf16[56,128,128]{2,1,0:T(8,128)(2,1)}, u32[]{:S(2)}, u32[]{:S(2)}) collective-permute-start(bf16[56,128,128]{2,1,0:T(8,128)(2,1)} %bitcast.1.refs_2_), channel_id=1, source_target_pairs={{0,1},{1,0},{2,3},{3,2},{4,5},{5,4},{6,7},{7,6},{8,9},{9,8},{10,11... | collective-permute-start | bytes 5505032 | tf_op jit(solution)/shard_map/ppermute | solution.py:259
  16.4 12.3 %collective-permute-done.4.refs_3_ = bf16[28,128,128]{2,1,0:T(8,128)(2,1)S(1)} collective-permute-done((bf16[28,128,128]{2,1,0:T(8,128)(2,1)S(1)}, bf16[28,128,128]{2,1,0:T(8,128)(2,1)S(1)}, u32[]{:S(2)}, u32[]{:S(2)}) %collective-permute-start.4) | collective-permute-done | bytes 917536 | tf_op jit(solution)/shard_map/ppermute | solution.py:324
  28.8 1.2 collective-permute-start.6
  30.5 20.4 %collective-permute-done.2.refs_9_ = bf16[64,128,128]{2,1,0:T(8,128)(2,1)} collective-permute-done((bf16[64,128,128]{2,1,0:T(8,128)(2,1)}, bf16[64,128,128]{2,1,0:T(8,128)(2,1)}, u32[]{:S(2)}, u32[]{:S(2)}) %collective-permute-start.2) | collective-permute-done | bytes 2097184 | tf_op jit(solution)/shard_map/ppermute | solution.py:317
  50.9 2.3 %collective-permute-start.8 = (s32[7,3,64]{2,0,1:T(8,128)S(1)}, s32[7,3,64]{2,0,1:T(8,128)S(1)}, u32[]{:S(2)}, u32[]{:S(2)}) collective-permute-start(s32[7,3,64]{2,0,1:T(8,128)S(1)} %bitcast.43), channel_id=1, source_target_pairs={{0,1},{1,0},{2,3},{3,2},{4,5},{5,4},{6,7},{7,6},{8,9},{9,8},{10,11... | collective-permute-start | bytes 16136 | tf_op jit(solution)/shard_map/ppermute | solution.py:259
  55.2 39.5 %collective-permute-done.refs_11_ = bf16[64,128,128]{2,1,0:T(8,128)(2,1)} collective-permute-done((bf16[64,128,128]{2,1,0:T(8,128)(2,1)}, bf16[64,128,128]{2,1,0:T(8,128)(2,1)}, u32[]{:S(2)}, u32[]{:S(2)}) %collective-permute-start) | collective-permute-done | bytes 2097184 | tf_op jit(solution)/shard_map/ppermute | solution.py:317
  94.8 1.3 collective-permute-start.9
  96.7 13.4 %shard_map.37 = (f32[28,128,128]{2,1,0:T(8,128)S(1)}, f32[28,128,128]{2,1,0:T(8,128)}, f32[28,128,128]{2,1,0:T(8,128)}, f32[28,128,128]{2,1,0:T(8,128)}, bf16[22...) custom-call(s32[448]{0:T(512)S(1)} %fusion.17.refs_0_, s32[7]{0:T(128)S(1)} %stack.33.refs_1_.scalars, ...), custom_call_target="tpu_custom_call" | custom-call | flops 1 | bytes 1 | tf_op jit(solution)/shard_map/pallas_call | solution.py:162
  110.2 2.4 %collective-permute-start.11 = (f32[28,128,128]{2,1,0:T(8,128)S(1)}, f32[28,128,128]{2,1,0:T(8,128)S(1)}, u32[]{:S(2)}, u32[]{:S(2)}) collective-permute-start(f32[28,128,128]{2,1,0:T(8,128)S(1)} %get-tuple-element.40), channel_id=1, source_target_pairs={{0,1},{1,0},{2,3},{3,2},{4,5},{5,4},{6,7},{7,6},{8,9},{9,8},{10,11... | collective-permute-start | bytes 5505032 | tf_op jit(solution)/shard_map/ppermute | solution.py:259
  113.2 4.7 %collective-permute-done.11.refs_0_ = f32[28,128,128]{2,1,0:T(8,128)S(1)} collective-permute-done((f32[28,128,128]{2,1,0:T(8,128)S(1)}, f32[28,128,128]{2,1,0:T(8,128)S(1)}, u32[]{:S(2)}, u32[]{:S(2)}) %collective-permute-start.11) | collective-permute-done | bytes 1835040 | tf_op jit(solution)/shard_map/ppermute | solution.py:259
  117.9 1.0 collective-permute-done.12.refs_1_
  118.9 2.6 %collective-permute-done.13.refs_2_ = f32[28,128,128]{2,1,0:T(8,128)S(1)} collective-permute-done((f32[28,128,128]{2,1,0:T(8,128)}, f32[28,128,128]{2,1,0:T(8,128)S(1)}, u32[]{:S(2)}, u32[]{:S(2)}) %collective-permute-start.13) | collective-permute-done | bytes 1835040 | tf_op jit(solution)/shard_map/ppermute | solution.py:259
  121.5 2.6 %collective-permute-done.14.refs_3_ = f32[28,128,128]{2,1,0:T(8,128)S(1)} collective-permute-done((f32[28,128,128]{2,1,0:T(8,128)}, f32[28,128,128]{2,1,0:T(8,128)S(1)}, u32[]{:S(2)}, u32[]{:S(2)}) %collective-permute-start.14) | collective-permute-done | bytes 1835040 | tf_op jit(solution)/shard_map/ppermute | solution.py:259
  125.1 17.1 %collective-permute-done.9.left = bf16[64,128,128]{2,1,0:T(8,128)(2,1)S(1)} collective-permute-done((bf16[64,128,128]{2,1,0:T(8,128)(2,1)}, bf16[64,128,128]{2,1,0:T(8,128)(2,1)S(1)}, u32[]{:S(2)}, u32[]{:S(2)}) %collective-permute-start.9) | collective-permute-done | bytes 2097184 | tf_op jit(solution)/shard_map/ppermute | solution.py:317
  142.1 2.8 %collective-permute-start.15 = (bf16[64,128,128]{2,1,0:T(8,128)(2,1)S(1)}, bf16[64,128,128]{2,1,0:T(8,128)(2,1)S(1)}, u32[]{:S(2)}, u32[]{:S(2)}) collective-permute-start(bf16[64,128,128]{2,1,0:T(8,128)(2,1)S(1)} %collective-permute-done.9.left), channel_id=1, source_target_pairs={{0,1},{1,0},{2,3},{3,2},{4,5},{5,4},{6,7},{7,6},{8,9},{9,8},{10,11... | collective-permute-start | bytes 6291464 | tf_op jit(solution)/shard_map/ppermute | solution.py:259
  144.9 2.5 %shard_map.39.given = f32[113,128,128]{2,1,0:T(8,128)S(1)} custom-call(s32[896]{0:T(1024)S(1)} %fusion.10.packed, s32[7]{0:T(128)S(1)} %stack.33.refs_1_.scalars, bf16[224,128,128]{2,1,0:T(8,128)(2,1)S(1)} %get-tuple-element.45.right, f32[113,128,128]{2,1,0:T(8,128)S(1)} %shard_map.38.given, ...), custom_call_target="tpu_custom_call", output_to_operand_aliasing={{}: (3, {})} | custom-call | flops 1 | bytes 1 | tf_op jit(solution)/shard_map/pallas_call | solution.py:242
  147.4 1.3 collective-permute-done.15.left
  148.7 4.7 %shard_map.40 = (bf16[112,128,128]{2,1,0:T(8,128)(2,1)}, f32[113,128,128]{2,1,0:T(8,128)S(1)}) custom-call(s32[896]{0:T(1024)S(1)} %fusion.10.packed, s32[7]{0:T(128)S(1)} %stack.33.refs_1_.scalars, bf16[224,128,128]{2,1,0:T(8,128)(2,1)S(1)} %get-tuple-element.45.right, f32[113,128,128]{2,1,0:T(8,128)S(1)} %shard_map.39.given, ...), custom_call_target="tpu_custom_call", output_to_operand_aliasing={{1}: (3, {})} | custom-call | flops 1 | bytes 1 | tf_op jit(solution)/shard_map/pallas_call | solution.py:242
  (40 shorter events, 4.7 us)
Async XLA Ops:
  0.0 30.0 %copy-start = (s32[1,1,1,7,3,64]{5,2,4,3,1,0:T(1,128)S(1)}, s32[1,1,1,7,3,64]{5,2,4,3,1,0:T(1,128)}, u32[]{:S(2)}) copy-start(s32[1,1,1,7,3,64]{5,2,4,3,1,0:T(1,128)} %param.5) | copy-start | bytes 16132
  0.0 13.6 %collective-permute-start.3 = (bf16[64,128,128]{2,1,0:T(8,128)(2,1)}, bf16[64,128,128]{2,1,0:T(8,128)(2,1)}, u32[]{:S(2)}, u32[]{:S(2)}) collective-permute-start(bf16[64,128,128]{2,1,0:T(8,128)(2,1)} %bitcast.refs_8_), channel_id=1, source_target_pairs={{2,4},{4,2},{3,5},{5,3},{10,12},{12,10},{11,13},{13,11},{18,20},{2... | collective-permute-start | bytes 6291464 | tf_op jit(solution)/shard_map/ppermute | solution.py:317
  2.1 48.7 %collective-permute-start.2 = (bf16[64,128,128]{2,1,0:T(8,128)(2,1)}, bf16[64,128,128]{2,1,0:T(8,128)(2,1)}, u32[]{:S(2)}, u32[]{:S(2)}) collective-permute-start(bf16[64,128,128]{2,1,0:T(8,128)(2,1)} %bitcast.refs_8_), channel_id=1, source_target_pairs={{0,2},{2,0},{4,6},{6,4},{1,3},{3,1},{5,7},{7,5},{8,10},{10,8},{12,... | collective-permute-start | bytes 6291464 | tf_op jit(solution)/shard_map/ppermute | solution.py:317
  8.1 20.7 %collective-permute-start.4 = (bf16[28,128,128]{2,1,0:T(8,128)(2,1)S(1)}, bf16[28,128,128]{2,1,0:T(8,128)(2,1)S(1)}, u32[]{:S(2)}, u32[]{:S(2)}) collective-permute-start(bf16[28,128,128]{2,1,0:T(8,128)(2,1)S(1)} %get-tuple-element.49), channel_id=1, source_target_pairs={{0,8},{8,0},{1,9},{9,1},{2,10},{10,2},{3,11},{11,3},{4,12},{12,4},... | collective-permute-start | bytes 2752520 | tf_op jit(solution)/shard_map/ppermute | solution.py:324
  9.3 85.5 %collective-permute-start = (bf16[64,128,128]{2,1,0:T(8,128)(2,1)}, bf16[64,128,128]{2,1,0:T(8,128)(2,1)}, u32[]{:S(2)}, u32[]{:S(2)}) collective-permute-start(bf16[64,128,128]{2,1,0:T(8,128)(2,1)} %bitcast.refs_8_), channel_id=1, source_target_pairs={{0,4},{6,2},{1,5},{7,3},{8,12},{14,10},{9,13},{15,11},{16,20},{22,... | collective-permute-start | bytes 6291464 | tf_op jit(solution)/shard_map/ppermute | solution.py:317
  13.6 83.2 %collective-permute-start.10 = (bf16[64,128,128]{2,1,0:T(8,128)(2,1)}, bf16[64,128,128]{2,1,0:T(8,128)(2,1)}, u32[]{:S(2)}, u32[]{:S(2)}) collective-permute-start(bf16[64,128,128]{2,1,0:T(8,128)(2,1)} %collective-permute-done.3.refs_10_), channel_id=1, source_target_pairs={{4,6},{2,0},{5,7},{3,1},{12,14},{10,8},{13,15},{11,9},{20,22},{18,... | collective-permute-start | bytes 6291464 | tf_op jit(solution)/shard_map/ppermute | solution.py:317
  14.9 40.4 %collective-permute-start.1 = (bf16[56,128,128]{2,1,0:T(8,128)(2,1)}, bf16[56,128,128]{2,1,0:T(8,128)(2,1)}, u32[]{:S(2)}, u32[]{:S(2)}) collective-permute-start(bf16[56,128,128]{2,1,0:T(8,128)(2,1)} %bitcast.1.refs_2_), channel_id=1, source_target_pairs={{0,1},{1,0},{2,3},{3,2},{4,5},{5,4},{6,7},{7,6},{8,9},{9,8},{10,11... | collective-permute-start | bytes 5505032 | tf_op jit(solution)/shard_map/ppermute | solution.py:259
  28.8 25.6 %collective-permute-start.6 = (bf16[28,128,128]{2,1,0:T(8,128)(2,1)}, bf16[28,128,128]{2,1,0:T(8,128)(2,1)S(1)}, u32[]{:S(2)}, u32[]{:S(2)}) collective-permute-start(bf16[28,128,128]{2,1,0:T(8,128)(2,1)} %get-tuple-element.29), channel_id=1, source_target_pairs={{0,8},{8,0},{1,9},{9,1},{2,10},{10,2},{3,11},{11,3},{4,12},{12,4},... | collective-permute-start | bytes 2752520 | tf_op jit(solution)/shard_map/ppermute | solution.py:326
  50.9 3.1 %collective-permute-start.8 = (s32[7,3,64]{2,0,1:T(8,128)S(1)}, s32[7,3,64]{2,0,1:T(8,128)S(1)}, u32[]{:S(2)}, u32[]{:S(2)}) collective-permute-start(s32[7,3,64]{2,0,1:T(8,128)S(1)} %bitcast.43), channel_id=1, source_target_pairs={{0,1},{1,0},{2,3},{3,2},{4,5},{5,4},{6,7},{7,6},{8,9},{9,8},{10,11... | collective-permute-start | bytes 16136 | tf_op jit(solution)/shard_map/ppermute | solution.py:259
  54.0 40.8 %collective-permute-start.5 = (bf16[28,128,128]{2,1,0:T(8,128)(2,1)S(1)}, bf16[28,128,128]{2,1,0:T(8,128)(2,1)S(1)}, u32[]{:S(2)}, u32[]{:S(2)}) collective-permute-start(bf16[28,128,128]{2,1,0:T(8,128)(2,1)S(1)} %collective-permute-done.4.refs_3_), channel_id=1, source_target_pairs={{0,1},{1,0},{2,3},{3,2},{4,5},{5,4},{6,7},{7,6},{8,9},{9,8},{10,11... | collective-permute-start | bytes 2752520 | tf_op jit(solution)/shard_map/ppermute | solution.py:259
  54.3 40.4 %collective-permute-start.7 = (bf16[28,128,128]{2,1,0:T(8,128)(2,1)S(1)}, bf16[28,128,128]{2,1,0:T(8,128)(2,1)}, u32[]{:S(2)}, u32[]{:S(2)}) collective-permute-start(bf16[28,128,128]{2,1,0:T(8,128)(2,1)S(1)} %collective-permute-done.6.refs_4_), channel_id=1, source_target_pairs={{0,1},{1,0},{2,3},{3,2},{4,5},{5,4},{6,7},{7,6},{8,9},{9,8},{10,11... | collective-permute-start | bytes 2752520 | tf_op jit(solution)/shard_map/ppermute | solution.py:259
  94.8 47.4 %collective-permute-start.9 = (bf16[64,128,128]{2,1,0:T(8,128)(2,1)}, bf16[64,128,128]{2,1,0:T(8,128)(2,1)S(1)}, u32[]{:S(2)}, u32[]{:S(2)}) collective-permute-start(bf16[64,128,128]{2,1,0:T(8,128)(2,1)} %collective-permute-done.refs_11_), channel_id=1, source_target_pairs={{4,6},{2,0},{5,7},{3,1},{12,14},{10,8},{13,15},{11,9},{20,22},{18,... | collective-permute-start | bytes 6291464 | tf_op jit(solution)/shard_map/ppermute | solution.py:317
  110.2 7.7 %collective-permute-start.11 = (f32[28,128,128]{2,1,0:T(8,128)S(1)}, f32[28,128,128]{2,1,0:T(8,128)S(1)}, u32[]{:S(2)}, u32[]{:S(2)}) collective-permute-start(f32[28,128,128]{2,1,0:T(8,128)S(1)} %get-tuple-element.40), channel_id=1, source_target_pairs={{0,1},{1,0},{2,3},{3,2},{4,5},{5,4},{6,7},{7,6},{8,9},{9,8},{10,11... | collective-permute-start | bytes 5505032 | tf_op jit(solution)/shard_map/ppermute | solution.py:259
  112.6 6.2 %collective-permute-start.12 = (f32[28,128,128]{2,1,0:T(8,128)}, f32[28,128,128]{2,1,0:T(8,128)S(1)}, u32[]{:S(2)}, u32[]{:S(2)}) collective-permute-start(f32[28,128,128]{2,1,0:T(8,128)} %get-tuple-element.41), channel_id=1, source_target_pairs={{0,1},{1,0},{2,3},{3,2},{4,5},{5,4},{6,7},{7,6},{8,9},{9,8},{10,11... | collective-permute-start | bytes 5505032 | tf_op jit(solution)/shard_map/ppermute | solution.py:259
  112.7 8.8 %collective-permute-start.13 = (f32[28,128,128]{2,1,0:T(8,128)}, f32[28,128,128]{2,1,0:T(8,128)S(1)}, u32[]{:S(2)}, u32[]{:S(2)}) collective-permute-start(f32[28,128,128]{2,1,0:T(8,128)} %get-tuple-element.42), channel_id=1, source_target_pairs={{0,1},{1,0},{2,3},{3,2},{4,5},{5,4},{6,7},{7,6},{8,9},{9,8},{10,11... | collective-permute-start | bytes 5505032 | tf_op jit(solution)/shard_map/ppermute | solution.py:259
  113.1 11.0 %collective-permute-start.14 = (f32[28,128,128]{2,1,0:T(8,128)}, f32[28,128,128]{2,1,0:T(8,128)S(1)}, u32[]{:S(2)}, u32[]{:S(2)}) collective-permute-start(f32[28,128,128]{2,1,0:T(8,128)} %get-tuple-element.43), channel_id=1, source_target_pairs={{0,1},{1,0},{2,3},{3,2},{4,5},{5,4},{6,7},{7,6},{8,9},{9,8},{10,11... | collective-permute-start | bytes 5505032 | tf_op jit(solution)/shard_map/ppermute | solution.py:259
  142.1 6.6 %collective-permute-start.15 = (bf16[64,128,128]{2,1,0:T(8,128)(2,1)S(1)}, bf16[64,128,128]{2,1,0:T(8,128)(2,1)S(1)}, u32[]{:S(2)}, u32[]{:S(2)}) collective-permute-start(bf16[64,128,128]{2,1,0:T(8,128)(2,1)S(1)} %collective-permute-done.9.left), channel_id=1, source_target_pairs={{0,1},{1,0},{2,3},{3,2},{4,5},{5,4},{6,7},{7,6},{8,9},{9,8},{10,11... | collective-permute-start | bytes 6291464 | tf_op jit(solution)/shard_map/ppermute | solution.py:259

commit v20 on v18

--- a/solution.py
+++ b/solution.py
@@ -10,7 +10,7 @@
 NBQ = 32
 UNROLL = 16
 PARTS = 4
-OUT_PARTS = 8
+PART_UNROLL = 8
 
 
 def chosen_products(packed, classes, panels, todo, shape, layers, spare, first_left=0):
@@ -37,9 +37,9 @@
     return count
 
 
-def add_chosen(todo, count, left, right, work, first_left=0):
+def add_chosen(todo, count, left, right, work, first_left=0, start=0, unroll=UNROLL):
     def several(group, carry):
-        entries = [todo[group * UNROLL + lane] for lane in range(UNROLL)]
+        entries = [todo[start + group * unroll + lane] for lane in range(unroll)]
         products = [
             jnp.dot(
                 left[((entry >> 10) & 1023) - first_left],
@@ -52,7 +52,40 @@
             work[entry & 1023] += product
         return carry
 
-    lax.fori_loop(0, (count + UNROLL - 1) // UNROLL, several, jnp.int32(0))
+    lax.fori_loop(0, (count + unroll - 1) // unroll, several, jnp.int32(0))
+
+
+def sort_products(packed, base, kind, shape, sorted_out, spare, first_left):
+    step_count, columns, slots = shape
+    room, counts, size = part_room(shape), PARTS * part_room(shape), spare // PARTS
+    for part in range(PARTS):
+        sorted_out[counts + part] = jnp.int32(0)
+    for extra in range(-(-step_count // columns)):
+        step = lax.rem(kind + step_count // 2, columns) + extra * columns
+        groups = jnp.where((kind >= 0) & (step < step_count), slots // 8, 0)
+        first = base + step * slots
+
+        def place(group, carry):
+            for lane in range(8):
+                entry = packed[first + group * 8 + lane]
+                result, part = entry & 1023, jnp.int32(0)
+                for bound in range(1, PARTS):
+                    part += (result >= bound * size).astype(jnp.int32)
+                count = sorted_out[counts + part]
+                sorted_out[part * room + count] = entry
+                sorted_out[counts + part] = count + (entry >= 0).astype(jnp.int32)
+            return carry
+
+        lax.fori_loop(0, groups, place, jnp.int32(0))
+    for part in range(PARTS):
+        count = sorted_out[counts + part]
+        for extra in range(PART_UNROLL - 1):
+            sorted_out[part * room + count + extra] = jnp.int32(first_left << 10 | spare)
+
+
+def part_room(shape):
+    step_count, columns, slots = shape
+    return -(-step_count // columns) * slots + PART_UNROLL
 
 
 def sum_kernel(panels, rights, givens, saved, mode, shape, layers, operand_count, layer_at, *refs):
@@ -207,48 +240,67 @@
     )(given, *pieces)
 
 
-def panel_kernel(shape, layer, kind_at, finish, packed, scalars, right, given, left, *refs):
+def own_kernel(shape, kind_at, packed, scalars, right, given, left, work, sorted_out, todo):
     del given
+    step_count, _, slots = shape
+    spare, kind = work.shape[0] - 1, scalars[kind_at]
+    count = chosen_products(packed, [kind], 1, todo, shape, 1, spare)
+    add_chosen(todo, count, left, right, work)
+    sort_products(packed, step_count * slots, kind, shape, sorted_out, spare, slots)
+
+
+def add_own(packed, scalars, kind_at, shape, panel, right, given):
     step_count, columns, slots = shape
-    work, todo = (refs[1], refs[2]) if finish else (refs[0], refs[1])
-    spare, first = work.shape[0] - 1, layer * slots
-    part = packed.at[pl.ds(layer * step_count * slots, step_count * slots)]
-    count = chosen_products(part, [scalars[kind_at]], 1, todo, shape, 1, spare, first)
-    add_chosen(todo, count, left, right, work, first)
-    if finish:
-        out, rounded, sems = refs[0], refs[3], refs[4]
-        size = spare // OUT_PARTS
-        copies = []
-        for index in range(OUT_PARTS):
-            span = pl.ds(index * size, size if index < OUT_PARTS - 1 else spare - index * size)
-            rounded[span] = work[span].astype(rounded.dtype)
-            copies.append(pltpu.make_async_copy(rounded.at[span], out.at[span], sems.at[index]))
-            copies[-1].start()
-        for copy in copies:
-            copy.wait()
-
-
-def add_panel(packed, scalars, kind_at, shape, layer, panel, right, given, finish):
-    step_count, columns, slots = shape
+    in_scalar, in_vector = pl.BlockSpec(memory_space=pltpu.SMEM), pl.BlockSpec(memory_space=pltpu.VMEM)
+    return pl.pallas_call(
+        functools.partial(own_kernel, shape, kind_at),
+        out_shape=[
+            pltpu.VMEM(given.shape, given.dtype),
+            jax.ShapeDtypeStruct((PARTS * part_room(shape) + PARTS,), jnp.int32),
+        ],
+        in_specs=[in_scalar] * 2 + [in_vector] * 3,
+        out_specs=[in_vector, in_scalar],
+        scratch_shapes=[pltpu.SMEM((-(-step_count // columns) * slots + UNROLL,), jnp.int32)],
+        input_output_aliases={3: 0},
+        compiler_params=pltpu.CompilerParams(vmem_limit_bytes=12 << 20),
+        cost_estimate=pl.CostEstimate(flops=1, bytes_accessed=1, transcendentals=0),
+    )(packed, scalars, right, given, panel)
+
+
+def other_kernel(shape, sorted_lists, right, given, left, out, work, rounded, sems):
+    del given
+    slots, room, spare = shape[2], part_room(shape), work.shape[0] - 1
+    size, copies = spare // PARTS, []
+    for part in range(PARTS):
+        count = sorted_lists[PARTS * room + part]
+        add_chosen(sorted_lists, count, left, right, work, slots, part * room, PART_UNROLL)
+        span = pl.ds(part * size, size if part < PARTS - 1 else spare - part * size)
+        rounded[span] = work[span].astype(rounded.dtype)
+        copies.append(pltpu.make_async_copy(rounded.at[span], out.at[span], sems.at[part]))
+        copies[-1].start()
+    for copy in copies:
+        copy.wait()
+
+
+def add_other(sorted_lists, shape, panel, right, given):
     result_slots, rows, width = given.shape[0] - 1, *given.shape[1:]
     in_scalar, in_vector = pl.BlockSpec(memory_space=pltpu.SMEM), pl.BlockSpec(memory_space=pltpu.VMEM)
-    out_shape, out_specs = [pltpu.VMEM(given.shape, given.dtype)], [in_vector]
-    scratch = [pltpu.SMEM((-(-step_count // columns) * slots + UNROLL,), jnp.int32)]
-    if finish:
-        out_shape.insert(0, jax.ShapeDtypeStruct((result_slots, rows, width), jnp.bfloat16))
-        out_specs.insert(0, pl.BlockSpec(memory_space=pl.ANY))
-        scratch.append(pltpu.VMEM((result_slots, rows, width), jnp.bfloat16))
-        scratch.append(pltpu.SemaphoreType.DMA((OUT_PARTS,)))
     return pl.pallas_call(
-        functools.partial(panel_kernel, shape, layer, kind_at, finish),
-        out_shape=out_shape,
-        in_specs=[in_scalar] * 2 + [in_vector] * 3,
-        out_specs=out_specs,
-        scratch_shapes=scratch,
-        input_output_aliases={3: len(out_shape) - 1},
+        functools.partial(other_kernel, shape),
+        out_shape=[
+            jax.ShapeDtypeStruct((result_slots, rows, width), jnp.bfloat16),
+            pltpu.VMEM(given.shape, given.dtype),
+        ],
+        in_specs=[in_scalar] + [in_vector] * 3,
+        out_specs=[pl.BlockSpec(memory_space=pl.ANY), in_vector],
+        scratch_shapes=[
+            pltpu.VMEM((result_slots, rows, width), jnp.bfloat16),
+            pltpu.SemaphoreType.DMA((PARTS,)),
+        ],
+        input_output_aliases={2: 1},
         compiler_params=pltpu.CompilerParams(vmem_limit_bytes=12 << 20),
         cost_estimate=pl.CostEstimate(flops=1, bytes_accessed=1, transcendentals=0),
-    )(packed, scalars, right, given, panel)[0]
+    )(sorted_lists, right, given, panel)[0]
 
 
 def scalar_list(*values):
@@ -344,8 +396,8 @@
 
     outer_three, total, right = fence((outer_three, total, right))
     kind_at = len(classes) + 1
-    total = add_panel(kept, scalars, kind_at, shape, 0, outer_three, right, total, False)
-    block = add_panel(kept, scalars, kind_at, shape, 1, swapped(outer_three), right, total, True)
+    total, sorted_lists = add_own(kept, scalars, kind_at, shape, outer_three, right, total)
+    block = add_other(sorted_lists, shape, swapped(outer_three), right, total)
     return block[None, None, None]
 
 

time: 153 us -> 154 us (level)
  transfers between devices with their start and end apart: 14 -> 14, of which waited for: 11 -> 10; matrix products, arithmetic and copies ran while one was open for 1% -> 1% of each run, Pallas kernels for 11% -> 12%
where the time goes in v20:
time: 154 us; the launch traced here: 153 us
  waiting for transfers between devices  106 us (69%)
  Pallas kernels  22.8 us (15%)
  starting transfers between devices  21.9 us (14%)
  local copies, waits for them, and re-layouts  1.93 us (1%)
    ppermute x5, waiting for transfers between devices, hop(): return lax.ppermute(value, 'col', pairs)  60.7 us
    ppermute x1, waiting for transfers between devices, line(): met = lax.ppermute(right_own, 'row', [(0, 1), (1, 0)])  32.1 us
    ppermute x8, waiting for transfers between devices, swapped(): return lax.ppermute(value, 'dep', [(0, 1), (1, 0)])  13.7 us
    pallas_call x1, Pallas kernels, product_sums(): pl.pallas_call(functools.partial(sum_kernel, panel_spans, right_spans, gi...  13.1 us
    ppermute x5, starting transfers between devices, hop(): return lax.ppermute(value, 'col', pairs)  11 us
    ppermute x8, starting transfers between devices, swapped(): return lax.ppermute(value, 'dep', [(0, 1), (1, 0)])  9.67 us
    pallas_call x1, Pallas kernels, add_other(): pl.pallas_call(functools.partial(other_kernel, shape), out_shape=[jax.Sha...  4.51 us
    pallas_call x1, Pallas kernels, add_own(): pl.pallas_call(functools.partial(own_kernel, shape, kind_at), out_shape=[...  4.18 us
  transfers between devices with their start and end apart: 14, of which 10 were waited for; matrix products, arithmetic and copies ran while one was open for 1% of the time, Pallas kernels for 12%

profile of v20, /device:TPU:1, one launch (start us, length us, event | category | flops | bytes accessed | tf_op | source)
XLA Modules:
  0.0 153.3 jit_solution(2645760737498582041)
XLA Ops:
  0.0 2.0 %collective-permute-start.3 = (bf16[64,128,128]{2,1,0:T(8,128)(2,1)}, bf16[64,128,128]{2,1,0:T(8,128)(2,1)}, u32[]{:S(2)}, u32[]{:S(2)}) collective-permute-start(bf16[64,128,128]{2,1,0:T(8,128)(2,1)} %bitcast.37), channel_id=1, source_target_pairs={{2,4},{4,2},{3,5},{5,3},{10,12},{12,10},{11,13},{13,11},{18,20},{2... | collective-permute-start | bytes 6291464 | tf_op jit(solution)/shard_map/ppermute | solution.py:369
  2.0 3.4 %collective-permute-start.2 = (bf16[64,128,128]{2,1,0:T(8,128)(2,1)}, bf16[64,128,128]{2,1,0:T(8,128)(2,1)}, u32[]{:S(2)}, u32[]{:S(2)}) collective-permute-start(bf16[64,128,128]{2,1,0:T(8,128)(2,1)} %bitcast.38), channel_id=1, source_target_pairs={{0,2},{2,0},{4,6},{6,4},{1,3},{3,1},{5,7},{7,5},{8,10},{10,8},{12,... | collective-permute-start | bytes 6291464 | tf_op jit(solution)/shard_map/ppermute | solution.py:369
  5.4 1.2 collective-permute-start.4
  6.6 3.0 %collective-permute-start = (bf16[64,128,128]{2,1,0:T(8,128)(2,1)}, bf16[64,128,128]{2,1,0:T(8,128)(2,1)S(1)}, u32[]{:S(2)}, u32[]{:S(2)}) collective-permute-start(bf16[64,128,128]{2,1,0:T(8,128)(2,1)} %bitcast.39), channel_id=1, source_target_pairs={{0,4},{6,2},{1,5},{7,3},{8,12},{14,10},{9,13},{15,11},{16,20},{22,... | collective-permute-start | bytes 6291464 | tf_op jit(solution)/shard_map/ppermute | solution.py:369
  9.7 1.6 %collective-permute-start.1 = (bf16[56,128,128]{2,1,0:T(8,128)(2,1)}, bf16[56,128,128]{2,1,0:T(8,128)(2,1)}, u32[]{:S(2)}, u32[]{:S(2)}) collective-permute-start(bf16[56,128,128]{2,1,0:T(8,128)(2,1)} %bitcast.42), channel_id=1, source_target_pairs={{0,1},{1,0},{2,3},{3,2},{4,5},{5,4},{6,7},{7,6},{8,9},{9,8},{10,11... | collective-permute-start | bytes 5505032 | tf_op jit(solution)/shard_map/ppermute | solution.py:311
  11.2 0.7 copy.13
  12.5 1.3 collective-permute-start.8
  13.9 32.1 %collective-permute-done.4.refs_3_ = bf16[56,128,128]{2,1,0:T(8,128)(2,1)} collective-permute-done((bf16[56,128,128]{2,1,0:T(8,128)(2,1)}, bf16[56,128,128]{2,1,0:T(8,128)(2,1)}, u32[]{:S(2)}, u32[]{:S(2)}) %collective-permute-start.4) | collective-permute-done | bytes 1835040 | tf_op jit(solution)/shard_map/ppermute | solution.py:375
  46.0 4.8 %collective-permute-done.2.refs_7_ = bf16[64,128,128]{2,1,0:T(8,128)(2,1)} collective-permute-done((bf16[64,128,128]{2,1,0:T(8,128)(2,1)}, bf16[64,128,128]{2,1,0:T(8,128)(2,1)}, u32[]{:S(2)}, u32[]{:S(2)}) %collective-permute-start.2) | collective-permute-done | bytes 2097184 | tf_op jit(solution)/shard_map/ppermute | solution.py:369
  50.8 2.3 %collective-permute-start.5 = (bf16[56,128,128]{2,1,0:T(8,128)(2,1)}, bf16[56,128,128]{2,1,0:T(8,128)(2,1)}, u32[]{:S(2)}, u32[]{:S(2)}) collective-permute-start(bf16[56,128,128]{2,1,0:T(8,128)(2,1)} %collective-permute-done.4.refs_3_), channel_id=1, source_target_pairs={{0,1},{1,0},{2,3},{3,2},{4,5},{5,4},{6,7},{7,6},{8,9},{9,8},{10,11... | collective-permute-start | bytes 5505032 | tf_op jit(solution)/shard_map/ppermute | solution.py:311
  53.3 3.0 %collective-permute-done.6 = s32[7,3,64]{2,0,1:T(8,128)S(1)} collective-permute-done((s32[7,3,64]{2,0,1:T(8,128)S(1)}, s32[7,3,64]{2,0,1:T(8,128)S(1)}, u32[]{:S(2)}, u32[]{:S(2)}) %collective-permute-start.6) | collective-permute-done | bytes 5408 | tf_op jit(solution)/shard_map/ppermute | solution.py:311
  56.7 37.9 %collective-permute-done.refs_9_ = bf16[64,128,128]{2,1,0:T(8,128)(2,1)S(1)} collective-permute-done((bf16[64,128,128]{2,1,0:T(8,128)(2,1)}, bf16[64,128,128]{2,1,0:T(8,128)(2,1)S(1)}, u32[]{:S(2)}, u32[]{:S(2)}) %collective-permute-start) | collective-permute-done | bytes 2097184 | tf_op jit(solution)/shard_map/ppermute | solution.py:369
  94.6 1.3 collective-permute-start.7
  95.9 0.7 collective-permute-done.8.refs_10_
  96.6 13.1 %shard_map.37 = (f32[28,128,128]{2,1,0:T(8,128)S(1)}, f32[28,128,128]{2,1,0:T(8,128)S(1)}, f32[28,128,128]{2,1,0:T(8,128)S(1)}, f32[28,128,128]{2,1,0:T(8,128)},...) custom-call(s32[448]{0:T(512)S(1)} %fusion.17.refs_0_, s32[7]{0:T(128)S(1)} %stack.33.refs_1_.scalars, ...), custom_call_target="tpu_custom_call" | custom-call | flops 1 | bytes 1 | tf_op jit(solution)/shard_map/pallas_call | solution.py:195
  109.8 2.4 %collective-permute-start.10 = (f32[28,128,128]{2,1,0:T(8,128)S(1)}, f32[28,128,128]{2,1,0:T(8,128)S(1)}, u32[]{:S(2)}, u32[]{:S(2)}) collective-permute-start(f32[28,128,128]{2,1,0:T(8,128)S(1)} %get-tuple-element.37), channel_id=1, source_target_pairs={{0,1},{1,0},{2,3},{3,2},{4,5},{5,4},{6,7},{7,6},{8,9},{9,8},{10,11... | collective-permute-start | bytes 5505032 | tf_op jit(solution)/shard_map/ppermute | solution.py:311
  112.8 2.8 %collective-permute-done.10.refs_1_ = f32[28,128,128]{2,1,0:T(8,128)S(1)} collective-permute-done((f32[28,128,128]{2,1,0:T(8,128)S(1)}, f32[28,128,128]{2,1,0:T(8,128)S(1)}, u32[]{:S(2)}, u32[]{:S(2)}) %collective-permute-start.10) | collective-permute-done | bytes 1835040 | tf_op jit(solution)/shard_map/ppermute | solution.py:311
  115.6 5.2 %collective-permute-done.11.refs_2_ = f32[28,128,128]{2,1,0:T(8,128)S(1)} collective-permute-done((f32[28,128,128]{2,1,0:T(8,128)S(1)}, f32[28,128,128]{2,1,0:T(8,128)S(1)}, u32[]{:S(2)}, u32[]{:S(2)}) %collective-permute-start.11) | collective-permute-done | bytes 1835040 | tf_op jit(solution)/shard_map/ppermute | solution.py:311
  121.1 2.4 %collective-permute-done.9.refs_0_ = f32[28,128,128]{2,1,0:T(8,128)S(1)} collective-permute-done((f32[28,128,128]{2,1,0:T(8,128)S(1)}, f32[28,128,128]{2,1,0:T(8,128)S(1)}, u32[]{:S(2)}, u32[]{:S(2)}) %collective-permute-start.9) | collective-permute-done | bytes 1835040 | tf_op jit(solution)/shard_map/ppermute | solution.py:311
  123.5 0.9 shard_map.38.given
  124.4 17.3 %collective-permute-done.7.left = bf16[64,128,128]{2,1,0:T(8,128)(2,1)S(1)} collective-permute-done((bf16[64,128,128]{2,1,0:T(8,128)(2,1)S(1)}, bf16[64,128,128]{2,1,0:T(8,128)(2,1)S(1)}, u32[]{:S(2)}, u32[]{:S(2)}) %collective-permute-start.7) | collective-permute-done | bytes 2097184 | tf_op jit(solution)/shard_map/ppermute | solution.py:369
  141.8 2.8 %collective-permute-start.13 = (bf16[64,128,128]{2,1,0:T(8,128)(2,1)S(1)}, bf16[64,128,128]{2,1,0:T(8,128)(2,1)S(1)}, u32[]{:S(2)}, u32[]{:S(2)}) collective-permute-start(bf16[64,128,128]{2,1,0:T(8,128)(2,1)S(1)} %collective-permute-done.7.left), channel_id=1, source_target_pairs={{0,1},{1,0},{2,3},{3,2},{4,5},{5,4},{6,7},{7,6},{8,9},{9,8},{10,11... | collective-permute-start | bytes 6291464 | tf_op jit(solution)/shard_map/ppermute | solution.py:311
  144.6 4.2 %shard_map.39 = (f32[113,128,128]{2,1,0:T(8,128)S(1)}, s32[548]{0:T(1024)S(1)}) custom-call(s32[896]{0:T(1024)S(1)} %fusion.10.packed, s32[7]{0:T(128)S(1)} %stack.33.refs_1_.scalars, bf16[224,128,128]{2,1,0:T(8,128)(2,1)S(1)} %get-tuple-element.41.right, f32[113,128,128]{2,1,0:T(8,128)S(1)} %shard_map.38.given, ...), custom_call_target="tpu_custom_call", output_to_operand_aliasing={{0}: (3, {})} | custom-call | flops 1 | bytes 1 | tf_op jit(solution)/shard_map/pallas_call | solution.py:255
  148.8 4.5 %shard_map.40 = (bf16[112,128,128]{2,1,0:T(8,128)(2,1)}, f32[113,128,128]{2,1,0:T(8,128)S(1)}) custom-call(s32[548]{0:T(1024)S(1)} %get-tuple-element.44.sorted_lists, bf16[224,128,128]{2,1,0:T(8,128)(2,1)S(1)} %get-tuple-element.41.right, f32[113,128,128]{2,1,0:T(8,128)S(1)} %get-tuple-element.45.given, ...), custom_call_target="tpu_custom_call", output_to_operand_aliasing={{1}: (2, {})} | custom-call | flops 1 | bytes 1 | tf_op jit(solution)/shard_map/pallas_call | solution.py:288
  (35 shorter events, 2.1 us)
Async XLA Ops:
  0.0 12.5 %collective-permute-start.3 = (bf16[64,128,128]{2,1,0:T(8,128)(2,1)}, bf16[64,128,128]{2,1,0:T(8,128)(2,1)}, u32[]{:S(2)}, u32[]{:S(2)}) collective-permute-start(bf16[64,128,128]{2,1,0:T(8,128)(2,1)} %bitcast.37), channel_id=1, source_target_pairs={{2,4},{4,2},{3,5},{5,3},{10,12},{12,10},{11,13},{13,11},{18,20},{2... | collective-permute-start | bytes 6291464 | tf_op jit(solution)/shard_map/ppermute | solution.py:369
  2.0 48.8 %collective-permute-start.2 = (bf16[64,128,128]{2,1,0:T(8,128)(2,1)}, bf16[64,128,128]{2,1,0:T(8,128)(2,1)}, u32[]{:S(2)}, u32[]{:S(2)}) collective-permute-start(bf16[64,128,128]{2,1,0:T(8,128)(2,1)} %bitcast.38), channel_id=1, source_target_pairs={{0,2},{2,0},{4,6},{6,4},{1,3},{3,1},{5,7},{7,5},{8,10},{10,8},{12,... | collective-permute-start | bytes 6291464 | tf_op jit(solution)/shard_map/ppermute | solution.py:369
  5.4 40.6 %collective-permute-start.4 = (bf16[56,128,128]{2,1,0:T(8,128)(2,1)}, bf16[56,128,128]{2,1,0:T(8,128)(2,1)}, u32[]{:S(2)}, u32[]{:S(2)}) collective-permute-start(bf16[56,128,128]{2,1,0:T(8,128)(2,1)} %bitcast.41), channel_id=1, source_target_pairs={{0,8},{8,0},{1,9},{9,1},{2,10},{10,2},{3,11},{11,3},{4,12},{12,4},... | collective-permute-start | bytes 5505032 | tf_op jit(solution)/shard_map/ppermute | solution.py:375
  6.6 88.0 %collective-permute-start = (bf16[64,128,128]{2,1,0:T(8,128)(2,1)}, bf16[64,128,128]{2,1,0:T(8,128)(2,1)S(1)}, u32[]{:S(2)}, u32[]{:S(2)}) collective-permute-start(bf16[64,128,128]{2,1,0:T(8,128)(2,1)} %bitcast.39), channel_id=1, source_target_pairs={{0,4},{6,2},{1,5},{7,3},{8,12},{14,10},{9,13},{15,11},{16,20},{22,... | collective-permute-start | bytes 6291464 | tf_op jit(solution)/shard_map/ppermute | solution.py:369
  9.7 47.1 %collective-permute-start.1 = (bf16[56,128,128]{2,1,0:T(8,128)(2,1)}, bf16[56,128,128]{2,1,0:T(8,128)(2,1)}, u32[]{:S(2)}, u32[]{:S(2)}) collective-permute-start(bf16[56,128,128]{2,1,0:T(8,128)(2,1)} %bitcast.42), channel_id=1, source_target_pairs={{0,1},{1,0},{2,3},{3,2},{4,5},{5,4},{6,7},{7,6},{8,9},{9,8},{10,11... | collective-permute-start | bytes 5505032 | tf_op jit(solution)/shard_map/ppermute | solution.py:311
  12.5 84.1 %collective-permute-start.8 = (bf16[64,128,128]{2,1,0:T(8,128)(2,1)}, bf16[64,128,128]{2,1,0:T(8,128)(2,1)}, u32[]{:S(2)}, u32[]{:S(2)}) collective-permute-start(bf16[64,128,128]{2,1,0:T(8,128)(2,1)} %collective-permute-done.3.refs_8_), channel_id=1, source_target_pairs={{4,6},{2,0},{5,7},{3,1},{12,14},{10,8},{13,15},{11,9},{20,22},{18,... | collective-permute-start | bytes 6291464 | tf_op jit(solution)/shard_map/ppermute | solution.py:369
  50.8 43.9 %collective-permute-start.5 = (bf16[56,128,128]{2,1,0:T(8,128)(2,1)}, bf16[56,128,128]{2,1,0:T(8,128)(2,1)}, u32[]{:S(2)}, u32[]{:S(2)}) collective-permute-start(bf16[56,128,128]{2,1,0:T(8,128)(2,1)} %collective-permute-done.4.refs_3_), channel_id=1, source_target_pairs={{0,1},{1,0},{2,3},{3,2},{4,5},{5,4},{6,7},{7,6},{8,9},{9,8},{10,11... | collective-permute-start | bytes 5505032 | tf_op jit(solution)/shard_map/ppermute | solution.py:311
  53.0 3.3 %collective-permute-start.6 = (s32[7,3,64]{2,0,1:T(8,128)S(1)}, s32[7,3,64]{2,0,1:T(8,128)S(1)}, u32[]{:S(2)}, u32[]{:S(2)}) collective-permute-start(s32[7,3,64]{2,0,1:T(8,128)S(1)} %bitcast.46), channel_id=1, source_target_pairs={{0,1},{1,0},{2,3},{3,2},{4,5},{5,4},{6,7},{7,6},{8,9},{9,8},{10,11... | collective-permute-start | bytes 16136 | tf_op jit(solution)/shard_map/ppermute | solution.py:311
  94.6 2.0 %copy-start = (bf16[64,128,128]{2,1,0:T(8,128)(2,1)}, bf16[64,128,128]{2,1,0:T(8,128)(2,1)S(1)}, u32[]{:S(2)}) copy-start(bf16[64,128,128]{2,1,0:T(8,128)(2,1)S(1)} %collective-permute-done.refs_9_) | copy-start | bytes 6291460
  94.6 47.1 %collective-permute-start.7 = (bf16[64,128,128]{2,1,0:T(8,128)(2,1)S(1)}, bf16[64,128,128]{2,1,0:T(8,128)(2,1)S(1)}, u32[]{:S(2)}, u32[]{:S(2)}) collective-permute-start(bf16[64,128,128]{2,1,0:T(8,128)(2,1)S(1)} %collective-permute-done.refs_9_), channel_id=1, source_target_pairs={{4,6},{2,0},{5,7},{3,1},{12,14},{10,8},{13,15},{11,9},{20,22},{18,... | collective-permute-start | bytes 6291464 | tf_op jit(solution)/shard_map/ppermute | solution.py:369
  109.8 5.9 %collective-permute-start.10 = (f32[28,128,128]{2,1,0:T(8,128)S(1)}, f32[28,128,128]{2,1,0:T(8,128)S(1)}, u32[]{:S(2)}, u32[]{:S(2)}) collective-permute-start(f32[28,128,128]{2,1,0:T(8,128)S(1)} %get-tuple-element.37), channel_id=1, source_target_pairs={{0,1},{1,0},{2,3},{3,2},{4,5},{5,4},{6,7},{7,6},{8,9},{9,8},{10,11... | collective-permute-start | bytes 5505032 | tf_op jit(solution)/shard_map/ppermute | solution.py:311
  112.2 8.7 %collective-permute-start.11 = (f32[28,128,128]{2,1,0:T(8,128)S(1)}, f32[28,128,128]{2,1,0:T(8,128)S(1)}, u32[]{:S(2)}, u32[]{:S(2)}) collective-permute-start(f32[28,128,128]{2,1,0:T(8,128)S(1)} %get-tuple-element.38), channel_id=1, source_target_pairs={{0,1},{1,0},{2,3},{3,2},{4,5},{5,4},{6,7},{7,6},{8,9},{9,8},{10,11... | collective-permute-start | bytes 5505032 | tf_op jit(solution)/shard_map/ppermute | solution.py:311
  112.3 8.8 %collective-permute-start.12 = (f32[28,128,128]{2,1,0:T(8,128)}, f32[28,128,128]{2,1,0:T(8,128)S(1)}, u32[]{:S(2)}, u32[]{:S(2)}) collective-permute-start(f32[28,128,128]{2,1,0:T(8,128)} %get-tuple-element.39), channel_id=1, source_target_pairs={{0,1},{1,0},{2,3},{3,2},{4,5},{5,4},{6,7},{7,6},{8,9},{9,8},{10,11... | collective-permute-start | bytes 5505032 | tf_op jit(solution)/shard_map/ppermute | solution.py:311
  112.7 10.8 %collective-permute-start.9 = (f32[28,128,128]{2,1,0:T(8,128)S(1)}, f32[28,128,128]{2,1,0:T(8,128)S(1)}, u32[]{:S(2)}, u32[]{:S(2)}) collective-permute-start(f32[28,128,128]{2,1,0:T(8,128)S(1)} %get-tuple-element.36), channel_id=1, source_target_pairs={{0,1},{1,0},{2,3},{3,2},{4,5},{5,4},{6,7},{7,6},{8,9},{9,8},{10,11... | collective-permute-start | bytes 5505032 | tf_op jit(solution)/shard_map/ppermute | solution.py:311
  141.8 7.0 %collective-permute-start.13 = (bf16[64,128,128]{2,1,0:T(8,128)(2,1)S(1)}, bf16[64,128,128]{2,1,0:T(8,128)(2,1)S(1)}, u32[]{:S(2)}, u32[]{:S(2)}) collective-permute-start(bf16[64,128,128]{2,1,0:T(8,128)(2,1)S(1)} %collective-permute-done.7.left), channel_id=1, source_target_pairs={{0,1},{1,0},{2,3},{3,2},{4,5},{5,4},{6,7},{7,6},{8,9},{9,8},{10,11... | collective-permute-start | bytes 6291464 | tf_op jit(solution)/shard_map/ppermute | solution.py:311

commit v21 on v20

--- a/solution.py
+++ b/solution.py
@@ -10,7 +10,9 @@
 NBQ = 32
 UNROLL = 16
 PARTS = 4
-PART_UNROLL = 8
+LAST_PARTS = 2
+PART_UNROLL = 16
+PIECES = 2
 
 
 def chosen_products(packed, classes, panels, todo, shape, layers, spare, first_left=0):
@@ -57,8 +59,8 @@
 
 def sort_products(packed, base, kind, shape, sorted_out, spare, first_left):
     step_count, columns, slots = shape
-    room, counts, size = part_room(shape), PARTS * part_room(shape), spare // PARTS
-    for part in range(PARTS):
+    room, counts, size = part_room(shape), LAST_PARTS * part_room(shape), spare // LAST_PARTS
+    for part in range(LAST_PARTS):
         sorted_out[counts + part] = jnp.int32(0)
     for extra in range(-(-step_count // columns)):
         step = lax.rem(kind + step_count // 2, columns) + extra * columns
@@ -69,7 +71,7 @@
             for lane in range(8):
                 entry = packed[first + group * 8 + lane]
                 result, part = entry & 1023, jnp.int32(0)
-                for bound in range(1, PARTS):
+                for bound in range(1, LAST_PARTS):
                     part += (result >= bound * size).astype(jnp.int32)
                 count = sorted_out[counts + part]
                 sorted_out[part * room + count] = entry
@@ -77,7 +79,7 @@
             return carry
 
         lax.fori_loop(0, groups, place, jnp.int32(0))
-    for part in range(PARTS):
+    for part in range(LAST_PARTS):
         count = sorted_out[counts + part]
         for extra in range(PART_UNROLL - 1):
             sorted_out[part * room + count + extra] = jnp.int32(first_left << 10 | spare)
@@ -256,7 +258,7 @@
         functools.partial(own_kernel, shape, kind_at),
         out_shape=[
             pltpu.VMEM(given.shape, given.dtype),
-            jax.ShapeDtypeStruct((PARTS * part_room(shape) + PARTS,), jnp.int32),
+            jax.ShapeDtypeStruct((LAST_PARTS * part_room(shape) + LAST_PARTS,), jnp.int32),
         ],
         in_specs=[in_scalar] * 2 + [in_vector] * 3,
         out_specs=[in_vector, in_scalar],
@@ -270,14 +272,17 @@
 def other_kernel(shape, sorted_lists, right, given, left, out, work, rounded, sems):
     del given
     slots, room, spare = shape[2], part_room(shape), work.shape[0] - 1
-    size, copies = spare // PARTS, []
-    for part in range(PARTS):
-        count = sorted_lists[PARTS * room + part]
+    size, copies = spare // LAST_PARTS, []
+    for part in range(LAST_PARTS):
+        count = sorted_lists[LAST_PARTS * room + part]
         add_chosen(sorted_lists, count, left, right, work, slots, part * room, PART_UNROLL)
-        span = pl.ds(part * size, size if part < PARTS - 1 else spare - part * size)
-        rounded[span] = work[span].astype(rounded.dtype)
-        copies.append(pltpu.make_async_copy(rounded.at[span], out.at[span], sems.at[part]))
-        copies[-1].start()
+        last = (part + 1) * size if part < LAST_PARTS - 1 else spare
+        cuts = [part * size + (last - part * size) * piece // PIECES for piece in range(PIECES + 1)]
+        for first, after in zip(cuts, cuts[1:]):
+            span = pl.ds(first, after - first)
+            rounded[span] = work[span].astype(rounded.dtype)
+            copies.append(pltpu.make_async_copy(rounded.at[span], out.at[span], sems.at[len(copies)]))
+            copies[-1].start()
     for copy in copies:
         copy.wait()
 
@@ -295,7 +300,7 @@
         out_specs=[pl.BlockSpec(memory_space=pl.ANY), in_vector],
         scratch_shapes=[
             pltpu.VMEM((result_slots, rows, width), jnp.bfloat16),
-            pltpu.SemaphoreType.DMA((PARTS,)),
+            pltpu.SemaphoreType.DMA((LAST_PARTS * PIECES,)),
         ],
         input_output_aliases={2: 1},
         compiler_params=pltpu.CompilerParams(vmem_limit_bytes=12 << 20),

time: 154 us -> 153 us (level)
  no operation moved by 1% of the time
where the time goes in v21:
time: 153 us; the launch traced here: 152 us
  waiting for transfers between devices  106 us (69%)
  starting transfers between devices  21.9 us (14%)
  Pallas kernels  21.9 us (14%)
  local copies, waits for them, and re-layouts  1.93 us (1%)
    ppermute x5, waiting for transfers between devices, hop(): return lax.ppermute(value, 'col', pairs)  60.7 us
    ppermute x1, waiting for transfers between devices, line(): met = lax.ppermute(right_own, 'row', [(0, 1), (1, 0)])  32.1 us
    ppermute x8, waiting for transfers between devices, swapped(): return lax.ppermute(value, 'dep', [(0, 1), (1, 0)])  13.7 us
    pallas_call x1, Pallas kernels, product_sums(): pl.pallas_call(functools.partial(sum_kernel, panel_spans, right_spans, gi...  13.1 us
    ppermute x5, starting transfers between devices, hop(): return lax.ppermute(value, 'col', pairs)  11 us
    ppermute x8, starting transfers between devices, swapped(): return lax.ppermute(value, 'dep', [(0, 1), (1, 0)])  9.67 us
    pallas_call x1, Pallas kernels, add_other(): pl.pallas_call(functools.partial(other_kernel, shape), out_shape=[jax.Sha...  3.95 us
    pallas_call x1, Pallas kernels, add_own(): pl.pallas_call(functools.partial(own_kernel, shape, kind_at), out_shape=[...  3.92 us
  transfers between devices with their start and end apart: 14, of which 10 were waited for; matrix products, arithmetic and copies ran while one was open for 1% of the time, Pallas kernels for 12%

profile of v21, /device:TPU:1, one launch (start us, length us, event | category | flops | bytes accessed | tf_op | source)
XLA Modules:
  0.0 152.5 jit_solution(15465941084591037342)
XLA Ops:
  0.0 2.0 %collective-permute-start.3 = (bf16[64,128,128]{2,1,0:T(8,128)(2,1)}, bf16[64,128,128]{2,1,0:T(8,128)(2,1)}, u32[]{:S(2)}, u32[]{:S(2)}) collective-permute-start(bf16[64,128,128]{2,1,0:T(8,128)(2,1)} %bitcast.37), channel_id=1, source_target_pairs={{2,4},{4,2},{3,5},{5,3},{10,12},{12,10},{11,13},{13,11},{18,20},{2... | collective-permute-start | bytes 6291464 | tf_op jit(solution)/shard_map/ppermute | solution.py:374
  2.0 3.4 %collective-permute-start.2 = (bf16[64,128,128]{2,1,0:T(8,128)(2,1)}, bf16[64,128,128]{2,1,0:T(8,128)(2,1)}, u32[]{:S(2)}, u32[]{:S(2)}) collective-permute-start(bf16[64,128,128]{2,1,0:T(8,128)(2,1)} %bitcast.38), channel_id=1, source_target_pairs={{0,2},{2,0},{4,6},{6,4},{1,3},{3,1},{5,7},{7,5},{8,10},{10,8},{12,... | collective-permute-start | bytes 6291464 | tf_op jit(solution)/shard_map/ppermute | solution.py:374
  5.4 1.2 collective-permute-start.4
  6.6 3.0 %collective-permute-start = (bf16[64,128,128]{2,1,0:T(8,128)(2,1)}, bf16[64,128,128]{2,1,0:T(8,128)(2,1)S(1)}, u32[]{:S(2)}, u32[]{:S(2)}) collective-permute-start(bf16[64,128,128]{2,1,0:T(8,128)(2,1)} %bitcast.39), channel_id=1, source_target_pairs={{0,4},{6,2},{1,5},{7,3},{8,12},{14,10},{9,13},{15,11},{16,20},{22,... | collective-permute-start | bytes 6291464 | tf_op jit(solution)/shard_map/ppermute | solution.py:374
  9.7 1.6 %collective-permute-start.1 = (bf16[56,128,128]{2,1,0:T(8,128)(2,1)}, bf16[56,128,128]{2,1,0:T(8,128)(2,1)}, u32[]{:S(2)}, u32[]{:S(2)}) collective-permute-start(bf16[56,128,128]{2,1,0:T(8,128)(2,1)} %bitcast.42), channel_id=1, source_target_pairs={{0,1},{1,0},{2,3},{3,2},{4,5},{5,4},{6,7},{7,6},{8,9},{9,8},{10,11... | collective-permute-start | bytes 5505032 | tf_op jit(solution)/shard_map/ppermute | solution.py:316
  11.2 0.7 copy.13
  12.5 1.3 collective-permute-start.8
  13.9 32.1 %collective-permute-done.4.refs_3_ = bf16[56,128,128]{2,1,0:T(8,128)(2,1)} collective-permute-done((bf16[56,128,128]{2,1,0:T(8,128)(2,1)}, bf16[56,128,128]{2,1,0:T(8,128)(2,1)}, u32[]{:S(2)}, u32[]{:S(2)}) %collective-permute-start.4) | collective-permute-done | bytes 1835040 | tf_op jit(solution)/shard_map/ppermute | solution.py:380
  46.0 4.8 %collective-permute-done.2.refs_7_ = bf16[64,128,128]{2,1,0:T(8,128)(2,1)} collective-permute-done((bf16[64,128,128]{2,1,0:T(8,128)(2,1)}, bf16[64,128,128]{2,1,0:T(8,128)(2,1)}, u32[]{:S(2)}, u32[]{:S(2)}) %collective-permute-start.2) | collective-permute-done | bytes 2097184 | tf_op jit(solution)/shard_map/ppermute | solution.py:374
  50.8 2.3 %collective-permute-start.5 = (bf16[56,128,128]{2,1,0:T(8,128)(2,1)}, bf16[56,128,128]{2,1,0:T(8,128)(2,1)}, u32[]{:S(2)}, u32[]{:S(2)}) collective-permute-start(bf16[56,128,128]{2,1,0:T(8,128)(2,1)} %collective-permute-done.4.refs_3_), channel_id=1, source_target_pairs={{0,1},{1,0},{2,3},{3,2},{4,5},{5,4},{6,7},{7,6},{8,9},{9,8},{10,11... | collective-permute-start | bytes 5505032 | tf_op jit(solution)/shard_map/ppermute | solution.py:316
  53.3 3.0 %collective-permute-done.6 = s32[7,3,64]{2,0,1:T(8,128)S(1)} collective-permute-done((s32[7,3,64]{2,0,1:T(8,128)S(1)}, s32[7,3,64]{2,0,1:T(8,128)S(1)}, u32[]{:S(2)}, u32[]{:S(2)}) %collective-permute-start.6) | collective-permute-done | bytes 5408 | tf_op jit(solution)/shard_map/ppermute | solution.py:316
  56.7 37.9 %collective-permute-done.refs_9_ = bf16[64,128,128]{2,1,0:T(8,128)(2,1)S(1)} collective-permute-done((bf16[64,128,128]{2,1,0:T(8,128)(2,1)}, bf16[64,128,128]{2,1,0:T(8,128)(2,1)S(1)}, u32[]{:S(2)}, u32[]{:S(2)}) %collective-permute-start) | collective-permute-done | bytes 2097184 | tf_op jit(solution)/shard_map/ppermute | solution.py:374
  94.6 1.3 collective-permute-start.7
  95.9 0.7 collective-permute-done.8.refs_10_
  96.6 13.1 %shard_map.37 = (f32[28,128,128]{2,1,0:T(8,128)S(1)}, f32[28,128,128]{2,1,0:T(8,128)S(1)}, f32[28,128,128]{2,1,0:T(8,128)S(1)}, f32[28,128,128]{2,1,0:T(8,128)},...) custom-call(s32[448]{0:T(512)S(1)} %fusion.17.refs_0_, s32[7]{0:T(128)S(1)} %stack.33.refs_1_.scalars, ...), custom_call_target="tpu_custom_call" | custom-call | flops 1 | bytes 1 | tf_op jit(solution)/shard_map/pallas_call | solution.py:197
  109.8 2.4 %collective-permute-start.10 = (f32[28,128,128]{2,1,0:T(8,128)S(1)}, f32[28,128,128]{2,1,0:T(8,128)S(1)}, u32[]{:S(2)}, u32[]{:S(2)}) collective-permute-start(f32[28,128,128]{2,1,0:T(8,128)S(1)} %get-tuple-element.37), channel_id=1, source_target_pairs={{0,1},{1,0},{2,3},{3,2},{4,5},{5,4},{6,7},{7,6},{8,9},{9,8},{10,11... | collective-permute-start | bytes 5505032 | tf_op jit(solution)/shard_map/ppermute | solution.py:316
  112.8 2.8 %collective-permute-done.10.refs_1_ = f32[28,128,128]{2,1,0:T(8,128)S(1)} collective-permute-done((f32[28,128,128]{2,1,0:T(8,128)S(1)}, f32[28,128,128]{2,1,0:T(8,128)S(1)}, u32[]{:S(2)}, u32[]{:S(2)}) %collective-permute-start.10) | collective-permute-done | bytes 1835040 | tf_op jit(solution)/shard_map/ppermute | solution.py:316
  115.6 5.2 %collective-permute-done.11.refs_2_ = f32[28,128,128]{2,1,0:T(8,128)S(1)} collective-permute-done((f32[28,128,128]{2,1,0:T(8,128)S(1)}, f32[28,128,128]{2,1,0:T(8,128)S(1)}, u32[]{:S(2)}, u32[]{:S(2)}) %collective-permute-start.11) | collective-permute-done | bytes 1835040 | tf_op jit(solution)/shard_map/ppermute | solution.py:316
  121.1 2.4 %collective-permute-done.9.refs_0_ = f32[28,128,128]{2,1,0:T(8,128)S(1)} collective-permute-done((f32[28,128,128]{2,1,0:T(8,128)S(1)}, f32[28,128,128]{2,1,0:T(8,128)S(1)}, u32[]{:S(2)}, u32[]{:S(2)}) %collective-permute-start.9) | collective-permute-done | bytes 1835040 | tf_op jit(solution)/shard_map/ppermute | solution.py:316
  123.5 0.9 shard_map.38.given
  124.4 17.3 %collective-permute-done.7.left = bf16[64,128,128]{2,1,0:T(8,128)(2,1)S(1)} collective-permute-done((bf16[64,128,128]{2,1,0:T(8,128)(2,1)S(1)}, bf16[64,128,128]{2,1,0:T(8,128)(2,1)S(1)}, u32[]{:S(2)}, u32[]{:S(2)}) %collective-permute-start.7) | collective-permute-done | bytes 2097184 | tf_op jit(solution)/shard_map/ppermute | solution.py:374
  141.8 2.8 %collective-permute-start.13 = (bf16[64,128,128]{2,1,0:T(8,128)(2,1)S(1)}, bf16[64,128,128]{2,1,0:T(8,128)(2,1)S(1)}, u32[]{:S(2)}, u32[]{:S(2)}) collective-permute-start(bf16[64,128,128]{2,1,0:T(8,128)(2,1)S(1)} %collective-permute-done.7.left), channel_id=1, source_target_pairs={{0,1},{1,0},{2,3},{3,2},{4,5},{5,4},{6,7},{7,6},{8,9},{9,8},{10,11... | collective-permute-start | bytes 6291464 | tf_op jit(solution)/shard_map/ppermute | solution.py:316
  144.6 3.9 %shard_map.39 = (f32[113,128,128]{2,1,0:T(8,128)S(1)}, s32[290]{0:T(512)S(1)}) custom-call(s32[896]{0:T(1024)S(1)} %fusion.10.packed, s32[7]{0:T(128)S(1)} %stack.33.refs_1_.scalars, bf16[224,128,128]{2,1,0:T(8,128)(2,1)S(1)} %get-tuple-element.41.right, f32[113,128,128]{2,1,0:T(8,128)S(1)} %shard_map.38.given, ...), custom_call_target="tpu_custom_call", output_to_operand_aliasing={{0}: (3, {})} | custom-call | flops 1 | bytes 1 | tf_op jit(solution)/shard_map/pallas_call | solution.py:257
  148.5 3.9 %shard_map.40 = (bf16[112,128,128]{2,1,0:T(8,128)(2,1)}, f32[113,128,128]{2,1,0:T(8,128)S(1)}) custom-call(s32[290]{0:T(512)S(1)} %get-tuple-element.44.sorted_lists, bf16[224,128,128]{2,1,0:T(8,128)(2,1)S(1)} %get-tuple-element.41.right, f32[113,128,128]{2,1,0:T(8,128)S(1)} %get-tuple-element.45.given, ...), custom_call_target="tpu_custom_call", output_to_operand_aliasing={{1}: (2, {})} | custom-call | flops 1 | bytes 1 | tf_op jit(solution)/shard_map/pallas_call | solution.py:293
  (35 shorter events, 2.1 us)
Async XLA Ops:
  0.0 12.5 %collective-permute-start.3 = (bf16[64,128,128]{2,1,0:T(8,128)(2,1)}, bf16[64,128,128]{2,1,0:T(8,128)(2,1)}, u32[]{:S(2)}, u32[]{:S(2)}) collective-permute-start(bf16[64,128,128]{2,1,0:T(8,128)(2,1)} %bitcast.37), channel_id=1, source_target_pairs={{2,4},{4,2},{3,5},{5,3},{10,12},{12,10},{11,13},{13,11},{18,20},{2... | collective-permute-start | bytes 6291464 | tf_op jit(solution)/shard_map/ppermute | solution.py:374
  2.0 48.8 %collective-permute-start.2 = (bf16[64,128,128]{2,1,0:T(8,128)(2,1)}, bf16[64,128,128]{2,1,0:T(8,128)(2,1)}, u32[]{:S(2)}, u32[]{:S(2)}) collective-permute-start(bf16[64,128,128]{2,1,0:T(8,128)(2,1)} %bitcast.38), channel_id=1, source_target_pairs={{0,2},{2,0},{4,6},{6,4},{1,3},{3,1},{5,7},{7,5},{8,10},{10,8},{12,... | collective-permute-start | bytes 6291464 | tf_op jit(solution)/shard_map/ppermute | solution.py:374
  5.4 40.6 %collective-permute-start.4 = (bf16[56,128,128]{2,1,0:T(8,128)(2,1)}, bf16[56,128,128]{2,1,0:T(8,128)(2,1)}, u32[]{:S(2)}, u32[]{:S(2)}) collective-permute-start(bf16[56,128,128]{2,1,0:T(8,128)(2,1)} %bitcast.41), channel_id=1, source_target_pairs={{0,8},{8,0},{1,9},{9,1},{2,10},{10,2},{3,11},{11,3},{4,12},{12,4},... | collective-permute-start | bytes 5505032 | tf_op jit(solution)/shard_map/ppermute | solution.py:380
  6.6 88.0 %collective-permute-start = (bf16[64,128,128]{2,1,0:T(8,128)(2,1)}, bf16[64,128,128]{2,1,0:T(8,128)(2,1)S(1)}, u32[]{:S(2)}, u32[]{:S(2)}) collective-permute-start(bf16[64,128,128]{2,1,0:T(8,128)(2,1)} %bitcast.39), channel_id=1, source_target_pairs={{0,4},{6,2},{1,5},{7,3},{8,12},{14,10},{9,13},{15,11},{16,20},{22,... | collective-permute-start | bytes 6291464 | tf_op jit(solution)/shard_map/ppermute | solution.py:374
  9.7 47.1 %collective-permute-start.1 = (bf16[56,128,128]{2,1,0:T(8,128)(2,1)}, bf16[56,128,128]{2,1,0:T(8,128)(2,1)}, u32[]{:S(2)}, u32[]{:S(2)}) collective-permute-start(bf16[56,128,128]{2,1,0:T(8,128)(2,1)} %bitcast.42), channel_id=1, source_target_pairs={{0,1},{1,0},{2,3},{3,2},{4,5},{5,4},{6,7},{7,6},{8,9},{9,8},{10,11... | collective-permute-start | bytes 5505032 | tf_op jit(solution)/shard_map/ppermute | solution.py:316
  12.5 84.1 %collective-permute-start.8 = (bf16[64,128,128]{2,1,0:T(8,128)(2,1)}, bf16[64,128,128]{2,1,0:T(8,128)(2,1)}, u32[]{:S(2)}, u32[]{:S(2)}) collective-permute-start(bf16[64,128,128]{2,1,0:T(8,128)(2,1)} %collective-permute-done.3.refs_8_), channel_id=1, source_target_pairs={{4,6},{2,0},{5,7},{3,1},{12,14},{10,8},{13,15},{11,9},{20,22},{18,... | collective-permute-start | bytes 6291464 | tf_op jit(solution)/shard_map/ppermute | solution.py:374
  50.8 43.9 %collective-permute-start.5 = (bf16[56,128,128]{2,1,0:T(8,128)(2,1)}, bf16[56,128,128]{2,1,0:T(8,128)(2,1)}, u32[]{:S(2)}, u32[]{:S(2)}) collective-permute-start(bf16[56,128,128]{2,1,0:T(8,128)(2,1)} %collective-permute-done.4.refs_3_), channel_id=1, source_target_pairs={{0,1},{1,0},{2,3},{3,2},{4,5},{5,4},{6,7},{7,6},{8,9},{9,8},{10,11... | collective-permute-start | bytes 5505032 | tf_op jit(solution)/shard_map/ppermute | solution.py:316
  53.0 3.3 %collective-permute-start.6 = (s32[7,3,64]{2,0,1:T(8,128)S(1)}, s32[7,3,64]{2,0,1:T(8,128)S(1)}, u32[]{:S(2)}, u32[]{:S(2)}) collective-permute-start(s32[7,3,64]{2,0,1:T(8,128)S(1)} %bitcast.46), channel_id=1, source_target_pairs={{0,1},{1,0},{2,3},{3,2},{4,5},{5,4},{6,7},{7,6},{8,9},{9,8},{10,11... | collective-permute-start | bytes 16136 | tf_op jit(solution)/shard_map/ppermute | solution.py:316
  94.6 2.0 %copy-start = (bf16[64,128,128]{2,1,0:T(8,128)(2,1)}, bf16[64,128,128]{2,1,0:T(8,128)(2,1)S(1)}, u32[]{:S(2)}) copy-start(bf16[64,128,128]{2,1,0:T(8,128)(2,1)S(1)} %collective-permute-done.refs_9_) | copy-start | bytes 6291460
  94.6 47.1 %collective-permute-start.7 = (bf16[64,128,128]{2,1,0:T(8,128)(2,1)S(1)}, bf16[64,128,128]{2,1,0:T(8,128)(2,1)S(1)}, u32[]{:S(2)}, u32[]{:S(2)}) collective-permute-start(bf16[64,128,128]{2,1,0:T(8,128)(2,1)S(1)} %collective-permute-done.refs_9_), channel_id=1, source_target_pairs={{4,6},{2,0},{5,7},{3,1},{12,14},{10,8},{13,15},{11,9},{20,22},{18,... | collective-permute-start | bytes 6291464 | tf_op jit(solution)/shard_map/ppermute | solution.py:374
  109.8 5.9 %collective-permute-start.10 = (f32[28,128,128]{2,1,0:T(8,128)S(1)}, f32[28,128,128]{2,1,0:T(8,128)S(1)}, u32[]{:S(2)}, u32[]{:S(2)}) collective-permute-start(f32[28,128,128]{2,1,0:T(8,128)S(1)} %get-tuple-element.37), channel_id=1, source_target_pairs={{0,1},{1,0},{2,3},{3,2},{4,5},{5,4},{6,7},{7,6},{8,9},{9,8},{10,11... | collective-permute-start | bytes 5505032 | tf_op jit(solution)/shard_map/ppermute | solution.py:316
  112.2 8.7 %collective-permute-start.11 = (f32[28,128,128]{2,1,0:T(8,128)S(1)}, f32[28,128,128]{2,1,0:T(8,128)S(1)}, u32[]{:S(2)}, u32[]{:S(2)}) collective-permute-start(f32[28,128,128]{2,1,0:T(8,128)S(1)} %get-tuple-element.38), channel_id=1, source_target_pairs={{0,1},{1,0},{2,3},{3,2},{4,5},{5,4},{6,7},{7,6},{8,9},{9,8},{10,11... | collective-permute-start | bytes 5505032 | tf_op jit(solution)/shard_map/ppermute | solution.py:316
  112.3 8.8 %collective-permute-start.12 = (f32[28,128,128]{2,1,0:T(8,128)}, f32[28,128,128]{2,1,0:T(8,128)S(1)}, u32[]{:S(2)}, u32[]{:S(2)}) collective-permute-start(f32[28,128,128]{2,1,0:T(8,128)} %get-tuple-element.39), channel_id=1, source_target_pairs={{0,1},{1,0},{2,3},{3,2},{4,5},{5,4},{6,7},{7,6},{8,9},{9,8},{10,11... | collective-permute-start | bytes 5505032 | tf_op jit(solution)/shard_map/ppermute | solution.py:316
  112.7 10.8 %collective-permute-start.9 = (f32[28,128,128]{2,1,0:T(8,128)S(1)}, f32[28,128,128]{2,1,0:T(8,128)S(1)}, u32[]{:S(2)}, u32[]{:S(2)}) collective-permute-start(f32[28,128,128]{2,1,0:T(8,128)S(1)} %get-tuple-element.36), channel_id=1, source_target_pairs={{0,1},{1,0},{2,3},{3,2},{4,5},{5,4},{6,7},{7,6},{8,9},{9,8},{10,11... | collective-permute-start | bytes 5505032 | tf_op jit(solution)/shard_map/ppermute | solution.py:316
  141.8 6.7 %collective-permute-start.13 = (bf16[64,128,128]{2,1,0:T(8,128)(2,1)S(1)}, bf16[64,128,128]{2,1,0:T(8,128)(2,1)S(1)}, u32[]{:S(2)}, u32[]{:S(2)}) collective-permute-start(bf16[64,128,128]{2,1,0:T(8,128)(2,1)S(1)} %collective-permute-done.7.left), channel_id=1, source_target_pairs={{0,1},{1,0},{2,3},{3,2},{4,5},{5,4},{6,7},{7,6},{8,9},{9,8},{10,11... | collective-permute-start | bytes 6291464 | tf_op jit(solution)/shard_map/ppermute | solution.py:316

commit v22 on v21

--- a/solution.py
+++ b/solution.py
@@ -11,8 +11,8 @@
 UNROLL = 16
 PARTS = 4
 LAST_PARTS = 2
-PART_UNROLL = 16
-PIECES = 2
+PART_UNROLL = 32
+PIECES = 4
 
 
 def chosen_products(packed, classes, panels, todo, shape, layers, spare, first_left=0):

time: 153 us -> 153 us (level)
  no operation moved by 1% of the time
where the time goes in v22:
time: 153 us; the launch traced here: 152 us
  waiting for transfers between devices  106 us (69%)
  starting transfers between devices  21.9 us (14%)
  Pallas kernels  21.6 us (14%)
  local copies, waits for them, and re-layouts  1.93 us (1%)
    ppermute x5, waiting for transfers between devices, hop(): return lax.ppermute(value, 'col', pairs)  60.7 us
    ppermute x1, waiting for transfers between devices, line(): met = lax.ppermute(right_own, 'row', [(0, 1), (1, 0)])  32.1 us
    ppermute x8, waiting for transfers between devices, swapped(): return lax.ppermute(value, 'dep', [(0, 1), (1, 0)])  13.7 us
    pallas_call x1, Pallas kernels, product_sums(): pl.pallas_call(functools.partial(sum_kernel, panel_spans, right_spans, gi...  13.1 us
    ppermute x5, starting transfers between devices, hop(): return lax.ppermute(value, 'col', pairs)  11 us
    ppermute x8, starting transfers between devices, swapped(): return lax.ppermute(value, 'dep', [(0, 1), (1, 0)])  9.67 us
    pallas_call x1, Pallas kernels, add_own(): pl.pallas_call(functools.partial(own_kernel, shape, kind_at), out_shape=[...  3.94 us
    pallas_call x1, Pallas kernels, add_other(): pl.pallas_call(functools.partial(other_kernel, shape), out_shape=[jax.Sha...  3.57 us
  transfers between devices with their start and end apart: 14, of which 10 were waited for; matrix products, arithmetic and copies ran while one was open for 1% of the time, Pallas kernels for 12%

profile of v22, /device:TPU:1, one launch (start us, length us, event | category | flops | bytes accessed | tf_op | source)
XLA Modules:
  0.0 152.1 jit_solution(16437938983631429039)
XLA Ops:
  0.0 2.0 %collective-permute-start.3 = (bf16[64,128,128]{2,1,0:T(8,128)(2,1)}, bf16[64,128,128]{2,1,0:T(8,128)(2,1)}, u32[]{:S(2)}, u32[]{:S(2)}) collective-permute-start(bf16[64,128,128]{2,1,0:T(8,128)(2,1)} %bitcast.37), channel_id=1, source_target_pairs={{2,4},{4,2},{3,5},{5,3},{10,12},{12,10},{11,13},{13,11},{18,20},{2... | collective-permute-start | bytes 6291464 | tf_op jit(solution)/shard_map/ppermute | solution.py:374
  2.0 3.4 %collective-permute-start.2 = (bf16[64,128,128]{2,1,0:T(8,128)(2,1)}, bf16[64,128,128]{2,1,0:T(8,128)(2,1)}, u32[]{:S(2)}, u32[]{:S(2)}) collective-permute-start(bf16[64,128,128]{2,1,0:T(8,128)(2,1)} %bitcast.38), channel_id=1, source_target_pairs={{0,2},{2,0},{4,6},{6,4},{1,3},{3,1},{5,7},{7,5},{8,10},{10,8},{12,... | collective-permute-start | bytes 6291464 | tf_op jit(solution)/shard_map/ppermute | solution.py:374
  5.4 1.2 collective-permute-start.4
  6.6 3.0 %collective-permute-start = (bf16[64,128,128]{2,1,0:T(8,128)(2,1)}, bf16[64,128,128]{2,1,0:T(8,128)(2,1)S(1)}, u32[]{:S(2)}, u32[]{:S(2)}) collective-permute-start(bf16[64,128,128]{2,1,0:T(8,128)(2,1)} %bitcast.39), channel_id=1, source_target_pairs={{0,4},{6,2},{1,5},{7,3},{8,12},{14,10},{9,13},{15,11},{16,20},{22,... | collective-permute-start | bytes 6291464 | tf_op jit(solution)/shard_map/ppermute | solution.py:374
  9.7 1.6 %collective-permute-start.1 = (bf16[56,128,128]{2,1,0:T(8,128)(2,1)}, bf16[56,128,128]{2,1,0:T(8,128)(2,1)}, u32[]{:S(2)}, u32[]{:S(2)}) collective-permute-start(bf16[56,128,128]{2,1,0:T(8,128)(2,1)} %bitcast.42), channel_id=1, source_target_pairs={{0,1},{1,0},{2,3},{3,2},{4,5},{5,4},{6,7},{7,6},{8,9},{9,8},{10,11... | collective-permute-start | bytes 5505032 | tf_op jit(solution)/shard_map/ppermute | solution.py:316
  11.2 0.7 copy.13
  12.5 1.3 collective-permute-start.8
  13.9 32.1 %collective-permute-done.4.refs_3_ = bf16[56,128,128]{2,1,0:T(8,128)(2,1)} collective-permute-done((bf16[56,128,128]{2,1,0:T(8,128)(2,1)}, bf16[56,128,128]{2,1,0:T(8,128)(2,1)}, u32[]{:S(2)}, u32[]{:S(2)}) %collective-permute-start.4) | collective-permute-done | bytes 1835040 | tf_op jit(solution)/shard_map/ppermute | solution.py:380
  46.0 4.8 %collective-permute-done.2.refs_7_ = bf16[64,128,128]{2,1,0:T(8,128)(2,1)} collective-permute-done((bf16[64,128,128]{2,1,0:T(8,128)(2,1)}, bf16[64,128,128]{2,1,0:T(8,128)(2,1)}, u32[]{:S(2)}, u32[]{:S(2)}) %collective-permute-start.2) | collective-permute-done | bytes 2097184 | tf_op jit(solution)/shard_map/ppermute | solution.py:374
  50.8 2.3 %collective-permute-start.5 = (bf16[56,128,128]{2,1,0:T(8,128)(2,1)}, bf16[56,128,128]{2,1,0:T(8,128)(2,1)}, u32[]{:S(2)}, u32[]{:S(2)}) collective-permute-start(bf16[56,128,128]{2,1,0:T(8,128)(2,1)} %collective-permute-done.4.refs_3_), channel_id=1, source_target_pairs={{0,1},{1,0},{2,3},{3,2},{4,5},{5,4},{6,7},{7,6},{8,9},{9,8},{10,11... | collective-permute-start | bytes 5505032 | tf_op jit(solution)/shard_map/ppermute | solution.py:316
  53.3 3.0 %collective-permute-done.6 = s32[7,3,64]{2,0,1:T(8,128)S(1)} collective-permute-done((s32[7,3,64]{2,0,1:T(8,128)S(1)}, s32[7,3,64]{2,0,1:T(8,128)S(1)}, u32[]{:S(2)}, u32[]{:S(2)}) %collective-permute-start.6) | collective-permute-done | bytes 5408 | tf_op jit(solution)/shard_map/ppermute | solution.py:316
  56.7 37.9 %collective-permute-done.refs_9_ = bf16[64,128,128]{2,1,0:T(8,128)(2,1)S(1)} collective-permute-done((bf16[64,128,128]{2,1,0:T(8,128)(2,1)}, bf16[64,128,128]{2,1,0:T(8,128)(2,1)S(1)}, u32[]{:S(2)}, u32[]{:S(2)}) %collective-permute-start) | collective-permute-done | bytes 2097184 | tf_op jit(solution)/shard_map/ppermute | solution.py:374
  94.6 1.3 collective-permute-start.7
  95.9 0.7 collective-permute-done.8.refs_10_
  96.6 13.1 %shard_map.37 = (f32[28,128,128]{2,1,0:T(8,128)S(1)}, f32[28,128,128]{2,1,0:T(8,128)S(1)}, f32[28,128,128]{2,1,0:T(8,128)S(1)}, f32[28,128,128]{2,1,0:T(8,128)},...) custom-call(s32[448]{0:T(512)S(1)} %fusion.17.refs_0_, s32[7]{0:T(128)S(1)} %stack.33.refs_1_.scalars, ...), custom_call_target="tpu_custom_call" | custom-call | flops 1 | bytes 1 | tf_op jit(solution)/shard_map/pallas_call | solution.py:197
  109.8 2.4 %collective-permute-start.10 = (f32[28,128,128]{2,1,0:T(8,128)S(1)}, f32[28,128,128]{2,1,0:T(8,128)S(1)}, u32[]{:S(2)}, u32[]{:S(2)}) collective-permute-start(f32[28,128,128]{2,1,0:T(8,128)S(1)} %get-tuple-element.37), channel_id=1, source_target_pairs={{0,1},{1,0},{2,3},{3,2},{4,5},{5,4},{6,7},{7,6},{8,9},{9,8},{10,11... | collective-permute-start | bytes 5505032 | tf_op jit(solution)/shard_map/ppermute | solution.py:316
  112.8 2.8 %collective-permute-done.10.refs_1_ = f32[28,128,128]{2,1,0:T(8,128)S(1)} collective-permute-done((f32[28,128,128]{2,1,0:T(8,128)S(1)}, f32[28,128,128]{2,1,0:T(8,128)S(1)}, u32[]{:S(2)}, u32[]{:S(2)}) %collective-permute-start.10) | collective-permute-done | bytes 1835040 | tf_op jit(solution)/shard_map/ppermute | solution.py:316
  115.6 5.2 %collective-permute-done.11.refs_2_ = f32[28,128,128]{2,1,0:T(8,128)S(1)} collective-permute-done((f32[28,128,128]{2,1,0:T(8,128)S(1)}, f32[28,128,128]{2,1,0:T(8,128)S(1)}, u32[]{:S(2)}, u32[]{:S(2)}) %collective-permute-start.11) | collective-permute-done | bytes 1835040 | tf_op jit(solution)/shard_map/ppermute | solution.py:316
  121.1 2.4 %collective-permute-done.9.refs_0_ = f32[28,128,128]{2,1,0:T(8,128)S(1)} collective-permute-done((f32[28,128,128]{2,1,0:T(8,128)S(1)}, f32[28,128,128]{2,1,0:T(8,128)S(1)}, u32[]{:S(2)}, u32[]{:S(2)}) %collective-permute-start.9) | collective-permute-done | bytes 1835040 | tf_op jit(solution)/shard_map/ppermute | solution.py:316
  123.5 0.9 shard_map.38.given
  124.4 17.3 %collective-permute-done.7.left = bf16[64,128,128]{2,1,0:T(8,128)(2,1)S(1)} collective-permute-done((bf16[64,128,128]{2,1,0:T(8,128)(2,1)S(1)}, bf16[64,128,128]{2,1,0:T(8,128)(2,1)S(1)}, u32[]{:S(2)}, u32[]{:S(2)}) %collective-permute-start.7) | collective-permute-done | bytes 2097184 | tf_op jit(solution)/shard_map/ppermute | solution.py:374
  141.8 2.8 %collective-permute-start.13 = (bf16[64,128,128]{2,1,0:T(8,128)(2,1)S(1)}, bf16[64,128,128]{2,1,0:T(8,128)(2,1)S(1)}, u32[]{:S(2)}, u32[]{:S(2)}) collective-permute-start(bf16[64,128,128]{2,1,0:T(8,128)(2,1)S(1)} %collective-permute-done.7.left), channel_id=1, source_target_pairs={{0,1},{1,0},{2,3},{3,2},{4,5},{5,4},{6,7},{7,6},{8,9},{9,8},{10,11... | collective-permute-start | bytes 6291464 | tf_op jit(solution)/shard_map/ppermute | solution.py:316
  144.6 3.9 %shard_map.39 = (f32[113,128,128]{2,1,0:T(8,128)S(1)}, s32[322]{0:T(512)S(1)}) custom-call(s32[896]{0:T(1024)S(1)} %fusion.10.packed, s32[7]{0:T(128)S(1)} %stack.33.refs_1_.scalars, bf16[224,128,128]{2,1,0:T(8,128)(2,1)S(1)} %get-tuple-element.41.right, f32[113,128,128]{2,1,0:T(8,128)S(1)} %shard_map.38.given, ...), custom_call_target="tpu_custom_call", output_to_operand_aliasing={{0}: (3, {})} | custom-call | flops 1 | bytes 1 | tf_op jit(solution)/shard_map/pallas_call | solution.py:257
  148.5 3.6 %shard_map.40 = (bf16[112,128,128]{2,1,0:T(8,128)(2,1)}, f32[113,128,128]{2,1,0:T(8,128)S(1)}) custom-call(s32[322]{0:T(512)S(1)} %get-tuple-element.44.sorted_lists, bf16[224,128,128]{2,1,0:T(8,128)(2,1)S(1)} %get-tuple-element.41.right, f32[113,128,128]{2,1,0:T(8,128)S(1)} %get-tuple-element.45.given, ...), custom_call_target="tpu_custom_call", output_to_operand_aliasing={{1}: (2, {})} | custom-call | flops 1 | bytes 1 | tf_op jit(solution)/shard_map/pallas_call | solution.py:293
  (35 shorter events, 2.1 us)
Async XLA Ops:
  0.0 12.5 %collective-permute-start.3 = (bf16[64,128,128]{2,1,0:T(8,128)(2,1)}, bf16[64,128,128]{2,1,0:T(8,128)(2,1)}, u32[]{:S(2)}, u32[]{:S(2)}) collective-permute-start(bf16[64,128,128]{2,1,0:T(8,128)(2,1)} %bitcast.37), channel_id=1, source_target_pairs={{2,4},{4,2},{3,5},{5,3},{10,12},{12,10},{11,13},{13,11},{18,20},{2... | collective-permute-start | bytes 6291464 | tf_op jit(solution)/shard_map/ppermute | solution.py:374
  2.0 48.8 %collective-permute-start.2 = (bf16[64,128,128]{2,1,0:T(8,128)(2,1)}, bf16[64,128,128]{2,1,0:T(8,128)(2,1)}, u32[]{:S(2)}, u32[]{:S(2)}) collective-permute-start(bf16[64,128,128]{2,1,0:T(8,128)(2,1)} %bitcast.38), channel_id=1, source_target_pairs={{0,2},{2,0},{4,6},{6,4},{1,3},{3,1},{5,7},{7,5},{8,10},{10,8},{12,... | collective-permute-start | bytes 6291464 | tf_op jit(solution)/shard_map/ppermute | solution.py:374
  5.4 40.6 %collective-permute-start.4 = (bf16[56,128,128]{2,1,0:T(8,128)(2,1)}, bf16[56,128,128]{2,1,0:T(8,128)(2,1)}, u32[]{:S(2)}, u32[]{:S(2)}) collective-permute-start(bf16[56,128,128]{2,1,0:T(8,128)(2,1)} %bitcast.41), channel_id=1, source_target_pairs={{0,8},{8,0},{1,9},{9,1},{2,10},{10,2},{3,11},{11,3},{4,12},{12,4},... | collective-permute-start | bytes 5505032 | tf_op jit(solution)/shard_map/ppermute | solution.py:380
  6.6 88.0 %collective-permute-start = (bf16[64,128,128]{2,1,0:T(8,128)(2,1)}, bf16[64,128,128]{2,1,0:T(8,128)(2,1)S(1)}, u32[]{:S(2)}, u32[]{:S(2)}) collective-permute-start(bf16[64,128,128]{2,1,0:T(8,128)(2,1)} %bitcast.39), channel_id=1, source_target_pairs={{0,4},{6,2},{1,5},{7,3},{8,12},{14,10},{9,13},{15,11},{16,20},{22,... | collective-permute-start | bytes 6291464 | tf_op jit(solution)/shard_map/ppermute | solution.py:374
  9.7 47.1 %collective-permute-start.1 = (bf16[56,128,128]{2,1,0:T(8,128)(2,1)}, bf16[56,128,128]{2,1,0:T(8,128)(2,1)}, u32[]{:S(2)}, u32[]{:S(2)}) collective-permute-start(bf16[56,128,128]{2,1,0:T(8,128)(2,1)} %bitcast.42), channel_id=1, source_target_pairs={{0,1},{1,0},{2,3},{3,2},{4,5},{5,4},{6,7},{7,6},{8,9},{9,8},{10,11... | collective-permute-start | bytes 5505032 | tf_op jit(solution)/shard_map/ppermute | solution.py:316
  12.5 84.1 %collective-permute-start.8 = (bf16[64,128,128]{2,1,0:T(8,128)(2,1)}, bf16[64,128,128]{2,1,0:T(8,128)(2,1)}, u32[]{:S(2)}, u32[]{:S(2)}) collective-permute-start(bf16[64,128,128]{2,1,0:T(8,128)(2,1)} %collective-permute-done.3.refs_8_), channel_id=1, source_target_pairs={{4,6},{2,0},{5,7},{3,1},{12,14},{10,8},{13,15},{11,9},{20,22},{18,... | collective-permute-start | bytes 6291464 | tf_op jit(solution)/shard_map/ppermute | solution.py:374
  50.8 43.9 %collective-permute-start.5 = (bf16[56,128,128]{2,1,0:T(8,128)(2,1)}, bf16[56,128,128]{2,1,0:T(8,128)(2,1)}, u32[]{:S(2)}, u32[]{:S(2)}) collective-permute-start(bf16[56,128,128]{2,1,0:T(8,128)(2,1)} %collective-permute-done.4.refs_3_), channel_id=1, source_target_pairs={{0,1},{1,0},{2,3},{3,2},{4,5},{5,4},{6,7},{7,6},{8,9},{9,8},{10,11... | collective-permute-start | bytes 5505032 | tf_op jit(solution)/shard_map/ppermute | solution.py:316
  53.0 3.3 %collective-permute-start.6 = (s32[7,3,64]{2,0,1:T(8,128)S(1)}, s32[7,3,64]{2,0,1:T(8,128)S(1)}, u32[]{:S(2)}, u32[]{:S(2)}) collective-permute-start(s32[7,3,64]{2,0,1:T(8,128)S(1)} %bitcast.46), channel_id=1, source_target_pairs={{0,1},{1,0},{2,3},{3,2},{4,5},{5,4},{6,7},{7,6},{8,9},{9,8},{10,11... | collective-permute-start | bytes 16136 | tf_op jit(solution)/shard_map/ppermute | solution.py:316
  94.6 2.0 %copy-start = (bf16[64,128,128]{2,1,0:T(8,128)(2,1)}, bf16[64,128,128]{2,1,0:T(8,128)(2,1)S(1)}, u32[]{:S(2)}) copy-start(bf16[64,128,128]{2,1,0:T(8,128)(2,1)S(1)} %collective-permute-done.refs_9_) | copy-start | bytes 6291460
  94.6 47.1 %collective-permute-start.7 = (bf16[64,128,128]{2,1,0:T(8,128)(2,1)S(1)}, bf16[64,128,128]{2,1,0:T(8,128)(2,1)S(1)}, u32[]{:S(2)}, u32[]{:S(2)}) collective-permute-start(bf16[64,128,128]{2,1,0:T(8,128)(2,1)S(1)} %collective-permute-done.refs_9_), channel_id=1, source_target_pairs={{4,6},{2,0},{5,7},{3,1},{12,14},{10,8},{13,15},{11,9},{20,22},{18,... | collective-permute-start | bytes 6291464 | tf_op jit(solution)/shard_map/ppermute | solution.py:374
  109.8 5.9 %collective-permute-start.10 = (f32[28,128,128]{2,1,0:T(8,128)S(1)}, f32[28,128,128]{2,1,0:T(8,128)S(1)}, u32[]{:S(2)}, u32[]{:S(2)}) collective-permute-start(f32[28,128,128]{2,1,0:T(8,128)S(1)} %get-tuple-element.37), channel_id=1, source_target_pairs={{0,1},{1,0},{2,3},{3,2},{4,5},{5,4},{6,7},{7,6},{8,9},{9,8},{10,11... | collective-permute-start | bytes 5505032 | tf_op jit(solution)/shard_map/ppermute | solution.py:316
  112.2 8.7 %collective-permute-start.11 = (f32[28,128,128]{2,1,0:T(8,128)S(1)}, f32[28,128,128]{2,1,0:T(8,128)S(1)}, u32[]{:S(2)}, u32[]{:S(2)}) collective-permute-start(f32[28,128,128]{2,1,0:T(8,128)S(1)} %get-tuple-element.38), channel_id=1, source_target_pairs={{0,1},{1,0},{2,3},{3,2},{4,5},{5,4},{6,7},{7,6},{8,9},{9,8},{10,11... | collective-permute-start | bytes 5505032 | tf_op jit(solution)/shard_map/ppermute | solution.py:316
  112.3 8.8 %collective-permute-start.12 = (f32[28,128,128]{2,1,0:T(8,128)}, f32[28,128,128]{2,1,0:T(8,128)S(1)}, u32[]{:S(2)}, u32[]{:S(2)}) collective-permute-start(f32[28,128,128]{2,1,0:T(8,128)} %get-tuple-element.39), channel_id=1, source_target_pairs={{0,1},{1,0},{2,3},{3,2},{4,5},{5,4},{6,7},{7,6},{8,9},{9,8},{10,11... | collective-permute-start | bytes 5505032 | tf_op jit(solution)/shard_map/ppermute | solution.py:316
  112.7 10.8 %collective-permute-start.9 = (f32[28,128,128]{2,1,0:T(8,128)S(1)}, f32[28,128,128]{2,1,0:T(8,128)S(1)}, u32[]{:S(2)}, u32[]{:S(2)}) collective-permute-start(f32[28,128,128]{2,1,0:T(8,128)S(1)} %get-tuple-element.36), channel_id=1, source_target_pairs={{0,1},{1,0},{2,3},{3,2},{4,5},{5,4},{6,7},{7,6},{8,9},{9,8},{10,11... | collective-permute-start | bytes 5505032 | tf_op jit(solution)/shard_map/ppermute | solution.py:316
  141.8 6.7 %collective-permute-start.13 = (bf16[64,128,128]{2,1,0:T(8,128)(2,1)S(1)}, bf16[64,128,128]{2,1,0:T(8,128)(2,1)S(1)}, u32[]{:S(2)}, u32[]{:S(2)}) collective-permute-start(bf16[64,128,128]{2,1,0:T(8,128)(2,1)S(1)} %collective-permute-done.7.left), channel_id=1, source_target_pairs={{0,1},{1,0},{2,3},{3,2},{4,5},{5,4},{6,7},{7,6},{8,9},{9,8},{10,11... | collective-permute-start | bytes 6291464 | tf_op jit(solution)/shard_map/ppermute | solution.py:316

commit v23 on v21

--- a/solution.py
+++ b/solution.py
@@ -10,9 +10,9 @@
 NBQ = 32
 UNROLL = 16
 PARTS = 4
-LAST_PARTS = 2
+LAST_PARTS = 4
 PART_UNROLL = 16
-PIECES = 2
+PIECES = 1
 
 
 def chosen_products(packed, classes, panels, todo, shape, layers, spare, first_left=0):

time: 153 us -> 153 us (level)
  no operation moved by 1% of the time
where the time goes in v23:
time: 153 us
  waiting for transfers between devices  106 us (69%)
  Pallas kernels  22.3 us (15%)
  starting transfers between devices  21.9 us (14%)
  local copies, waits for them, and re-layouts  1.93 us (1%)
    ppermute x5, waiting for transfers between devices, hop(): return lax.ppermute(value, 'col', pairs)  60.7 us
    ppermute x1, waiting for transfers between devices, line(): met = lax.ppermute(right_own, 'row', [(0, 1), (1, 0)])  32.1 us
    ppermute x8, waiting for transfers between devices, swapped(): return lax.ppermute(value, 'dep', [(0, 1), (1, 0)])  13.7 us
    pallas_call x1, Pallas kernels, product_sums(): pl.pallas_call(functools.partial(sum_kernel, panel_spans, right_spans, gi...  13.1 us
    ppermute x5, starting transfers between devices, hop(): return lax.ppermute(value, 'col', pairs)  11 us
    ppermute x8, starting transfers between devices, swapped(): return lax.ppermute(value, 'dep', [(0, 1), (1, 0)])  9.67 us
    pallas_call x1, Pallas kernels, add_own(): pl.pallas_call(functools.partial(own_kernel, shape, kind_at), out_shape=[...  4.49 us
    pallas_call x1, Pallas kernels, add_other(): pl.pallas_call(functools.partial(other_kernel, shape), out_shape=[jax.Sha...  3.76 us
  transfers between devices with their start and end apart: 14, of which 10 were waited for; matrix products, arithmetic and copies ran while one was open for 1% of the time, Pallas kernels for 12%

profile of v23, /device:TPU:1, one launch (start us, length us, event | category | flops | bytes accessed | tf_op | source)
XLA Modules:
  0.0 152.8 jit_solution(4866541405342411198)
XLA Ops:
  0.0 2.0 %collective-permute-start.3 = (bf16[64,128,128]{2,1,0:T(8,128)(2,1)}, bf16[64,128,128]{2,1,0:T(8,128)(2,1)}, u32[]{:S(2)}, u32[]{:S(2)}) collective-permute-start(bf16[64,128,128]{2,1,0:T(8,128)(2,1)} %bitcast.37), channel_id=1, source_target_pairs={{2,4},{4,2},{3,5},{5,3},{10,12},{12,10},{11,13},{13,11},{18,20},{2... | collective-permute-start | bytes 6291464 | tf_op jit(solution)/shard_map/ppermute | solution.py:374
  2.0 3.4 %collective-permute-start.2 = (bf16[64,128,128]{2,1,0:T(8,128)(2,1)}, bf16[64,128,128]{2,1,0:T(8,128)(2,1)}, u32[]{:S(2)}, u32[]{:S(2)}) collective-permute-start(bf16[64,128,128]{2,1,0:T(8,128)(2,1)} %bitcast.38), channel_id=1, source_target_pairs={{0,2},{2,0},{4,6},{6,4},{1,3},{3,1},{5,7},{7,5},{8,10},{10,8},{12,... | collective-permute-start | bytes 6291464 | tf_op jit(solution)/shard_map/ppermute | solution.py:374
  5.4 1.2 collective-permute-start.4
  6.6 3.0 %collective-permute-start = (bf16[64,128,128]{2,1,0:T(8,128)(2,1)}, bf16[64,128,128]{2,1,0:T(8,128)(2,1)S(1)}, u32[]{:S(2)}, u32[]{:S(2)}) collective-permute-start(bf16[64,128,128]{2,1,0:T(8,128)(2,1)} %bitcast.39), channel_id=1, source_target_pairs={{0,4},{6,2},{1,5},{7,3},{8,12},{14,10},{9,13},{15,11},{16,20},{22,... | collective-permute-start | bytes 6291464 | tf_op jit(solution)/shard_map/ppermute | solution.py:374
  9.7 1.6 %collective-permute-start.1 = (bf16[56,128,128]{2,1,0:T(8,128)(2,1)}, bf16[56,128,128]{2,1,0:T(8,128)(2,1)}, u32[]{:S(2)}, u32[]{:S(2)}) collective-permute-start(bf16[56,128,128]{2,1,0:T(8,128)(2,1)} %bitcast.42), channel_id=1, source_target_pairs={{0,1},{1,0},{2,3},{3,2},{4,5},{5,4},{6,7},{7,6},{8,9},{9,8},{10,11... | collective-permute-start | bytes 5505032 | tf_op jit(solution)/shard_map/ppermute | solution.py:316
  11.2 0.7 copy.13
  12.5 1.3 collective-permute-start.8
  13.9 32.1 %collective-permute-done.4.refs_3_ = bf16[56,128,128]{2,1,0:T(8,128)(2,1)} collective-permute-done((bf16[56,128,128]{2,1,0:T(8,128)(2,1)}, bf16[56,128,128]{2,1,0:T(8,128)(2,1)}, u32[]{:S(2)}, u32[]{:S(2)}) %collective-permute-start.4) | collective-permute-done | bytes 1835040 | tf_op jit(solution)/shard_map/ppermute | solution.py:380
  46.0 4.8 %collective-permute-done.2.refs_7_ = bf16[64,128,128]{2,1,0:T(8,128)(2,1)} collective-permute-done((bf16[64,128,128]{2,1,0:T(8,128)(2,1)}, bf16[64,128,128]{2,1,0:T(8,128)(2,1)}, u32[]{:S(2)}, u32[]{:S(2)}) %collective-permute-start.2) | collective-permute-done | bytes 2097184 | tf_op jit(solution)/shard_map/ppermute | solution.py:374
  50.8 2.3 %collective-permute-start.5 = (bf16[56,128,128]{2,1,0:T(8,128)(2,1)}, bf16[56,128,128]{2,1,0:T(8,128)(2,1)}, u32[]{:S(2)}, u32[]{:S(2)}) collective-permute-start(bf16[56,128,128]{2,1,0:T(8,128)(2,1)} %collective-permute-done.4.refs_3_), channel_id=1, source_target_pairs={{0,1},{1,0},{2,3},{3,2},{4,5},{5,4},{6,7},{7,6},{8,9},{9,8},{10,11... | collective-permute-start | bytes 5505032 | tf_op jit(solution)/shard_map/ppermute | solution.py:316
  53.3 3.0 %collective-permute-done.6 = s32[7,3,64]{2,0,1:T(8,128)S(1)} collective-permute-done((s32[7,3,64]{2,0,1:T(8,128)S(1)}, s32[7,3,64]{2,0,1:T(8,128)S(1)}, u32[]{:S(2)}, u32[]{:S(2)}) %collective-permute-start.6) | collective-permute-done | bytes 5408 | tf_op jit(solution)/shard_map/ppermute | solution.py:316
  56.7 37.9 %collective-permute-done.refs_9_ = bf16[64,128,128]{2,1,0:T(8,128)(2,1)S(1)} collective-permute-done((bf16[64,128,128]{2,1,0:T(8,128)(2,1)}, bf16[64,128,128]{2,1,0:T(8,128)(2,1)S(1)}, u32[]{:S(2)}, u32[]{:S(2)}) %collective-permute-start) | collective-permute-done | bytes 2097184 | tf_op jit(solution)/shard_map/ppermute | solution.py:374
  94.6 1.3 collective-permute-start.7
  95.9 0.7 collective-permute-done.8.refs_10_
  96.6 13.1 %shard_map.37 = (f32[28,128,128]{2,1,0:T(8,128)S(1)}, f32[28,128,128]{2,1,0:T(8,128)S(1)}, f32[28,128,128]{2,1,0:T(8,128)S(1)}, f32[28,128,128]{2,1,0:T(8,128)},...) custom-call(s32[448]{0:T(512)S(1)} %fusion.17.refs_0_, s32[7]{0:T(128)S(1)} %stack.33.refs_1_.scalars, ...), custom_call_target="tpu_custom_call" | custom-call | flops 1 | bytes 1 | tf_op jit(solution)/shard_map/pallas_call | solution.py:197
  109.8 2.4 %collective-permute-start.10 = (f32[28,128,128]{2,1,0:T(8,128)S(1)}, f32[28,128,128]{2,1,0:T(8,128)S(1)}, u32[]{:S(2)}, u32[]{:S(2)}) collective-permute-start(f32[28,128,128]{2,1,0:T(8,128)S(1)} %get-tuple-element.37), channel_id=1, source_target_pairs={{0,1},{1,0},{2,3},{3,2},{4,5},{5,4},{6,7},{7,6},{8,9},{9,8},{10,11... | collective-permute-start | bytes 5505032 | tf_op jit(solution)/shard_map/ppermute | solution.py:316
  112.8 2.8 %collective-permute-done.10.refs_1_ = f32[28,128,128]{2,1,0:T(8,128)S(1)} collective-permute-done((f32[28,128,128]{2,1,0:T(8,128)S(1)}, f32[28,128,128]{2,1,0:T(8,128)S(1)}, u32[]{:S(2)}, u32[]{:S(2)}) %collective-permute-start.10) | collective-permute-done | bytes 1835040 | tf_op jit(solution)/shard_map/ppermute | solution.py:316
  115.6 5.2 %collective-permute-done.11.refs_2_ = f32[28,128,128]{2,1,0:T(8,128)S(1)} collective-permute-done((f32[28,128,128]{2,1,0:T(8,128)S(1)}, f32[28,128,128]{2,1,0:T(8,128)S(1)}, u32[]{:S(2)}, u32[]{:S(2)}) %collective-permute-start.11) | collective-permute-done | bytes 1835040 | tf_op jit(solution)/shard_map/ppermute | solution.py:316
  121.1 2.4 %collective-permute-done.9.refs_0_ = f32[28,128,128]{2,1,0:T(8,128)S(1)} collective-permute-done((f32[28,128,128]{2,1,0:T(8,128)S(1)}, f32[28,128,128]{2,1,0:T(8,128)S(1)}, u32[]{:S(2)}, u32[]{:S(2)}) %collective-permute-start.9) | collective-permute-done | bytes 1835040 | tf_op jit(solution)/shard_map/ppermute | solution.py:316
  123.5 0.9 shard_map.38.given
  124.4 17.3 %collective-permute-done.7.left = bf16[64,128,128]{2,1,0:T(8,128)(2,1)S(1)} collective-permute-done((bf16[64,128,128]{2,1,0:T(8,128)(2,1)S(1)}, bf16[64,128,128]{2,1,0:T(8,128)(2,1)S(1)}, u32[]{:S(2)}, u32[]{:S(2)}) %collective-permute-start.7) | collective-permute-done | bytes 2097184 | tf_op jit(solution)/shard_map/ppermute | solution.py:374
  141.8 2.8 %collective-permute-start.13 = (bf16[64,128,128]{2,1,0:T(8,128)(2,1)S(1)}, bf16[64,128,128]{2,1,0:T(8,128)(2,1)S(1)}, u32[]{:S(2)}, u32[]{:S(2)}) collective-permute-start(bf16[64,128,128]{2,1,0:T(8,128)(2,1)S(1)} %collective-permute-done.7.left), channel_id=1, source_target_pairs={{0,1},{1,0},{2,3},{3,2},{4,5},{5,4},{6,7},{7,6},{8,9},{9,8},{10,11... | collective-permute-start | bytes 6291464 | tf_op jit(solution)/shard_map/ppermute | solution.py:316
  144.6 4.5 %shard_map.39 = (f32[113,128,128]{2,1,0:T(8,128)S(1)}, s32[580]{0:T(1024)S(1)}) custom-call(s32[896]{0:T(1024)S(1)} %fusion.10.packed, s32[7]{0:T(128)S(1)} %stack.33.refs_1_.scalars, bf16[224,128,128]{2,1,0:T(8,128)(2,1)S(1)} %get-tuple-element.41.right, f32[113,128,128]{2,1,0:T(8,128)S(1)} %shard_map.38.given, ...), custom_call_target="tpu_custom_call", output_to_operand_aliasing={{0}: (3, {})} | custom-call | flops 1 | bytes 1 | tf_op jit(solution)/shard_map/pallas_call | solution.py:257
  149.1 3.8 %shard_map.40 = (bf16[112,128,128]{2,1,0:T(8,128)(2,1)}, f32[113,128,128]{2,1,0:T(8,128)S(1)}) custom-call(s32[580]{0:T(1024)S(1)} %get-tuple-element.44.sorted_lists, bf16[224,128,128]{2,1,0:T(8,128)(2,1)S(1)} %get-tuple-element.41.right, f32[113,128,128]{2,1,0:T(8,128)S(1)} %get-tuple-element.45.given, ...), custom_call_target="tpu_custom_call", output_to_operand_aliasing={{1}: (2, {})} | custom-call | flops 1 | bytes 1 | tf_op jit(solution)/shard_map/pallas_call | solution.py:293
  (35 shorter events, 2.1 us)
Async XLA Ops:
  0.0 12.5 %collective-permute-start.3 = (bf16[64,128,128]{2,1,0:T(8,128)(2,1)}, bf16[64,128,128]{2,1,0:T(8,128)(2,1)}, u32[]{:S(2)}, u32[]{:S(2)}) collective-permute-start(bf16[64,128,128]{2,1,0:T(8,128)(2,1)} %bitcast.37), channel_id=1, source_target_pairs={{2,4},{4,2},{3,5},{5,3},{10,12},{12,10},{11,13},{13,11},{18,20},{2... | collective-permute-start | bytes 6291464 | tf_op jit(solution)/shard_map/ppermute | solution.py:374
  2.0 48.8 %collective-permute-start.2 = (bf16[64,128,128]{2,1,0:T(8,128)(2,1)}, bf16[64,128,128]{2,1,0:T(8,128)(2,1)}, u32[]{:S(2)}, u32[]{:S(2)}) collective-permute-start(bf16[64,128,128]{2,1,0:T(8,128)(2,1)} %bitcast.38), channel_id=1, source_target_pairs={{0,2},{2,0},{4,6},{6,4},{1,3},{3,1},{5,7},{7,5},{8,10},{10,8},{12,... | collective-permute-start | bytes 6291464 | tf_op jit(solution)/shard_map/ppermute | solution.py:374
  5.4 40.6 %collective-permute-start.4 = (bf16[56,128,128]{2,1,0:T(8,128)(2,1)}, bf16[56,128,128]{2,1,0:T(8,128)(2,1)}, u32[]{:S(2)}, u32[]{:S(2)}) collective-permute-start(bf16[56,128,128]{2,1,0:T(8,128)(2,1)} %bitcast.41), channel_id=1, source_target_pairs={{0,8},{8,0},{1,9},{9,1},{2,10},{10,2},{3,11},{11,3},{4,12},{12,4},... | collective-permute-start | bytes 5505032 | tf_op jit(solution)/shard_map/ppermute | solution.py:380
  6.6 88.0 %collective-permute-start = (bf16[64,128,128]{2,1,0:T(8,128)(2,1)}, bf16[64,128,128]{2,1,0:T(8,128)(2,1)S(1)}, u32[]{:S(2)}, u32[]{:S(2)}) collective-permute-start(bf16[64,128,128]{2,1,0:T(8,128)(2,1)} %bitcast.39), channel_id=1, source_target_pairs={{0,4},{6,2},{1,5},{7,3},{8,12},{14,10},{9,13},{15,11},{16,20},{22,... | collective-permute-start | bytes 6291464 | tf_op jit(solution)/shard_map/ppermute | solution.py:374
  9.7 47.1 %collective-permute-start.1 = (bf16[56,128,128]{2,1,0:T(8,128)(2,1)}, bf16[56,128,128]{2,1,0:T(8,128)(2,1)}, u32[]{:S(2)}, u32[]{:S(2)}) collective-permute-start(bf16[56,128,128]{2,1,0:T(8,128)(2,1)} %bitcast.42), channel_id=1, source_target_pairs={{0,1},{1,0},{2,3},{3,2},{4,5},{5,4},{6,7},{7,6},{8,9},{9,8},{10,11... | collective-permute-start | bytes 5505032 | tf_op jit(solution)/shard_map/ppermute | solution.py:316
  12.5 84.1 %collective-permute-start.8 = (bf16[64,128,128]{2,1,0:T(8,128)(2,1)}, bf16[64,128,128]{2,1,0:T(8,128)(2,1)}, u32[]{:S(2)}, u32[]{:S(2)}) collective-permute-start(bf16[64,128,128]{2,1,0:T(8,128)(2,1)} %collective-permute-done.3.refs_8_), channel_id=1, source_target_pairs={{4,6},{2,0},{5,7},{3,1},{12,14},{10,8},{13,15},{11,9},{20,22},{18,... | collective-permute-start | bytes 6291464 | tf_op jit(solution)/shard_map/ppermute | solution.py:374
  50.8 43.9 %collective-permute-start.5 = (bf16[56,128,128]{2,1,0:T(8,128)(2,1)}, bf16[56,128,128]{2,1,0:T(8,128)(2,1)}, u32[]{:S(2)}, u32[]{:S(2)}) collective-permute-start(bf16[56,128,128]{2,1,0:T(8,128)(2,1)} %collective-permute-done.4.refs_3_), channel_id=1, source_target_pairs={{0,1},{1,0},{2,3},{3,2},{4,5},{5,4},{6,7},{7,6},{8,9},{9,8},{10,11... | collective-permute-start | bytes 5505032 | tf_op jit(solution)/shard_map/ppermute | solution.py:316
  53.0 3.3 %collective-permute-start.6 = (s32[7,3,64]{2,0,1:T(8,128)S(1)}, s32[7,3,64]{2,0,1:T(8,128)S(1)}, u32[]{:S(2)}, u32[]{:S(2)}) collective-permute-start(s32[7,3,64]{2,0,1:T(8,128)S(1)} %bitcast.46), channel_id=1, source_target_pairs={{0,1},{1,0},{2,3},{3,2},{4,5},{5,4},{6,7},{7,6},{8,9},{9,8},{10,11... | collective-permute-start | bytes 16136 | tf_op jit(solution)/shard_map/ppermute | solution.py:316
  94.6 2.0 %copy-start = (bf16[64,128,128]{2,1,0:T(8,128)(2,1)}, bf16[64,128,128]{2,1,0:T(8,128)(2,1)S(1)}, u32[]{:S(2)}) copy-start(bf16[64,128,128]{2,1,0:T(8,128)(2,1)S(1)} %collective-permute-done.refs_9_) | copy-start | bytes 6291460
  94.6 47.1 %collective-permute-start.7 = (bf16[64,128,128]{2,1,0:T(8,128)(2,1)S(1)}, bf16[64,128,128]{2,1,0:T(8,128)(2,1)S(1)}, u32[]{:S(2)}, u32[]{:S(2)}) collective-permute-start(bf16[64,128,128]{2,1,0:T(8,128)(2,1)S(1)} %collective-permute-done.refs_9_), channel_id=1, source_target_pairs={{4,6},{2,0},{5,7},{3,1},{12,14},{10,8},{13,15},{11,9},{20,22},{18,... | collective-permute-start | bytes 6291464 | tf_op jit(solution)/shard_map/ppermute | solution.py:374
  109.8 5.9 %collective-permute-start.10 = (f32[28,128,128]{2,1,0:T(8,128)S(1)}, f32[28,128,128]{2,1,0:T(8,128)S(1)}, u32[]{:S(2)}, u32[]{:S(2)}) collective-permute-start(f32[28,128,128]{2,1,0:T(8,128)S(1)} %get-tuple-element.37), channel_id=1, source_target_pairs={{0,1},{1,0},{2,3},{3,2},{4,5},{5,4},{6,7},{7,6},{8,9},{9,8},{10,11... | collective-permute-start | bytes 5505032 | tf_op jit(solution)/shard_map/ppermute | solution.py:316
  112.2 8.7 %collective-permute-start.11 = (f32[28,128,128]{2,1,0:T(8,128)S(1)}, f32[28,128,128]{2,1,0:T(8,128)S(1)}, u32[]{:S(2)}, u32[]{:S(2)}) collective-permute-start(f32[28,128,128]{2,1,0:T(8,128)S(1)} %get-tuple-element.38), channel_id=1, source_target_pairs={{0,1},{1,0},{2,3},{3,2},{4,5},{5,4},{6,7},{7,6},{8,9},{9,8},{10,11... | collective-permute-start | bytes 5505032 | tf_op jit(solution)/shard_map/ppermute | solution.py:316
  112.3 8.8 %collective-permute-start.12 = (f32[28,128,128]{2,1,0:T(8,128)}, f32[28,128,128]{2,1,0:T(8,128)S(1)}, u32[]{:S(2)}, u32[]{:S(2)}) collective-permute-start(f32[28,128,128]{2,1,0:T(8,128)} %get-tuple-element.39), channel_id=1, source_target_pairs={{0,1},{1,0},{2,3},{3,2},{4,5},{5,4},{6,7},{7,6},{8,9},{9,8},{10,11... | collective-permute-start | bytes 5505032 | tf_op jit(solution)/shard_map/ppermute | solution.py:316
  112.7 10.8 %collective-permute-start.9 = (f32[28,128,128]{2,1,0:T(8,128)S(1)}, f32[28,128,128]{2,1,0:T(8,128)S(1)}, u32[]{:S(2)}, u32[]{:S(2)}) collective-permute-start(f32[28,128,128]{2,1,0:T(8,128)S(1)} %get-tuple-element.36), channel_id=1, source_target_pairs={{0,1},{1,0},{2,3},{3,2},{4,5},{5,4},{6,7},{7,6},{8,9},{9,8},{10,11... | collective-permute-start | bytes 5505032 | tf_op jit(solution)/shard_map/ppermute | solution.py:316
  141.8 7.3 %collective-permute-start.13 = (bf16[64,128,128]{2,1,0:T(8,128)(2,1)S(1)}, bf16[64,128,128]{2,1,0:T(8,128)(2,1)S(1)}, u32[]{:S(2)}, u32[]{:S(2)}) collective-permute-start(bf16[64,128,128]{2,1,0:T(8,128)(2,1)S(1)} %collective-permute-done.7.left), channel_id=1, source_target_pairs={{0,1},{1,0},{2,3},{3,2},{4,5},{5,4},{6,7},{7,6},{8,9},{9,8},{10,11... | collective-permute-start | bytes 6291464 | tf_op jit(solution)/shard_map/ppermute | solution.py:316

commit v24 on v21

--- a/solution.py
+++ b/solution.py
@@ -10,8 +10,8 @@
 NBQ = 32
 UNROLL = 16
 PARTS = 4
-LAST_PARTS = 2
-PART_UNROLL = 16
+LAST_PARTS = 3
+PART_UNROLL = 24
 PIECES = 2
 
 

time: 153 us -> 153 us (level)
  no operation moved by 1% of the time
where the time goes in v24:
time: 153 us; the launch traced here: 152 us
  waiting for transfers between devices  106 us (69%)
  starting transfers between devices  21.9 us (14%)
  Pallas kernels  21.6 us (14%)
  local copies, waits for them, and re-layouts  1.93 us (1%)
    ppermute x5, waiting for transfers between devices, hop(): return lax.ppermute(value, 'col', pairs)  60.7 us
    ppermute x1, waiting for transfers between devices, line(): met = lax.ppermute(right_own, 'row', [(0, 1), (1, 0)])  32.1 us
    ppermute x8, waiting for transfers between devices, swapped(): return lax.ppermute(value, 'dep', [(0, 1), (1, 0)])  13.7 us
    pallas_call x1, Pallas kernels, product_sums(): pl.pallas_call(functools.partial(sum_kernel, panel_spans, right_spans, gi...  13.1 us
    ppermute x5, starting transfers between devices, hop(): return lax.ppermute(value, 'col', pairs)  11 us
    ppermute x8, starting transfers between devices, swapped(): return lax.ppermute(value, 'dep', [(0, 1), (1, 0)])  9.67 us
    pallas_call x1, Pallas kernels, add_own(): pl.pallas_call(functools.partial(own_kernel, shape, kind_at), out_shape=[...  4.03 us
    pallas_call x1, Pallas kernels, add_other(): pl.pallas_call(functools.partial(other_kernel, shape), out_shape=[jax.Sha...  3.53 us
  transfers between devices with their start and end apart: 14, of which 10 were waited for; matrix products, arithmetic and copies ran while one was open for 1% of the time, Pallas kernels for 12%

profile of v24, /device:TPU:1, one launch (start us, length us, event | category | flops | bytes accessed | tf_op | source)
XLA Modules:
  0.0 152.1 jit_solution(2830590335590270480)
XLA Ops:
  0.0 2.0 %collective-permute-start.3 = (bf16[64,128,128]{2,1,0:T(8,128)(2,1)}, bf16[64,128,128]{2,1,0:T(8,128)(2,1)}, u32[]{:S(2)}, u32[]{:S(2)}) collective-permute-start(bf16[64,128,128]{2,1,0:T(8,128)(2,1)} %bitcast.37), channel_id=1, source_target_pairs={{2,4},{4,2},{3,5},{5,3},{10,12},{12,10},{11,13},{13,11},{18,20},{2... | collective-permute-start | bytes 6291464 | tf_op jit(solution)/shard_map/ppermute | solution.py:374
  2.0 3.4 %collective-permute-start.2 = (bf16[64,128,128]{2,1,0:T(8,128)(2,1)}, bf16[64,128,128]{2,1,0:T(8,128)(2,1)}, u32[]{:S(2)}, u32[]{:S(2)}) collective-permute-start(bf16[64,128,128]{2,1,0:T(8,128)(2,1)} %bitcast.38), channel_id=1, source_target_pairs={{0,2},{2,0},{4,6},{6,4},{1,3},{3,1},{5,7},{7,5},{8,10},{10,8},{12,... | collective-permute-start | bytes 6291464 | tf_op jit(solution)/shard_map/ppermute | solution.py:374
  5.4 1.2 collective-permute-start.4
  6.6 3.0 %collective-permute-start = (bf16[64,128,128]{2,1,0:T(8,128)(2,1)}, bf16[64,128,128]{2,1,0:T(8,128)(2,1)S(1)}, u32[]{:S(2)}, u32[]{:S(2)}) collective-permute-start(bf16[64,128,128]{2,1,0:T(8,128)(2,1)} %bitcast.39), channel_id=1, source_target_pairs={{0,4},{6,2},{1,5},{7,3},{8,12},{14,10},{9,13},{15,11},{16,20},{22,... | collective-permute-start | bytes 6291464 | tf_op jit(solution)/shard_map/ppermute | solution.py:374
  9.7 1.6 %collective-permute-start.1 = (bf16[56,128,128]{2,1,0:T(8,128)(2,1)}, bf16[56,128,128]{2,1,0:T(8,128)(2,1)}, u32[]{:S(2)}, u32[]{:S(2)}) collective-permute-start(bf16[56,128,128]{2,1,0:T(8,128)(2,1)} %bitcast.42), channel_id=1, source_target_pairs={{0,1},{1,0},{2,3},{3,2},{4,5},{5,4},{6,7},{7,6},{8,9},{9,8},{10,11... | collective-permute-start | bytes 5505032 | tf_op jit(solution)/shard_map/ppermute | solution.py:316
  11.2 0.7 copy.13
  12.5 1.3 collective-permute-start.8
  13.9 32.1 %collective-permute-done.4.refs_3_ = bf16[56,128,128]{2,1,0:T(8,128)(2,1)} collective-permute-done((bf16[56,128,128]{2,1,0:T(8,128)(2,1)}, bf16[56,128,128]{2,1,0:T(8,128)(2,1)}, u32[]{:S(2)}, u32[]{:S(2)}) %collective-permute-start.4) | collective-permute-done | bytes 1835040 | tf_op jit(solution)/shard_map/ppermute | solution.py:380
  46.0 4.8 %collective-permute-done.2.refs_7_ = bf16[64,128,128]{2,1,0:T(8,128)(2,1)} collective-permute-done((bf16[64,128,128]{2,1,0:T(8,128)(2,1)}, bf16[64,128,128]{2,1,0:T(8,128)(2,1)}, u32[]{:S(2)}, u32[]{:S(2)}) %collective-permute-start.2) | collective-permute-done | bytes 2097184 | tf_op jit(solution)/shard_map/ppermute | solution.py:374
  50.8 2.3 %collective-permute-start.5 = (bf16[56,128,128]{2,1,0:T(8,128)(2,1)}, bf16[56,128,128]{2,1,0:T(8,128)(2,1)}, u32[]{:S(2)}, u32[]{:S(2)}) collective-permute-start(bf16[56,128,128]{2,1,0:T(8,128)(2,1)} %collective-permute-done.4.refs_3_), channel_id=1, source_target_pairs={{0,1},{1,0},{2,3},{3,2},{4,5},{5,4},{6,7},{7,6},{8,9},{9,8},{10,11... | collective-permute-start | bytes 5505032 | tf_op jit(solution)/shard_map/ppermute | solution.py:316
  53.3 3.0 %collective-permute-done.6 = s32[7,3,64]{2,0,1:T(8,128)S(1)} collective-permute-done((s32[7,3,64]{2,0,1:T(8,128)S(1)}, s32[7,3,64]{2,0,1:T(8,128)S(1)}, u32[]{:S(2)}, u32[]{:S(2)}) %collective-permute-start.6) | collective-permute-done | bytes 5408 | tf_op jit(solution)/shard_map/ppermute | solution.py:316
  56.7 37.9 %collective-permute-done.refs_9_ = bf16[64,128,128]{2,1,0:T(8,128)(2,1)S(1)} collective-permute-done((bf16[64,128,128]{2,1,0:T(8,128)(2,1)}, bf16[64,128,128]{2,1,0:T(8,128)(2,1)S(1)}, u32[]{:S(2)}, u32[]{:S(2)}) %collective-permute-start) | collective-permute-done | bytes 2097184 | tf_op jit(solution)/shard_map/ppermute | solution.py:374
  94.6 1.3 collective-permute-start.7
  95.9 0.7 collective-permute-done.8.refs_10_
  96.6 13.1 %shard_map.37 = (f32[28,128,128]{2,1,0:T(8,128)S(1)}, f32[28,128,128]{2,1,0:T(8,128)S(1)}, f32[28,128,128]{2,1,0:T(8,128)S(1)}, f32[28,128,128]{2,1,0:T(8,128)},...) custom-call(s32[448]{0:T(512)S(1)} %fusion.17.refs_0_, s32[7]{0:T(128)S(1)} %stack.33.refs_1_.scalars, ...), custom_call_target="tpu_custom_call" | custom-call | flops 1 | bytes 1 | tf_op jit(solution)/shard_map/pallas_call | solution.py:197
  109.8 2.4 %collective-permute-start.10 = (f32[28,128,128]{2,1,0:T(8,128)S(1)}, f32[28,128,128]{2,1,0:T(8,128)S(1)}, u32[]{:S(2)}, u32[]{:S(2)}) collective-permute-start(f32[28,128,128]{2,1,0:T(8,128)S(1)} %get-tuple-element.37), channel_id=1, source_target_pairs={{0,1},{1,0},{2,3},{3,2},{4,5},{5,4},{6,7},{7,6},{8,9},{9,8},{10,11... | collective-permute-start | bytes 5505032 | tf_op jit(solution)/shard_map/ppermute | solution.py:316
  112.8 2.8 %collective-permute-done.10.refs_1_ = f32[28,128,128]{2,1,0:T(8,128)S(1)} collective-permute-done((f32[28,128,128]{2,1,0:T(8,128)S(1)}, f32[28,128,128]{2,1,0:T(8,128)S(1)}, u32[]{:S(2)}, u32[]{:S(2)}) %collective-permute-start.10) | collective-permute-done | bytes 1835040 | tf_op jit(solution)/shard_map/ppermute | solution.py:316
  115.6 5.2 %collective-permute-done.11.refs_2_ = f32[28,128,128]{2,1,0:T(8,128)S(1)} collective-permute-done((f32[28,128,128]{2,1,0:T(8,128)S(1)}, f32[28,128,128]{2,1,0:T(8,128)S(1)}, u32[]{:S(2)}, u32[]{:S(2)}) %collective-permute-start.11) | collective-permute-done | bytes 1835040 | tf_op jit(solution)/shard_map/ppermute | solution.py:316
  121.1 2.4 %collective-permute-done.9.refs_0_ = f32[28,128,128]{2,1,0:T(8,128)S(1)} collective-permute-done((f32[28,128,128]{2,1,0:T(8,128)S(1)}, f32[28,128,128]{2,1,0:T(8,128)S(1)}, u32[]{:S(2)}, u32[]{:S(2)}) %collective-permute-start.9) | collective-permute-done | bytes 1835040 | tf_op jit(solution)/shard_map/ppermute | solution.py:316
  123.5 0.9 shard_map.38.given
  124.4 17.3 %collective-permute-done.7.left = bf16[64,128,128]{2,1,0:T(8,128)(2,1)S(1)} collective-permute-done((bf16[64,128,128]{2,1,0:T(8,128)(2,1)S(1)}, bf16[64,128,128]{2,1,0:T(8,128)(2,1)S(1)}, u32[]{:S(2)}, u32[]{:S(2)}) %collective-permute-start.7) | collective-permute-done | bytes 2097184 | tf_op jit(solution)/shard_map/ppermute | solution.py:374
  141.8 2.8 %collective-permute-start.13 = (bf16[64,128,128]{2,1,0:T(8,128)(2,1)S(1)}, bf16[64,128,128]{2,1,0:T(8,128)(2,1)S(1)}, u32[]{:S(2)}, u32[]{:S(2)}) collective-permute-start(bf16[64,128,128]{2,1,0:T(8,128)(2,1)S(1)} %collective-permute-done.7.left), channel_id=1, source_target_pairs={{0,1},{1,0},{2,3},{3,2},{4,5},{5,4},{6,7},{7,6},{8,9},{9,8},{10,11... | collective-permute-start | bytes 6291464 | tf_op jit(solution)/shard_map/ppermute | solution.py:316
  144.6 4.0 %shard_map.39 = (f32[113,128,128]{2,1,0:T(8,128)S(1)}, s32[459]{0:T(512)S(1)}) custom-call(s32[896]{0:T(1024)S(1)} %fusion.10.packed, s32[7]{0:T(128)S(1)} %stack.33.refs_1_.scalars, bf16[224,128,128]{2,1,0:T(8,128)(2,1)S(1)} %get-tuple-element.41.right, f32[113,128,128]{2,1,0:T(8,128)S(1)} %shard_map.38.given, ...), custom_call_target="tpu_custom_call", output_to_operand_aliasing={{0}: (3, {})} | custom-call | flops 1 | bytes 1 | tf_op jit(solution)/shard_map/pallas_call | solution.py:257
  148.6 3.5 %shard_map.40 = (bf16[112,128,128]{2,1,0:T(8,128)(2,1)}, f32[113,128,128]{2,1,0:T(8,128)S(1)}) custom-call(s32[459]{0:T(512)S(1)} %get-tuple-element.44.sorted_lists, bf16[224,128,128]{2,1,0:T(8,128)(2,1)S(1)} %get-tuple-element.41.right, f32[113,128,128]{2,1,0:T(8,128)S(1)} %get-tuple-element.45.given, ...), custom_call_target="tpu_custom_call", output_to_operand_aliasing={{1}: (2, {})} | custom-call | flops 1 | bytes 1 | tf_op jit(solution)/shard_map/pallas_call | solution.py:293
  (35 shorter events, 2.1 us)
Async XLA Ops:
  0.0 12.5 %collective-permute-start.3 = (bf16[64,128,128]{2,1,0:T(8,128)(2,1)}, bf16[64,128,128]{2,1,0:T(8,128)(2,1)}, u32[]{:S(2)}, u32[]{:S(2)}) collective-permute-start(bf16[64,128,128]{2,1,0:T(8,128)(2,1)} %bitcast.37), channel_id=1, source_target_pairs={{2,4},{4,2},{3,5},{5,3},{10,12},{12,10},{11,13},{13,11},{18,20},{2... | collective-permute-start | bytes 6291464 | tf_op jit(solution)/shard_map/ppermute | solution.py:374
  2.0 48.8 %collective-permute-start.2 = (bf16[64,128,128]{2,1,0:T(8,128)(2,1)}, bf16[64,128,128]{2,1,0:T(8,128)(2,1)}, u32[]{:S(2)}, u32[]{:S(2)}) collective-permute-start(bf16[64,128,128]{2,1,0:T(8,128)(2,1)} %bitcast.38), channel_id=1, source_target_pairs={{0,2},{2,0},{4,6},{6,4},{1,3},{3,1},{5,7},{7,5},{8,10},{10,8},{12,... | collective-permute-start | bytes 6291464 | tf_op jit(solution)/shard_map/ppermute | solution.py:374
  5.4 40.6 %collective-permute-start.4 = (bf16[56,128,128]{2,1,0:T(8,128)(2,1)}, bf16[56,128,128]{2,1,0:T(8,128)(2,1)}, u32[]{:S(2)}, u32[]{:S(2)}) collective-permute-start(bf16[56,128,128]{2,1,0:T(8,128)(2,1)} %bitcast.41), channel_id=1, source_target_pairs={{0,8},{8,0},{1,9},{9,1},{2,10},{10,2},{3,11},{11,3},{4,12},{12,4},... | collective-permute-start | bytes 5505032 | tf_op jit(solution)/shard_map/ppermute | solution.py:380
  6.6 88.0 %collective-permute-start = (bf16[64,128,128]{2,1,0:T(8,128)(2,1)}, bf16[64,128,128]{2,1,0:T(8,128)(2,1)S(1)}, u32[]{:S(2)}, u32[]{:S(2)}) collective-permute-start(bf16[64,128,128]{2,1,0:T(8,128)(2,1)} %bitcast.39), channel_id=1, source_target_pairs={{0,4},{6,2},{1,5},{7,3},{8,12},{14,10},{9,13},{15,11},{16,20},{22,... | collective-permute-start | bytes 6291464 | tf_op jit(solution)/shard_map/ppermute | solution.py:374
  9.7 47.1 %collective-permute-start.1 = (bf16[56,128,128]{2,1,0:T(8,128)(2,1)}, bf16[56,128,128]{2,1,0:T(8,128)(2,1)}, u32[]{:S(2)}, u32[]{:S(2)}) collective-permute-start(bf16[56,128,128]{2,1,0:T(8,128)(2,1)} %bitcast.42), channel_id=1, source_target_pairs={{0,1},{1,0},{2,3},{3,2},{4,5},{5,4},{6,7},{7,6},{8,9},{9,8},{10,11... | collective-permute-start | bytes 5505032 | tf_op jit(solution)/shard_map/ppermute | solution.py:316
  12.5 84.1 %collective-permute-start.8 = (bf16[64,128,128]{2,1,0:T(8,128)(2,1)}, bf16[64,128,128]{2,1,0:T(8,128)(2,1)}, u32[]{:S(2)}, u32[]{:S(2)}) collective-permute-start(bf16[64,128,128]{2,1,0:T(8,128)(2,1)} %collective-permute-done.3.refs_8_), channel_id=1, source_target_pairs={{4,6},{2,0},{5,7},{3,1},{12,14},{10,8},{13,15},{11,9},{20,22},{18,... | collective-permute-start | bytes 6291464 | tf_op jit(solution)/shard_map/ppermute | solution.py:374
  50.8 43.9 %collective-permute-start.5 = (bf16[56,128,128]{2,1,0:T(8,128)(2,1)}, bf16[56,128,128]{2,1,0:T(8,128)(2,1)}, u32[]{:S(2)}, u32[]{:S(2)}) collective-permute-start(bf16[56,128,128]{2,1,0:T(8,128)(2,1)} %collective-permute-done.4.refs_3_), channel_id=1, source_target_pairs={{0,1},{1,0},{2,3},{3,2},{4,5},{5,4},{6,7},{7,6},{8,9},{9,8},{10,11... | collective-permute-start | bytes 5505032 | tf_op jit(solution)/shard_map/ppermute | solution.py:316
  53.0 3.3 %collective-permute-start.6 = (s32[7,3,64]{2,0,1:T(8,128)S(1)}, s32[7,3,64]{2,0,1:T(8,128)S(1)}, u32[]{:S(2)}, u32[]{:S(2)}) collective-permute-start(s32[7,3,64]{2,0,1:T(8,128)S(1)} %bitcast.46), channel_id=1, source_target_pairs={{0,1},{1,0},{2,3},{3,2},{4,5},{5,4},{6,7},{7,6},{8,9},{9,8},{10,11... | collective-permute-start | bytes 16136 | tf_op jit(solution)/shard_map/ppermute | solution.py:316
  94.6 2.0 %copy-start = (bf16[64,128,128]{2,1,0:T(8,128)(2,1)}, bf16[64,128,128]{2,1,0:T(8,128)(2,1)S(1)}, u32[]{:S(2)}) copy-start(bf16[64,128,128]{2,1,0:T(8,128)(2,1)S(1)} %collective-permute-done.refs_9_) | copy-start | bytes 6291460
  94.6 47.1 %collective-permute-start.7 = (bf16[64,128,128]{2,1,0:T(8,128)(2,1)S(1)}, bf16[64,128,128]{2,1,0:T(8,128)(2,1)S(1)}, u32[]{:S(2)}, u32[]{:S(2)}) collective-permute-start(bf16[64,128,128]{2,1,0:T(8,128)(2,1)S(1)} %collective-permute-done.refs_9_), channel_id=1, source_target_pairs={{4,6},{2,0},{5,7},{3,1},{12,14},{10,8},{13,15},{11,9},{20,22},{18,... | collective-permute-start | bytes 6291464 | tf_op jit(solution)/shard_map/ppermute | solution.py:374
  109.8 5.9 %collective-permute-start.10 = (f32[28,128,128]{2,1,0:T(8,128)S(1)}, f32[28,128,128]{2,1,0:T(8,128)S(1)}, u32[]{:S(2)}, u32[]{:S(2)}) collective-permute-start(f32[28,128,128]{2,1,0:T(8,128)S(1)} %get-tuple-element.37), channel_id=1, source_target_pairs={{0,1},{1,0},{2,3},{3,2},{4,5},{5,4},{6,7},{7,6},{8,9},{9,8},{10,11... | collective-permute-start | bytes 5505032 | tf_op jit(solution)/shard_map/ppermute | solution.py:316
  112.2 8.7 %collective-permute-start.11 = (f32[28,128,128]{2,1,0:T(8,128)S(1)}, f32[28,128,128]{2,1,0:T(8,128)S(1)}, u32[]{:S(2)}, u32[]{:S(2)}) collective-permute-start(f32[28,128,128]{2,1,0:T(8,128)S(1)} %get-tuple-element.38), channel_id=1, source_target_pairs={{0,1},{1,0},{2,3},{3,2},{4,5},{5,4},{6,7},{7,6},{8,9},{9,8},{10,11... | collective-permute-start | bytes 5505032 | tf_op jit(solution)/shard_map/ppermute | solution.py:316
  112.3 8.8 %collective-permute-start.12 = (f32[28,128,128]{2,1,0:T(8,128)}, f32[28,128,128]{2,1,0:T(8,128)S(1)}, u32[]{:S(2)}, u32[]{:S(2)}) collective-permute-start(f32[28,128,128]{2,1,0:T(8,128)} %get-tuple-element.39), channel_id=1, source_target_pairs={{0,1},{1,0},{2,3},{3,2},{4,5},{5,4},{6,7},{7,6},{8,9},{9,8},{10,11... | collective-permute-start | bytes 5505032 | tf_op jit(solution)/shard_map/ppermute | solution.py:316
  112.7 10.8 %collective-permute-start.9 = (f32[28,128,128]{2,1,0:T(8,128)S(1)}, f32[28,128,128]{2,1,0:T(8,128)S(1)}, u32[]{:S(2)}, u32[]{:S(2)}) collective-permute-start(f32[28,128,128]{2,1,0:T(8,128)S(1)} %get-tuple-element.36), channel_id=1, source_target_pairs={{0,1},{1,0},{2,3},{3,2},{4,5},{5,4},{6,7},{7,6},{8,9},{9,8},{10,11... | collective-permute-start | bytes 5505032 | tf_op jit(solution)/shard_map/ppermute | solution.py:316
  141.8 6.8 %collective-permute-start.13 = (bf16[64,128,128]{2,1,0:T(8,128)(2,1)S(1)}, bf16[64,128,128]{2,1,0:T(8,128)(2,1)S(1)}, u32[]{:S(2)}, u32[]{:S(2)}) collective-permute-start(bf16[64,128,128]{2,1,0:T(8,128)(2,1)S(1)} %collective-permute-done.7.left), channel_id=1, source_target_pairs={{0,1},{1,0},{2,3},{3,2},{4,5},{5,4},{6,7},{7,6},{8,9},{9,8},{10,11... | collective-permute-start | bytes 6291464 | tf_op jit(solution)/shard_map/ppermute | solution.py:316
